TPU v7x, 32 devices: a whole 2x2x4 slice. The times are simulated.
32 devices in a mesh: dp: 8 (over z, y), ep: 4 (over x, core).
Axes of the slice: x: 2, y: 2, z: 4, core: 2. Of those that a mesh axis runs over, the one named last changes fastest.
Arguments:
- states: bfloat16 [256, 16, 128, 128], P(('dp', 'ep')), may hold values from -4 to 4
- query_rows: bfloat16 [256, 4, 1024], P(('dp', 'ep')), may hold values from -6 to 6
- key_rows: bfloat16 [256, 4, 1024], P(('dp', 'ep')), may hold values from -6 to 6
- value_rows: bfloat16 [256, 4, 2048], P(('dp', 'ep')), may hold values from -6 to 6
- gate_rows: bfloat16 [256, 4, 2048], P(('dp', 'ep')), may hold values from -6 to 6
- beta_logit: bfloat16 [256, 4, 16], P(('dp', 'ep')), may hold values from -6 to 6
- decay_logit: bfloat16 [256, 4, 16], P(('dp', 'ep')), may hold values from -8 to 8
- residual: bfloat16 [256, 4, 2048], P(('dp', 'ep')), may hold values from -6 to 6
- route_ids: int32 [256, 4, 10], P(('dp', 'ep')), may hold values from 0 to 31, all different within a row; in each aligned block of 32 rows (0 to 31, 32 to 63, ..., all dimensions but the last counted through in order) at most 11 rows name the same one
- route_prob: float32 [256, 4, 10], P(('dp', 'ep')), may hold values from 0.05 to 1
- out_weight: bfloat16 [2048, 2048], P(None, 'ep'), may hold values from -0.125 to 0.125
- core_gain: float32 [128], replicated, may hold values from 0.1 to 1.9
- moe_gain: float32 [2048], replicated, may hold values from 0.1 to 1.9
- gate_up: bfloat16 [32, 2048, 512], P(('dp', 'ep')), may hold values from -0.125 to 0.125
- down_weight: bfloat16 [32, 256, 2048], P(('dp', 'ep')), may hold values from -0.375 to 0.375
- new_home: int32 [256], P(('dp', 'ep')), may hold values from 0 to 255, as said below
Outputs:
- mixed_out: bfloat16 [256, 4, 2048], P(('dp', 'ep'))
- moved_out: bfloat16 [256, 16, 128, 128], P(('dp', 'ep'))
Inputs may be any that keep to these rules, and one draw needn't show every extreme that they name: `route_ids`: each row names 10 different experts; among the 32 rows of one device (its requests, each with its 4 tokens) no expert is named more than 11 times, a bound that some block reaches. `new_home`: A permutation of the request positions; a request stays among the 4 devices of its dp index, and every device hands exactly 2 of its requests to each device of that group, itself included.
All inputs are finite; a program needn't handle non-finite values.
Results may differ from a plain program's by a relative error of at most 0.01.
Values may be sent and summed in bfloat16 or wider, within the bound.
No kernel may reach another device: no remote copies, remote signals or barrier semaphores. Data moves between devices by JAX's collectives and lax.ppermute only.
A program may use at most 128 MiB of HBM per device.

v0:
```python
import jax
import jax.numpy as jnp
from jax import lax
from jax.sharding import PartitionSpec as P

epsilon = 1e-06


def unit_rows(values):
    return values * lax.rsqrt(jnp.sum(values * values, -1, keepdims=True) + epsilon)


def delta_block(
    state_in, query_rows, key_rows, value_rows, gate_rows, beta_logit, decay_logit, core_gain
):
    batch_size = state_in.shape[0]
    head_count = decay_logit.shape[-1]
    head_width = state_in.shape[-1]
    key_heads = query_rows.shape[-1] // head_width
    repeats = head_count // key_heads
    memory_state = state_in.astype(jnp.float32)
    outputs = []
    for position in range(query_rows.shape[1]):
        queries = unit_rows(
            query_rows[:, position].astype(jnp.float32).reshape(batch_size, key_heads, head_width)
        )
        queries = jnp.repeat(queries, repeats, axis=1) * head_width ** (-0.5)
        key_units = unit_rows(
            key_rows[:, position].astype(jnp.float32).reshape(batch_size, key_heads, head_width)
        )
        key_units = jnp.repeat(key_units, repeats, axis=1)
        values = (
            value_rows[:, position].astype(jnp.float32).reshape(batch_size, head_count, head_width)
        )
        decays = jax.nn.sigmoid(decay_logit[:, position].astype(jnp.float32))
        strength = jax.nn.sigmoid(beta_logit[:, position].astype(jnp.float32))
        memory_state = memory_state * decays[:, :, None, None]
        memory = jnp.einsum(
            "bhkv,bhk->bhv", memory_state, key_units, precision=lax.Precision.HIGHEST
        )
        update = (values - memory) * strength[:, :, None]
        memory_state = memory_state + key_units[:, :, :, None] * update[:, :, None, :]
        reading = jnp.einsum(
            "bhkv,bhk->bhv", memory_state, queries, precision=lax.Precision.HIGHEST
        )
        scaled = reading * lax.rsqrt(jnp.mean(reading * reading, -1, keepdims=True) + epsilon)
        gate_vals = (
            gate_rows[:, position].astype(jnp.float32).reshape(batch_size, head_count, head_width)
        )
        gated_out = scaled * core_gain * jax.nn.silu(gate_vals)
        outputs.append(gated_out.reshape(batch_size, head_count * head_width).astype(jnp.bfloat16))
    return (memory_state.astype(jnp.bfloat16), jnp.stack(outputs, axis=1))


def rms_scale(values, gain):
    return values * lax.rsqrt(jnp.mean(values * values, -1, keepdims=True) + epsilon) * gain


def expert_apply(chosen_rows, gate_up, down_weight):
    hidden_units = down_weight.shape[0]
    joined = jnp.dot(chosen_rows, gate_up, preferred_element_type=jnp.float32)
    active = (jax.nn.silu(joined[:, :hidden_units]) * joined[:, hidden_units:]).astype(jnp.bfloat16)
    return jnp.dot(active, down_weight, preferred_element_type=jnp.float32).astype(jnp.bfloat16)


def pack(values, positions, lane_count):
    zeroed = jnp.zeros(values.shape, values.dtype)
    placed = zeroed.at[positions].set(values)
    return placed.reshape((lane_count, values.shape[0] // lane_count) + values.shape[1:])


def unpack(values):
    return values.reshape((values.shape[0] * values.shape[1],) + values.shape[2:])


def shards(
    states,
    query_rows,
    key_rows,
    value_rows,
    gate_rows,
    beta_logit,
    decay_logit,
    residual,
    route_ids,
    route_prob,
    out_weight,
    core_gain,
    moe_gain,
    gate_up,
    down_weight,
    new_home,
):
    req_count = states.shape[0]
    step_count = query_rows.shape[1]
    model_width = residual.shape[-1]
    ep_size = lax.axis_size("ep")
    dp_size = lax.axis_size("dp")
    target = new_home // req_count % ep_size
    new_place = new_home % req_count
    order_ids = jnp.arange(req_count, dtype=jnp.int32)
    earlier = (target[:, None] == target[None, :]) & (order_ids[None, :] < order_ids[:, None])
    lane_rank = jnp.sum(earlier.astype(jnp.int32), axis=1)
    lane_cap = req_count // ep_size
    buffer_index = target * lane_cap + lane_rank
    fresh_states, core_out = delta_block(
        states, query_rows, key_rows, value_rows, gate_rows, beta_logit, decay_logit, core_gain
    )
    received = (
        lax.all_to_all(
            pack(fresh_states, buffer_index, ep_size), "ep", split_axis=0, concat_axis=0, tiled=True
        ),
        lax.all_to_all(
            pack(new_place, buffer_index, ep_size), "ep", split_axis=0, concat_axis=0, tiled=True
        ),
    )
    moved_out = jnp.zeros_like(states).at[unpack(received[1])].set(unpack(received[0]), mode="drop")
    token_count = req_count * step_count
    core_flat = core_out.reshape(token_count, core_out.shape[-1])
    columns = jnp.dot(
        lax.all_gather(core_flat, "ep", axis=0, tiled=True),
        out_weight,
        preferred_element_type=jnp.float32,
    ).astype(jnp.bfloat16)
    attention = lax.all_to_all(columns, "ep", split_axis=0, concat_axis=1, tiled=True)
    hidden = (
        residual.reshape(token_count, model_width).astype(jnp.float32)
        + attention.astype(jnp.float32)
    ).astype(jnp.bfloat16)
    normed = rms_scale(hidden.astype(jnp.float32), moe_gain).astype(jnp.bfloat16)
    top_count = route_ids.shape[-1]
    experts = dp_size * ep_size
    capacity = (token_count * top_count + experts - 1) // experts + 1
    flat_ids = route_ids.reshape(-1)
    onehot = (flat_ids[:, None] == jnp.arange(experts, dtype=jnp.int32)[None, :]).astype(jnp.int32)
    route_rank = jnp.sum(jnp.cumsum(onehot, axis=0) * onehot, axis=1) - 1
    slot_index = flat_ids * capacity + route_rank
    outgoing = (
        jnp.zeros((experts * capacity, model_width), jnp.bfloat16)
        .at[slot_index]
        .set(jnp.repeat(normed, top_count, axis=0))
    )
    arrived = lax.all_to_all(
        lax.all_to_all(
            outgoing.reshape(dp_size, ep_size, capacity, model_width),
            "dp",
            split_axis=0,
            concat_axis=0,
            tiled=True,
        ),
        "ep",
        split_axis=1,
        concat_axis=1,
        tiled=True,
    )
    result = expert_apply(arrived.reshape(-1, model_width), gate_up[0], down_weight[0]).reshape(
        dp_size, ep_size, capacity, model_width
    )
    returned = lax.all_to_all(
        lax.all_to_all(result, "dp", split_axis=0, concat_axis=0, tiled=True),
        "ep",
        split_axis=1,
        concat_axis=1,
        tiled=True,
    )
    routed = returned.reshape(experts * capacity, model_width)[slot_index]
    weights = route_prob.reshape(token_count, top_count)
    weights = weights / jnp.sum(weights, -1, keepdims=True)
    combined = jnp.sum(
        routed.reshape(token_count, top_count, model_width).astype(jnp.float32)
        * weights[:, :, None],
        axis=1,
    )
    mixed_out = (
        (hidden.astype(jnp.float32) + combined)
        .astype(jnp.bfloat16)
        .reshape(req_count, step_count, model_width)
    )
    return (mixed_out, moved_out)


def solution(mesh):
    placed = (
        P(("dp", "ep"), None, None, None),
        P(("dp", "ep"), None, None),
        P(("dp", "ep"), None, None),
        P(("dp", "ep"), None, None),
        P(("dp", "ep"), None, None),
        P(("dp", "ep"), None, None),
        P(("dp", "ep"), None, None),
        P(("dp", "ep"), None, None),
        P(("dp", "ep"), None, None),
        P(("dp", "ep"), None, None),
        P(None, "ep"),
        P(),
        P(),
        P(("dp", "ep"), None, None),
        P(("dp", "ep"), None, None),
        P(("dp", "ep")),
    )
    return jax.shard_map(
        shards,
        mesh=mesh,
        in_specs=placed,
        out_specs=(P(("dp", "ep"), None, None), P(("dp", "ep"), None, None, None)),
        check_vma=False,
    )
```

profile of v0, /device:TPU:0, one launch (start us, length us, event | category | flops | bytes accessed | tf_op | source)
XLA Modules:
  0.0 358.4 jit_solution(125876590752649854)
XLA Ops:
  7.6 9.6 %fusion = f32[8,16,1,128]{3,2,1,0:T(1,128)S(1)} fusion(f32[8,16,128,1]{2,3,1,0:T(1,128)S(1)} %bitcast.152, bf16[8,16,128,128]{3,2,1,0:T(8,128)(2,1)} %param.16, f32[8,16]{1,0:T(8,128)S(1)} %get-tuple-element.37), kind=kOutput, calls=%fused_computation.10 | convolution fusion | flops 29360128 | bytes 4325888 | tf_op jit(solution)/shard_map/bhkv,bhk->bhv/dot_general | solution.py:38
  17.4 8.3 %fusion.2 = f32[8,16,1,128]{3,2,1,0:T(1,128)S(1)} fusion(f32[8,16,128,1]{2,3,1,0:T(1,128)S(1)} %bitcast.196, bf16[8,16,128,128]{3,2,1,0:T(8,128)(2,1)S(1)} %copy-done.1, f32[8,16,128]{2,1,0:T(8,128)S(1)} %subtract_multiply_fusion.3, f32[8,16,128]{2,1,0:T(8,128)S(1)} %bitcast.153, f32[8,16]{1,0:T(8,128)S(1)} %get-tuple-element.37), kind=kOutput, calls=%fused_computation.12 | convolution fusion | flops 33554432 | bytes 4456960 | tf_op jit(solution)/shard_map/bhkv,bhk->bhv/dot_general | solution.py:43
  25.9 8.8 %fusion.3 = f32[8,16,1,128]{3,2,1,0:T(1,128)S(1)} fusion(f32[8,16,128,1]{2,3,1,0:T(1,128)S(1)} %bitcast.161, bf16[8,16,128,128]{3,2,1,0:T(8,128)(2,1)S(1)} %copy-done.1, f32[8,16]{1,0:T(8,128)S(1)} %get-tuple-element.36, f32[8,16,128]{2,1,0:T(8,128)S(1)} %subtract_multiply_fusion.3, f32[8,16,128]{2,1,0:T(8,128)S(1)} %bitcast.154, ...), kind=kOutput, calls=%fused_computation.13 | convolution fusion | flops 35651584 | bytes 4457472 | tf_op jit(solution)/shard_map/bhkv,bhk->bhv/dot_general | solution.py:38
  34.8 11.6 %fusion.11 = f32[8,16,1,128]{3,2,1,0:T(1,128)S(1)} fusion(f32[8,16,128,1]{2,3,1,0:T(1,128)S(1)} %bitcast.197, bf16[8,16,128,128]{3,2,1,0:T(8,128)(2,1)S(1)} %copy-done.1, f32[8,16,128]{2,1,0:T(8,128)S(1)} %subtract_multiply_fusion.2, f32[8,16,128]{2,1,0:T(8,128)S(1)} %bitcast.162, f32[8,16]{1,0:T(8,128)S(1)} %get-tuple-element.36, ...), kind=kOutput, calls=%fused_computation.20 | convolution fusion | flops 39845888 | bytes 4588544 | tf_op jit(solution)/shard_map/bhkv,bhk->bhv/dot_general | solution.py:43
  46.5 11.7 %fusion.7 = f32[8,16,1,128]{3,2,1,0:T(1,128)S(1)} fusion(f32[8,16,128,1]{2,3,1,0:T(1,128)S(1)} %bitcast.168, bf16[8,16,128,128]{3,2,1,0:T(8,128)(2,1)S(1)} %copy-done.1, f32[8,16]{1,0:T(8,128)S(1)} %get-tuple-element.35, f32[8,16,128]{2,1,0:T(8,128)S(1)} %subtract_multiply_fusion.2, f32[8,16,128]{2,1,0:T(8,128)S(1)} %bitcast.163, ...), kind=kOutput, calls=%fused_computation.16 | convolution fusion | flops 41943040 | bytes 4589056 | tf_op jit(solution)/shard_map/bhkv,bhk->bhv/dot_general | solution.py:38
  58.4 15.5 %fusion.42 = f32[8,16,1,128]{3,2,1,0:T(1,128)S(1)} fusion(f32[8,16,128,1]{2,3,1,0:T(1,128)S(1)} %bitcast.198, bf16[8,16,128,128]{3,2,1,0:T(8,128)(2,1)S(1)} %copy-done.1, f32[8,16,128]{2,1,0:T(8,128)S(1)} %subtract_multiply_fusion.1, f32[8,16,128]{2,1,0:T(8,128)S(1)} %bitcast.169, f32[8,16]{1,0:T(8,128)S(1)} %get-tuple-element.35, ...), kind=kOutput, calls=%fused_computation.54 | convolution fusion | flops 46137344 | bytes 4720128 | tf_op jit(solution)/shard_map/bhkv,bhk->bhv/dot_general | solution.py:43
  74.0 15.6 %fusion.5 = f32[8,16,1,128]{3,2,1,0:T(1,128)S(1)} fusion(f32[8,16,128,1]{2,3,1,0:T(1,128)S(1)} %bitcast.173, f32[8,16]{1,0:T(8,128)S(1)} %get-tuple-element.34, bf16[8,16,128,128]{3,2,1,0:T(8,128)(2,1)S(1)} %copy-done.1, f32[8,16,128]{2,1,0:T(8,128)S(1)} %subtract_multiply_fusion.1, f32[8,16,128]{2,1,0:T(8,128)S(1)} %bitcast.170, ...), kind=kOutput, calls=%fused_computation.14 | convolution fusion | flops 48234496 | bytes 4720640 | tf_op jit(solution)/shard_map/bhkv,bhk->bhv/dot_general | solution.py:38
  89.9 21.1 %fusion.10 = f32[8,16,1,128]{3,2,1,0:T(1,128)S(1)} fusion(f32[8,16,128,1]{2,3,1,0:T(1,128)S(1)} %bitcast.199, f32[8,16,128]{2,1,0:T(8,128)S(1)} %subtract_multiply_fusion, f32[8,16,128]{2,1,0:T(8,128)S(1)} %bitcast.174, f32[8,16]{1,0:T(8,128)S(1)} %get-tuple-element.34, bf16[8,16,128,128]{3,2,1,0:T(8,128)(2,1)S(1)} %copy-done.1, ...), kind=kOutput, calls=%fused_computation.19 | convolution fusion | flops 52428800 | bytes 4851712 | tf_op jit(solution)/shard_map/bhkv,bhk->bhv/dot_general | solution.py:43
  111.8 8.6 %all_gather.3 = bf16[128,2048]{1,0:T(8,128)(2,1)S(1)} all-gather(bf16[32,2048]{1,0:T(8,128)(2,1)S(1)} %reshape.504), channel_id=1, replica_groups=mesh['dp'=8,'ep'=4] {'ep'}, dimensions={0}, use_global_device_ids=true | all-gather | bytes 655360 | tf_op jit(solution)/shard_map/all_gather | solution.py:121
  120.4 2.7 convolution_convert_fusion.1
  123.1 3.7 %all-to-all-start = ((bf16[4,32,512]{2,1,0:T(8,128)(2,1)}), bf16[4,32,512]{2,1,0:T(8,128)(2,1)S(1)}, u32[]{:S(2)}, u32[]{:S(2)}) async-start(bf16[4,32,512]{2,1,0:T(8,128)(2,1)} %bitcast.64), calls=%async_computation | async-start | bytes 262144 | tf_op jit(solution)/shard_map/all_to_all | solution.py:125
  133.9 3.6 %reshape.565 = bf16[320,2048]{1,0:T(8,128)(2,1)} reshape(bf16[32,10,2048]{2,1,0:T(8,128)(2,1)} %broadcast_in_dim.31) | data formatting | bytes 2621440 | tf_op jit(solution)/shard_map/reshape | solution.py:141
  137.5 3.7 %scatter_custom_fusion = bf16[352,2048]{1,0:T(8,128)(2,1)S(1)} fusion(s32[320]{0:T(512)} %fusion.50, bf16[320,2048]{1,0:T(8,128)(2,1)} %reshape.565, bf16[]{:T(256)} %constant.72.clone.1), kind=kCustom, calls=%fused_computation.52 | custom fusion | bytes 1442304 | tf_op jit(solution)/shard_map/scatter | solution.py:141
  142.8 2.8 copy.102
  145.5 39.8 %all_to_all.47 = bf16[8,4,11,2048]{3,1,2,0:T(4,128)(2,1)S(1)} all-to-all(bf16[8,4,11,2048]{3,1,2,0:T(4,128)(2,1)S(1)} %copy.102), channel_id=1, replica_groups=mesh['dp'=8,'ep'=4] {'dp'}, dimensions={0} | all-to-all | bytes 2883584 | tf_op jit(solution)/shard_map/all_to_all | solution.py:144
  187.3 3.6 all-to-all-start.2
  195.2 14.2 %all-to-all-done.2 = bf16[8,4,11,2048]{3,0,2,1:T(8,128)(2,1)S(1)} async-done(((bf16[8,4,11,2048]{3,0,2,1:T(8,128)(2,1)}), bf16[8,4,11,2048]{3,0,2,1:T(8,128)(2,1)S(1)}, u32[]{:S(2)}, u32[]{:S(2)}) %all-to-all-start.2) | async-done | bytes 1441824 | tf_op jit(solution)/shard_map/all_to_all | solution.py:143
  209.5 3.8 %all-to-all-start.5 = ((s32[4,1,2]{2,1,0:T(1,128)}), s32[4,1,2]{2,1,0:T(1,128)}, u32[]{:S(2)}, u32[]{:S(2)}) async-start(s32[4,1,2]{2,1,0:T(1,128)} %bitcast.202), calls=%async_computation.5 | async-start | bytes 4096 | tf_op jit(solution)/shard_map/all_to_all | solution.py:113
  220.6 3.9 %copy.105 = bf16[8,4,11,2048]{3,1,2,0:T(4,128)(2,1)} copy(bf16[8,4,11,2048]{3,2,1,0:T(8,128)(2,1)} %reshape.510) | data formatting | bytes 2883584 | tf_op jit(solution)/shard_map/reshape | solution.py:156
  224.5 3.7 %all-to-all-start.3 = ((bf16[8,4,11,2048]{3,1,2,0:T(4,128)(2,1)}), bf16[8,4,11,2048]{3,1,2,0:T(4,128)(2,1)S(1)}, u32[]{:S(2)}, u32[]{:S(2)}) async-start(bf16[8,4,11,2048]{3,1,2,0:T(4,128)(2,1)} %copy.105), calls=%async_computation.3 | async-start | bytes 2883584 | tf_op jit(solution)/shard_map/all_to_all | solution.py:160
  228.3 14.0 %fusion.9 = bf16[8,16,128,128]{3,2,1,0:T(8,128)(2,1)} fusion(f32[8,16,128]{2,1,0:T(8,128)} %copy-done.10, f32[8,16,128]{2,1,0:T(8,128)} %bitcast.175, f32[8,16]{1,0:T(8,128)S(1)} %get-tuple-element.34, f32[8,16,128]{2,1,0:T(8,128)} %copy-done.9, f32[8,16,128]{2,1,0:T(8,128)} %bitcast.172, f32[8,16]{1,0:T(8,128)S(1)} %get-tuple-element.35, ...), kind=kLoop, calls=%fused_computation.18 | loop fusion | flops 29360128 | bytes 8914944 | tf_op jit(solution)/shard_map/convert_element_type | solution.py:52
  242.3 3.1 broadcast.335.clone
  245.3 10.9 %scatter_fusion = bf16[8,16,128,128]{3,2,1,0:T(8,128)(2,1)} fusion(bf16[8,16,128,128]{3,2,1,0:T(8,128)(2,1)} %broadcast.335.clone, s32[8]{0:T(128)S(1)} %copy-done.19, bf16[8,16,128,128]{3,2,1,0:T(8,128)(2,1)} %fusion.9), kind=kCustom, calls=%fused_computation.3 | custom fusion | bytes 12582944 | tf_op jit(solution)/shard_map/scatter | solution.py:68
  256.2 7.1 %all-to-all-done.3 = bf16[8,4,11,2048]{3,1,2,0:T(4,128)(2,1)S(1)} async-done(((bf16[8,4,11,2048]{3,1,2,0:T(4,128)(2,1)}), bf16[8,4,11,2048]{3,1,2,0:T(4,128)(2,1)S(1)}, u32[]{:S(2)}, u32[]{:S(2)}) %all-to-all-start.3) | async-done | bytes 1441824 | tf_op jit(solution)/shard_map/all_to_all | solution.py:160
  263.3 4.9 %all-to-all-start.6 = ((bf16[4,2,16,128,128]{4,3,2,1,0:T(8,128)(2,1)}), bf16[4,2,16,128,128]{4,3,2,1,0:T(8,128)(2,1)}, u32[]{:S(2)}, u32[]{:S(2)}) async-start(bf16[4,2,16,128,128]{4,3,2,1,0:T(8,128)(2,1)} %bitcast.134), calls=%async_computation.6 | async-start | bytes 8388608 | tf_op jit(solution)/shard_map/all_to_all | solution.py:110
  270.1 46.3 %all-to-all-done.6 = bf16[4,2,16,128,128]{4,3,2,1,0:T(8,128)(2,1)} async-done(((bf16[4,2,16,128,128]{4,3,2,1,0:T(8,128)(2,1)}), bf16[4,2,16,128,128]{4,3,2,1,0:T(8,128)(2,1)}, u32[]{:S(2)}, u32[]{:S(2)}) %all-to-all-start.6) | async-done | bytes 4194336 | tf_op jit(solution)/shard_map/all_to_all | solution.py:110
  316.4 3.6 all-to-all-start.4
  329.0 3.1 broadcast.335
  332.1 11.0 %scatter_fusion.1 = bf16[8,16,128,128]{3,2,1,0:T(8,128)(2,1)} fusion(bf16[8,16,128,128]{3,2,1,0:T(8,128)(2,1)} %broadcast.335, s32[8]{0:T(128)} %fusion.52, bf16[8,16,128,128]{3,2,1,0:T(8,128)(2,1)} %bitcast.73), kind=kCustom, calls=%fused_computation.4 | custom fusion | bytes 12582944 | tf_op jit(solution)/shard_map/scatter | solution.py:117
  347.1 3.2 gather_fusion
  350.3 3.5 reshape.552
  353.8 3.6 multiply_reduce_fusion
  (154 shorter events, 46.4 us)
Async XLA Ops:
  0.6 216.6 %copy-start = (bf16[1,2048,512]{2,1,0:T(8,128)(2,1)S(1)}, bf16[1,2048,512]{2,1,0:T(8,128)(2,1)}, u32[]{:S(2)}) copy-start(bf16[1,2048,512]{2,1,0:T(8,128)(2,1)} %param.29) | copy-start | bytes 6291460
  2.4 15.0 %copy-start.1 = (bf16[8,16,128,128]{3,2,1,0:T(8,128)(2,1)S(1)}, bf16[8,16,128,128]{3,2,1,0:T(8,128)(2,1)}, u32[]{:S(2)}) copy-start(bf16[8,16,128,128]{3,2,1,0:T(8,128)(2,1)} %param.16) | copy-start | bytes 12582916
  7.6 82.2 %copy-start.11 = (f32[8,8,2,128]{3,2,1,0:T(2,128)}, f32[8,8,2,128]{3,2,1,0:T(2,128)S(1)}, u32[]{:S(2)}) copy-start(f32[8,8,2,128]{3,2,1,0:T(2,128)S(1)} %broadcast_in_dim.22) | copy-start | bytes 196612
  17.4 72.4 %copy-start.7 = (f32[8,16,128]{2,1,0:T(8,128)}, f32[8,16,128]{2,1,0:T(8,128)S(1)}, u32[]{:S(2)}) copy-start(f32[8,16,128]{2,1,0:T(8,128)S(1)} %subtract_multiply_fusion.3) | copy-start | bytes 196612
  25.9 63.9 %copy-start.12 = (f32[8,8,2,128]{3,2,1,0:T(2,128)}, f32[8,8,2,128]{3,2,1,0:T(2,128)S(1)}, u32[]{:S(2)}) copy-start(f32[8,8,2,128]{3,2,1,0:T(2,128)S(1)} %broadcast_in_dim.24) | copy-start | bytes 196612
  34.8 55.1 %copy-start.8 = (f32[8,16,128]{2,1,0:T(8,128)}, f32[8,16,128]{2,1,0:T(8,128)S(1)}, u32[]{:S(2)}) copy-start(f32[8,16,128]{2,1,0:T(8,128)S(1)} %subtract_multiply_fusion.2) | copy-start | bytes 196612
  46.5 43.3 %copy-start.13 = (f32[8,8,2,128]{3,2,1,0:T(2,128)}, f32[8,8,2,128]{3,2,1,0:T(2,128)S(1)}, u32[]{:S(2)}) copy-start(f32[8,8,2,128]{3,2,1,0:T(2,128)S(1)} %broadcast_in_dim.26) | copy-start | bytes 196612
  58.3 31.5 %copy-start.9 = (f32[8,16,128]{2,1,0:T(8,128)}, f32[8,16,128]{2,1,0:T(8,128)S(1)}, u32[]{:S(2)}) copy-start(f32[8,16,128]{2,1,0:T(8,128)S(1)} %subtract_multiply_fusion.1) | copy-start | bytes 196612
  74.0 15.8 %copy-start.14 = (f32[8,8,2,128]{3,2,1,0:T(2,128)}, f32[8,8,2,128]{3,2,1,0:T(2,128)S(1)}, u32[]{:S(2)}) copy-start(f32[8,8,2,128]{3,2,1,0:T(2,128)S(1)} %broadcast_in_dim.28) | copy-start | bytes 196612
  89.7 21.3 %copy-start.10 = (f32[8,16,128]{2,1,0:T(8,128)}, f32[8,16,128]{2,1,0:T(8,128)S(1)}, u32[]{:S(2)}) copy-start(f32[8,16,128]{2,1,0:T(8,128)S(1)} %subtract_multiply_fusion) | copy-start | bytes 196612
  89.9 21.3 %copy-start.6 = (bf16[8,4,2048]{2,1,0:T(4,128)(2,1)S(1)}, bf16[8,4,2048]{2,1,0:T(4,128)(2,1)}, u32[]{:S(2)}) copy-start(bf16[8,4,2048]{2,1,0:T(4,128)(2,1)} %param.20) | copy-start | bytes 393220
  89.9 21.5 %copy-start.18 = (f32[128]{0:T(128)S(1)}, f32[128]{0:T(128)}, u32[]{:S(2)}) copy-start(f32[128]{0:T(128)} %param.27) | copy-start | bytes 1540
  111.0 15.9 %copy-start.15 = (s32[8,4,10]{2,1,0:T(4,128)S(1)}, s32[8,4,10]{2,1,0:T(4,128)}, u32[]{:S(2)}) copy-start(s32[8,4,10]{2,1,0:T(4,128)} %param.24) | copy-start | bytes 3844
  111.0 17.4 %copy-start.4 = (bf16[8,4,2048]{2,1,0:T(4,128)(2,1)S(1)}, bf16[8,4,2048]{2,1,0:T(4,128)(2,1)}, u32[]{:S(2)}) copy-start(bf16[8,4,2048]{2,1,0:T(4,128)(2,1)} %param.23) | copy-start | bytes 393220
  111.5 20.7 %copy-start.17 = (f32[2048]{0:T(1024)S(1)}, f32[2048]{0:T(1024)}, u32[]{:S(2)}) copy-start(f32[2048]{0:T(1024)} %param.28) | copy-start | bytes 24580
  123.1 8.3 %all-to-all-start = ((bf16[4,32,512]{2,1,0:T(8,128)(2,1)}), bf16[4,32,512]{2,1,0:T(8,128)(2,1)S(1)}, u32[]{:S(2)}, u32[]{:S(2)}) async-start(bf16[4,32,512]{2,1,0:T(8,128)(2,1)} %bitcast.64), calls=%async_computation | async-start | bytes 262144 | tf_op jit(solution)/shard_map/all_to_all | solution.py:125
  131.9 2.0 copy-start.2
  187.3 22.2 %all-to-all-start.2 = ((bf16[8,4,11,2048]{3,0,2,1:T(8,128)(2,1)}), bf16[8,4,11,2048]{3,0,2,1:T(8,128)(2,1)S(1)}, u32[]{:S(2)}, u32[]{:S(2)}) async-start(bf16[8,4,11,2048]{3,0,2,1:T(8,128)(2,1)} %copy.103), calls=%async_computation.2 | async-start | bytes 2883584 | tf_op jit(solution)/shard_map/all_to_all | solution.py:143
  209.5 15.1 %all-to-all-start.5 = ((s32[4,1,2]{2,1,0:T(1,128)}), s32[4,1,2]{2,1,0:T(1,128)}, u32[]{:S(2)}, u32[]{:S(2)}) async-start(s32[4,1,2]{2,1,0:T(1,128)} %bitcast.202), calls=%async_computation.5 | async-start | bytes 4096 | tf_op jit(solution)/shard_map/all_to_all | solution.py:113
  217.2 1.2 copy-start.20
  224.5 38.8 %all-to-all-start.3 = ((bf16[8,4,11,2048]{3,1,2,0:T(4,128)(2,1)}), bf16[8,4,11,2048]{3,1,2,0:T(4,128)(2,1)S(1)}, u32[]{:S(2)}, u32[]{:S(2)}) async-start(bf16[8,4,11,2048]{3,1,2,0:T(4,128)(2,1)} %copy.105), calls=%async_computation.3 | async-start | bytes 2883584 | tf_op jit(solution)/shard_map/all_to_all | solution.py:160
  242.3 3.1 copy-start.19
  263.3 53.1 %all-to-all-start.6 = ((bf16[4,2,16,128,128]{4,3,2,1,0:T(8,128)(2,1)}), bf16[4,2,16,128,128]{4,3,2,1,0:T(8,128)(2,1)}, u32[]{:S(2)}, u32[]{:S(2)}) async-start(bf16[4,2,16,128,128]{4,3,2,1,0:T(8,128)(2,1)} %bitcast.134), calls=%async_computation.6 | async-start | bytes 8388608 | tf_op jit(solution)/shard_map/all_to_all | solution.py:110
  268.2 51.8 %copy-start.16 = (f32[8,4,10]{2,1,0:T(4,128)S(1)}, f32[8,4,10]{2,1,0:T(4,128)}, u32[]{:S(2)}) copy-start(f32[8,4,10]{2,1,0:T(4,128)} %param.25) | copy-start | bytes 3844
  316.4 26.7 %all-to-all-start.4 = ((bf16[8,4,11,2048]{3,0,2,1:T(8,128)(2,1)}), bf16[8,4,11,2048]{3,0,2,1:T(8,128)(2,1)S(1)}, u32[]{:S(2)}, u32[]{:S(2)}) async-start(bf16[8,4,11,2048]{3,0,2,1:T(8,128)(2,1)} %copy.106), calls=%async_computation.4 | async-start | bytes 2883584 | tf_op jit(solution)/shard_map/all_to_all | solution.py:159
  350.3 7.2 %copy-start.3 = (f32[8,4,2048]{2,1,0:T(4,128)S(1)}, f32[8,4,2048]{2,1,0:T(4,128)}, u32[]{:S(2)}) copy-start(f32[8,4,2048]{2,1,0:T(4,128)} %copy-done.2) | copy-start | bytes 786436
  350.3 7.2 %copy-start.5 = (bf16[8,4,2048]{2,1,0:T(4,128)(2,1)S(1)}, bf16[8,4,2048]{2,1,0:T(4,128)(2,1)}, u32[]{:S(2)}) copy-start(bf16[8,4,2048]{2,1,0:T(4,128)(2,1)} %param.23) | copy-start | bytes 393220
where the time goes:
time: 364 us; the launch traced here: 358 us
  matrix products  106 us (29%)
  local copies, waits for them, and re-layouts  74.4 us (20%)
  waiting for transfers between devices  70.1 us (19%)
  blocking collectives  48.4 us (13%)
  other arithmetic  34.2 us (9%)
  starting transfers between devices  23.2 us (6%)
    dot_general x4, matrix products, delta_block(): jnp.einsum('bhkv,bhk->bhv', memory_state, queries, precision=lax.Precisio...  56.5 us
    all_to_all x1, waiting for transfers between devices, shards(): lax.all_to_all(pack(fresh_states, buffer_index, ep_size), 'ep', split_axi...  46.3 us
    dot_general x4, matrix products, delta_block(): jnp.einsum('bhkv,bhk->bhv', memory_state, key_units, precision=lax.Precis...  45.7 us
    all_to_all x1, blocking collectives, shards(): lax.all_to_all(outgoing.reshape(dp_size, ep_size, capacity, model_width),...  39.8 us
    all_to_all x1, waiting for transfers between devices, shards(): lax.all_to_all(lax.all_to_all(outgoing.reshape(dp_size, ep_size, capacity...  14.2 us
    convert_element_type x1, other arithmetic, delta_block(): return (memory_state.astype(jnp.bfloat16), jnp.stack(outputs, axis=1))  14 us
    scatter x2, local copies, waits for them, and re-layouts, pack(): placed = zeroed.at[positions].set(values)  12.1 us
    scatter x1, local copies, waits for them, and re-layouts, shards(): jnp.zeros_like(states).at[unpack(received[1])]  11 us
  transfers between devices with their start and end apart: 6, of which 4 were waited for; matrix products, arithmetic and copies ran while one was open for 19% of the time, Pallas kernels for 0%

commit v1 on v0

v1 whole, which is shorter than its diff:
```python
import functools

import jax
import jax.numpy as jnp
from jax import lax
from jax.experimental import pallas as pl
from jax.experimental.pallas import tpu as pltpu
from jax.sharding import PartitionSpec as P

EPS = 1e-06
F32 = jnp.float32
BF16 = jnp.bfloat16
MIB = 1 << 20


def row_sum(x):
    return jnp.sum(x, axis=-1, keepdims=True)


def spread_rows(ref, scratch, requests, steps):
    for r in range(requests):
        split_heads(ref[r].astype(F32), scratch, r, steps)


def split_heads(values, scratch, r, steps):
    hd = scratch.shape[-1]
    for h in range(scratch.shape[0]):
        scratch[h, r * steps : (r + 1) * steps, :] = values[:, h * hd : (h + 1) * hd]


def at_step(scratch, t, requests, steps, head=None):
    if head is None:
        return scratch[pl.ds(t, requests, stride=steps), :]
    return scratch[head, pl.ds(t, requests, stride=steps), :]


def recurrence(kh, repeats, steps, requests, hd, k_s, q_s, v_s, a_s, b_s, m_s, emit_out, emit_state):
    per = m_s.shape[1] // requests
    ks = [at_step(k_s, t, requests, steps, kh) for t in range(steps)]
    rk = [lax.rsqrt(row_sum(k * k) + EPS) for k in ks]
    kn = [k * r for k, r in zip(ks, rk)]
    kk = {(i, t): row_sum(kn[i] * kn[t]) for t in range(steps) for i in range(t)}
    if emit_out is not None:
        qs = [at_step(q_s, t, requests, steps, kh) for t in range(steps)]
        rq = [lax.rsqrt(row_sum(q * q) + EPS) * hd**-0.5 for q in qs]
        qn = [q * r for q, r in zip(qs, rq)]
        kq = {(i, t): row_sum(kn[i] * qn[t]) for t in range(steps) for i in range(t + 1)}
    for h in range(kh * repeats, (kh + 1) * repeats):
        decayed = []
        c = None
        for t in range(steps):
            a = at_step(a_s, t, requests, steps)[:, h : h + 1]
            b = at_step(b_s, t, requests, steps)[:, h : h + 1]
            decayed = [w * a for w in decayed]
            c = a if c is None else c * a
            m = (c * rk[t]) * at_step(m_s, t, requests, per, h)
            for i in range(t):
                m = m + kk[i, t] * decayed[i]
            decayed.append((at_step(v_s, t, requests, steps, h) - m) * b)
            if emit_out is not None:
                o = (c * rq[t]) * at_step(m_s, steps + t, requests, per, h)
                for i in range(t + 1):
                    o = o + kq[i, t] * decayed[i]
                emit_out(t, h, o)
        if emit_state is not None:
            emit_state(h, c, [w * r for w, r in zip(decayed, rk)])


def sigmoid_rows(ref, scratch, requests, steps):
    for r in range(requests):
        scratch[r * steps : (r + 1) * steps, : ref.shape[-1]] = jax.nn.sigmoid(ref[r].astype(F32))


def core_kernel(
    state_ref, q_ref, k_ref, v_ref, g_ref, b_ref, a_ref, gain_ref, out_ref,
    k_s, q_s, v_s, g_s, a_s, b_s, m_s, o_s,
):
    r = pl.program_id(0)
    requests, steps, key_width = k_ref.shape
    heads, hd = state_ref.shape[1], state_ref.shape[-1]
    key_heads = key_width // hd
    repeats = heads // key_heads
    rows = jnp.concatenate([k_ref[r].astype(F32), q_ref[r].astype(F32)], axis=0).astype(BF16)
    base = pl.multiple_of(r * 2 * steps, 2 * steps)
    for h in range(heads):
        kh = h // repeats
        m_s[h, pl.ds(base, 2 * steps), :] = jnp.dot(
            rows[:, kh * hd : (kh + 1) * hd], state_ref[0, h], preferred_element_type=F32
        )

    @pl.when(r == requests - 1)
    def _():
        spread_rows(k_ref, k_s, requests, steps)
        spread_rows(q_ref, q_s, requests, steps)
        spread_rows(v_ref, v_s, requests, steps)
        spread_rows(g_ref, g_s, requests, steps)
        sigmoid_rows(a_ref, a_s, requests, steps)
        sigmoid_rows(b_ref, b_s, requests, steps)
        gain = gain_ref[...]

        def emit(t, h, o):
            gate = at_step(g_s, t, requests, steps, h)
            scaled = o * lax.rsqrt(row_sum(o * o) * (1.0 / hd) + EPS)
            o_s[h, pl.ds(t, requests, stride=steps), :] = scaled * gain * jax.nn.silu(gate)

        for kh in range(key_heads):
            recurrence(kh, repeats, steps, requests, hd, k_s, q_s, v_s, a_s, b_s, m_s, emit, None)
        for h in range(heads):
            out_ref[:, h * hd : (h + 1) * hd] = o_s[h].astype(BF16)


def core_rows(states, query_rows, key_rows, value_rows, gate_rows, beta_logit, decay_logit, core_gain):
    requests, heads, hd, _ = states.shape
    steps = key_rows.shape[1]
    kw, vw = key_rows.shape[-1], value_rows.shape[-1]
    whole = lambda x: pl.BlockSpec(x.shape, lambda r: (0,) * x.ndim)
    tokens = requests * steps
    gain = core_gain.reshape(1, hd)
    small = (query_rows, key_rows, value_rows, gate_rows, beta_logit, decay_logit, gain)
    return pl.pallas_call(
        core_kernel,
        grid=(requests,),
        in_specs=[pl.BlockSpec((1, heads, hd, hd), lambda r: (r, 0, 0, 0))] + [whole(x) for x in small],
        out_specs=pl.BlockSpec((tokens, vw), lambda r: (0, 0)),
        out_shape=jax.ShapeDtypeStruct((tokens, vw), BF16),
        scratch_shapes=[
            pltpu.VMEM((kw // hd, tokens, hd), F32),
            pltpu.VMEM((kw // hd, tokens, hd), F32),
            pltpu.VMEM((heads, tokens, hd), F32),
            pltpu.VMEM((heads, tokens, hd), F32),
            pltpu.VMEM((tokens, 128), F32),
            pltpu.VMEM((tokens, 128), F32),
            pltpu.VMEM((heads, 2 * tokens, hd), F32),
            pltpu.VMEM((heads, tokens, hd), F32),
        ],
        compiler_params=pltpu.CompilerParams(vmem_limit_bytes=32 * MIB),
        cost_estimate=pl.CostEstimate(flops=20_000_000, bytes_accessed=5 * MIB, transcendentals=100_000),
        name="core_rows",
    )(states, *small)


def pack_kernel(order_ref, state_ref, pay_ref, *rest):
    groups = len(rest) // 2
    outs, sems = rest[:-1], rest[-1]
    cap = outs[0].shape[0]
    half = len(outs) // 2
    copies = []
    for d in range(half):
        for j in range(cap):
            source = order_ref[(d + 1) * cap + j]
            copies.append(
                pltpu.make_async_copy(state_ref.at[source], outs[d].at[j], sems.at[0, d * cap + j])
            )
            copies.append(
                pltpu.make_async_copy(pay_ref.at[source], outs[half + d].at[j], sems.at[1, d * cap + j])
            )
    for c in copies:
        c.start()
    for c in copies:
        c.wait()


def pack_lanes(order, states, payload, lanes):
    requests = states.shape[0]
    cap = requests // lanes
    hbm = pl.BlockSpec(memory_space=pl.ANY)
    outs = pl.pallas_call(
        pack_kernel,
        in_specs=[pl.BlockSpec(memory_space=pltpu.SMEM), hbm, hbm],
        out_specs=[hbm] * (2 * (lanes - 1)),
        out_shape=[jax.ShapeDtypeStruct((cap,) + states.shape[1:], BF16)] * (lanes - 1)
        + [jax.ShapeDtypeStruct((cap,) + payload.shape[1:], BF16)] * (lanes - 1),
        scratch_shapes=[pltpu.SemaphoreType.DMA((2, (lanes - 1) * cap))],
        cost_estimate=pl.CostEstimate(flops=0, bytes_accessed=6 * MIB, transcendentals=0),
        name="pack_lanes",
    )(order, states, payload)
    return outs[: lanes - 1], outs[lanes - 1 :]


def state_kernel(kw, vw, heads, order_ref, place_ref, own_ref, *rest):
    lanes = len(rest) - 13 + 1
    sources = (own_ref,) + rest[: lanes - 1]
    pay_ref, out_ref = rest[lanes - 1], rest[lanes]
    k_s, v_s, a_s, b_s, m_s, u_s, c_s, held, ready, in_sem, out_sem = rest[lanes + 1 :]
    requests, steps, _ = pay_ref.shape
    hd = held.shape[-1]
    repeats = heads // (kw // hd)
    cap = requests // lanes
    copies = []
    for r in range(requests):
        d, j = divmod(r, cap)
        source = own_ref.at[order_ref[j]] if d == 0 else sources[d].at[j]
        copies.append(pltpu.make_async_copy(source, held.at[r], in_sem.at[r]))
        copies[-1].start()
    for r in range(requests):
        rows = slice(r * steps, (r + 1) * steps)
        pay = pay_ref[r].astype(F32)
        split_heads(pay[:, :kw], k_s, r, steps)
        split_heads(pay[:, kw : kw + vw], v_s, r, steps)
        a_s[rows, :] = jax.nn.sigmoid(pay[:, kw + vw : kw + vw + 128])
        b_s[rows, :] = jax.nn.sigmoid(pay[:, kw + vw + 128 : kw + vw + 256])
    for r in range(requests):
        copies[r].wait()
        rows = slice(r * steps, (r + 1) * steps)
        for h in range(heads):
            m_s[h, rows, :] = jnp.dot(
                k_s[h // repeats, rows, :].astype(BF16), held[r, h], preferred_element_type=F32
            )

    def emit(h, c, updates):
        c_s[h] = jnp.broadcast_to(c, (requests, hd))
        for t, u in enumerate(updates):
            u_s[h, pl.ds(t, requests, stride=steps), :] = u

    for kh in range(kw // hd):
        recurrence(kh, repeats, steps, requests, hd, k_s, None, v_s, a_s, b_s, m_s, None, emit)
    sent = []
    for r in range(requests):
        slot = r % 2
        if r >= 2:
            sent[r - 2].wait()
        rows = slice(r * steps, (r + 1) * steps)
        for h in range(heads):
            k4 = k_s[h // repeats, rows, :]
            k8 = jnp.concatenate([k4, k4], axis=0).astype(BF16)
            u4 = u_s[h, rows, :]
            high = u4.astype(BF16).astype(F32)
            u8 = jnp.concatenate([high, u4 - high], axis=0).astype(BF16)
            added = lax.dot_general(
                k8, u8, (((0,), (0,)), ((), ())), preferred_element_type=F32
            )
            kept = held[r, h].astype(F32) * c_s[h, r : r + 1, :]
            ready[slot, h] = (kept + added).astype(BF16)
        sent.append(pltpu.make_async_copy(ready.at[slot], out_ref.at[place_ref[r]], out_sem.at[slot]))
        sent[-1].start()
    for c in sent[-2:]:
        c.wait()


def landed_states(order, place, own, arrived, payload, kw, vw):
    requests, heads, hd, _ = own.shape
    steps = payload.shape[1]
    tokens = requests * steps
    hbm = pl.BlockSpec(memory_space=pl.ANY)
    smem = pl.BlockSpec(memory_space=pltpu.SMEM)
    return pl.pallas_call(
        functools.partial(state_kernel, kw, vw, heads),
        in_specs=[smem, smem, hbm] + [hbm] * len(arrived) + [pl.BlockSpec(memory_space=pltpu.VMEM)],
        out_specs=hbm,
        out_shape=jax.ShapeDtypeStruct(own.shape, BF16),
        scratch_shapes=[
            pltpu.VMEM((kw // hd, tokens, hd), F32),
            pltpu.VMEM((heads, tokens, hd), F32),
            pltpu.VMEM((tokens, 128), F32),
            pltpu.VMEM((tokens, 128), F32),
            pltpu.VMEM((heads, tokens, hd), F32),
            pltpu.VMEM((heads, tokens, hd), F32),
            pltpu.VMEM((heads, requests, hd), F32),
            pltpu.VMEM(own.shape, BF16),
            pltpu.VMEM((2, heads, hd, hd), BF16),
            pltpu.SemaphoreType.DMA((requests,)),
            pltpu.SemaphoreType.DMA((2,)),
        ],
        compiler_params=pltpu.CompilerParams(vmem_limit_bytes=40 * MIB),
        cost_estimate=pl.CostEstimate(flops=20_000_000, bytes_accessed=9 * MIB, transcendentals=10_000),
        name="landed_states",
    )(order, place, own, *arrived, payload)


def expert_kernel(me_ref, h_ref, route_ref, gain_ref, up_ref, down_ref, out_ref):
    groups, parts, tokens, cols = h_ref.shape
    rows = groups * tokens
    hidden_units = down_ref.shape[1]
    pieces = [h_ref[:, e].reshape(rows, cols).astype(F32) for e in range(parts)]
    total = sum(row_sum(p * p) for p in pieces)
    scale = lax.rsqrt(total * (1.0 / (parts * cols)) + EPS)
    joined = None
    for e in range(parts):
        span = slice(e * cols, (e + 1) * cols)
        normed = (pieces[e] * scale * gain_ref[:, span]).astype(BF16)
        term = jnp.dot(normed, up_ref[0, span, :], preferred_element_type=F32)
        joined = term if joined is None else joined + term
    active = (jax.nn.silu(joined[:, :hidden_units]) * joined[:, hidden_units:]).astype(BF16)
    result = jnp.dot(active, down_ref[0], preferred_element_type=F32).astype(BF16)
    route = route_ref[...]
    top = route.shape[1] // 2
    named = route[:, :top] == me_ref[0].astype(F32)
    weight = row_sum(jnp.where(named, route[:, top:], 0.0))
    out_ref[...] = (result.astype(F32) * weight).astype(BF16)


def expert_all(me, hidden, routes, moe_gain, gate_up, down_weight):
    groups, parts, tokens, cols = hidden.shape
    width = parts * cols
    step = max(1, min(groups, 256 // tokens))
    rows = step * tokens
    const = lambda x: pl.BlockSpec(x.shape, lambda i: (0,) * x.ndim)
    gain = moe_gain.reshape(1, width)
    return pl.pallas_call(
        expert_kernel,
        grid=(groups // step,),
        in_specs=[
            pl.BlockSpec(memory_space=pltpu.SMEM),
            pl.BlockSpec((step, parts, tokens, cols), lambda i: (i, 0, 0, 0)),
            pl.BlockSpec((rows, routes.shape[1]), lambda i: (i, 0)),
            const(gain),
            const(gate_up),
            const(down_weight),
        ],
        out_specs=pl.BlockSpec((rows, width), lambda i: (i, 0)),
        out_shape=jax.ShapeDtypeStruct((groups * tokens, width), BF16),
        compiler_params=pltpu.CompilerParams(vmem_limit_bytes=40 * MIB),
        cost_estimate=pl.CostEstimate(
            flops=6 * groups * tokens * width * 256, bytes_accessed=12 * MIB, transcendentals=0
        ),
        name="expert_all",
    )(me, hidden, routes, gain, gate_up, down_weight)


def shards(
    states, query_rows, key_rows, value_rows, gate_rows, beta_logit, decay_logit, residual,
    route_ids, route_prob, out_weight, core_gain, moe_gain, gate_up, down_weight, new_home,
):
    requests, heads, hd, _ = states.shape
    steps = query_rows.shape[1]
    width = residual.shape[-1]
    tokens = requests * steps
    lanes = lax.axis_size("ep")
    groups = lax.axis_size("dp")
    my_lane = lax.axis_index("ep")
    me = lax.axis_index("dp") * lanes + my_lane
    cap = requests // lanes
    kw, vw = key_rows.shape[-1], value_rows.shape[-1]
    top = route_ids.shape[-1]

    with jax.named_scope("order"):
        lane = (new_home // requests % lanes) ^ my_lane
        ids = jnp.arange(requests, dtype=jnp.int32)
        earlier = (lane[:, None] == lane[None, :]) & (ids[None, :] < ids[:, None])
        slot = lane * cap + jnp.sum(earlier.astype(jnp.int32), axis=1)
        order = jnp.sum(jnp.where(slot[:, None] == ids[None, :], ids[:, None], 0), axis=0)
        place = (new_home % requests).astype(BF16)
        place = jnp.broadcast_to(place[:, None, None], (requests, steps, 1))
        fill = lambda n: jnp.zeros((requests, steps, n), BF16)
        payload = jnp.concatenate(
            [key_rows, value_rows, decay_logit, place, fill(127 - heads), beta_logit, fill(128 - heads)],
            axis=-1,
        )
    with jax.named_scope("send_states"):
        packed, pays = pack_lanes(order, states, payload, lanes)
        swap = lambda x, d: lax.ppermute(x, "ep", [(i, i ^ d) for i in range(lanes)])
        arrived = [swap(packed[d - 1], d) for d in range(1, lanes)]
        arrived_pay = [swap(pays[d - 1], d) for d in range(1, lanes)]

    with jax.named_scope("routes"):
        weights = route_prob.reshape(tokens, top)
        weights = weights / jnp.sum(weights, -1, keepdims=True)
        routes = jnp.concatenate([route_ids.reshape(tokens, top).astype(F32), weights], axis=-1)
        routes = lax.all_gather(routes, ("dp", "ep"), axis=0, tiled=True)
        group_residual = lax.all_gather(residual.reshape(tokens, width), "ep", axis=0, tiled=True)

    with jax.named_scope("core"):
        core = core_rows(
            states, query_rows, key_rows, value_rows, gate_rows, beta_logit, decay_logit, core_gain
        )
        group_core = lax.all_gather(core, "ep", axis=0, tiled=True)
    with jax.named_scope("attention"):
        cols = out_weight.shape[1]
        attention = jnp.dot(group_core, out_weight, preferred_element_type=F32).astype(BF16)
        before = lax.dynamic_slice_in_dim(group_residual, my_lane * cols, cols, axis=1)
        hidden_cols = (before.astype(F32) + attention.astype(F32)).astype(BF16)
        gathered = lax.all_gather(hidden_cols, ("dp", "ep"), axis=0, tiled=False)
        gathered = gathered.reshape(groups, lanes, tokens * lanes, cols)

    with jax.named_scope("experts"):
        partial = expert_all(me.reshape(1), gathered, routes, moe_gain, gate_up, down_weight)
        combined = lax.psum_scatter(partial, ("dp", "ep"), scatter_dimension=0, tiled=True)
        own = lax.dynamic_slice(
            gathered,
            (lax.axis_index("dp"), 0, my_lane * tokens, 0),
            (1, lanes, tokens, cols),
        )[0]
        own = own.transpose(1, 0, 2).reshape(tokens, width)
        mixed_out = (own.astype(F32) + combined.astype(F32)).astype(BF16)

    with jax.named_scope("landed"):
        own_pay = payload[order[:cap]]
        all_pay = jnp.concatenate([own_pay] + arrived_pay, axis=0)
        place = all_pay[:, 0, kw + vw + heads].astype(jnp.int32)
        moved_out = landed_states(order, place, states, arrived, all_pay, kw, vw)
    return mixed_out.reshape(requests, steps, width), moved_out


def solution(mesh):
    row = P(("dp", "ep"), None, None)
    placed = (P(("dp", "ep"), None, None, None),) + (row,) * 9 + (
        P(None, "ep"), P(), P(), row, row, P(("dp", "ep")),
    )
    return jax.shard_map(
        shards,
        mesh=mesh,
        in_specs=placed,
        out_specs=(row, P(("dp", "ep"), None, None, None)),
        check_vma=False,
    )
```

time: 364 us -> 299 us (0.82); the launches traced: 358 us -> 298 us
  Pallas kernels: 0 us -> 123 us
  matrix products: 106 us -> 1.11 us
  local copies, waits for them, and re-layouts: 74.4 us -> 22.5 us
  other arithmetic: 34.2 us -> 3.2 us
  starting transfers between devices: 23.2 us -> 3.97 us
  between operations: 1.68 us -> 14.3 us
  blocking collectives: 48.4 us -> 58.6 us
    pallas_call x0 -> x4, Pallas kernels: none -> 123 us  [the longest x1 102 us: pack_lanes(): pl.pallas_call(pack_kernel, in_specs=[pl.BlockSpec(memory_space=pltpu.SME...]
    dot_general x11 -> x1, matrix products: 106 us -> 1.11 us  [shards(): jnp.dot(group_core, out_weight, preferred_element_type=F32).astype(BF16)]
    all_to_all x6 -> x0, waiting for transfers between devices: 70.1 us -> none  [the longest x1 46.3 us: shards(): lax.all_to_all(pack(fresh_states, buffer_index, ep_size), 'ep', split_axi...]
    ppermute x0 -> x6, waiting for transfers between devices: none -> 51.7 us  [shards(): lax.ppermute(x, 'ep', [(i, i ^ d) for i in range(lanes)])]
    all_gather x1 -> x3, blocking collectives: 8.62 us -> 58.6 us  [the longest x1 42.7 us: shards(): routes = lax.all_gather(routes, ('dp', 'ep'), axis=0, tiled=True)]
    all_to_all x1 -> x0, blocking collectives: 39.8 us -> none  [shards(): lax.all_to_all(outgoing.reshape(dp_size, ep_size, capacity, model_width),...]
    scatter x4 -> x0, local copies, waits for them, and re-layouts: 26.7 us -> none  [the longest x2 12.1 us: pack(): placed = zeroed.at[positions].set(values)]
    all_to_all x6 -> x0, starting transfers between devices: 23.2 us -> none  [the longest x1 4.86 us: shards(): lax.all_to_all(pack(fresh_states, buffer_index, ep_size), 'ep', split_axi...]
  transfers between devices with their start and end apart: 6 -> 8, of which waited for: 4 -> 3; matrix products, arithmetic and copies ran while one was open for 19% -> 2% of each run, Pallas kernels for 0% -> 37%
where the time goes in v1:
time: 299 us; the launch traced here: 298 us
  Pallas kernels  123 us (41%)
  waiting for transfers between devices  71.7 us (24%)
  blocking collectives  58.6 us (20%)
  local copies, waits for them, and re-layouts  22.5 us (8%)
  between operations  14.3 us (5%)
  starting transfers between devices  3.97 us (1%)
  other arithmetic  3.2 us (1%)
    pallas_call x1, Pallas kernels, pack_lanes(): pl.pallas_call(pack_kernel, in_specs=[pl.BlockSpec(memory_space=pltpu.SME...  102 us
    ppermute x6, waiting for transfers between devices, shards(): lax.ppermute(x, 'ep', [(i, i ^ d) for i in range(lanes)])  51.7 us
    all_gather x1, blocking collectives, shards(): routes = lax.all_gather(routes, ('dp', 'ep'), axis=0, tiled=True)  42.7 us
    all_gather x1, waiting for transfers between devices, shards(): gathered = lax.all_gather(hidden_cols, ('dp', 'ep'), axis=0, tiled=False)  19.9 us
    unnamed x52, local copies, waits for them, and re-layouts  18.8 us
    pallas_call x1, Pallas kernels, landed_states(): pl.pallas_call(functools.partial(state_kernel, kw, vw, heads), in_specs=[...  8.8 us
    all_gather x1, blocking collectives, shards(): group_core = lax.all_gather(core, 'ep', axis=0, tiled=True)  8.62 us
    all_gather x1, blocking collectives, shards(): lax.all_gather(residual.reshape(tokens, width), 'ep', axis=0, tiled=True)  7.29 us
  transfers between devices with their start and end apart: 8, of which 3 were waited for; matrix products, arithmetic and copies ran while one was open for 2% of the time, Pallas kernels for 37%

profile of v1, /device:TPU:0, one launch (start us, length us, event | category | flops | bytes accessed | tf_op | source)
XLA Modules:
  0.0 298.0 jit_solution(4984636760841817540)
XLA Ops:
  7.2 2.3 copy-done.1
  9.6 0.9 copy-done.7
  10.5 0.8 copy-done.9
  11.3 0.9 copy-done.11
  12.2 0.8 copy-done.12
  13.1 0.7 copy-done.13
  13.7 0.7 copy-done.15
  14.4 0.7 copy-done.19
  15.1 6.5 %core_rows.1 = bf16[32,2048]{1,0:T(8,128)(2,1)S(1)} custom-call(bf16[8,16,128,128]{3,2,1,0:T(8,128)(2,1)S(1)} %copy-done.1, bf16[8,4,1024]{2,1,0:T(4,128)(2,1)S(1)} %copy-done.12, bf16[8,4,1024]{2,1,0:T(4,128)(2,1)S(1)} %copy-done.9, bf16[8,4,2048]{2,1,0:T(4,128)(2,1)S(1)} %copy-done.7, bf16[8,4,2048]{2,1,0:T(4,128)(2,1)S(1)} %copy-done.11, ...), custom_call_target="tpu_custom_call" | custom-call | flops 20000000 | bytes 5242880 | tf_op jit(solution)/shard_map/core/core_rows/pallas_call | solution.py:120
  21.6 8.6 %all_gather.16 = bf16[128,2048]{1,0:T(8,128)(2,1)S(1)} all-gather(bf16[32,2048]{1,0:T(8,128)(2,1)S(1)} %core_rows.1), channel_id=1, replica_groups=mesh['dp'=8,'ep'=4] {'ep'}, dimensions={0}, use_global_device_ids=true | all-gather | bytes 655360 | tf_op jit(solution)/shard_map/core/all_gather | solution.py:366
  30.3 7.3 %all_gather.15 = bf16[128,2048]{1,0:T(8,128)(2,1)S(1)} all-gather(bf16[32,2048]{1,0:T(8,128)(2,1)S(1)} %reshape.43), channel_id=1, replica_groups=mesh['dp'=8,'ep'=4] {'ep'}, dimensions={0}, use_global_device_ids=true | all-gather | bytes 655360 | tf_op jit(solution)/shard_map/routes/all_gather | solution.py:360
  37.6 1.1 fusion.2
  39.2 42.7 %all-gather.1 = f32[32,32,20]{1,2,0:T(8,128)S(1)} all-gather(f32[1,32,20]{1,2,0:T(8,128)S(1)} %copy.27), channel_id=1, replica_groups=mesh['dp'=8,'ep'=4] {'dp','ep'}, dimensions={0}, use_global_device_ids=true | all-gather | bytes 84480 | tf_op jit(solution)/shard_map/routes/all_gather | solution.py:359
  82.2 19.9 %all-gather.4.cloned.1.call-done = bf16[4096,512]{1,0:T(8,128)(2,1)} async-done(((bf16[128,512]{1,0:T(8,128)(2,1)}), bf16[4096,512]{1,0:T(8,128)(2,1)}) %all-gather.4.cloned.1.call-update) | async-done | bytes 4194320 | tf_op jit(solution)/shard_map/attention/all_gather | solution.py:372
  102.1 2.2 copy-done.4
  104.3 1.6 copy-done.5
  105.9 1.2 copy-done.6
  107.2 5.2 %expert_all.1 = bf16[1024,2048]{1,0:T(8,128)(2,1)S(1)} custom-call(s32[1]{0:T(128)} %bitcast.4.me_ref, bf16[8,4,128,512]{3,2,1,0:T(8,128)(2,1)S(1)} %bitcast.19, f32[1024,20]{1,0:T(8,128)S(1)} %bitcast.20, f32[1,2048]{1,0:T(1,128)S(1)} %bitcast.21, bf16[1,2048,512]{2,1,0:T(8,128)(2,1)S(1)} %copy-done.5, bf16[1,256,2048]{2,1,0:T(8,128)(2,1)S(1)} %copy-done.6), custom_call_target="tpu_custom_call" | custom-call | flops 3221225472 | bytes 12582912 | tf_op jit(solution)/shard_map/experts/expert_all/pallas_call | solution.py:299
  112.4 2.0 copy-done.3
  115.3 0.9 concatenate.10.pay_ref
  117.0 102.1 %pack_lanes.1 = (bf16[2,16,128,128]{3,2,1,0:T(8,128)(2,1)}, bf16[2,16,128,128]{3,2,1,0:T(8,128)(2,1)}, bf16[2,16,128,128]{3,2,1,0:T(8,128)(2,1)}, bf16[2,4,3328]...) custom-call(s32[8]{0:T(128)} %select_reduce_fusion.order_ref, ...), custom_call_target="tpu_custom_call" | custom-call | bytes 6291456 | tf_op jit(solution)/shard_map/send_states/pack_lanes/pallas_call | solution.py:167
  219.4 1.2 collective-permute-start.1
  221.6 1.2 collective-permute-start.4
  222.8 1.5 gather_fusion
  224.6 0.8 constant_dynamic-update-slice_fusion.2
  225.8 29.6 %collective-permute-done.4.rest_1_ = bf16[2,16,128,128]{3,2,1,0:T(8,128)(2,1)} collective-permute-done((bf16[2,16,128,128]{3,2,1,0:T(8,128)(2,1)}, bf16[2,16,128,128]{3,2,1,0:T(8,128)(2,1)}, u32[]{:S(2)}, u32[]{:S(2)}) %collective-permute-start.4) | collective-permute-done | bytes 1048608 | tf_op jit(solution)/shard_map/send_states/ppermute | solution.py:351
  255.5 22.1 %collective-permute-done.5.rest_2_ = bf16[2,16,128,128]{3,2,1,0:T(8,128)(2,1)S(1)} collective-permute-done((bf16[2,16,128,128]{3,2,1,0:T(8,128)(2,1)}, bf16[2,16,128,128]{3,2,1,0:T(8,128)(2,1)S(1)}, u32[]{:S(2)}, u32[]{:S(2)}) %collective-permute-start.5) | collective-permute-done | bytes 1048608 | tf_op jit(solution)/shard_map/send_states/ppermute | solution.py:351
  277.5 2.2 copy-done.2
  279.7 8.8 %landed_states.1 = bf16[8,16,128,128]{3,2,1,0:T(8,128)(2,1)} custom-call(s32[8]{0:T(128)S(1)} %copy-done.18, s32[8]{0:T(128)S(1)} %fusion.3.place_ref, bf16[8,16,128,128]{3,2,1,0:T(8,128)(2,1)S(1)} %copy-done.2, bf16[2,16,128,128]{3,2,1,0:T(8,128)(2,1)S(1)} %collective-permute-done.3.rest_0_, bf16[2,16,128,128]{3,2,1,0:T(8,128)(2,1)} %collective-permute-done.4.rest_1_, ...), custom_call_target="tpu_custom_call" | custom-call | flops 20000000 | bytes 9437184 | tf_op jit(solution)/shard_map/landed/landed_states/pallas_call | solution.py:246
  288.5 0.9 convert_bitcast_fusion
  289.5 0.9 add_convert_fusion
  290.5 0.7 reshape.49
  (70 shorter events, 4.3 us)
Async XLA Ops:
  7.2 30.4 %copy-start = (bf16[2048,512]{1,0:T(8,128)(2,1)S(1)}, bf16[2048,512]{1,0:T(8,128)(2,1)}, u32[]{:S(2)}) copy-start(bf16[2048,512]{1,0:T(8,128)(2,1)} %param.26) | copy-start | bytes 6291460
  7.2 95.0 %all-gather.4.cloned.1.call-start = ((), (), s32[]{:S(2)}) async-start(), calls=%async_computation.2 | async-start | bytes 4325376 | tf_op jit(solution)/shard_map/attention/all_gather | solution.py:372
  7.2 2.3 copy-start.1
  9.6 0.9 copy-start.7
  10.5 0.8 copy-start.9
  11.3 0.9 copy-start.11
  12.2 0.8 copy-start.12
  13.1 0.7 copy-start.13
  13.7 0.7 copy-start.15
  14.4 0.7 copy-start.19
  15.1 15.2 %copy-start.20 = (bf16[8,4,2048]{2,1,0:T(4,128)(2,1)S(1)}, bf16[8,4,2048]{2,1,0:T(4,128)(2,1)}, u32[]{:S(2)}) copy-start(bf16[8,4,2048]{2,1,0:T(4,128)(2,1)} %param.23) | copy-start | bytes 393220
  15.1 23.7 %copy-start.21 = (f32[8,4,10]{2,1,0:T(4,128)S(1)}, f32[8,4,10]{2,1,0:T(4,128)}, u32[]{:S(2)}) copy-start(f32[8,4,10]{2,1,0:T(4,128)} %param.25) | copy-start | bytes 3844
  15.1 23.9 %copy-start.22 = (s32[8,4,10]{2,1,0:T(4,128)S(1)}, s32[8,4,10]{2,1,0:T(4,128)}, u32[]{:S(2)}) copy-start(s32[8,4,10]{2,1,0:T(4,128)} %param.24) | copy-start | bytes 3844
  21.6 80.5 %copy-start.17 = (f32[2048]{0:T(1024)S(1)}, f32[2048]{0:T(1024)}, u32[]{:S(2)}) copy-start(f32[2048]{0:T(1024)} %param.28) | copy-start | bytes 24580
  38.7 250.8 %reduce-scatter.2.cloned.1.call-start = ((), (), s32[]{:S(2)}) async-start(), calls=%async_computation.1 | async-start | bytes 4325376 | tf_op jit(solution)/shard_map/experts/reduce_scatter | solution.py:377
  102.1 2.2 copy-start.4
  104.3 1.6 copy-start.5
  105.9 1.2 copy-start.6
  112.4 2.0 copy-start.3
  114.4 0.7 copy-start.23
  114.4 0.9 copy-start.8
  114.4 0.9 copy-start.10
  114.4 0.9 copy-start.14
  114.4 0.9 copy-start.16
  117.0 105.9 %copy-start.18 = (s32[8]{0:T(128)S(1)}, s32[8]{0:T(128)}, u32[]{:S(2)}) copy-start(s32[8]{0:T(128)} %select_reduce_fusion.order_ref) | copy-start | bytes 100
  219.1 5.3 %collective-permute-start = (bf16[2,4,3328]{2,1,0:T(4,128)(2,1)}, bf16[2,4,3328]{2,1,0:T(4,128)(2,1)}, u32[]{:S(2)}, u32[]{:S(2)}) collective-permute-start(bf16[2,4,3328]{2,1,0:T(4,128)(2,1)} %get-tuple-element.8), channel_id=1, source_target_pairs={{0,1},{1,0},{2,3},{3,2},{4,5},{5,4},{6,7},{7,6},{8,9},{9,8},{10,11... | collective-permute-start | bytes 159752 | tf_op jit(solution)/shard_map/send_states/ppermute | solution.py:351
  219.4 6.0 %collective-permute-start.1 = (bf16[2,4,3328]{2,1,0:T(4,128)(2,1)}, bf16[2,4,3328]{2,1,0:T(4,128)(2,1)S(1)}, u32[]{:S(2)}, u32[]{:S(2)}) collective-permute-start(bf16[2,4,3328]{2,1,0:T(4,128)(2,1)} %get-tuple-element.9), channel_id=1, source_target_pairs={{0,2},{1,3},{2,0},{3,1},{4,6},{5,7},{6,4},{7,5},{8,10},{9,11},{10,... | collective-permute-start | bytes 159752 | tf_op jit(solution)/shard_map/send_states/ppermute | solution.py:351
  220.7 4.8 %collective-permute-start.2 = (bf16[2,4,3328]{2,1,0:T(4,128)(2,1)}, bf16[2,4,3328]{2,1,0:T(4,128)(2,1)S(1)}, u32[]{:S(2)}, u32[]{:S(2)}) collective-permute-start(bf16[2,4,3328]{2,1,0:T(4,128)(2,1)} %get-tuple-element.10), channel_id=1, source_target_pairs={{0,3},{1,2},{2,1},{3,0},{4,7},{5,6},{6,5},{7,4},{8,11},{9,10},{10,... | collective-permute-start | bytes 159752 | tf_op jit(solution)/shard_map/send_states/ppermute | solution.py:351
  221.0 4.8 %collective-permute-start.3 = (bf16[2,16,128,128]{3,2,1,0:T(8,128)(2,1)}, bf16[2,16,128,128]{3,2,1,0:T(8,128)(2,1)S(1)}, u32[]{:S(2)}, u32[]{:S(2)}) collective-permute-start(bf16[2,16,128,128]{3,2,1,0:T(8,128)(2,1)} %get-tuple-element.11), channel_id=1, source_target_pairs={{0,1},{1,0},{2,3},{3,2},{4,5},{5,4},{6,7},{7,6},{8,9},{9,8},{10,11... | collective-permute-start | bytes 3145736 | tf_op jit(solution)/shard_map/send_states/ppermute | solution.py:351
  221.6 33.9 %collective-permute-start.4 = (bf16[2,16,128,128]{3,2,1,0:T(8,128)(2,1)}, bf16[2,16,128,128]{3,2,1,0:T(8,128)(2,1)}, u32[]{:S(2)}, u32[]{:S(2)}) collective-permute-start(bf16[2,16,128,128]{3,2,1,0:T(8,128)(2,1)} %get-tuple-element.12), channel_id=1, source_target_pairs={{0,2},{1,3},{2,0},{3,1},{4,6},{5,7},{6,4},{7,5},{8,10},{9,11},{10,... | collective-permute-start | bytes 3145736 | tf_op jit(solution)/shard_map/send_states/ppermute | solution.py:351
  224.4 53.1 %collective-permute-start.5 = (bf16[2,16,128,128]{3,2,1,0:T(8,128)(2,1)}, bf16[2,16,128,128]{3,2,1,0:T(8,128)(2,1)S(1)}, u32[]{:S(2)}, u32[]{:S(2)}) collective-permute-start(bf16[2,16,128,128]{3,2,1,0:T(8,128)(2,1)} %get-tuple-element.13), channel_id=1, source_target_pairs={{0,3},{1,2},{2,1},{3,0},{4,7},{5,6},{6,5},{7,4},{8,11},{9,10},{10,... | collective-permute-start | bytes 3145736 | tf_op jit(solution)/shard_map/send_states/ppermute | solution.py:351
  277.5 2.2 copy-start.2
Sparse Core Ops, SparseCore 0:
  38.9 63.2 all-gather.3
  114.5 140.0 reduce-scatter.1

commit v2 on v1

v2 whole, which is shorter than its diff:
```python
import functools

import jax
import jax.numpy as jnp
from jax import lax
from jax.experimental import pallas as pl
from jax.experimental.pallas import tpu as pltpu
from jax.sharding import PartitionSpec as P

EPS = 1e-06
F32 = jnp.float32
BF16 = jnp.bfloat16
MIB = 1 << 20


def row_sum(x):
    return jnp.sum(x, axis=-1, keepdims=True)


def spread_rows(ref, scratch, requests, steps):
    for r in range(requests):
        split_heads(ref[r].astype(F32), scratch, r, steps)


def split_heads(values, scratch, r, steps):
    hd = scratch.shape[-1]
    for h in range(scratch.shape[0]):
        scratch[h, r * steps : (r + 1) * steps, :] = values[:, h * hd : (h + 1) * hd]


def at_step(scratch, t, requests, steps, head=None):
    if head is None:
        return scratch[pl.ds(t, requests, stride=steps), :]
    return scratch[head, pl.ds(t, requests, stride=steps), :]


def recurrence(kh, repeats, steps, requests, hd, k_s, q_s, v_s, a_s, b_s, m_s, emit_out, emit_state):
    per = m_s.shape[1] // requests
    ks = [at_step(k_s, t, requests, steps, kh) for t in range(steps)]
    rk = [lax.rsqrt(row_sum(k * k) + EPS) for k in ks]
    kn = [k * r for k, r in zip(ks, rk)]
    kk = {(i, t): row_sum(kn[i] * kn[t]) for t in range(steps) for i in range(t)}
    if emit_out is not None:
        qs = [at_step(q_s, t, requests, steps, kh) for t in range(steps)]
        rq = [lax.rsqrt(row_sum(q * q) + EPS) * hd**-0.5 for q in qs]
        qn = [q * r for q, r in zip(qs, rq)]
        kq = {(i, t): row_sum(kn[i] * qn[t]) for t in range(steps) for i in range(t + 1)}
    for h in range(kh * repeats, (kh + 1) * repeats):
        decayed = []
        c = None
        for t in range(steps):
            a = at_step(a_s, t, requests, steps)[:, h : h + 1]
            b = at_step(b_s, t, requests, steps)[:, h : h + 1]
            decayed = [w * a for w in decayed]
            c = a if c is None else c * a
            m = (c * rk[t]) * at_step(m_s, t, requests, per, h)
            for i in range(t):
                m = m + kk[i, t] * decayed[i]
            decayed.append((at_step(v_s, t, requests, steps, h) - m) * b)
            if emit_out is not None:
                o = (c * rq[t]) * at_step(m_s, steps + t, requests, per, h)
                for i in range(t + 1):
                    o = o + kq[i, t] * decayed[i]
                emit_out(t, h, o)
        if emit_state is not None:
            emit_state(h, c, [w * r for w, r in zip(decayed, rk)])


def sigmoid_rows(ref, scratch, requests, steps):
    for r in range(requests):
        scratch[r * steps : (r + 1) * steps, : ref.shape[-1]] = jax.nn.sigmoid(ref[r].astype(F32))


def core_kernel(
    lanes, order_ref, home_ref,
    state_ref, q_ref, k_ref, v_ref, g_ref, b_ref, a_ref, gain_ref, out_ref, *rest,
):
    packed, pays = rest[: lanes - 1], rest[lanes - 1 : 2 * lanes - 1]
    k_s, q_s, v_s, g_s, a_s, b_s, m_s, o_s = rest[2 * lanes - 1 :]
    i = pl.program_id(0)
    r = order_ref[i]
    requests, steps, key_width = k_ref.shape
    heads, hd = state_ref.shape[1], state_ref.shape[-1]
    value_width = v_ref.shape[-1]
    key_heads = key_width // hd
    repeats = heads // key_heads
    cap = requests // lanes
    rows = jnp.concatenate([k_ref[r].astype(F32), q_ref[r].astype(F32)], axis=0).astype(BF16)
    base = pl.multiple_of(r * 2 * steps, 2 * steps)
    for h in range(heads):
        kh = h // repeats
        m_s[h, pl.ds(base, 2 * steps), :] = jnp.dot(
            rows[:, kh * hd : (kh + 1) * hd], state_ref[0, h], preferred_element_type=F32
        )
    home = jnp.full((steps, 128), home_ref[i].astype(F32), F32).astype(BF16)
    for d in range(lanes):

        @pl.when(i // cap == d)
        def _():
            if d:
                packed[d - 1][...] = state_ref[...]
            pay = pays[d]
            pay[0, :, :key_width] = k_ref[r]
            pay[0, :, key_width : key_width + value_width] = v_ref[r]
            tail = key_width + value_width
            pay[0, :, tail : tail + heads] = a_ref[r]
            pay[0, :, tail + 128 : tail + 128 + heads] = b_ref[r]
            pay[0, :, tail + 256 : tail + 384] = home

    @pl.when(i == requests - 1)
    def _():
        spread_rows(k_ref, k_s, requests, steps)
        spread_rows(q_ref, q_s, requests, steps)
        spread_rows(v_ref, v_s, requests, steps)
        spread_rows(g_ref, g_s, requests, steps)
        sigmoid_rows(a_ref, a_s, requests, steps)
        sigmoid_rows(b_ref, b_s, requests, steps)
        gain = gain_ref[...]

        def emit(t, h, o):
            gate = at_step(g_s, t, requests, steps, h)
            scaled = o * lax.rsqrt(row_sum(o * o) * (1.0 / hd) + EPS)
            o_s[h, pl.ds(t, requests, stride=steps), :] = scaled * gain * jax.nn.silu(gate)

        for kh in range(key_heads):
            recurrence(kh, repeats, steps, requests, hd, k_s, q_s, v_s, a_s, b_s, m_s, emit, None)
        for h in range(heads):
            out_ref[:, h * hd : (h + 1) * hd] = o_s[h].astype(BF16)


def core_rows(
    order, home, lanes, states, query_rows, key_rows, value_rows, gate_rows, beta_logit, decay_logit, core_gain
):
    requests, heads, hd, _ = states.shape
    steps = key_rows.shape[1]
    kw, vw = key_rows.shape[-1], value_rows.shape[-1]
    cap = requests // lanes
    pay_width = kw + vw + 384
    whole = lambda x: pl.BlockSpec(x.shape, lambda i, *_: (0,) * x.ndim)
    tokens = requests * steps
    gain = core_gain.reshape(1, hd)
    small = (query_rows, key_rows, value_rows, gate_rows, beta_logit, decay_logit, gain)
    slot = lambda d: lambda i, *_: jnp.clip(i - d * cap, 0, cap - 1)
    state_out = lambda d: pl.BlockSpec((1, heads, hd, hd), lambda i, *_: (slot(d)(i), 0, 0, 0))
    pay_out = lambda d: pl.BlockSpec((1, steps, pay_width), lambda i, *_: (slot(d)(i), 0, 0))
    outs = pl.pallas_call(
        functools.partial(core_kernel, lanes),
        grid_spec=pltpu.PrefetchScalarGridSpec(
            num_scalar_prefetch=2,
            grid=(requests,),
            in_specs=[pl.BlockSpec((1, heads, hd, hd), lambda i, order, home: (order[i], 0, 0, 0))]
            + [whole(x) for x in small],
            out_specs=[pl.BlockSpec((tokens, vw), lambda i, *_: (0, 0))]
            + [state_out(d) for d in range(1, lanes)]
            + [pay_out(d) for d in range(lanes)],
            scratch_shapes=[
                pltpu.VMEM((kw // hd, tokens, hd), F32),
                pltpu.VMEM((kw // hd, tokens, hd), F32),
                pltpu.VMEM((heads, tokens, hd), F32),
                pltpu.VMEM((heads, tokens, hd), F32),
                pltpu.VMEM((tokens, 128), F32),
                pltpu.VMEM((tokens, 128), F32),
                pltpu.VMEM((heads, 2 * tokens, hd), F32),
                pltpu.VMEM((heads, tokens, hd), F32),
            ],
        ),
        out_shape=[jax.ShapeDtypeStruct((tokens, vw), BF16)]
        + [jax.ShapeDtypeStruct((cap, heads, hd, hd), BF16)] * (lanes - 1)
        + [jax.ShapeDtypeStruct((cap, steps, pay_width), BF16)] * lanes,
        compiler_params=pltpu.CompilerParams(vmem_limit_bytes=60 * MIB),
        cost_estimate=pl.CostEstimate(flops=20_000_000, bytes_accessed=8 * MIB, transcendentals=100_000),
        name="core_rows",
    )(order, home, states, *small)
    return outs[0], outs[1:lanes], outs[lanes:]


def state_kernel(lanes, kw, vw, heads, order_ref, place_ref, own_ref, *rest):
    sources = (own_ref,) + rest[: lanes - 1]
    pays, out_ref = rest[lanes - 1 : 2 * lanes - 1], rest[2 * lanes - 1]
    k_s, v_s, a_s, b_s, m_s, u_s, c_s, held, ready, in_sem, out_sem = rest[2 * lanes :]
    requests = held.shape[0]
    steps = pays[0].shape[1]
    hd = held.shape[-1]
    repeats = heads // (kw // hd)
    cap = requests // lanes
    copies = []
    for r in range(requests):
        d, j = divmod(r, cap)
        source = own_ref.at[order_ref[j]] if d == 0 else sources[d].at[j]
        copies.append(pltpu.make_async_copy(source, held.at[r], in_sem.at[r]))
        copies[-1].start()
    for r in range(requests):
        rows = slice(r * steps, (r + 1) * steps)
        pay = pays[r // cap][r % cap].astype(F32)
        split_heads(pay[:, :kw], k_s, r, steps)
        split_heads(pay[:, kw : kw + vw], v_s, r, steps)
        a_s[rows, :] = jax.nn.sigmoid(pay[:, kw + vw : kw + vw + 128])
        b_s[rows, :] = jax.nn.sigmoid(pay[:, kw + vw + 128 : kw + vw + 256])
    for r in range(requests):
        copies[r].wait()
        rows = slice(r * steps, (r + 1) * steps)
        for h in range(heads):
            m_s[h, rows, :] = jnp.dot(
                k_s[h // repeats, rows, :].astype(BF16), held[r, h], preferred_element_type=F32
            )

    def emit(h, c, updates):
        c_s[h] = jnp.broadcast_to(c, (requests, hd))
        for t, u in enumerate(updates):
            u_s[h, pl.ds(t, requests, stride=steps), :] = u

    for kh in range(kw // hd):
        recurrence(kh, repeats, steps, requests, hd, k_s, None, v_s, a_s, b_s, m_s, None, emit)
    sent = []
    for r in range(requests):
        slot = r % 2
        if r >= 2:
            sent[r - 2].wait()
        rows = slice(r * steps, (r + 1) * steps)
        for h in range(heads):
            k4 = k_s[h // repeats, rows, :]
            k8 = jnp.concatenate([k4, k4], axis=0).astype(BF16)
            u4 = u_s[h, rows, :]
            high = u4.astype(BF16).astype(F32)
            u8 = jnp.concatenate([high, u4 - high], axis=0).astype(BF16)
            added = lax.dot_general(
                k8, u8, (((0,), (0,)), ((), ())), preferred_element_type=F32
            )
            kept = held[r, h].astype(F32) * c_s[h, r : r + 1, :]
            ready[slot, h] = (kept + added).astype(BF16)
        sent.append(pltpu.make_async_copy(ready.at[slot], out_ref.at[place_ref[r]], out_sem.at[slot]))
        sent[-1].start()
    for c in sent[-2:]:
        c.wait()


def landed_states(order, place, own, arrived, pays, kw, vw):
    requests, heads, hd, _ = own.shape
    steps = pays[0].shape[1]
    lanes = len(pays)
    tokens = requests * steps
    hbm = pl.BlockSpec(memory_space=pl.ANY)
    smem = pl.BlockSpec(memory_space=pltpu.SMEM)
    return pl.pallas_call(
        functools.partial(state_kernel, lanes, kw, vw, heads),
        in_specs=[smem, smem, hbm] + [hbm] * len(arrived) + [pl.BlockSpec(memory_space=pltpu.VMEM)] * lanes,
        out_specs=hbm,
        out_shape=jax.ShapeDtypeStruct(own.shape, BF16),
        scratch_shapes=[
            pltpu.VMEM((kw // hd, tokens, hd), F32),
            pltpu.VMEM((heads, tokens, hd), F32),
            pltpu.VMEM((tokens, 128), F32),
            pltpu.VMEM((tokens, 128), F32),
            pltpu.VMEM((heads, tokens, hd), F32),
            pltpu.VMEM((heads, tokens, hd), F32),
            pltpu.VMEM((heads, requests, hd), F32),
            pltpu.VMEM(own.shape, BF16),
            pltpu.VMEM((2, heads, hd, hd), BF16),
            pltpu.SemaphoreType.DMA((requests,)),
            pltpu.SemaphoreType.DMA((2,)),
        ],
        compiler_params=pltpu.CompilerParams(vmem_limit_bytes=40 * MIB),
        cost_estimate=pl.CostEstimate(flops=20_000_000, bytes_accessed=9 * MIB, transcendentals=10_000),
        name="landed_states",
    )(order, place, own, *arrived, *pays)


def expert_kernel(sides, own_out, where_ref, *rest):
    pieces = rest[: 2 * sides]
    weight_ref, gain_ref, up_ref, down_ref = rest[2 * sides : 2 * sides + 4]
    keeps = rest[2 * sides + 4 : 3 * sides + 4]
    give_ref = rest[3 * sides + 4]
    result_s = rest[-1]
    spans, group_rows, cols = pieces[0].shape
    tokens = give_ref.shape[2]
    width = down_ref.shape[-1]
    hidden_units = down_ref.shape[1]
    e = where_ref[0]
    blocks = [(x, c) for x in range(spans) for c in range(2)]
    values = {}
    for x, c in blocks:
        parts = [pieces[2 * y + c][x] for y in range(sides)]
        values[x, c] = jnp.concatenate(parts, axis=0).astype(F32)
    total = sum(row_sum(values[b] * values[b]) for b in blocks)
    scale = lax.rsqrt(total * (1.0 / width) + EPS)
    joined = None
    for x, c in blocks:
        block = e ^ (2 * x + c)
        normed = (values[x, c] * scale * gain_ref[pl.ds(block, 1), :]).astype(BF16)
        up = up_ref[0, pl.ds(pl.multiple_of(block * cols, cols), cols), :]
        term = jnp.dot(normed, up, preferred_element_type=F32)
        joined = term if joined is None else joined + term
        if own_out:
            rest[3 * sides + 5][:, pl.ds(pl.multiple_of(block * cols, cols), cols)] = pieces[c][
                x, pl.ds(pl.multiple_of(e * tokens, tokens), tokens), :
            ]
    active = (jax.nn.silu(joined[:, :hidden_units]) * joined[:, hidden_units:]).astype(BF16)
    result = jnp.dot(active, down_ref[0], preferred_element_type=F32).astype(BF16)
    eye = lax.broadcasted_iota(jnp.int32, (group_rows, group_rows), 0) == lax.broadcasted_iota(
        jnp.int32, (group_rows, group_rows), 1
    )
    weights = []
    for y in range(sides):
        line = weight_ref[pl.ds(where_ref[1 + y], 1), :]
        weights.append(row_sum(jnp.where(eye, jnp.broadcast_to(line, eye.shape), 0.0)))
    result_s[...] = (result.astype(F32) * jnp.concatenate(weights, axis=0)).astype(BF16)
    for y in range(sides):
        for x in range(spans):
            for c in range(2):
                start = y * group_rows + (e ^ (2 * x + c)) * tokens
                rows = result_s[pl.ds(pl.multiple_of(start, tokens), tokens), :]
                if c:
                    give_ref[y, x] = rows
                else:
                    keeps[y][x] = rows


def expert_chunk(where, pieces, weights, gain, gate_up, down_weight, tokens, own_out):
    sides = len(pieces) // 2
    spans, group_rows, cols = pieces[0].shape
    width = down_weight.shape[-1]
    vmem = pl.BlockSpec(memory_space=pltpu.VMEM)
    keep = jax.ShapeDtypeStruct((spans, tokens, width), BF16)
    give = jax.ShapeDtypeStruct((sides, spans, tokens, width), BF16)
    own = [jax.ShapeDtypeStruct((tokens, width), BF16)] if own_out else []
    rows = sides * group_rows
    outs = pl.pallas_call(
        functools.partial(expert_kernel, sides, own_out),
        in_specs=[pl.BlockSpec(memory_space=pltpu.SMEM)] + [vmem] * (len(pieces) + 4),
        out_specs=[vmem] * (sides + 1 + len(own)),
        out_shape=[keep] * sides + [give] + own,
        scratch_shapes=[pltpu.VMEM((rows, width), BF16)],
        compiler_params=pltpu.CompilerParams(vmem_limit_bytes=32 * MIB),
        cost_estimate=pl.CostEstimate(
            flops=6 * rows * width * down_weight.shape[1], bytes_accessed=6 * MIB, transcendentals=0
        ),
        name="expert_chunk",
    )(where, *pieces, weights, gain, gate_up, down_weight)
    return outs


def swap(x, axis, d):
    size = lax.axis_size(axis)
    return lax.ppermute(x, axis, [(i, i ^ d) for i in range(size)])


def summed(*terms):
    return functools.reduce(lambda p, q: p + q, [t.astype(F32) for t in terms])


def shards(
    states, query_rows, key_rows, value_rows, gate_rows, beta_logit, decay_logit, residual,
    route_ids, route_prob, out_weight, core_gain, moe_gain, gate_up, down_weight, new_home,
):
    requests, heads, hd, _ = states.shape
    steps = query_rows.shape[1]
    width = residual.shape[-1]
    tokens = requests * steps
    lanes = lax.axis_size("ep")
    groups = lax.axis_size("dp")
    my_lane = lax.axis_index("ep")
    my_group = lax.axis_index("dp")
    cap = requests // lanes
    kw, vw = key_rows.shape[-1], value_rows.shape[-1]
    top = route_ids.shape[-1]

    with jax.named_scope("order"):
        lane = (new_home // requests % lanes) ^ my_lane
        ids = jnp.arange(requests, dtype=jnp.int32)
        earlier = (lane[:, None] == lane[None, :]) & (ids[None, :] < ids[:, None])
        slot = lane * cap + jnp.sum(earlier.astype(jnp.int32), axis=1)
        placed = slot[:, None] == ids[None, :]
        order = jnp.sum(jnp.where(placed, ids[:, None], 0), axis=0)
        home = jnp.sum(jnp.where(placed, new_home[:, None] % requests, 0), axis=0)

    with jax.named_scope("routes"):
        weights = route_prob.reshape(tokens, top)
        weights = weights / jnp.sum(weights, -1, keepdims=True)
        named = route_ids.reshape(tokens, top)[None] == jnp.arange(groups * lanes, dtype=jnp.int32)[:, None, None]
        weights = jnp.sum(jnp.where(named, weights[None], 0.0), axis=-1)
        weights = lax.all_to_all(weights, ("dp", "ep"), split_axis=0, concat_axis=0, tiled=True)
        weights = weights.reshape(groups, lanes * tokens)

    with jax.named_scope("core"):
        group_residual = lax.all_gather(residual.reshape(tokens, width), "ep", axis=0, tiled=True)
        core, packed, pays = core_rows(
            order, home, lanes, states, query_rows, key_rows, value_rows, gate_rows, beta_logit,
            decay_logit, core_gain,
        )
        core, group_residual, weights = lax.optimization_barrier((core, group_residual, weights))
        group_core = lax.all_gather(core, "ep", axis=0, tiled=True)
    with jax.named_scope("attention"):
        cols = out_weight.shape[1]
        attention = jnp.dot(group_core, out_weight, preferred_element_type=F32).astype(BF16)
        before = lax.dynamic_slice_in_dim(group_residual, my_lane * cols, cols, axis=1)
        hidden_cols = (before.astype(F32) + attention.astype(F32)).astype(BF16)
        held = jnp.stack([hidden_cols] + [swap(hidden_cols, "ep", d) for d in range(2, lanes, 2)])
        held, packed, pays = lax.optimization_barrier((held, packed, pays))

    with jax.named_scope("send_states"):
        arrived = [swap(packed[d - 1], "ep", d) for d in range(1, lanes)]
        arrived_pays = [pays[0]] + [swap(pays[d], "ep", d) for d in range(1, lanes)]

    gain = moe_gain.reshape(lanes, cols)
    sums = []
    own_rows = None
    for d in range(0, groups, 2):
        with jax.named_scope("tokens"):
            near = swap(held, "dp", d) if d else held
            across = swap(near, "dp", 1)
            pieces = [near, swap(near, "ep", 1), across, swap(across, "ep", 1)]
        with jax.named_scope("experts"):
            where = jnp.stack([my_lane, my_group ^ d, my_group ^ d ^ 1])
            outs = expert_chunk(where, pieces, weights, gain, gate_up, down_weight, tokens, d == 0)
            keep_near, keep_across, give = outs[:3]
            if d == 0:
                own_rows = outs[3]
        with jax.named_scope("way_back"):
            got = swap(give, "ep", 1)
            back = swap(summed(keep_across, got[1]).astype(BF16), "dp", 1)
            chunk = summed(keep_near, got[0], back)
            sums.append(swap(chunk.astype(BF16), "dp", d) if d else chunk)
    with jax.named_scope("mixed"):
        mixed = summed(own_rows, *[s[0] for s in sums])
        for x in range(1, lanes // 2):
            mixed = mixed + swap(summed(*[s[x] for s in sums]).astype(BF16), "ep", 2 * x).astype(F32)
        mixed_out = mixed.astype(BF16)

    with jax.named_scope("landed"):
        place = jnp.concatenate([p[:, 0, kw + vw + 256] for p in arrived_pays]).astype(jnp.int32)
        moved_out = landed_states(order, place, states, arrived, arrived_pays, kw, vw)
    return mixed_out.reshape(requests, steps, width), moved_out


def solution(mesh):
    row = P(("dp", "ep"), None, None)
    placed = (P(("dp", "ep"), None, None, None),) + (row,) * 9 + (
        P(None, "ep"), P(), P(), row, row, P(("dp", "ep")),
    )
    return jax.shard_map(
        shards,
        mesh=mesh,
        in_specs=placed,
        out_specs=(row, P(("dp", "ep"), None, None, None)),
        check_vma=False,
    )
```

time: 299 us -> 172 us (0.58)
  Pallas kernels: 123 us -> 32.2 us
  blocking collectives: 58.6 us -> 15.4 us
  starting transfers between devices: 3.97 us -> 40.6 us
  local copies, waits for them, and re-layouts: 22.5 us -> 5.34 us
  between operations: 14.3 us -> 0.96 us
    pallas_call x4 -> x6, Pallas kernels: 123 us -> 32.2 us  [the longest x1 13.1 us: core_rows(): pl.pallas_call(functools.partial(core_kernel, lanes), grid_spec=pltpu.Pre...]
    all_gather x1 -> x0, blocking collectives: 42.7 us -> none  [shards(): routes = lax.all_gather(routes, ('dp', 'ep'), axis=0, tiled=True)]
    ppermute x6 -> x34, starting transfers between devices: 3.89 us -> 33.3 us  [swap(): return lax.ppermute(x, axis, [(i, i ^ d) for i in range(size)])]
    all_gather x1 -> x0, waiting for transfers between devices: 19.9 us -> none  [shards(): gathered = lax.all_gather(hidden_cols, ('dp', 'ep'), axis=0, tiled=False)]
    ppermute x6 -> x34, waiting for transfers between devices: 51.7 us -> 69.7 us  [swap(): return lax.ppermute(x, axis, [(i, i ^ d) for i in range(size)])]
    unnamed x52 -> x26, local copies, waits for them, and re-layouts: 18.8 us -> 1.64 us
    all_to_all x0 -> x1, starting transfers between devices: none -> 7.3 us  [shards(): lax.all_to_all(weights, ('dp', 'ep'), split_axis=0, concat_axis=0, tiled=...]
  transfers between devices with their start and end apart: 8 -> 35, of which waited for: 3 -> 14; matrix products, arithmetic and copies ran while one was open for 2% -> 2% of each run, Pallas kernels for 37% -> 19%
where the time goes in v2:
time: 172 us
  waiting for transfers between devices  69.7 us (41%)
  starting transfers between devices  40.6 us (24%)
  Pallas kernels  32.2 us (19%)
  blocking collectives  15.4 us (9%)
  other arithmetic  6 us (3%)
  local copies, waits for them, and re-layouts  5.34 us (3%)
    ppermute x34, waiting for transfers between devices, swap(): return lax.ppermute(x, axis, [(i, i ^ d) for i in range(size)])  69.7 us
    ppermute x34, starting transfers between devices, swap(): return lax.ppermute(x, axis, [(i, i ^ d) for i in range(size)])  33.3 us
    pallas_call x1, Pallas kernels, core_rows(): pl.pallas_call(functools.partial(core_kernel, lanes), grid_spec=pltpu.Pre...  13.1 us
    pallas_call x4, Pallas kernels, expert_chunk(): pl.pallas_call(functools.partial(expert_kernel, sides, own_out), in_specs...  10 us
    pallas_call x1, Pallas kernels, landed_states(): pl.pallas_call(functools.partial(state_kernel, lanes, kw, vw, heads), in_...  9.07 us
    all_gather x1, blocking collectives, shards(): lax.all_gather(residual.reshape(tokens, width), 'ep', axis=0, tiled=True)  7.94 us
    all_gather x1, blocking collectives, shards(): group_core = lax.all_gather(core, 'ep', axis=0, tiled=True)  7.49 us
    all_to_all x1, starting transfers between devices, shards(): lax.all_to_all(weights, ('dp', 'ep'), split_axis=0, concat_axis=0, tiled=...  7.3 us
  transfers between devices with their start and end apart: 35, of which 14 were waited for; matrix products, arithmetic and copies ran while one was open for 2% of the time, Pallas kernels for 19%

profile of v2, /device:TPU:0, one launch (start us, length us, event | category | flops | bytes accessed | tf_op | source)
XLA Modules:
  0.0 171.5 jit_solution(1948746927257417257)
XLA Ops:
  4.0 7.3 %all-to-all-start = ((f32[32,1,32]{2,1,0:T(1,128)}), f32[32,1,32]{2,1,0:T(1,128)S(1)}, u32[]{:S(2)}, u32[]{:S(2)}) async-start(f32[32,1,32]{2,1,0:T(1,128)} %bitcast.7), calls=%async_computation | async-start | bytes 32768 | tf_op jit(solution)/shard_map/routes/all_to_all | solution.py:381
  13.1 7.9 %all_gather.6 = bf16[128,2048]{1,0:T(8,128)(2,1)} all-gather(bf16[32,2048]{1,0:T(8,128)(2,1)S(1)} %reshape.88), channel_id=1, replica_groups=mesh['dp'=8,'ep'=4] {'ep'}, dimensions={0}, use_global_device_ids=true | all-gather | bytes 655360 | tf_op jit(solution)/shard_map/core/all_gather | solution.py:385
  21.7 13.1 %core_rows.1 = (bf16[32,2048]{1,0:T(8,128)(2,1)}, bf16[2,16,128,128]{3,2,1,0:T(8,128)(2,1)}, bf16[2,16,128,128]{3,2,1,0:T(8,128)(2,1)}, bf16[2,16,128,128]{3,2,1...) custom-call(s32[8]{0:T(128)} %get-tuple-element.67.order_ref, ...), custom_call_target="tpu_custom_call" | custom-call | flops 20000000 | bytes 8388608 | tf_op jit(solution)/shard_map/core/core_rows/pallas_call | solution.py:146
  36.4 7.5 %all_gather.7 = bf16[128,2048]{1,0:T(8,128)(2,1)S(1)} all-gather(bf16[32,2048]{1,0:T(8,128)(2,1)} %get-tuple-element.36), channel_id=1, replica_groups=mesh['dp'=8,'ep'=4] {'ep'}, dimensions={0}, use_global_device_ids=true | all-gather | bytes 655360 | tf_op jit(solution)/shard_map/core/all_gather | solution.py:391
  45.2 1.4 collective-permute-start
  46.6 4.4 %collective-permute-done = bf16[128,512]{1,0:T(8,128)(2,1)S(1)} collective-permute-done((bf16[128,512]{1,0:T(8,128)(2,1)S(1)}, bf16[128,512]{1,0:T(8,128)(2,1)S(1)}, u32[]{:S(2)}, u32[]{:S(2)}) %collective-permute-start) | collective-permute-done | bytes 131104 | tf_op jit(solution)/shard_map/attention/ppermute | solution.py:344
  51.1 1.5 collective-permute-start.2
  52.6 3.3 %collective-permute-start.20 = (bf16[2,128,512]{2,1,0:T(8,128)(2,1)S(1)}, bf16[2,128,512]{2,1,0:T(8,128)(2,1)}, u32[]{:S(2)}, u32[]{:S(2)}) collective-permute-start(bf16[2,128,512]{2,1,0:T(8,128)(2,1)S(1)} %pad_maximum_fusion.rest_0_), channel_id=1, source_target_pairs={{0,24},{4,28},{8,16},{12,20},{16,8},{20,12},{24,0},{28,4},{1,25},{... | collective-permute-start | bytes 786440 | tf_op jit(solution)/shard_map/tokens/ppermute | solution.py:344
  55.9 1.5 collective-permute-start.30
  57.5 2.2 %collective-permute-done.30.rest_6_ = bf16[2,4,3456]{2,1,0:T(4,128)(2,1)S(1)} collective-permute-done((bf16[2,4,3456]{2,1,0:T(4,128)(2,1)}, bf16[2,4,3456]{2,1,0:T(4,128)(2,1)S(1)}, u32[]{:S(2)}, u32[]{:S(2)}) %collective-permute-start.30) | collective-permute-done | bytes 55328 | tf_op jit(solution)/shard_map/send_states/ppermute | solution.py:344
  61.0 2.7 %collective-permute-done.20.rest_0_ = bf16[2,128,512]{2,1,0:T(8,128)(2,1)} collective-permute-done((bf16[2,128,512]{2,1,0:T(8,128)(2,1)S(1)}, bf16[2,128,512]{2,1,0:T(8,128)(2,1)}, u32[]{:S(2)}, u32[]{:S(2)}) %collective-permute-start.20) | collective-permute-done | bytes 262176 | tf_op jit(solution)/shard_map/tokens/ppermute | solution.py:344
  64.5 13.3 %collective-permute-done.13.rest_0_ = bf16[2,128,512]{2,1,0:T(8,128)(2,1)} collective-permute-done((bf16[2,128,512]{2,1,0:T(8,128)(2,1)S(1)}, bf16[2,128,512]{2,1,0:T(8,128)(2,1)}, u32[]{:S(2)}, u32[]{:S(2)}) %collective-permute-start.13) | collective-permute-done | bytes 262176 | tf_op jit(solution)/shard_map/tokens/ppermute | solution.py:344
  78.5 1.5 collective-permute-start.29
  80.0 1.5 collective-permute-start.8
  81.5 1.6 copy-done.1
  83.1 2.7 %expert_chunk.4 = (bf16[2,32,2048]{2,1,0:T(8,128)(2,1)S(1)}, bf16[2,32,2048]{2,1,0:T(8,128)(2,1)S(1)}, bf16[2,2,32,2048]{3,2,1,0:T(8,128)(2,1)S(1)}, bf16[32,2048]{1,0:T(8,128)(2,1)S(1)}) custom-call(s32[3]{0:T(128)S(1)} %pad_add_fusion.where_ref, bf16[2,128,512]{2,1,0:T(8,128)(2,1)S(1)} %pad_maximum_fusion.rest_0_, ...), custom_call_target="tpu_custom_call" | custom-call | flops 805306368 | bytes 6291456 | tf_op jit(solution)/shard_map/experts/expert_chunk/pallas_call | solution.py:327
  87.4 3.5 %collective-permute-done.8.rest_2_ = bf16[2,128,512]{2,1,0:T(8,128)(2,1)S(1)} collective-permute-done((bf16[2,128,512]{2,1,0:T(8,128)(2,1)}, bf16[2,128,512]{2,1,0:T(8,128)(2,1)S(1)}, u32[]{:S(2)}, u32[]{:S(2)}) %collective-permute-start.8) | collective-permute-done | bytes 262176 | tf_op jit(solution)/shard_map/tokens/ppermute | solution.py:344
  91.6 2.6 %expert_chunk.7 = (bf16[2,32,2048]{2,1,0:T(8,128)(2,1)S(1)}, bf16[2,32,2048]{2,1,0:T(8,128)(2,1)S(1)}, bf16[2,2,32,2048]{3,2,1,0:T(8,128)(2,1)S(1)}) custom-call(s32[3]{0:T(128)S(1)} %pad_add_fusion.3.where_ref, bf16[2,128,512]{2,1,0:T(8,128)(2,1)} %collective-permute-done.20.rest_0_, bf16[2,128,512]{2,1,0:T(8,128)(2,1)S(1)} %collective-permute-done.21.rest_1_, ...), custom_call_target="tpu_custom_call" | custom-call | flops 805306368 | bytes 6291456 | tf_op jit(solution)/shard_map/experts/expert_chunk/pallas_call | solution.py:327
  94.3 1.5 collective-permute-start.32
  95.8 2.4 %expert_chunk.6 = (bf16[2,32,2048]{2,1,0:T(8,128)(2,1)S(1)}, bf16[2,32,2048]{2,1,0:T(8,128)(2,1)S(1)}, bf16[2,2,32,2048]{3,2,1,0:T(8,128)(2,1)S(1)}) custom-call(s32[3]{0:T(128)S(1)} %pad_add_fusion.2.where_ref, bf16[2,128,512]{2,1,0:T(8,128)(2,1)} %collective-permute-done.13.rest_0_, bf16[2,128,512]{2,1,0:T(8,128)(2,1)S(1)} %collective-permute-done.14.rest_1_, ...), custom_call_target="tpu_custom_call" | custom-call | flops 805306368 | bytes 6291456 | tf_op jit(solution)/shard_map/experts/expert_chunk/pallas_call | solution.py:327
  99.0 2.4 %expert_chunk.5 = (bf16[2,32,2048]{2,1,0:T(8,128)(2,1)S(1)}, bf16[2,32,2048]{2,1,0:T(8,128)(2,1)S(1)}, bf16[2,2,32,2048]{3,2,1,0:T(8,128)(2,1)S(1)}) custom-call(s32[3]{0:T(128)S(1)} %pad_add_fusion.1.where_ref, bf16[2,128,512]{2,1,0:T(8,128)(2,1)} %collective-permute-done.6.rest_0_, bf16[2,128,512]{2,1,0:T(8,128)(2,1)S(1)} %collective-permute-done.7.rest_1_, ...), custom_call_target="tpu_custom_call" | custom-call | flops 805306368 | bytes 6291456 | tf_op jit(solution)/shard_map/experts/expert_chunk/pallas_call | solution.py:327
  104.1 1.4 collective-permute-start.25
  105.6 11.7 %collective-permute-done.25 = bf16[2,32,2048]{2,1,0:T(8,128)(2,1)S(1)} collective-permute-done((bf16[2,32,2048]{2,1,0:T(8,128)(2,1)S(1)}, bf16[2,32,2048]{2,1,0:T(8,128)(2,1)S(1)}, u32[]{:S(2)}, u32[]{:S(2)}) %collective-permute-start.25) | collective-permute-done | bytes 262176 | tf_op jit(solution)/shard_map/way_back/ppermute | solution.py:344
  117.9 6.9 %collective-permute-done.18 = bf16[2,32,2048]{2,1,0:T(8,128)(2,1)S(1)} collective-permute-done((bf16[2,32,2048]{2,1,0:T(8,128)(2,1)S(1)}, bf16[2,32,2048]{2,1,0:T(8,128)(2,1)S(1)}, u32[]{:S(2)}, u32[]{:S(2)}) %collective-permute-start.18) | collective-permute-done | bytes 262176 | tf_op jit(solution)/shard_map/way_back/ppermute | solution.py:344
  125.5 6.0 %collective-permute-done.11 = bf16[2,32,2048]{2,1,0:T(8,128)(2,1)S(1)} collective-permute-done((bf16[2,32,2048]{2,1,0:T(8,128)(2,1)S(1)}, bf16[2,32,2048]{2,1,0:T(8,128)(2,1)S(1)}, u32[]{:S(2)}, u32[]{:S(2)}) %collective-permute-start.11) | collective-permute-done | bytes 262176 | tf_op jit(solution)/shard_map/way_back/ppermute | solution.py:344
  131.5 1.7 %collective-permute-start.26 = (bf16[2,32,2048]{2,1,0:T(8,128)(2,1)S(1)}, bf16[2,32,2048]{2,1,0:T(8,128)(2,1)S(1)}, u32[]{:S(2)}, u32[]{:S(2)}) collective-permute-start(bf16[2,32,2048]{2,1,0:T(8,128)(2,1)S(1)} %fusion.5), channel_id=1, source_target_pairs={{0,24},{4,28},{8,16},{12,20},{16,8},{20,12},{24,0},{28,4},{1,25},{... | collective-permute-start | bytes 786440 | tf_op jit(solution)/shard_map/way_back/ppermute | solution.py:344
  134.0 7.8 %collective-permute-done.26 = bf16[2,32,2048]{2,1,0:T(8,128)(2,1)S(1)} collective-permute-done((bf16[2,32,2048]{2,1,0:T(8,128)(2,1)S(1)}, bf16[2,32,2048]{2,1,0:T(8,128)(2,1)S(1)}, u32[]{:S(2)}, u32[]{:S(2)}) %collective-permute-start.26) | collective-permute-done | bytes 262176 | tf_op jit(solution)/shard_map/way_back/ppermute | solution.py:344
  141.9 9.1 %collective-permute-start.12 = (bf16[2,32,2048]{2,1,0:T(8,128)(2,1)S(1)}, bf16[2,32,2048]{2,1,0:T(8,128)(2,1)S(1)}, u32[]{:S(2)}, u32[]{:S(2)}) collective-permute-start(bf16[2,32,2048]{2,1,0:T(8,128)(2,1)S(1)} %fusion.11), channel_id=1, source_target_pairs={{0,8},{4,12},{8,0},{12,4},{16,24},{20,28},{24,16},{28,20},{1,9},{5... | collective-permute-start | bytes 786440 | tf_op jit(solution)/shard_map/way_back/ppermute | solution.py:344
  151.0 3.8 %collective-permute-done.19 = bf16[2,32,2048]{2,1,0:T(8,128)(2,1)S(1)} collective-permute-done((bf16[2,32,2048]{2,1,0:T(8,128)(2,1)S(1)}, bf16[2,32,2048]{2,1,0:T(8,128)(2,1)S(1)}, u32[]{:S(2)}, u32[]{:S(2)}) %collective-permute-start.19) | collective-permute-done | bytes 262176 | tf_op jit(solution)/shard_map/way_back/ppermute | solution.py:344
  154.8 5.1 %collective-permute-done.12 = bf16[2,32,2048]{2,1,0:T(8,128)(2,1)S(1)} collective-permute-done((bf16[2,32,2048]{2,1,0:T(8,128)(2,1)S(1)}, bf16[2,32,2048]{2,1,0:T(8,128)(2,1)S(1)}, u32[]{:S(2)}, u32[]{:S(2)}) %collective-permute-start.12) | collective-permute-done | bytes 262176 | tf_op jit(solution)/shard_map/way_back/ppermute | solution.py:344
  159.9 1.5 collective-permute-start.27
  161.6 9.1 %landed_states.1 = bf16[8,16,128,128]{3,2,1,0:T(8,128)(2,1)} custom-call(s32[8]{0:T(128)S(1)} %copy-done.6, s32[8]{0:T(128)S(1)} %maximum_convert_fusion.place_ref, bf16[8,16,128,128]{3,2,1,0:T(8,128)(2,1)S(1)} %copy-done.4, bf16[2,16,128,128]{3,2,1,0:T(8,128)(2,1)S(1)} %collective-permute-done.31.rest_0_, ...), custom_call_target="tpu_custom_call" | custom-call | flops 20000000 | bytes 9437184 | tf_op jit(solution)/shard_map/landed/landed_states/pallas_call | solution.py:244
  (109 shorter events, 20.7 us)
Async XLA Ops:
  4.0 30.8 %all-to-all-start = ((f32[32,1,32]{2,1,0:T(1,128)}), f32[32,1,32]{2,1,0:T(1,128)S(1)}, u32[]{:S(2)}, u32[]{:S(2)}) async-start(f32[32,1,32]{2,1,0:T(1,128)} %bitcast.7), calls=%async_computation | async-start | bytes 32768 | tf_op jit(solution)/shard_map/routes/all_to_all | solution.py:381
  45.2 5.8 %collective-permute-start = (bf16[128,512]{1,0:T(8,128)(2,1)S(1)}, bf16[128,512]{1,0:T(8,128)(2,1)S(1)}, u32[]{:S(2)}, u32[]{:S(2)}) collective-permute-start(bf16[128,512]{1,0:T(8,128)(2,1)S(1)} %fusion.2), channel_id=1, source_target_pairs={{0,2},{1,3},{2,0},{3,1},{4,6},{5,7},{6,4},{7,5},{8,10},{9,11},{10,... | collective-permute-start | bytes 393224 | tf_op jit(solution)/shard_map/attention/ppermute | solution.py:344
  51.1 10.0 %collective-permute-start.2 = (bf16[2,128,512]{2,1,0:T(8,128)(2,1)S(1)}, bf16[2,128,512]{2,1,0:T(8,128)(2,1)}, u32[]{:S(2)}, u32[]{:S(2)}) collective-permute-start(bf16[2,128,512]{2,1,0:T(8,128)(2,1)S(1)} %pad_maximum_fusion.rest_0_), channel_id=1, source_target_pairs={{0,4},{4,0},{8,12},{12,8},{16,20},{20,16},{24,28},{28,24},{1,5},{5... | collective-permute-start | bytes 786440 | tf_op jit(solution)/shard_map/tokens/ppermute | solution.py:344
  52.6 11.2 %collective-permute-start.20 = (bf16[2,128,512]{2,1,0:T(8,128)(2,1)S(1)}, bf16[2,128,512]{2,1,0:T(8,128)(2,1)}, u32[]{:S(2)}, u32[]{:S(2)}) collective-permute-start(bf16[2,128,512]{2,1,0:T(8,128)(2,1)S(1)} %pad_maximum_fusion.rest_0_), channel_id=1, source_target_pairs={{0,24},{4,28},{8,16},{12,20},{16,8},{20,12},{24,0},{28,4},{1,25},{... | collective-permute-start | bytes 786440 | tf_op jit(solution)/shard_map/tokens/ppermute | solution.py:344
  55.9 8.6 %collective-permute-start.1 = (bf16[2,128,512]{2,1,0:T(8,128)(2,1)S(1)}, bf16[2,128,512]{2,1,0:T(8,128)(2,1)}, u32[]{:S(2)}, u32[]{:S(2)}) collective-permute-start(bf16[2,128,512]{2,1,0:T(8,128)(2,1)S(1)} %pad_maximum_fusion.rest_0_), channel_id=1, source_target_pairs={{0,1},{1,0},{2,3},{3,2},{4,5},{5,4},{6,7},{7,6},{8,9},{9,8},{10,11... | collective-permute-start | bytes 786440 | tf_op jit(solution)/shard_map/tokens/ppermute | solution.py:344
  55.9 22.0 %collective-permute-start.13 = (bf16[2,128,512]{2,1,0:T(8,128)(2,1)S(1)}, bf16[2,128,512]{2,1,0:T(8,128)(2,1)}, u32[]{:S(2)}, u32[]{:S(2)}) collective-permute-start(bf16[2,128,512]{2,1,0:T(8,128)(2,1)S(1)} %pad_maximum_fusion.rest_0_), channel_id=1, source_target_pairs={{0,16},{4,20},{8,24},{12,28},{16,0},{20,4},{24,8},{28,12},{1,17},{... | collective-permute-start | bytes 786440 | tf_op jit(solution)/shard_map/tokens/ppermute | solution.py:344
  55.9 3.8 %collective-permute-start.30 = (bf16[2,4,3456]{2,1,0:T(4,128)(2,1)}, bf16[2,4,3456]{2,1,0:T(4,128)(2,1)S(1)}, u32[]{:S(2)}, u32[]{:S(2)}) collective-permute-start(bf16[2,4,3456]{2,1,0:T(4,128)(2,1)} %get-tuple-element.62), channel_id=1, source_target_pairs={{0,3},{1,2},{2,1},{3,0},{4,7},{5,6},{6,5},{7,4},{8,11},{9,10},{10,... | collective-permute-start | bytes 165896 | tf_op jit(solution)/shard_map/send_states/ppermute | solution.py:344
  59.7 18.8 %collective-permute-start.6 = (bf16[2,128,512]{2,1,0:T(8,128)(2,1)S(1)}, bf16[2,128,512]{2,1,0:T(8,128)(2,1)}, u32[]{:S(2)}, u32[]{:S(2)}) collective-permute-start(bf16[2,128,512]{2,1,0:T(8,128)(2,1)S(1)} %pad_maximum_fusion.rest_0_), channel_id=1, source_target_pairs={{0,8},{4,12},{8,0},{12,4},{16,24},{20,28},{24,16},{28,20},{1,9},{5... | collective-permute-start | bytes 786440 | tf_op jit(solution)/shard_map/tokens/ppermute | solution.py:344
  61.0 18.9 %collective-permute-start.3 = (bf16[2,128,512]{2,1,0:T(8,128)(2,1)}, bf16[2,128,512]{2,1,0:T(8,128)(2,1)}, u32[]{:S(2)}, u32[]{:S(2)}) collective-permute-start(bf16[2,128,512]{2,1,0:T(8,128)(2,1)} %collective-permute-done.2.rest_2_), channel_id=1, source_target_pairs={{0,1},{1,0},{2,3},{3,2},{4,5},{5,4},{6,7},{7,6},{8,9},{9,8},{10,11... | collective-permute-start | bytes 786440 | tf_op jit(solution)/shard_map/tokens/ppermute | solution.py:344
  63.8 17.7 %collective-permute-start.22 = (bf16[2,128,512]{2,1,0:T(8,128)(2,1)}, bf16[2,128,512]{2,1,0:T(8,128)(2,1)}, u32[]{:S(2)}, u32[]{:S(2)}) collective-permute-start(bf16[2,128,512]{2,1,0:T(8,128)(2,1)} %collective-permute-done.20.rest_0_), channel_id=1, source_target_pairs={{0,4},{4,0},{8,12},{12,8},{16,20},{20,16},{24,28},{28,24},{1,5},{5... | collective-permute-start | bytes 786440 | tf_op jit(solution)/shard_map/tokens/ppermute | solution.py:344
  64.5 21.9 %collective-permute-start.21 = (bf16[2,128,512]{2,1,0:T(8,128)(2,1)}, bf16[2,128,512]{2,1,0:T(8,128)(2,1)S(1)}, u32[]{:S(2)}, u32[]{:S(2)}) collective-permute-start(bf16[2,128,512]{2,1,0:T(8,128)(2,1)} %collective-permute-done.20.rest_0_), channel_id=1, source_target_pairs={{0,1},{1,0},{2,3},{3,2},{4,5},{5,4},{6,7},{7,6},{8,9},{9,8},{10,11... | collective-permute-start | bytes 786440 | tf_op jit(solution)/shard_map/tokens/ppermute | solution.py:344
  77.9 9.5 %collective-permute-start.15 = (bf16[2,128,512]{2,1,0:T(8,128)(2,1)}, bf16[2,128,512]{2,1,0:T(8,128)(2,1)S(1)}, u32[]{:S(2)}, u32[]{:S(2)}) collective-permute-start(bf16[2,128,512]{2,1,0:T(8,128)(2,1)} %collective-permute-done.13.rest_0_), channel_id=1, source_target_pairs={{0,4},{4,0},{8,12},{12,8},{16,20},{20,16},{24,28},{28,24},{1,5},{5... | collective-permute-start | bytes 786440 | tf_op jit(solution)/shard_map/tokens/ppermute | solution.py:344
  78.5 7.2 %collective-permute-start.29 = (bf16[2,4,3456]{2,1,0:T(4,128)(2,1)S(1)}, bf16[2,4,3456]{2,1,0:T(4,128)(2,1)S(1)}, u32[]{:S(2)}, u32[]{:S(2)}) collective-permute-start(bf16[2,4,3456]{2,1,0:T(4,128)(2,1)S(1)} %copy-done.12), channel_id=1, source_target_pairs={{0,2},{1,3},{2,0},{3,1},{4,6},{5,7},{6,4},{7,5},{8,10},{9,11},{10,... | collective-permute-start | bytes 165896 | tf_op jit(solution)/shard_map/send_states/ppermute | solution.py:344
  80.0 11.0 %collective-permute-start.8 = (bf16[2,128,512]{2,1,0:T(8,128)(2,1)}, bf16[2,128,512]{2,1,0:T(8,128)(2,1)S(1)}, u32[]{:S(2)}, u32[]{:S(2)}) collective-permute-start(bf16[2,128,512]{2,1,0:T(8,128)(2,1)} %collective-permute-done.6.rest_0_), channel_id=1, source_target_pairs={{0,4},{4,0},{8,12},{12,8},{16,20},{20,16},{24,28},{28,24},{1,5},{5... | collective-permute-start | bytes 786440 | tf_op jit(solution)/shard_map/tokens/ppermute | solution.py:344
  81.4 9.5 %collective-permute-start.23 = (bf16[2,128,512]{2,1,0:T(8,128)(2,1)}, bf16[2,128,512]{2,1,0:T(8,128)(2,1)S(1)}, u32[]{:S(2)}, u32[]{:S(2)}) collective-permute-start(bf16[2,128,512]{2,1,0:T(8,128)(2,1)} %collective-permute-done.22.rest_2_), channel_id=1, source_target_pairs={{0,1},{1,0},{2,3},{3,2},{4,5},{5,4},{6,7},{7,6},{8,9},{9,8},{10,11... | collective-permute-start | bytes 786440 | tf_op jit(solution)/shard_map/tokens/ppermute | solution.py:344
  85.8 15.6 %collective-permute-start.4 = (bf16[2,2,32,2048]{3,2,1,0:T(8,128)(2,1)S(1)}, bf16[2,2,32,2048]{3,2,1,0:T(8,128)(2,1)S(1)}, u32[]{:S(2)}, u32[]{:S(2)}) collective-permute-start(bf16[2,2,32,2048]{3,2,1,0:T(8,128)(2,1)S(1)} %get-tuple-element.48), channel_id=1, source_target_pairs={{0,1},{1,0},{2,3},{3,2},{4,5},{5,4},{6,7},{7,6},{8,9},{9,8},{10,11... | collective-permute-start | bytes 1572872 | tf_op jit(solution)/shard_map/way_back/ppermute | solution.py:344
  86.4 7.8 %collective-permute-start.14 = (bf16[2,128,512]{2,1,0:T(8,128)(2,1)}, bf16[2,128,512]{2,1,0:T(8,128)(2,1)S(1)}, u32[]{:S(2)}, u32[]{:S(2)}) collective-permute-start(bf16[2,128,512]{2,1,0:T(8,128)(2,1)} %collective-permute-done.13.rest_0_), channel_id=1, source_target_pairs={{0,1},{1,0},{2,3},{3,2},{4,5},{5,4},{6,7},{7,6},{8,9},{9,8},{10,11... | collective-permute-start | bytes 786440 | tf_op jit(solution)/shard_map/tokens/ppermute | solution.py:344
  87.3 7.0 %collective-permute-start.16 = (bf16[2,128,512]{2,1,0:T(8,128)(2,1)S(1)}, bf16[2,128,512]{2,1,0:T(8,128)(2,1)S(1)}, u32[]{:S(2)}, u32[]{:S(2)}) collective-permute-start(bf16[2,128,512]{2,1,0:T(8,128)(2,1)S(1)} %collective-permute-done.15.rest_2_), channel_id=1, source_target_pairs={{0,1},{1,0},{2,3},{3,2},{4,5},{5,4},{6,7},{7,6},{8,9},{9,8},{10,11... | collective-permute-start | bytes 786440 | tf_op jit(solution)/shard_map/tokens/ppermute | solution.py:344
  90.9 7.3 %collective-permute-start.7 = (bf16[2,128,512]{2,1,0:T(8,128)(2,1)}, bf16[2,128,512]{2,1,0:T(8,128)(2,1)S(1)}, u32[]{:S(2)}, u32[]{:S(2)}) collective-permute-start(bf16[2,128,512]{2,1,0:T(8,128)(2,1)} %collective-permute-done.6.rest_0_), channel_id=1, source_target_pairs={{0,1},{1,0},{2,3},{3,2},{4,5},{5,4},{6,7},{7,6},{8,9},{9,8},{10,11... | collective-permute-start | bytes 786440 | tf_op jit(solution)/shard_map/tokens/ppermute | solution.py:344
  91.0 7.7 %collective-permute-start.9 = (bf16[2,128,512]{2,1,0:T(8,128)(2,1)S(1)}, bf16[2,128,512]{2,1,0:T(8,128)(2,1)S(1)}, u32[]{:S(2)}, u32[]{:S(2)}) collective-permute-start(bf16[2,128,512]{2,1,0:T(8,128)(2,1)S(1)} %collective-permute-done.8.rest_2_), channel_id=1, source_target_pairs={{0,1},{1,0},{2,3},{3,2},{4,5},{5,4},{6,7},{7,6},{8,9},{9,8},{10,11... | collective-permute-start | bytes 786440 | tf_op jit(solution)/shard_map/tokens/ppermute | solution.py:344
  94.2 67.4 %collective-permute-start.31 = (bf16[2,16,128,128]{3,2,1,0:T(8,128)(2,1)S(1)}, bf16[2,16,128,128]{3,2,1,0:T(8,128)(2,1)S(1)}, u32[]{:S(2)}, u32[]{:S(2)}) collective-permute-start(bf16[2,16,128,128]{3,2,1,0:T(8,128)(2,1)S(1)} %copy-done.10), channel_id=1, source_target_pairs={{0,1},{1,0},{2,3},{3,2},{4,5},{5,4},{6,7},{7,6},{8,9},{9,8},{10,11... | collective-permute-start | bytes 3145736 | tf_op jit(solution)/shard_map/send_states/ppermute | solution.py:344
  94.3 67.3 %collective-permute-start.32 = (bf16[2,16,128,128]{3,2,1,0:T(8,128)(2,1)S(1)}, bf16[2,16,128,128]{3,2,1,0:T(8,128)(2,1)S(1)}, u32[]{:S(2)}, u32[]{:S(2)}) collective-permute-start(bf16[2,16,128,128]{3,2,1,0:T(8,128)(2,1)S(1)} %copy-done.9), channel_id=1, source_target_pairs={{0,2},{1,3},{2,0},{3,1},{4,6},{5,7},{6,4},{7,5},{8,10},{9,11},{10,... | collective-permute-start | bytes 3145736 | tf_op jit(solution)/shard_map/send_states/ppermute | solution.py:344
  98.2 63.4 %collective-permute-start.33 = (bf16[2,16,128,128]{3,2,1,0:T(8,128)(2,1)S(1)}, bf16[2,16,128,128]{3,2,1,0:T(8,128)(2,1)S(1)}, u32[]{:S(2)}, u32[]{:S(2)}) collective-permute-start(bf16[2,16,128,128]{3,2,1,0:T(8,128)(2,1)S(1)} %copy-done.8), channel_id=1, source_target_pairs={{0,3},{1,2},{2,1},{3,0},{4,7},{5,6},{6,5},{7,4},{8,11},{9,10},{10,... | collective-permute-start | bytes 3145736 | tf_op jit(solution)/shard_map/send_states/ppermute | solution.py:344
  103.3 30.0 %collective-permute-start.5 = (bf16[2,32,2048]{2,1,0:T(8,128)(2,1)S(1)}, bf16[2,32,2048]{2,1,0:T(8,128)(2,1)S(1)}, u32[]{:S(2)}, u32[]{:S(2)}) collective-permute-start(bf16[2,32,2048]{2,1,0:T(8,128)(2,1)S(1)} %fusion.12), channel_id=1, source_target_pairs={{0,4},{4,0},{8,12},{12,8},{16,20},{20,16},{24,28},{28,24},{1,5},{5... | collective-permute-start | bytes 786440 | tf_op jit(solution)/shard_map/way_back/ppermute | solution.py:344
  104.1 13.2 %collective-permute-start.25 = (bf16[2,32,2048]{2,1,0:T(8,128)(2,1)S(1)}, bf16[2,32,2048]{2,1,0:T(8,128)(2,1)S(1)}, u32[]{:S(2)}, u32[]{:S(2)}) collective-permute-start(bf16[2,32,2048]{2,1,0:T(8,128)(2,1)S(1)} %fusion.3), channel_id=1, source_target_pairs={{0,4},{4,0},{8,12},{12,8},{16,20},{20,16},{24,28},{28,24},{1,5},{5... | collective-permute-start | bytes 786440 | tf_op jit(solution)/shard_map/way_back/ppermute | solution.py:344
  117.3 7.5 %collective-permute-start.18 = (bf16[2,32,2048]{2,1,0:T(8,128)(2,1)S(1)}, bf16[2,32,2048]{2,1,0:T(8,128)(2,1)S(1)}, u32[]{:S(2)}, u32[]{:S(2)}) collective-permute-start(bf16[2,32,2048]{2,1,0:T(8,128)(2,1)S(1)} %fusion.6), channel_id=1, source_target_pairs={{0,4},{4,0},{8,12},{12,8},{16,20},{20,16},{24,28},{28,24},{1,5},{5... | collective-permute-start | bytes 786440 | tf_op jit(solution)/shard_map/way_back/ppermute | solution.py:344
  124.8 6.6 %collective-permute-start.11 = (bf16[2,32,2048]{2,1,0:T(8,128)(2,1)S(1)}, bf16[2,32,2048]{2,1,0:T(8,128)(2,1)S(1)}, u32[]{:S(2)}, u32[]{:S(2)}) collective-permute-start(bf16[2,32,2048]{2,1,0:T(8,128)(2,1)S(1)} %fusion.9), channel_id=1, source_target_pairs={{0,4},{4,0},{8,12},{12,8},{16,20},{20,16},{24,28},{28,24},{1,5},{5... | collective-permute-start | bytes 786440 | tf_op jit(solution)/shard_map/way_back/ppermute | solution.py:344
  131.5 10.4 %collective-permute-start.26 = (bf16[2,32,2048]{2,1,0:T(8,128)(2,1)S(1)}, bf16[2,32,2048]{2,1,0:T(8,128)(2,1)S(1)}, u32[]{:S(2)}, u32[]{:S(2)}) collective-permute-start(bf16[2,32,2048]{2,1,0:T(8,128)(2,1)S(1)} %fusion.5), channel_id=1, source_target_pairs={{0,24},{4,28},{8,16},{12,20},{16,8},{20,12},{24,0},{28,4},{1,25},{... | collective-permute-start | bytes 786440 | tf_op jit(solution)/shard_map/way_back/ppermute | solution.py:344
  133.3 21.5 %collective-permute-start.19 = (bf16[2,32,2048]{2,1,0:T(8,128)(2,1)S(1)}, bf16[2,32,2048]{2,1,0:T(8,128)(2,1)S(1)}, u32[]{:S(2)}, u32[]{:S(2)}) collective-permute-start(bf16[2,32,2048]{2,1,0:T(8,128)(2,1)S(1)} %fusion.8), channel_id=1, source_target_pairs={{0,16},{4,20},{8,24},{12,28},{16,0},{20,4},{24,8},{28,12},{1,17},{... | collective-permute-start | bytes 786440 | tf_op jit(solution)/shard_map/way_back/ppermute | solution.py:344
  141.9 18.0 %collective-permute-start.12 = (bf16[2,32,2048]{2,1,0:T(8,128)(2,1)S(1)}, bf16[2,32,2048]{2,1,0:T(8,128)(2,1)S(1)}, u32[]{:S(2)}, u32[]{:S(2)}) collective-permute-start(bf16[2,32,2048]{2,1,0:T(8,128)(2,1)S(1)} %fusion.11), channel_id=1, source_target_pairs={{0,8},{4,12},{8,0},{12,4},{16,24},{20,28},{24,16},{28,20},{1,9},{5... | collective-permute-start | bytes 786440 | tf_op jit(solution)/shard_map/way_back/ppermute | solution.py:344
  154.8 6.6 %collective-permute-start.28 = (bf16[2,4,3456]{2,1,0:T(4,128)(2,1)S(1)}, bf16[2,4,3456]{2,1,0:T(4,128)(2,1)S(1)}, u32[]{:S(2)}, u32[]{:S(2)}) collective-permute-start(bf16[2,4,3456]{2,1,0:T(4,128)(2,1)S(1)} %copy-done.11), channel_id=1, source_target_pairs={{0,1},{1,0},{2,3},{3,2},{4,5},{5,4},{6,7},{7,6},{8,9},{9,8},{10,11... | collective-permute-start | bytes 165896 | tf_op jit(solution)/shard_map/send_states/ppermute | solution.py:344
  159.9 10.8 %collective-permute-start.27 = (bf16[32,2048]{1,0:T(8,128)(2,1)S(1)}, bf16[32,2048]{1,0:T(8,128)(2,1)S(1)}, u32[]{:S(2)}, u32[]{:S(2)}) collective-permute-start(bf16[32,2048]{1,0:T(8,128)(2,1)S(1)} %fusion.23), channel_id=1, source_target_pairs={{0,2},{1,3},{2,0},{3,1},{4,6},{5,7},{6,4},{7,5},{8,10},{9,11},{10,... | collective-permute-start | bytes 393224 | tf_op jit(solution)/shard_map/mixed/ppermute | solution.py:344
  (16 other events, 301.5 us)

commit v3 on v2

v3 whole, which is shorter than its diff:
```python
import functools

import jax
import jax.numpy as jnp
from jax import lax
from jax.experimental import pallas as pl
from jax.experimental.pallas import tpu as pltpu
from jax.sharding import PartitionSpec as P

EPS = 1e-06
F32 = jnp.float32
BF16 = jnp.bfloat16
MIB = 1 << 20


def row_sum(x):
    return jnp.sum(x, axis=-1, keepdims=True)


def spread_rows(ref, scratch, requests, steps):
    for r in range(requests):
        split_heads(ref[r].astype(F32), scratch, r, steps)


def split_heads(values, scratch, r, steps):
    hd = scratch.shape[-1]
    for h in range(scratch.shape[0]):
        scratch[h, r * steps : (r + 1) * steps, :] = values[:, h * hd : (h + 1) * hd]


def at_step(scratch, t, requests, steps, head=None):
    if head is None:
        return scratch[pl.ds(t, requests, stride=steps), :]
    return scratch[head, pl.ds(t, requests, stride=steps), :]


def recurrence(kh, repeats, steps, requests, hd, k_s, q_s, v_s, a_s, b_s, m_s, emit_out, emit_state):
    per = m_s.shape[1] // requests
    ks = [at_step(k_s, t, requests, steps, kh) for t in range(steps)]
    rk = [lax.rsqrt(row_sum(k * k) + EPS) for k in ks]
    kn = [k * r for k, r in zip(ks, rk)]
    kk = {(i, t): row_sum(kn[i] * kn[t]) for t in range(steps) for i in range(t)}
    if emit_out is not None:
        qs = [at_step(q_s, t, requests, steps, kh) for t in range(steps)]
        rq = [lax.rsqrt(row_sum(q * q) + EPS) * hd**-0.5 for q in qs]
        qn = [q * r for q, r in zip(qs, rq)]
        kq = {(i, t): row_sum(kn[i] * qn[t]) for t in range(steps) for i in range(t + 1)}
    for h in range(kh * repeats, (kh + 1) * repeats):
        decayed = []
        c = None
        for t in range(steps):
            a = at_step(a_s, t, requests, steps)[:, h : h + 1]
            b = at_step(b_s, t, requests, steps)[:, h : h + 1]
            decayed = [w * a for w in decayed]
            c = a if c is None else c * a
            m = (c * rk[t]) * at_step(m_s, t, requests, per, h)
            for i in range(t):
                m = m + kk[i, t] * decayed[i]
            decayed.append((at_step(v_s, t, requests, steps, h) - m) * b)
            if emit_out is not None:
                o = (c * rq[t]) * at_step(m_s, steps + t, requests, per, h)
                for i in range(t + 1):
                    o = o + kq[i, t] * decayed[i]
                emit_out(t, h, o)
        if emit_state is not None:
            emit_state(h, c, [w * r for w, r in zip(decayed, rk)])


def sigmoid_rows(ref, scratch, requests, steps):
    for r in range(requests):
        scratch[r * steps : (r + 1) * steps, : ref.shape[-1]] = jax.nn.sigmoid(ref[r].astype(F32))


def packed_rows(key_heads, heads, steps):
    used = (key_heads + heads + 3) * steps
    return used, -(-used // 16) * 16


def core_kernel(
    lanes, home_ref, state_ref, q_ref, k_ref, v_ref, g_ref, b_ref, a_ref, gain_ref, out_ref, packed_ref,
    k_s, q_s, v_s, g_s, a_s, b_s, m_s, o_s, held, pay_f, pay_s, in_sem, out_sem,
):
    requests, steps, _ = k_ref.shape
    hd = held.shape[-1]
    heads, key_heads = v_s.shape[0], k_s.shape[0]
    repeats = heads // key_heads
    cap = requests // lanes
    copies = []
    for r in range(requests):
        copies.append(pltpu.make_async_copy(state_ref.at[r], held.at[r], in_sem.at[r]))
        copies[-1].start()
    spread_rows(k_ref, k_s, requests, steps)
    spread_rows(q_ref, q_s, requests, steps)
    spread_rows(v_ref, v_s, requests, steps)
    spread_rows(g_ref, g_s, requests, steps)
    sigmoid_rows(a_ref, a_s, requests, steps)
    sigmoid_rows(b_ref, b_s, requests, steps)
    target = [lax.rem(lax.div(home_ref[r], requests), lanes) for r in range(requests)]
    slots = [
        target[r] * cap + sum([(target[p] == target[r]).astype(jnp.int32) for p in range(r)], jnp.int32(0))
        for r in range(requests)
    ]
    state_rows = heads * hd
    sent = []
    pay_f[...] = jnp.zeros_like(pay_f)
    for r in range(requests):
        rows = slice(r * steps, (r + 1) * steps)
        for kh in range(key_heads):
            pay_f[kh * steps : (kh + 1) * steps, :] = k_s[kh, rows, :]
        for h in range(heads):
            at = (key_heads + h) * steps
            pay_f[at : at + steps, :] = v_s[h, rows, :]
        at = (key_heads + heads) * steps
        pay_f[at : at + steps, :heads] = a_ref[r].astype(F32)
        pay_f[at + steps : at + 2 * steps, :heads] = b_ref[r].astype(F32)
        place = lax.rem(home_ref[r], requests).astype(F32)
        pay_f[at + 2 * steps : at + 3 * steps, :] = jnp.full((steps, hd), place, F32)
        pay_s[r] = pay_f[...].astype(BF16)
        sent.append(
            pltpu.make_async_copy(
                pay_s.at[r], packed_ref.at[slots[r], pl.ds(state_rows, pay_s.shape[1])], out_sem.at[0, r]
            )
        )
        sent[-1].start()
    for r in range(requests):
        copies[r].wait()
        rows = slice(r * steps, (r + 1) * steps)
        for kh in range(key_heads):
            left = jnp.concatenate([k_s[kh, rows, :], q_s[kh, rows, :]], axis=0).astype(BF16)
            for h in range(kh * repeats, (kh + 1) * repeats):
                m_s[h, r * 2 * steps : (r + 1) * 2 * steps, :] = jnp.dot(
                    left, held[r, h * hd : (h + 1) * hd, :], preferred_element_type=F32
                )
        sent.append(
            pltpu.make_async_copy(
                held.at[r], packed_ref.at[slots[r], pl.ds(0, state_rows)], out_sem.at[1, r]
            )
        )
        sent[-1].start()
    gain = gain_ref[...]

    def emit(t, h, o):
        gate = at_step(g_s, t, requests, steps, h)
        scaled = o * lax.rsqrt(row_sum(o * o) * (1.0 / hd) + EPS)
        o_s[h, pl.ds(t, requests, stride=steps), :] = scaled * gain * jax.nn.silu(gate)

    for kh in range(key_heads):
        recurrence(kh, repeats, steps, requests, hd, k_s, q_s, v_s, a_s, b_s, m_s, emit, None)
    for h in range(heads):
        out_ref[:, h * hd : (h + 1) * hd] = o_s[h].astype(BF16)
    for c in sent:
        c.wait()


def core_rows(
    home, lanes, states, query_rows, key_rows, value_rows, gate_rows, beta_logit, decay_logit, core_gain
):
    requests, heads, hd, _ = states.shape
    steps = key_rows.shape[1]
    kw, vw = key_rows.shape[-1], value_rows.shape[-1]
    tokens = requests * steps
    _, pay_rows = packed_rows(kw // hd, heads, steps)
    vmem, hbm = pl.BlockSpec(memory_space=pltpu.VMEM), pl.BlockSpec(memory_space=pl.ANY)
    return pl.pallas_call(
        functools.partial(core_kernel, lanes),
        in_specs=[pl.BlockSpec(memory_space=pltpu.SMEM), hbm] + [vmem] * 7,
        out_specs=[vmem, hbm],
        out_shape=[
            jax.ShapeDtypeStruct((tokens, vw), BF16),
            jax.ShapeDtypeStruct((requests, heads * hd + pay_rows, hd), BF16),
        ],
        scratch_shapes=[
            pltpu.VMEM((kw // hd, tokens, hd), F32),
            pltpu.VMEM((kw // hd, tokens, hd), F32),
            pltpu.VMEM((heads, tokens, hd), F32),
            pltpu.VMEM((heads, tokens, hd), F32),
            pltpu.VMEM((tokens, 128), F32),
            pltpu.VMEM((tokens, 128), F32),
            pltpu.VMEM((heads, 2 * tokens, hd), F32),
            pltpu.VMEM((heads, tokens, hd), F32),
            pltpu.VMEM((requests, heads * hd, hd), BF16),
            pltpu.VMEM((pay_rows, hd), F32),
            pltpu.VMEM((requests, pay_rows, hd), BF16),
            pltpu.SemaphoreType.DMA((requests,)),
            pltpu.SemaphoreType.DMA((2, requests)),
        ],
        compiler_params=pltpu.CompilerParams(vmem_limit_bytes=60 * MIB),
        cost_estimate=pl.CostEstimate(flops=20_000_000, bytes_accessed=9 * MIB, transcendentals=100_000),
        name="core_rows",
    )(
        home, states.reshape(requests, heads * hd, hd), query_rows, key_rows, value_rows, gate_rows,
        beta_logit, decay_logit, core_gain.reshape(1, hd),
    )


def state_kernel(
    key_heads, heads, steps, place_ref, arrived_ref, out_ref,
    k_s, v_s, a_s, b_s, m_s, u_s, c_s, held, pay_s, ready, in_sem, pay_sem, out_sem,
):
    requests, state_rows, hd = held.shape
    repeats = heads // key_heads
    pays, copies = [], []
    for r in range(requests):
        pays.append(
            pltpu.make_async_copy(
                arrived_ref.at[r, pl.ds(state_rows, pay_s.shape[1])], pay_s.at[r], pay_sem.at[r]
            )
        )
        pays[-1].start()
    for r in range(requests):
        copies.append(
            pltpu.make_async_copy(arrived_ref.at[r, pl.ds(0, state_rows)], held.at[r], in_sem.at[r])
        )
        copies[-1].start()
    for r in range(requests):
        pays[r].wait()
        rows = slice(r * steps, (r + 1) * steps)
        pay = pay_s[r].astype(F32)
        for kh in range(key_heads):
            k_s[kh, rows, :] = pay[kh * steps : (kh + 1) * steps]
        for h in range(heads):
            v_s[h, rows, :] = pay[(key_heads + h) * steps : (key_heads + h + 1) * steps]
        at = (key_heads + heads) * steps
        a_s[rows, :] = jax.nn.sigmoid(pay[at : at + steps])
        b_s[rows, :] = jax.nn.sigmoid(pay[at + steps : at + 2 * steps])
    for r in range(requests):
        copies[r].wait()
        rows = slice(r * steps, (r + 1) * steps)
        for h in range(heads):
            m_s[h, rows, :] = jnp.dot(
                k_s[h // repeats, rows, :].astype(BF16),
                held[r, h * hd : (h + 1) * hd, :],
                preferred_element_type=F32,
            )

    def emit(h, c, updates):
        c_s[h] = jnp.broadcast_to(c, (requests, hd))
        for t, u in enumerate(updates):
            u_s[h, pl.ds(t, requests, stride=steps), :] = u

    for kh in range(key_heads):
        recurrence(kh, repeats, steps, requests, hd, k_s, None, v_s, a_s, b_s, m_s, None, emit)
    sent = []
    for r in range(requests):
        slot = r % 2
        if r >= 2:
            sent[r - 2].wait()
        rows = slice(r * steps, (r + 1) * steps)
        for h in range(heads):
            k4 = k_s[h // repeats, rows, :]
            k8 = jnp.concatenate([k4, k4], axis=0).astype(BF16)
            u4 = u_s[h, rows, :]
            high = u4.astype(BF16).astype(F32)
            u8 = jnp.concatenate([high, u4 - high], axis=0).astype(BF16)
            added = lax.dot_general(
                k8, u8, (((0,), (0,)), ((), ())), preferred_element_type=F32
            )
            kept = held[r, h * hd : (h + 1) * hd, :].astype(F32) * c_s[h, r : r + 1, :]
            ready[slot, h * hd : (h + 1) * hd, :] = (kept + added).astype(BF16)
        sent.append(pltpu.make_async_copy(ready.at[slot], out_ref.at[place_ref[r]], out_sem.at[slot]))
        sent[-1].start()
    for c in sent[-2:]:
        c.wait()


def landed_states(place, arrived, key_heads, heads, steps):
    requests, all_rows, hd = arrived.shape
    tokens = requests * steps
    state_rows = heads * hd
    hbm = pl.BlockSpec(memory_space=pl.ANY)
    out = pl.pallas_call(
        functools.partial(state_kernel, key_heads, heads, steps),
        in_specs=[pl.BlockSpec(memory_space=pltpu.SMEM), hbm],
        out_specs=hbm,
        out_shape=jax.ShapeDtypeStruct((requests, state_rows, hd), BF16),
        scratch_shapes=[
            pltpu.VMEM((key_heads, tokens, hd), F32),
            pltpu.VMEM((heads, tokens, hd), F32),
            pltpu.VMEM((tokens, hd), F32),
            pltpu.VMEM((tokens, hd), F32),
            pltpu.VMEM((heads, tokens, hd), F32),
            pltpu.VMEM((heads, tokens, hd), F32),
            pltpu.VMEM((heads, requests, hd), F32),
            pltpu.VMEM((requests, state_rows, hd), BF16),
            pltpu.VMEM((requests, all_rows - state_rows, hd), BF16),
            pltpu.VMEM((2, state_rows, hd), BF16),
            pltpu.SemaphoreType.DMA((requests,)),
            pltpu.SemaphoreType.DMA((requests,)),
            pltpu.SemaphoreType.DMA((2,)),
        ],
        compiler_params=pltpu.CompilerParams(vmem_limit_bytes=32 * MIB),
        cost_estimate=pl.CostEstimate(flops=20_000_000, bytes_accessed=9 * MIB, transcendentals=10_000),
        name="landed_states",
    )(place, arrived)
    return out.reshape(requests, heads, hd, hd)


def expert_kernel(sides, own_out, where_ref, *rest):
    pieces = rest[: 2 * sides]
    weight_ref, gain_ref, up_ref, down_ref = rest[2 * sides : 2 * sides + 4]
    keeps = rest[2 * sides + 4 : 3 * sides + 4]
    give_ref = rest[3 * sides + 4]
    result_s = rest[-1]
    spans, group_rows, cols = pieces[0].shape
    tokens = give_ref.shape[2]
    width = down_ref.shape[-1]
    hidden_units = down_ref.shape[1]
    e = where_ref[0]
    blocks = [(x, c) for x in range(spans) for c in range(2)]
    values = {}
    for x, c in blocks:
        parts = [pieces[2 * y + c][x] for y in range(sides)]
        values[x, c] = jnp.concatenate(parts, axis=0).astype(F32)
    total = sum(row_sum(values[b] * values[b]) for b in blocks)
    scale = lax.rsqrt(total * (1.0 / width) + EPS)
    joined = None
    for x, c in blocks:
        block = e ^ (2 * x + c)
        normed = (values[x, c] * scale * gain_ref[pl.ds(block, 1), :]).astype(BF16)
        up = up_ref[0, pl.ds(pl.multiple_of(block * cols, cols), cols), :]
        term = jnp.dot(normed, up, preferred_element_type=F32)
        joined = term if joined is None else joined + term
        if own_out:
            rest[3 * sides + 5][:, pl.ds(pl.multiple_of(block * cols, cols), cols)] = pieces[c][
                x, pl.ds(pl.multiple_of(e * tokens, tokens), tokens), :
            ]
    active = (jax.nn.silu(joined[:, :hidden_units]) * joined[:, hidden_units:]).astype(BF16)
    result = jnp.dot(active, down_ref[0], preferred_element_type=F32).astype(BF16)
    eye = lax.broadcasted_iota(jnp.int32, (group_rows, group_rows), 0) == lax.broadcasted_iota(
        jnp.int32, (group_rows, group_rows), 1
    )
    weights = []
    for y in range(sides):
        line = weight_ref[pl.ds(where_ref[1 + y], 1), :]
        weights.append(row_sum(jnp.where(eye, jnp.broadcast_to(line, eye.shape), 0.0)))
    result_s[...] = (result.astype(F32) * jnp.concatenate(weights, axis=0)).astype(BF16)
    for y in range(sides):
        for x in range(spans):
            for c in range(2):
                start = y * group_rows + (e ^ (2 * x + c)) * tokens
                rows = result_s[pl.ds(pl.multiple_of(start, tokens), tokens), :]
                if c:
                    give_ref[y, x] = rows
                else:
                    keeps[y][x] = rows


def expert_chunk(where, pieces, weights, gain, gate_up, down_weight, tokens, own_out):
    sides = len(pieces) // 2
    spans, group_rows, cols = pieces[0].shape
    width = down_weight.shape[-1]
    vmem = pl.BlockSpec(memory_space=pltpu.VMEM)
    keep = jax.ShapeDtypeStruct((spans, tokens, width), BF16)
    give = jax.ShapeDtypeStruct((sides, spans, tokens, width), BF16)
    own = [jax.ShapeDtypeStruct((tokens, width), BF16)] if own_out else []
    rows = sides * group_rows
    outs = pl.pallas_call(
        functools.partial(expert_kernel, sides, own_out),
        in_specs=[pl.BlockSpec(memory_space=pltpu.SMEM)] + [vmem] * (len(pieces) + 4),
        out_specs=[vmem] * (sides + 1 + len(own)),
        out_shape=[keep] * sides + [give] + own,
        scratch_shapes=[pltpu.VMEM((rows, width), BF16)],
        compiler_params=pltpu.CompilerParams(vmem_limit_bytes=32 * MIB),
        cost_estimate=pl.CostEstimate(
            flops=6 * rows * width * down_weight.shape[1], bytes_accessed=6 * MIB, transcendentals=0
        ),
        name="expert_chunk",
    )(where, *pieces, weights, gain, gate_up, down_weight)
    return outs


def swap(x, axis, d):
    size = lax.axis_size(axis)
    return lax.ppermute(x, axis, [(i, i ^ d) for i in range(size)])


def summed(*terms):
    return functools.reduce(lambda p, q: p + q, [t.astype(F32) for t in terms])


def shards(
    states, query_rows, key_rows, value_rows, gate_rows, beta_logit, decay_logit, residual,
    route_ids, route_prob, out_weight, core_gain, moe_gain, gate_up, down_weight, new_home,
):
    requests, heads, hd, _ = states.shape
    steps = query_rows.shape[1]
    width = residual.shape[-1]
    tokens = requests * steps
    lanes = lax.axis_size("ep")
    groups = lax.axis_size("dp")
    my_lane = lax.axis_index("ep")
    my_group = lax.axis_index("dp")
    kw, vw = key_rows.shape[-1], value_rows.shape[-1]
    top = route_ids.shape[-1]

    experts = groups * lanes
    cols = out_weight.shape[1]
    everyone = functools.partial(lax.all_to_all, split_axis=0, concat_axis=0, tiled=True)

    with jax.named_scope("core"):
        before = lax.all_to_all(
            residual.reshape(tokens, width), "ep", split_axis=1, concat_axis=0, tiled=True
        )
        core, packed = core_rows(
            new_home, lanes, states, query_rows, key_rows, value_rows, gate_rows, beta_logit,
            decay_logit, core_gain,
        )
        group_core = lax.all_gather(core, "ep", axis=0, tiled=True)
    with jax.named_scope("attention"):
        attention = jnp.dot(group_core, out_weight, preferred_element_type=F32).astype(BF16)
        hidden_cols = (before.astype(F32) + attention.astype(F32)).astype(BF16)
        held = jnp.stack([hidden_cols] + [swap(hidden_cols, "ep", d) for d in range(2, lanes, 2)])
        held, packed = lax.optimization_barrier((held, packed))
        first_across = swap(held, "dp", 1)
    with jax.named_scope("send_states"):
        arrived = everyone(packed, "ep")
    with jax.named_scope("routes"):
        route_prob, first_across = lax.optimization_barrier((route_prob, first_across))
        weights = route_prob.reshape(tokens, top)
        weights = weights / jnp.sum(weights, -1, keepdims=True)
        named = route_ids.reshape(tokens, top)[None] == jnp.arange(experts, dtype=jnp.int32)[:, None, None]
        weights = jnp.sum(jnp.where(named, weights[None], 0.0), axis=-1)
        weights = everyone(weights, ("dp", "ep")).reshape(groups, lanes * tokens)

    gain = moe_gain.reshape(lanes, cols)
    sums = []
    own_rows = None
    for d in range(0, groups, 2):
        with jax.named_scope("tokens"):
            near = swap(held, "dp", d) if d else held
            across = swap(near, "dp", 1) if d else first_across
            pieces = [near, swap(near, "ep", 1), across, swap(across, "ep", 1)]
        with jax.named_scope("experts"):
            where = jnp.stack([my_lane, my_group ^ d, my_group ^ d ^ 1])
            outs = expert_chunk(where, pieces, weights, gain, gate_up, down_weight, tokens, d == 0)
            keep_near, keep_across, give = outs[:3]
            if d == 0:
                own_rows = outs[3]
        with jax.named_scope("way_back"):
            got = swap(give, "ep", 1)
            back = swap(summed(keep_across, got[1]).astype(BF16), "dp", 1)
            chunk = summed(keep_near, got[0], back)
            sums.append(swap(chunk.astype(BF16), "dp", d) if d else chunk)
    with jax.named_scope("landed"):
        place_row = heads * hd + (kw // hd + heads + 2) * steps
        place = arrived[:, place_row, 0].astype(jnp.int32)
        moved_out = landed_states(place, arrived, kw // hd, heads, steps)
        sums, moved_out = lax.optimization_barrier((sums, moved_out))
    with jax.named_scope("mixed"):
        mixed = summed(own_rows, *[s[0] for s in sums])
        for x in range(1, lanes // 2):
            mixed = mixed + swap(summed(*[s[x] for s in sums]).astype(BF16), "ep", 2 * x).astype(F32)
        mixed_out = mixed.astype(BF16)
    return mixed_out.reshape(requests, steps, width), moved_out


def solution(mesh):
    row = P(("dp", "ep"), None, None)
    placed = (P(("dp", "ep"), None, None, None),) + (row,) * 9 + (
        P(None, "ep"), P(), P(), row, row, P(("dp", "ep")),
    )
    return jax.shard_map(
        shards,
        mesh=mesh,
        in_specs=placed,
        out_specs=(row, P(("dp", "ep"), None, None, None)),
        check_vma=False,
    )
```

time: 172 us -> 156 us (0.907)
  waiting for transfers between devices: 69.7 us -> 51.3 us
  blocking collectives: 15.4 us -> 9.61 us
  local copies, waits for them, and re-layouts: 5.34 us -> 9.34 us
  other arithmetic: 6 us -> 8.56 us
  starting transfers between devices: 40.6 us -> 42.9 us
    ppermute x34 -> x28, waiting for transfers between devices: 69.7 us -> 35.1 us  [swap(): return lax.ppermute(x, axis, [(i, i ^ d) for i in range(size)])]
    all_to_all x1 -> x3, waiting for transfers between devices: 0.01 us -> 16.2 us  [the longest x1 11.3 us: shards(): arrived = everyone(packed, 'ep')]
    all_to_all x1 -> x3, starting transfers between devices: 7.3 us -> 22.9 us  [the longest x1 13.5 us: shards(): weights = everyone(weights, ('dp', 'ep')).reshape(groups, lanes * tokens)]
    ppermute x34 -> x28, starting transfers between devices: 33.3 us -> 20 us  [swap(): return lax.ppermute(x, axis, [(i, i ^ d) for i in range(size)])]
    all_gather x1 -> x0, blocking collectives: 7.94 us -> none  [shards(): lax.all_gather(residual.reshape(tokens, width), 'ep', axis=0, tiled=True)]
    unnamed x26 -> x30, local copies, waits for them, and re-layouts: 1.64 us -> 5.98 us
    all_gather x1, blocking collectives: 7.49 us -> 9.61 us  [shards(): group_core = lax.all_gather(core, 'ep', axis=0, tiled=True)]
    pallas_call x2, Pallas kernels: 22.1 us -> 20.1 us  [the longest x1 10.5 us: landed_states(): pl.pallas_call(functools.partial(state_kernel, key_heads, heads, steps),...]
  transfers between devices with their start and end apart: 35 -> 31, of which waited for: 14 -> 9; matrix products, arithmetic and copies ran while one was open for 2% -> 5% of each run, Pallas kernels for 19% -> 20%
where the time goes in v3:
time: 156 us; the launch traced here: 155 us
  waiting for transfers between devices  51.3 us (33%)
  starting transfers between devices  42.9 us (28%)
  Pallas kernels  31.1 us (20%)
  blocking collectives  9.61 us (6%)
  local copies, waits for them, and re-layouts  9.34 us (6%)
  other arithmetic  8.56 us (5%)
    ppermute x28, waiting for transfers between devices, swap(): return lax.ppermute(x, axis, [(i, i ^ d) for i in range(size)])  35.1 us
    ppermute x28, starting transfers between devices, swap(): return lax.ppermute(x, axis, [(i, i ^ d) for i in range(size)])  20 us
    all_to_all x1, starting transfers between devices, shards(): weights = everyone(weights, ('dp', 'ep')).reshape(groups, lanes * tokens)  13.5 us
    all_to_all x1, waiting for transfers between devices, shards(): arrived = everyone(packed, 'ep')  11.3 us
    pallas_call x4, Pallas kernels, expert_chunk(): pl.pallas_call(functools.partial(expert_kernel, sides, own_out), in_specs...  11 us
    pallas_call x1, Pallas kernels, landed_states(): pl.pallas_call(functools.partial(state_kernel, key_heads, heads, steps),...  10.5 us
    all_gather x1, blocking collectives, shards(): group_core = lax.all_gather(core, 'ep', axis=0, tiled=True)  9.61 us
    pallas_call x1, Pallas kernels, core_rows(): pl.pallas_call(functools.partial(core_kernel, lanes), in_specs=[pl.BlockS...  9.54 us
  transfers between devices with their start and end apart: 31, of which 9 were waited for; matrix products, arithmetic and copies ran while one was open for 5% of the time, Pallas kernels for 20%

profile of v3, /device:TPU:0, one launch (start us, length us, event | category | flops | bytes accessed | tf_op | source)
XLA Modules:
  0.0 155.2 jit_solution(9703032601283395311)
XLA Ops:
  0.6 1.1 all_to_all.19
  2.5 4.2 %all-to-all-start = ((bf16[32,4,512]{2,0,1:T(8,128)(2,1)}), bf16[32,4,512]{2,0,1:T(8,128)(2,1)S(1)}, u32[]{:S(2)}, u32[]{:S(2)}) async-start(bf16[32,4,512]{2,0,1:T(8,128)(2,1)} %copy.21), calls=%async_computation | async-start | bytes 262144 | tf_op jit(solution)/shard_map/core/all_to_all | solution.py:401
  6.7 9.5 %core_rows.1 = (bf16[32,2048]{1,0:T(8,128)(2,1)}, bf16[8,2160,128]{2,1,0:T(8,128)(2,1)}) custom-call(s32[8]{0:T(128)} %home_ref.1, bf16[8,2048,128]{2,1,0:T(8,128)(2,1)} %bitcast.79, bf16[8,4,1024]{2,1,0:T(4,128)(2,1)} %q_ref.1, bf16[8,4,1024]{2,1,0:T(4,128)(2,1)} %k_ref.1, bf16[8,4,2048]{2,1,0:T(4,128)(2,1)} %v_ref.1, bf16[8,4,2048]{2,1,0:T(4,128)(2,1)} %g_ref.1, ...), custom_call_target="tpu_custom_call" | custom-call | flops 20000000 | bytes 9437184 | tf_op jit(solution)/shard_map/core/core_rows/pallas_call | solution.py:164
  16.2 9.6 %all_gather.3 = bf16[128,2048]{1,0:T(8,128)(2,1)} all-gather(bf16[32,2048]{1,0:T(8,128)(2,1)} %get-tuple-element.26), channel_id=1, replica_groups=mesh['dp'=8,'ep'=4] {'ep'}, dimensions={0}, use_global_device_ids=true | all-gather | bytes 655360 | tf_op jit(solution)/shard_map/core/all_gather | solution.py:408
  25.9 1.5 fusion.2
  27.8 5.4 %collective-permute-done = bf16[128,512]{1,0:T(8,128)(2,1)S(1)} collective-permute-done((bf16[128,512]{1,0:T(8,128)(2,1)S(1)}, bf16[128,512]{1,0:T(8,128)(2,1)S(1)}, u32[]{:S(2)}, u32[]{:S(2)}) %collective-permute-start) | collective-permute-done | bytes 131104 | tf_op jit(solution)/shard_map/attention/ppermute | solution.py:374
  33.2 2.1 %collective-permute-start.2 = (bf16[2,128,512]{2,1,0:T(8,128)(2,1)S(1)}, bf16[2,128,512]{2,1,0:T(8,128)(2,1)}, u32[]{:S(2)}, u32[]{:S(2)}) collective-permute-start(bf16[2,128,512]{2,1,0:T(8,128)(2,1)S(1)} %pad_maximum_fusion.rest_0_), channel_id=1, source_target_pairs={{0,4},{4,0},{8,12},{12,8},{16,20},{20,16},{24,28},{28,24},{1,5},{5... | collective-permute-start | bytes 786440 | tf_op jit(solution)/shard_map/attention/ppermute | solution.py:374
  35.4 3.6 %collective-permute-start.20 = (bf16[2,128,512]{2,1,0:T(8,128)(2,1)S(1)}, bf16[2,128,512]{2,1,0:T(8,128)(2,1)}, u32[]{:S(2)}, u32[]{:S(2)}) collective-permute-start(bf16[2,128,512]{2,1,0:T(8,128)(2,1)S(1)} %pad_maximum_fusion.rest_0_), channel_id=1, source_target_pairs={{0,24},{4,28},{8,16},{12,20},{16,8},{20,12},{24,0},{28,4},{1,25},{... | collective-permute-start | bytes 786440 | tf_op jit(solution)/shard_map/tokens/ppermute | solution.py:374
  39.8 1.6 %collective-permute-done.2.rest_2_ = bf16[2,128,512]{2,1,0:T(8,128)(2,1)} collective-permute-done((bf16[2,128,512]{2,1,0:T(8,128)(2,1)S(1)}, bf16[2,128,512]{2,1,0:T(8,128)(2,1)}, u32[]{:S(2)}, u32[]{:S(2)}) %collective-permute-start.2) | collective-permute-done | bytes 262176 | tf_op jit(solution)/shard_map/attention/ppermute | solution.py:374
  41.7 4.9 %collective-permute-done.20.rest_0_ = bf16[2,128,512]{2,1,0:T(8,128)(2,1)} collective-permute-done((bf16[2,128,512]{2,1,0:T(8,128)(2,1)S(1)}, bf16[2,128,512]{2,1,0:T(8,128)(2,1)}, u32[]{:S(2)}, u32[]{:S(2)}) %collective-permute-start.20) | collective-permute-done | bytes 262176 | tf_op jit(solution)/shard_map/tokens/ppermute | solution.py:374
  47.7 13.5 %all-to-all-start.1 = ((f32[32,1,32]{2,1,0:T(1,128)}), f32[32,1,32]{2,1,0:T(1,128)S(1)}, u32[]{:S(2)}, u32[]{:S(2)}) async-start(f32[32,1,32]{2,1,0:T(1,128)} %bitcast.12), calls=%async_computation.1 | async-start | bytes 32768 | tf_op jit(solution)/shard_map/routes/all_to_all | solution.py:423
  61.5 1.7 %collective-permute-start.15 = (bf16[2,128,512]{2,1,0:T(8,128)(2,1)}, bf16[2,128,512]{2,1,0:T(8,128)(2,1)}, u32[]{:S(2)}, u32[]{:S(2)}) collective-permute-start(bf16[2,128,512]{2,1,0:T(8,128)(2,1)} %collective-permute-done.13.rest_0_), channel_id=1, source_target_pairs={{0,4},{4,0},{8,12},{12,8},{16,20},{20,16},{24,28},{28,24},{1,5},{5... | collective-permute-start | bytes 786440 | tf_op jit(solution)/shard_map/tokens/ppermute | solution.py:374
  63.3 5.0 %all-to-all-done.1 = f32[32,1,32]{2,1,0:T(1,128)S(1)} async-done(((f32[32,1,32]{2,1,0:T(1,128)}), f32[32,1,32]{2,1,0:T(1,128)S(1)}, u32[]{:S(2)}, u32[]{:S(2)}) %all-to-all-start.1) | async-done | bytes 4128 | tf_op jit(solution)/shard_map/routes/all_to_all | solution.py:423
  70.1 1.6 %copy-done.1 = bf16[1,2048,512]{2,1,0:T(8,128)(2,1)S(1)} copy-done((bf16[1,2048,512]{2,1,0:T(8,128)(2,1)S(1)}, bf16[1,2048,512]{2,1,0:T(8,128)(2,1)}, u32[]{:S(2)}) %copy-start.1) | copy-done | bytes 2097176
  71.7 3.3 %expert_chunk.4 = (bf16[2,32,2048]{2,1,0:T(8,128)(2,1)S(1)}, bf16[2,32,2048]{2,1,0:T(8,128)(2,1)S(1)}, bf16[2,2,32,2048]{3,2,1,0:T(8,128)(2,1)}, bf16[32,2048]{1,0:T(8,128)(2,1)S(1)}) custom-call(s32[3]{0:T(128)S(1)} %pad_add_fusion.where_ref, bf16[2,128,512]{2,1,0:T(8,128)(2,1)S(1)} %pad_maximum_fusion.rest_0_, ...), custom_call_target="tpu_custom_call" | custom-call | flops 805306368 | bytes 6291456 | tf_op jit(solution)/shard_map/experts/expert_chunk/pallas_call | solution.py:357
  79.9 5.2 %all-to-all-start.2 = ((bf16[8,2160,128]{2,1,0:T(8,128)(2,1)}), bf16[8,2160,128]{2,1,0:T(8,128)(2,1)}, u32[]{:S(2)}, u32[]{:S(2)}) async-start(bf16[8,2160,128]{2,1,0:T(8,128)(2,1)} %get-tuple-element.44), calls=%async_computation.2 | async-start | bytes 8847360 | tf_op jit(solution)/shard_map/send_states/all_to_all | solution.py:416
  85.1 1.6 %copy-done.2 = bf16[1,2048,512]{2,1,0:T(8,128)(2,1)S(1)} copy-done((bf16[1,2048,512]{2,1,0:T(8,128)(2,1)S(1)}, bf16[1,2048,512]{2,1,0:T(8,128)(2,1)}, u32[]{:S(2)}) %copy-start.2) | copy-done | bytes 2097176
  87.4 2.5 %expert_chunk.7 = (bf16[2,32,2048]{2,1,0:T(8,128)(2,1)S(1)}, bf16[2,32,2048]{2,1,0:T(8,128)(2,1)S(1)}, bf16[2,2,32,2048]{3,2,1,0:T(8,128)(2,1)S(1)}) custom-call(s32[3]{0:T(128)S(1)} %copy-done.11, bf16[2,128,512]{2,1,0:T(8,128)(2,1)} %collective-permute-done.20.rest_0_, bf16[2,128,512]{2,1,0:T(8,128)(2,1)} %collective-permute-done.21.rest_1_, ...), custom_call_target="tpu_custom_call" | custom-call | flops 805306368 | bytes 6291456 | tf_op jit(solution)/shard_map/experts/expert_chunk/pallas_call | solution.py:357
  90.3 2.6 %expert_chunk.6 = (bf16[2,32,2048]{2,1,0:T(8,128)(2,1)S(1)}, bf16[2,32,2048]{2,1,0:T(8,128)(2,1)S(1)}, bf16[2,2,32,2048]{3,2,1,0:T(8,128)(2,1)S(1)}) custom-call(s32[3]{0:T(128)S(1)} %copy-done.10, bf16[2,128,512]{2,1,0:T(8,128)(2,1)} %collective-permute-done.13.rest_0_, bf16[2,128,512]{2,1,0:T(8,128)(2,1)} %collective-permute-done.14.rest_1_, ...), custom_call_target="tpu_custom_call" | custom-call | flops 805306368 | bytes 6291456 | tf_op jit(solution)/shard_map/experts/expert_chunk/pallas_call | solution.py:357
  93.2 2.6 %expert_chunk.5 = (bf16[2,32,2048]{2,1,0:T(8,128)(2,1)S(1)}, bf16[2,32,2048]{2,1,0:T(8,128)(2,1)S(1)}, bf16[2,2,32,2048]{3,2,1,0:T(8,128)(2,1)S(1)}) custom-call(s32[3]{0:T(128)S(1)} %pad_add_fusion.1.where_ref, bf16[2,128,512]{2,1,0:T(8,128)(2,1)} %collective-permute-done.6.rest_0_, bf16[2,128,512]{2,1,0:T(8,128)(2,1)} %collective-permute-done.7.rest_1_, ...), custom_call_target="tpu_custom_call" | custom-call | flops 805306368 | bytes 6291456 | tf_op jit(solution)/shard_map/experts/expert_chunk/pallas_call | solution.py:357
  97.2 1.6 %collective-permute-start.5 = (bf16[2,32,2048]{2,1,0:T(8,128)(2,1)S(1)}, bf16[2,32,2048]{2,1,0:T(8,128)(2,1)S(1)}, u32[]{:S(2)}, u32[]{:S(2)}) collective-permute-start(bf16[2,32,2048]{2,1,0:T(8,128)(2,1)S(1)} %fusion.12), channel_id=1, source_target_pairs={{0,4},{4,0},{8,12},{12,8},{16,20},{20,16},{24,28},{28,24},{1,5},{5... | collective-permute-start | bytes 786440 | tf_op jit(solution)/shard_map/way_back/ppermute | solution.py:374
  99.5 1.6 %collective-permute-start.18 = (bf16[2,32,2048]{2,1,0:T(8,128)(2,1)S(1)}, bf16[2,32,2048]{2,1,0:T(8,128)(2,1)S(1)}, u32[]{:S(2)}, u32[]{:S(2)}) collective-permute-start(bf16[2,32,2048]{2,1,0:T(8,128)(2,1)S(1)} %fusion.6), channel_id=1, source_target_pairs={{0,4},{4,0},{8,12},{12,8},{16,20},{20,16},{24,28},{28,24},{1,5},{5... | collective-permute-start | bytes 786440 | tf_op jit(solution)/shard_map/way_back/ppermute | solution.py:374
  101.7 10.3 %collective-permute-done.25 = bf16[2,32,2048]{2,1,0:T(8,128)(2,1)S(1)} collective-permute-done((bf16[2,32,2048]{2,1,0:T(8,128)(2,1)S(1)}, bf16[2,32,2048]{2,1,0:T(8,128)(2,1)S(1)}, u32[]{:S(2)}, u32[]{:S(2)}) %collective-permute-start.25) | collective-permute-done | bytes 262176 | tf_op jit(solution)/shard_map/way_back/ppermute | solution.py:374
  112.1 1.6 %collective-permute-start.26 = (bf16[2,32,2048]{2,1,0:T(8,128)(2,1)S(1)}, bf16[2,32,2048]{2,1,0:T(8,128)(2,1)}, u32[]{:S(2)}, u32[]{:S(2)}) collective-permute-start(bf16[2,32,2048]{2,1,0:T(8,128)(2,1)S(1)} %fusion.5), channel_id=1, source_target_pairs={{0,24},{4,28},{8,16},{12,20},{16,8},{20,12},{24,0},{28,4},{1,25},{... | collective-permute-start | bytes 786440 | tf_op jit(solution)/shard_map/way_back/ppermute | solution.py:374
  113.7 3.9 %collective-permute-done.18 = bf16[2,32,2048]{2,1,0:T(8,128)(2,1)S(1)} collective-permute-done((bf16[2,32,2048]{2,1,0:T(8,128)(2,1)S(1)}, bf16[2,32,2048]{2,1,0:T(8,128)(2,1)S(1)}, u32[]{:S(2)}, u32[]{:S(2)}) %collective-permute-start.18) | collective-permute-done | bytes 262176 | tf_op jit(solution)/shard_map/way_back/ppermute | solution.py:374
  118.4 4.1 %collective-permute-done.11 = bf16[2,32,2048]{2,1,0:T(8,128)(2,1)S(1)} collective-permute-done((bf16[2,32,2048]{2,1,0:T(8,128)(2,1)S(1)}, bf16[2,32,2048]{2,1,0:T(8,128)(2,1)S(1)}, u32[]{:S(2)}, u32[]{:S(2)}) %collective-permute-start.11) | collective-permute-done | bytes 262176 | tf_op jit(solution)/shard_map/way_back/ppermute | solution.py:374
  123.3 1.0 fusion.13
  124.4 11.3 %all-to-all-done.2.arrived_ref = bf16[8,2160,128]{2,1,0:T(8,128)(2,1)} async-done(((bf16[8,2160,128]{2,1,0:T(8,128)(2,1)}), bf16[8,2160,128]{2,1,0:T(8,128)(2,1)}, u32[]{:S(2)}, u32[]{:S(2)}) %all-to-all-start.2) | async-done | bytes 4423712 | tf_op jit(solution)/shard_map/send_states/all_to_all | solution.py:416
  136.6 10.5 %landed_states.1 = bf16[8,2048,128]{2,1,0:T(8,128)(2,1)} custom-call(s32[8]{0:T(128)S(1)} %fusion.17.place_ref, bf16[8,2160,128]{2,1,0:T(8,128)(2,1)} %all-to-all-done.2.arrived_ref), custom_call_target="tpu_custom_call" | custom-call | flops 20000000 | bytes 9437184 | tf_op jit(solution)/shard_map/landed/landed_states/pallas_call | solution.py:271
  147.1 1.1 fusion.16
  148.7 4.7 %collective-permute-done.27 = bf16[32,2048]{1,0:T(8,128)(2,1)S(1)} collective-permute-done((bf16[32,2048]{1,0:T(8,128)(2,1)S(1)}, bf16[32,2048]{1,0:T(8,128)(2,1)S(1)}, u32[]{:S(2)}, u32[]{:S(2)}) %collective-permute-start.27) | collective-permute-done | bytes 131104 | tf_op jit(solution)/shard_map/mixed/ppermute | solution.py:374
  153.4 1.1 fusion.15
  (98 shorter events, 18.2 us)
Async XLA Ops:
  2.5 23.4 %all-to-all-start = ((bf16[32,4,512]{2,0,1:T(8,128)(2,1)}), bf16[32,4,512]{2,0,1:T(8,128)(2,1)S(1)}, u32[]{:S(2)}, u32[]{:S(2)}) async-start(bf16[32,4,512]{2,0,1:T(8,128)(2,1)} %copy.21), calls=%async_computation | async-start | bytes 262144 | tf_op jit(solution)/shard_map/core/all_to_all | solution.py:401
  6.7 63.4 %copy-start.3 = (bf16[1,256,2048]{2,1,0:T(8,128)(2,1)S(1)}, bf16[1,256,2048]{2,1,0:T(8,128)(2,1)}, u32[]{:S(2)}) copy-start(bf16[1,256,2048]{2,1,0:T(8,128)(2,1)} %rest_7_.7) | copy-start | bytes 3145732
  27.4 5.8 %collective-permute-start = (bf16[128,512]{1,0:T(8,128)(2,1)S(1)}, bf16[128,512]{1,0:T(8,128)(2,1)S(1)}, u32[]{:S(2)}, u32[]{:S(2)}) collective-permute-start(bf16[128,512]{1,0:T(8,128)(2,1)S(1)} %fusion.2), channel_id=1, source_target_pairs={{0,2},{1,3},{2,0},{3,1},{4,6},{5,7},{6,4},{7,5},{8,10},{9,11},{10,... | collective-permute-start | bytes 393224 | tf_op jit(solution)/shard_map/attention/ppermute | solution.py:374
  33.2 8.2 %collective-permute-start.2 = (bf16[2,128,512]{2,1,0:T(8,128)(2,1)S(1)}, bf16[2,128,512]{2,1,0:T(8,128)(2,1)}, u32[]{:S(2)}, u32[]{:S(2)}) collective-permute-start(bf16[2,128,512]{2,1,0:T(8,128)(2,1)S(1)} %pad_maximum_fusion.rest_0_), channel_id=1, source_target_pairs={{0,4},{4,0},{8,12},{12,8},{16,20},{20,16},{24,28},{28,24},{1,5},{5... | collective-permute-start | bytes 786440 | tf_op jit(solution)/shard_map/attention/ppermute | solution.py:374
  35.4 11.2 %collective-permute-start.20 = (bf16[2,128,512]{2,1,0:T(8,128)(2,1)S(1)}, bf16[2,128,512]{2,1,0:T(8,128)(2,1)}, u32[]{:S(2)}, u32[]{:S(2)}) collective-permute-start(bf16[2,128,512]{2,1,0:T(8,128)(2,1)S(1)} %pad_maximum_fusion.rest_0_), channel_id=1, source_target_pairs={{0,24},{4,28},{8,16},{12,20},{16,8},{20,12},{24,0},{28,4},{1,25},{... | collective-permute-start | bytes 786440 | tf_op jit(solution)/shard_map/tokens/ppermute | solution.py:374
  39.0 22.1 %collective-permute-start.13 = (bf16[2,128,512]{2,1,0:T(8,128)(2,1)S(1)}, bf16[2,128,512]{2,1,0:T(8,128)(2,1)}, u32[]{:S(2)}, u32[]{:S(2)}) collective-permute-start(bf16[2,128,512]{2,1,0:T(8,128)(2,1)S(1)} %pad_maximum_fusion.rest_0_), channel_id=1, source_target_pairs={{0,16},{4,20},{8,24},{12,28},{16,0},{20,4},{24,8},{28,12},{1,17},{... | collective-permute-start | bytes 786440 | tf_op jit(solution)/shard_map/tokens/ppermute | solution.py:374
  39.1 22.4 %collective-permute-start.6 = (bf16[2,128,512]{2,1,0:T(8,128)(2,1)S(1)}, bf16[2,128,512]{2,1,0:T(8,128)(2,1)}, u32[]{:S(2)}, u32[]{:S(2)}) collective-permute-start(bf16[2,128,512]{2,1,0:T(8,128)(2,1)S(1)} %pad_maximum_fusion.rest_0_), channel_id=1, source_target_pairs={{0,8},{4,12},{8,0},{12,4},{16,24},{20,28},{24,16},{28,20},{1,9},{5... | collective-permute-start | bytes 786440 | tf_op jit(solution)/shard_map/tokens/ppermute | solution.py:374
  39.8 29.7 %collective-permute-start.1 = (bf16[2,128,512]{2,1,0:T(8,128)(2,1)S(1)}, bf16[2,128,512]{2,1,0:T(8,128)(2,1)}, u32[]{:S(2)}, u32[]{:S(2)}) collective-permute-start(bf16[2,128,512]{2,1,0:T(8,128)(2,1)S(1)} %pad_maximum_fusion.rest_0_), channel_id=1, source_target_pairs={{0,1},{1,0},{2,3},{3,2},{4,5},{5,4},{6,7},{7,6},{8,9},{9,8},{10,11... | collective-permute-start | bytes 786440 | tf_op jit(solution)/shard_map/tokens/ppermute | solution.py:374
  41.6 28.5 %collective-permute-start.3 = (bf16[2,128,512]{2,1,0:T(8,128)(2,1)}, bf16[2,128,512]{2,1,0:T(8,128)(2,1)}, u32[]{:S(2)}, u32[]{:S(2)}) collective-permute-start(bf16[2,128,512]{2,1,0:T(8,128)(2,1)} %collective-permute-done.2.rest_2_), channel_id=1, source_target_pairs={{0,1},{1,0},{2,3},{3,2},{4,5},{5,4},{6,7},{7,6},{8,9},{9,8},{10,11... | collective-permute-start | bytes 786440 | tf_op jit(solution)/shard_map/tokens/ppermute | solution.py:374
  46.6 23.5 %collective-permute-start.22 = (bf16[2,128,512]{2,1,0:T(8,128)(2,1)}, bf16[2,128,512]{2,1,0:T(8,128)(2,1)}, u32[]{:S(2)}, u32[]{:S(2)}) collective-permute-start(bf16[2,128,512]{2,1,0:T(8,128)(2,1)} %collective-permute-done.20.rest_0_), channel_id=1, source_target_pairs={{0,4},{4,0},{8,12},{12,8},{16,20},{20,16},{24,28},{28,24},{1,5},{5... | collective-permute-start | bytes 786440 | tf_op jit(solution)/shard_map/tokens/ppermute | solution.py:374
  47.7 20.6 %all-to-all-start.1 = ((f32[32,1,32]{2,1,0:T(1,128)}), f32[32,1,32]{2,1,0:T(1,128)S(1)}, u32[]{:S(2)}, u32[]{:S(2)}) async-start(f32[32,1,32]{2,1,0:T(1,128)} %bitcast.12), calls=%async_computation.1 | async-start | bytes 32768 | tf_op jit(solution)/shard_map/routes/all_to_all | solution.py:423
  61.2 15.8 %collective-permute-start.21 = (bf16[2,128,512]{2,1,0:T(8,128)(2,1)}, bf16[2,128,512]{2,1,0:T(8,128)(2,1)}, u32[]{:S(2)}, u32[]{:S(2)}) collective-permute-start(bf16[2,128,512]{2,1,0:T(8,128)(2,1)} %collective-permute-done.20.rest_0_), channel_id=1, source_target_pairs={{0,1},{1,0},{2,3},{3,2},{4,5},{5,4},{6,7},{7,6},{8,9},{9,8},{10,11... | collective-permute-start | bytes 786440 | tf_op jit(solution)/shard_map/tokens/ppermute | solution.py:374
  61.5 15.5 %collective-permute-start.15 = (bf16[2,128,512]{2,1,0:T(8,128)(2,1)}, bf16[2,128,512]{2,1,0:T(8,128)(2,1)}, u32[]{:S(2)}, u32[]{:S(2)}) collective-permute-start(bf16[2,128,512]{2,1,0:T(8,128)(2,1)} %collective-permute-done.13.rest_0_), channel_id=1, source_target_pairs={{0,4},{4,0},{8,12},{12,8},{16,20},{20,16},{24,28},{28,24},{1,5},{5... | collective-permute-start | bytes 786440 | tf_op jit(solution)/shard_map/tokens/ppermute | solution.py:374
  69.5 8.5 %collective-permute-start.8 = (bf16[2,128,512]{2,1,0:T(8,128)(2,1)}, bf16[2,128,512]{2,1,0:T(8,128)(2,1)}, u32[]{:S(2)}, u32[]{:S(2)}) collective-permute-start(bf16[2,128,512]{2,1,0:T(8,128)(2,1)} %collective-permute-done.6.rest_0_), channel_id=1, source_target_pairs={{0,4},{4,0},{8,12},{12,8},{16,20},{20,16},{24,28},{28,24},{1,5},{5... | collective-permute-start | bytes 786440 | tf_op jit(solution)/shard_map/tokens/ppermute | solution.py:374
  70.1 8.1 %collective-permute-start.23 = (bf16[2,128,512]{2,1,0:T(8,128)(2,1)}, bf16[2,128,512]{2,1,0:T(8,128)(2,1)S(1)}, u32[]{:S(2)}, u32[]{:S(2)}) collective-permute-start(bf16[2,128,512]{2,1,0:T(8,128)(2,1)} %collective-permute-done.22.rest_2_), channel_id=1, source_target_pairs={{0,1},{1,0},{2,3},{3,2},{4,5},{5,4},{6,7},{7,6},{8,9},{9,8},{10,11... | collective-permute-start | bytes 786440 | tf_op jit(solution)/shard_map/tokens/ppermute | solution.py:374
  76.4 19.8 %collective-permute-start.4 = (bf16[2,2,32,2048]{3,2,1,0:T(8,128)(2,1)}, bf16[2,2,32,2048]{3,2,1,0:T(8,128)(2,1)}, u32[]{:S(2)}, u32[]{:S(2)}) collective-permute-start(bf16[2,2,32,2048]{3,2,1,0:T(8,128)(2,1)} %get-tuple-element.33), channel_id=1, source_target_pairs={{0,1},{1,0},{2,3},{3,2},{4,5},{5,4},{6,7},{7,6},{8,9},{9,8},{10,11... | collective-permute-start | bytes 1572872 | tf_op jit(solution)/shard_map/way_back/ppermute | solution.py:374
  77.0 12.9 %collective-permute-start.14 = (bf16[2,128,512]{2,1,0:T(8,128)(2,1)}, bf16[2,128,512]{2,1,0:T(8,128)(2,1)}, u32[]{:S(2)}, u32[]{:S(2)}) collective-permute-start(bf16[2,128,512]{2,1,0:T(8,128)(2,1)} %collective-permute-done.13.rest_0_), channel_id=1, source_target_pairs={{0,1},{1,0},{2,3},{3,2},{4,5},{5,4},{6,7},{7,6},{8,9},{9,8},{10,11... | collective-permute-start | bytes 786440 | tf_op jit(solution)/shard_map/tokens/ppermute | solution.py:374
  77.0 13.3 %collective-permute-start.16 = (bf16[2,128,512]{2,1,0:T(8,128)(2,1)}, bf16[2,128,512]{2,1,0:T(8,128)(2,1)}, u32[]{:S(2)}, u32[]{:S(2)}) collective-permute-start(bf16[2,128,512]{2,1,0:T(8,128)(2,1)} %collective-permute-done.15.rest_2_), channel_id=1, source_target_pairs={{0,1},{1,0},{2,3},{3,2},{4,5},{5,4},{6,7},{7,6},{8,9},{9,8},{10,11... | collective-permute-start | bytes 786440 | tf_op jit(solution)/shard_map/tokens/ppermute | solution.py:374
  78.1 15.1 %collective-permute-start.7 = (bf16[2,128,512]{2,1,0:T(8,128)(2,1)}, bf16[2,128,512]{2,1,0:T(8,128)(2,1)}, u32[]{:S(2)}, u32[]{:S(2)}) collective-permute-start(bf16[2,128,512]{2,1,0:T(8,128)(2,1)} %collective-permute-done.6.rest_0_), channel_id=1, source_target_pairs={{0,1},{1,0},{2,3},{3,2},{4,5},{5,4},{6,7},{7,6},{8,9},{9,8},{10,11... | collective-permute-start | bytes 786440 | tf_op jit(solution)/shard_map/tokens/ppermute | solution.py:374
  78.9 14.3 %collective-permute-start.9 = (bf16[2,128,512]{2,1,0:T(8,128)(2,1)}, bf16[2,128,512]{2,1,0:T(8,128)(2,1)}, u32[]{:S(2)}, u32[]{:S(2)}) collective-permute-start(bf16[2,128,512]{2,1,0:T(8,128)(2,1)} %collective-permute-done.8.rest_2_), channel_id=1, source_target_pairs={{0,1},{1,0},{2,3},{3,2},{4,5},{5,4},{6,7},{7,6},{8,9},{9,8},{10,11... | collective-permute-start | bytes 786440 | tf_op jit(solution)/shard_map/tokens/ppermute | solution.py:374
  79.9 55.8 %all-to-all-start.2 = ((bf16[8,2160,128]{2,1,0:T(8,128)(2,1)}), bf16[8,2160,128]{2,1,0:T(8,128)(2,1)}, u32[]{:S(2)}, u32[]{:S(2)}) async-start(bf16[8,2160,128]{2,1,0:T(8,128)(2,1)} %get-tuple-element.44), calls=%async_computation.2 | async-start | bytes 8847360 | tf_op jit(solution)/shard_map/send_states/all_to_all | solution.py:416
  89.9 8.8 %collective-permute-start.24 = (bf16[2,2,32,2048]{3,2,1,0:T(8,128)(2,1)S(1)}, bf16[2,2,32,2048]{3,2,1,0:T(8,128)(2,1)S(1)}, u32[]{:S(2)}, u32[]{:S(2)}) collective-permute-start(bf16[2,2,32,2048]{3,2,1,0:T(8,128)(2,1)S(1)} %get-tuple-element.42), channel_id=1, source_target_pairs={{0,1},{1,0},{2,3},{3,2},{4,5},{5,4},{6,7},{7,6},{8,9},{9,8},{10,11... | collective-permute-start | bytes 1572872 | tf_op jit(solution)/shard_map/way_back/ppermute | solution.py:374
  92.9 6.5 %collective-permute-start.17 = (bf16[2,2,32,2048]{3,2,1,0:T(8,128)(2,1)S(1)}, bf16[2,2,32,2048]{3,2,1,0:T(8,128)(2,1)S(1)}, u32[]{:S(2)}, u32[]{:S(2)}) collective-permute-start(bf16[2,2,32,2048]{3,2,1,0:T(8,128)(2,1)S(1)} %get-tuple-element.39), channel_id=1, source_target_pairs={{0,1},{1,0},{2,3},{3,2},{4,5},{5,4},{6,7},{7,6},{8,9},{9,8},{10,11... | collective-permute-start | bytes 1572872 | tf_op jit(solution)/shard_map/way_back/ppermute | solution.py:374
  95.8 5.3 %collective-permute-start.10 = (bf16[2,2,32,2048]{3,2,1,0:T(8,128)(2,1)S(1)}, bf16[2,2,32,2048]{3,2,1,0:T(8,128)(2,1)S(1)}, u32[]{:S(2)}, u32[]{:S(2)}) collective-permute-start(bf16[2,2,32,2048]{3,2,1,0:T(8,128)(2,1)S(1)} %get-tuple-element.36), channel_id=1, source_target_pairs={{0,1},{1,0},{2,3},{3,2},{4,5},{5,4},{6,7},{7,6},{8,9},{9,8},{10,11... | collective-permute-start | bytes 1572872 | tf_op jit(solution)/shard_map/way_back/ppermute | solution.py:374
  97.2 26.1 %collective-permute-start.5 = (bf16[2,32,2048]{2,1,0:T(8,128)(2,1)S(1)}, bf16[2,32,2048]{2,1,0:T(8,128)(2,1)S(1)}, u32[]{:S(2)}, u32[]{:S(2)}) collective-permute-start(bf16[2,32,2048]{2,1,0:T(8,128)(2,1)S(1)} %fusion.12), channel_id=1, source_target_pairs={{0,4},{4,0},{8,12},{12,8},{16,20},{20,16},{24,28},{28,24},{1,5},{5... | collective-permute-start | bytes 786440 | tf_op jit(solution)/shard_map/way_back/ppermute | solution.py:374
  98.8 13.2 %collective-permute-start.25 = (bf16[2,32,2048]{2,1,0:T(8,128)(2,1)S(1)}, bf16[2,32,2048]{2,1,0:T(8,128)(2,1)S(1)}, u32[]{:S(2)}, u32[]{:S(2)}) collective-permute-start(bf16[2,32,2048]{2,1,0:T(8,128)(2,1)S(1)} %fusion.3), channel_id=1, source_target_pairs={{0,4},{4,0},{8,12},{12,8},{16,20},{20,16},{24,28},{28,24},{1,5},{5... | collective-permute-start | bytes 786440 | tf_op jit(solution)/shard_map/way_back/ppermute | solution.py:374
  99.5 18.1 %collective-permute-start.18 = (bf16[2,32,2048]{2,1,0:T(8,128)(2,1)S(1)}, bf16[2,32,2048]{2,1,0:T(8,128)(2,1)S(1)}, u32[]{:S(2)}, u32[]{:S(2)}) collective-permute-start(bf16[2,32,2048]{2,1,0:T(8,128)(2,1)S(1)} %fusion.6), channel_id=1, source_target_pairs={{0,4},{4,0},{8,12},{12,8},{16,20},{20,16},{24,28},{28,24},{1,5},{5... | collective-permute-start | bytes 786440 | tf_op jit(solution)/shard_map/way_back/ppermute | solution.py:374
  101.1 21.4 %collective-permute-start.11 = (bf16[2,32,2048]{2,1,0:T(8,128)(2,1)S(1)}, bf16[2,32,2048]{2,1,0:T(8,128)(2,1)S(1)}, u32[]{:S(2)}, u32[]{:S(2)}) collective-permute-start(bf16[2,32,2048]{2,1,0:T(8,128)(2,1)S(1)} %fusion.9), channel_id=1, source_target_pairs={{0,4},{4,0},{8,12},{12,8},{16,20},{20,16},{24,28},{28,24},{1,5},{5... | collective-permute-start | bytes 786440 | tf_op jit(solution)/shard_map/way_back/ppermute | solution.py:374
  112.1 35.0 %collective-permute-start.26 = (bf16[2,32,2048]{2,1,0:T(8,128)(2,1)S(1)}, bf16[2,32,2048]{2,1,0:T(8,128)(2,1)}, u32[]{:S(2)}, u32[]{:S(2)}) collective-permute-start(bf16[2,32,2048]{2,1,0:T(8,128)(2,1)S(1)} %fusion.5), channel_id=1, source_target_pairs={{0,24},{4,28},{8,16},{12,20},{16,8},{20,12},{24,0},{28,4},{1,25},{... | collective-permute-start | bytes 786440 | tf_op jit(solution)/shard_map/way_back/ppermute | solution.py:374
  117.7 29.4 %collective-permute-start.19 = (bf16[2,32,2048]{2,1,0:T(8,128)(2,1)S(1)}, bf16[2,32,2048]{2,1,0:T(8,128)(2,1)}, u32[]{:S(2)}, u32[]{:S(2)}) collective-permute-start(bf16[2,32,2048]{2,1,0:T(8,128)(2,1)S(1)} %fusion.8), channel_id=1, source_target_pairs={{0,16},{4,20},{8,24},{12,28},{16,0},{20,4},{24,8},{28,12},{1,17},{... | collective-permute-start | bytes 786440 | tf_op jit(solution)/shard_map/way_back/ppermute | solution.py:374
  122.7 24.5 %collective-permute-start.12 = (bf16[2,32,2048]{2,1,0:T(8,128)(2,1)S(1)}, bf16[2,32,2048]{2,1,0:T(8,128)(2,1)}, u32[]{:S(2)}, u32[]{:S(2)}) collective-permute-start(bf16[2,32,2048]{2,1,0:T(8,128)(2,1)S(1)} %fusion.11), channel_id=1, source_target_pairs={{0,8},{4,12},{8,0},{12,4},{16,24},{20,28},{24,16},{28,20},{1,9},{5... | collective-permute-start | bytes 786440 | tf_op jit(solution)/shard_map/way_back/ppermute | solution.py:374
  148.2 5.1 %collective-permute-start.27 = (bf16[32,2048]{1,0:T(8,128)(2,1)S(1)}, bf16[32,2048]{1,0:T(8,128)(2,1)S(1)}, u32[]{:S(2)}, u32[]{:S(2)}) collective-permute-start(bf16[32,2048]{1,0:T(8,128)(2,1)S(1)} %fusion.16), channel_id=1, source_target_pairs={{0,2},{1,3},{2,0},{3,1},{4,6},{5,7},{6,4},{7,5},{8,10},{9,11},{10,... | collective-permute-start | bytes 393224 | tf_op jit(solution)/shard_map/mixed/ppermute | solution.py:374
  (14 other events, 196.8 us)

commit v4 on v3

--- a/solution.py
+++ b/solution.py
@@ -77,9 +77,11 @@
 
 
 def core_kernel(
-    lanes, home_ref, state_ref, q_ref, k_ref, v_ref, g_ref, b_ref, a_ref, gain_ref, out_ref, packed_ref,
-    k_s, q_s, v_s, g_s, a_s, b_s, m_s, o_s, held, pay_f, pay_s, in_sem, out_sem,
+    lanes, experts, home_ref, lane_ref, state_ref, q_ref, k_ref, v_ref, g_ref, b_ref, a_ref, gain_ref,
+    res_ref, ids_ref, prob_ref, out_ref, *rest,
 ):
+    packed = rest[:lanes]
+    k_s, q_s, v_s, g_s, a_s, b_s, m_s, o_s, r_s, w_s, held, pay_f, pay_s, in_sem, out_sem = rest[lanes:]
     requests, steps, _ = k_ref.shape
     hd = held.shape[-1]
     heads, key_heads = v_s.shape[0], k_s.shape[0]
@@ -95,12 +97,25 @@
     spread_rows(g_ref, g_s, requests, steps)
     sigmoid_rows(a_ref, a_s, requests, steps)
     sigmoid_rows(b_ref, b_s, requests, steps)
-    target = [lax.rem(lax.div(home_ref[r], requests), lanes) for r in range(requests)]
-    slots = [
-        target[r] * cap + sum([(target[p] == target[r]).astype(jnp.int32) for p in range(r)], jnp.int32(0))
+    target = [lax.rem(lax.div(home_ref[r], requests), lanes) ^ lane_ref[0] for r in range(requests)]
+    ranks = [
+        sum([(target[p] == target[r]).astype(jnp.int32) for p in range(r)], jnp.int32(0))
         for r in range(requests)
     ]
     state_rows = heads * hd
+
+    def send(source, r, start, kind):
+        rows = pl.ds(start, source.shape[0])
+        for d in range(lanes):
+
+            @pl.when(target[r] == d)
+            def _():
+                pltpu.make_async_copy(
+                    source, packed[d].at[ranks[r], rows], out_sem.at[kind, r]
+                ).start()
+
+        return pltpu.make_async_copy(source, packed[0].at[0, rows], out_sem.at[kind, r])
+
     sent = []
     pay_f[...] = jnp.zeros_like(pay_f)
     for r in range(requests):
@@ -116,12 +131,7 @@
         place = lax.rem(home_ref[r], requests).astype(F32)
         pay_f[at + 2 * steps : at + 3 * steps, :] = jnp.full((steps, hd), place, F32)
         pay_s[r] = pay_f[...].astype(BF16)
-        sent.append(
-            pltpu.make_async_copy(
-                pay_s.at[r], packed_ref.at[slots[r], pl.ds(state_rows, pay_s.shape[1])], out_sem.at[0, r]
-            )
-        )
-        sent[-1].start()
+        sent.append(send(pay_s.at[r], r, state_rows, 0))
     for r in range(requests):
         copies[r].wait()
         rows = slice(r * steps, (r + 1) * steps)
@@ -131,12 +141,7 @@
                 m_s[h, r * 2 * steps : (r + 1) * 2 * steps, :] = jnp.dot(
                     left, held[r, h * hd : (h + 1) * hd, :], preferred_element_type=F32
                 )
-        sent.append(
-            pltpu.make_async_copy(
-                held.at[r], packed_ref.at[slots[r], pl.ds(0, state_rows)], out_sem.at[1, r]
-            )
-        )
-        sent[-1].start()
+        sent.append(send(held.at[r], r, 0, 1))
     gain = gain_ref[...]
 
     def emit(t, h, o):
@@ -146,29 +151,50 @@
 
     for kh in range(key_heads):
         recurrence(kh, repeats, steps, requests, hd, k_s, q_s, v_s, a_s, b_s, m_s, emit, None)
-    for h in range(heads):
-        out_ref[:, h * hd : (h + 1) * hd] = o_s[h].astype(BF16)
+    top = ids_ref.shape[-1]
+    place = lax.broadcasted_iota(jnp.int32, (steps, w_s.shape[-1]), 1)
+    for r in range(requests):
+        rows = slice(r * steps, (r + 1) * steps)
+        r_s[rows, :] = res_ref[r].astype(F32)
+        prob = prob_ref[r]
+        prob = prob / row_sum(prob)
+        weight = jnp.zeros(place.shape, F32)
+        ids = ids_ref[r]
+        for j in range(top):
+            high = prob[:, j : j + 1].astype(BF16).astype(F32)
+            weight = jnp.where(place == ids[:, j : j + 1], high, weight)
+            weight = jnp.where(place == ids[:, j : j + 1] + experts, prob[:, j : j + 1] - high, weight)
+        w_s[rows, :] = weight
+    width = heads * hd
+    cols = res_ref.shape[-1] // lanes
+    for p in range(lanes):
+        for h in range(heads):
+            out_ref[p, :, h * hd : (h + 1) * hd] = o_s[h].astype(BF16)
+        out_ref[p, :, width : width + cols] = r_s[:, p * cols : (p + 1) * cols].astype(BF16)
+        out_ref[p, :, width + cols :] = w_s[...].astype(BF16)
     for c in sent:
         c.wait()
 
 
 def core_rows(
-    home, lanes, states, query_rows, key_rows, value_rows, gate_rows, beta_logit, decay_logit, core_gain
+    home, lane, lanes, experts, states, query_rows, key_rows, value_rows, gate_rows, beta_logit, decay_logit,
+    core_gain, residual, route_ids, route_prob,
 ):
     requests, heads, hd, _ = states.shape
     steps = key_rows.shape[1]
     kw, vw = key_rows.shape[-1], value_rows.shape[-1]
     tokens = requests * steps
     _, pay_rows = packed_rows(kw // hd, heads, steps)
+    width = residual.shape[-1]
+    weight_lanes = -(-2 * experts // 128) * 128
     vmem, hbm = pl.BlockSpec(memory_space=pltpu.VMEM), pl.BlockSpec(memory_space=pl.ANY)
+    smem = pl.BlockSpec(memory_space=pltpu.SMEM)
     return pl.pallas_call(
-        functools.partial(core_kernel, lanes),
-        in_specs=[pl.BlockSpec(memory_space=pltpu.SMEM), hbm] + [vmem] * 7,
-        out_specs=[vmem, hbm],
-        out_shape=[
-            jax.ShapeDtypeStruct((tokens, vw), BF16),
-            jax.ShapeDtypeStruct((requests, heads * hd + pay_rows, hd), BF16),
-        ],
+        functools.partial(core_kernel, lanes, experts),
+        in_specs=[smem, smem, hbm] + [vmem] * 10,
+        out_specs=[vmem] + [hbm] * lanes,
+        out_shape=[jax.ShapeDtypeStruct((lanes, tokens, vw + width // lanes + weight_lanes), BF16)]
+        + [jax.ShapeDtypeStruct((requests // lanes, heads * hd + pay_rows, hd), BF16)] * lanes,
         scratch_shapes=[
             pltpu.VMEM((kw // hd, tokens, hd), F32),
             pltpu.VMEM((kw // hd, tokens, hd), F32),
@@ -178,6 +204,8 @@
             pltpu.VMEM((tokens, 128), F32),
             pltpu.VMEM((heads, 2 * tokens, hd), F32),
             pltpu.VMEM((heads, tokens, hd), F32),
+            pltpu.VMEM((tokens, width), F32),
+            pltpu.VMEM((tokens, weight_lanes), F32),
             pltpu.VMEM((requests, heads * hd, hd), BF16),
             pltpu.VMEM((pay_rows, hd), F32),
             pltpu.VMEM((requests, pay_rows, hd), BF16),
@@ -188,28 +216,32 @@
         cost_estimate=pl.CostEstimate(flops=20_000_000, bytes_accessed=9 * MIB, transcendentals=100_000),
         name="core_rows",
     )(
-        home, states.reshape(requests, heads * hd, hd), query_rows, key_rows, value_rows, gate_rows,
-        beta_logit, decay_logit, core_gain.reshape(1, hd),
+        home, lane, states.reshape(requests, heads * hd, hd), query_rows, key_rows, value_rows, gate_rows,
+        beta_logit, decay_logit, core_gain.reshape(1, hd), residual, route_ids, route_prob,
     )
 
 
 def state_kernel(
-    key_heads, heads, steps, place_ref, arrived_ref, out_ref,
-    k_s, v_s, a_s, b_s, m_s, u_s, c_s, held, pay_s, ready, in_sem, pay_sem, out_sem,
+    key_heads, heads, steps, count, place_ref, *rest
 ):
+    arrived = rest[:count]
+    out_ref, k_s, v_s, a_s, b_s, m_s, u_s, c_s, held, pay_s, ready, in_sem, pay_sem, out_sem = rest[-14:]
     requests, state_rows, hd = held.shape
+    cap = requests // count
     repeats = heads // key_heads
     pays, copies = [], []
     for r in range(requests):
         pays.append(
             pltpu.make_async_copy(
-                arrived_ref.at[r, pl.ds(state_rows, pay_s.shape[1])], pay_s.at[r], pay_sem.at[r]
+                arrived[r // cap].at[r % cap, pl.ds(state_rows, pay_s.shape[1])], pay_s.at[r], pay_sem.at[r]
             )
         )
         pays[-1].start()
     for r in range(requests):
         copies.append(
-            pltpu.make_async_copy(arrived_ref.at[r, pl.ds(0, state_rows)], held.at[r], in_sem.at[r])
+            pltpu.make_async_copy(
+                arrived[r // cap].at[r % cap, pl.ds(0, state_rows)], held.at[r], in_sem.at[r]
+            )
         )
         copies[-1].start()
     for r in range(requests):
@@ -263,16 +295,20 @@
         c.wait()
 
 
-def landed_states(place, arrived, key_heads, heads, steps):
-    requests, all_rows, hd = arrived.shape
+def landed_states(arrived, before, total, key_heads, heads, steps):
+    cap, all_rows, hd = arrived[0].shape
+    place_row = heads * hd + (key_heads + heads + 2) * steps
+    place = jnp.concatenate([a[:, place_row, 0] for a in arrived]).astype(jnp.int32)
+    requests = cap * len(arrived)
     tokens = requests * steps
     state_rows = heads * hd
     hbm = pl.BlockSpec(memory_space=pl.ANY)
     out = pl.pallas_call(
-        functools.partial(state_kernel, key_heads, heads, steps),
-        in_specs=[pl.BlockSpec(memory_space=pltpu.SMEM), hbm],
+        functools.partial(state_kernel, key_heads, heads, steps, len(arrived)),
+        in_specs=[pl.BlockSpec(memory_space=pltpu.SMEM)] + [hbm] * (len(arrived) + len(before)),
         out_specs=hbm,
-        out_shape=jax.ShapeDtypeStruct((requests, state_rows, hd), BF16),
+        out_shape=jax.ShapeDtypeStruct((total, state_rows, hd), BF16),
+        input_output_aliases={len(arrived) + 1: 0} if before else {},
         scratch_shapes=[
             pltpu.VMEM((key_heads, tokens, hd), F32),
             pltpu.VMEM((heads, tokens, hd), F32),
@@ -289,19 +325,21 @@
             pltpu.SemaphoreType.DMA((2,)),
         ],
         compiler_params=pltpu.CompilerParams(vmem_limit_bytes=32 * MIB),
-        cost_estimate=pl.CostEstimate(flops=20_000_000, bytes_accessed=9 * MIB, transcendentals=10_000),
+        cost_estimate=pl.CostEstimate(flops=20_000_000, bytes_accessed=requests * MIB, transcendentals=10_000),
         name="landed_states",
-    )(place, arrived)
-    return out.reshape(requests, heads, hd, hd)
-
-
-def expert_kernel(sides, own_out, where_ref, *rest):
+    )(place, *arrived, *before)
+    return out
+
+
+def expert_kernel(sides, own_out, experts, where_ref, *rest):
     pieces = rest[: 2 * sides]
-    weight_ref, gain_ref, up_ref, down_ref = rest[2 * sides : 2 * sides + 4]
-    keeps = rest[2 * sides + 4 : 3 * sides + 4]
-    give_ref = rest[3 * sides + 4]
+    gain_ref, up_ref, down_ref = rest[2 * sides : 2 * sides + 3]
+    keeps = rest[2 * sides + 3 : 3 * sides + 3]
+    give_ref = rest[3 * sides + 3]
     result_s = rest[-1]
-    spans, group_rows, cols = pieces[0].shape
+    group_rows = pieces[0].shape[0]
+    cols = gain_ref.shape[-1]
+    spans = give_ref.shape[1]
     tokens = give_ref.shape[2]
     width = down_ref.shape[-1]
     hidden_units = down_ref.shape[1]
@@ -309,7 +347,7 @@
     blocks = [(x, c) for x in range(spans) for c in range(2)]
     values = {}
     for x, c in blocks:
-        parts = [pieces[2 * y + c][x] for y in range(sides)]
+        parts = [pieces[2 * y + c][:, x * cols : (x + 1) * cols] for y in range(sides)]
         values[x, c] = jnp.concatenate(parts, axis=0).astype(F32)
     total = sum(row_sum(values[b] * values[b]) for b in blocks)
     scale = lax.rsqrt(total * (1.0 / width) + EPS)
@@ -321,19 +359,17 @@
         term = jnp.dot(normed, up, preferred_element_type=F32)
         joined = term if joined is None else joined + term
         if own_out:
-            rest[3 * sides + 5][:, pl.ds(pl.multiple_of(block * cols, cols), cols)] = pieces[c][
-                x, pl.ds(pl.multiple_of(e * tokens, tokens), tokens), :
+            rest[3 * sides + 4][:, pl.ds(pl.multiple_of(block * cols, cols), cols)] = pieces[c][
+                pl.ds(pl.multiple_of(e * tokens, tokens), tokens), x * cols : (x + 1) * cols
             ]
     active = (jax.nn.silu(joined[:, :hidden_units]) * joined[:, hidden_units:]).astype(BF16)
     result = jnp.dot(active, down_ref[0], preferred_element_type=F32).astype(BF16)
-    eye = lax.broadcasted_iota(jnp.int32, (group_rows, group_rows), 0) == lax.broadcasted_iota(
-        jnp.int32, (group_rows, group_rows), 1
-    )
-    weights = []
-    for y in range(sides):
-        line = weight_ref[pl.ds(where_ref[1 + y], 1), :]
-        weights.append(row_sum(jnp.where(eye, jnp.broadcast_to(line, eye.shape), 0.0)))
-    result_s[...] = (result.astype(F32) * jnp.concatenate(weights, axis=0)).astype(BF16)
+    marks = [pieces[2 * y][:, spans * cols :].astype(F32) for y in range(sides)]
+    marks = jnp.concatenate(marks, axis=0)
+    place = lax.broadcasted_iota(jnp.int32, marks.shape, 1)
+    mine = (place == where_ref[1]) | (place == where_ref[1] + experts)
+    weight = row_sum(jnp.where(mine, marks, 0.0))
+    result_s[...] = (result.astype(F32) * weight).astype(BF16)
     for y in range(sides):
         for x in range(spans):
             for c in range(2):
@@ -345,9 +381,9 @@
                     keeps[y][x] = rows
 
 
-def expert_chunk(where, pieces, weights, gain, gate_up, down_weight, tokens, own_out):
+def expert_chunk(where, pieces, gain, gate_up, down_weight, tokens, experts, own_out):
     sides = len(pieces) // 2
-    spans, group_rows, cols = pieces[0].shape
+    spans, group_rows = gain.shape[0] // 2, pieces[0].shape[0]
     width = down_weight.shape[-1]
     vmem = pl.BlockSpec(memory_space=pltpu.VMEM)
     keep = jax.ShapeDtypeStruct((spans, tokens, width), BF16)
@@ -355,8 +391,8 @@
     own = [jax.ShapeDtypeStruct((tokens, width), BF16)] if own_out else []
     rows = sides * group_rows
     outs = pl.pallas_call(
-        functools.partial(expert_kernel, sides, own_out),
-        in_specs=[pl.BlockSpec(memory_space=pltpu.SMEM)] + [vmem] * (len(pieces) + 4),
+        functools.partial(expert_kernel, sides, own_out, experts),
+        in_specs=[pl.BlockSpec(memory_space=pltpu.SMEM)] + [vmem] * (len(pieces) + 3),
         out_specs=[vmem] * (sides + 1 + len(own)),
         out_shape=[keep] * sides + [give] + own,
         scratch_shapes=[pltpu.VMEM((rows, width), BF16)],
@@ -365,7 +401,7 @@
             flops=6 * rows * width * down_weight.shape[1], bytes_accessed=6 * MIB, transcendentals=0
         ),
         name="expert_chunk",
-    )(where, *pieces, weights, gain, gate_up, down_weight)
+    )(where, *pieces, gain, gate_up, down_weight)
     return outs
 
 
@@ -395,57 +431,65 @@
 
     experts = groups * lanes
     cols = out_weight.shape[1]
-    everyone = functools.partial(lax.all_to_all, split_axis=0, concat_axis=0, tiled=True)
+    me = my_group * lanes + my_lane
 
     with jax.named_scope("core"):
-        before = lax.all_to_all(
-            residual.reshape(tokens, width), "ep", split_axis=1, concat_axis=0, tiled=True
+        sent, *packed = core_rows(
+            new_home, my_lane.reshape(1), lanes, experts, states, query_rows, key_rows, value_rows,
+            gate_rows, beta_logit, decay_logit, core_gain, residual, route_ids, route_prob,
         )
-        core, packed = core_rows(
-            new_home, lanes, states, query_rows, key_rows, value_rows, gate_rows, beta_logit,
-            decay_logit, core_gain,
-        )
-        group_core = lax.all_gather(core, "ep", axis=0, tiled=True)
+        got = lax.all_to_all(sent, "ep", split_axis=0, concat_axis=0, tiled=True)
+        got = got.reshape(lanes * tokens, got.shape[-1])
     with jax.named_scope("attention"):
-        attention = jnp.dot(group_core, out_weight, preferred_element_type=F32).astype(BF16)
+        attention = jnp.dot(got[:, :vw], out_weight, preferred_element_type=F32).astype(BF16)
+        before = got[:, vw : vw + cols]
         hidden_cols = (before.astype(F32) + attention.astype(F32)).astype(BF16)
-        held = jnp.stack([hidden_cols] + [swap(hidden_cols, "ep", d) for d in range(2, lanes, 2)])
+        others = [swap(hidden_cols, "ep", d) for d in range(2, lanes, 2)]
+        held = jnp.concatenate([hidden_cols] + others + [got[:, vw + cols :]], axis=1)
         held, packed = lax.optimization_barrier((held, packed))
-        first_across = swap(held, "dp", 1)
+
     with jax.named_scope("send_states"):
-        arrived = everyone(packed, "ep")
-    with jax.named_scope("routes"):
-        route_prob, first_across = lax.optimization_barrier((route_prob, first_across))
-        weights = route_prob.reshape(tokens, top)
-        weights = weights / jnp.sum(weights, -1, keepdims=True)
-        named = route_ids.reshape(tokens, top)[None] == jnp.arange(experts, dtype=jnp.int32)[:, None, None]
-        weights = jnp.sum(jnp.where(named, weights[None], 0.0), axis=-1)
-        weights = everyone(weights, ("dp", "ep")).reshape(groups, lanes * tokens)
+        arrived = [packed[0]]
+        for d in range(1, lanes):
+            if d > 2:
+                packed, arrived[-1] = lax.optimization_barrier((packed, arrived[-1]))
+            arrived.append(swap(packed[d], "ep", d))
 
     gain = moe_gain.reshape(lanes, cols)
-    sums = []
+    where = jnp.stack([my_lane, me])
+    far = groups // 2
+    chunks = [0] + [d for d in range(groups - 2, 0, -2) if d != far] + [far]
+    sums, asides = {}, []
     own_rows = None
-    for d in range(0, groups, 2):
+    with jax.named_scope("tokens"):
+        near = {d: swap(held, "dp", d) if d else held for d in chunks}
+    for d in chunks:
         with jax.named_scope("tokens"):
-            near = swap(held, "dp", d) if d else held
-            across = swap(near, "dp", 1) if d else first_across
-            pieces = [near, swap(near, "ep", 1), across, swap(across, "ep", 1)]
+            across = swap(near[d], "dp", 1)
+            pieces = [near[d], swap(near[d], "ep", 1), across, swap(across, "ep", 1)]
+            if d == far:
+                pieces, asides, arrived[2:3] = lax.optimization_barrier((pieces, asides, arrived[2:3]))
         with jax.named_scope("experts"):
-            where = jnp.stack([my_lane, my_group ^ d, my_group ^ d ^ 1])
-            outs = expert_chunk(where, pieces, weights, gain, gate_up, down_weight, tokens, d == 0)
+            outs = expert_chunk(where, pieces, gain, gate_up, down_weight, tokens, experts, d == 0)
             keep_near, keep_across, give = outs[:3]
             if d == 0:
                 own_rows = outs[3]
         with jax.named_scope("way_back"):
-            got = swap(give, "ep", 1)
-            back = swap(summed(keep_across, got[1]).astype(BF16), "dp", 1)
-            chunk = summed(keep_near, got[0], back)
-            sums.append(swap(chunk.astype(BF16), "dp", d) if d else chunk)
+            taken = swap(give, "ep", 1)
+            asides.append(summed(keep_across, taken[1]).astype(BF16))
+            sums[d] = (keep_near, taken)
+    with jax.named_scope("way_back"):
+        for d, aside in zip(chunks, asides):
+            keep_near, taken = sums[d]
+            chunk = summed(keep_near, taken[0], swap(aside, "dp", 1))
+            sums[d] = swap(chunk.astype(BF16), "dp", d) if d else chunk
+        sums = [sums[d] for d in chunks]
     with jax.named_scope("landed"):
-        place_row = heads * hd + (kw // hd + heads + 2) * steps
-        place = arrived[:, place_row, 0].astype(jnp.int32)
-        moved_out = landed_states(place, arrived, kw // hd, heads, steps)
+        sizes = (requests, kw // hd, heads, steps)
+        moved_out = landed_states(arrived[:-1], [], *sizes)
         sums, moved_out = lax.optimization_barrier((sums, moved_out))
+        moved_out = landed_states(arrived[-1:], [moved_out], *sizes)
+        moved_out = moved_out.reshape(requests, heads, hd, hd)
     with jax.named_scope("mixed"):
         mixed = summed(own_rows, *[s[0] for s in sums])
         for x in range(1, lanes // 2):

time: 156 us -> 136 us (0.87)
  starting transfers between devices: 42.9 us -> 23.2 us
  other arithmetic: 8.56 us -> 1.12 us
  blocking collectives: 9.61 us -> 14.9 us
  waiting for transfers between devices: 51.3 us -> 53.7 us
    all_to_all x3 -> x0, starting transfers between devices: 22.9 us -> none  [the longest x1 13.5 us: shards(): weights = everyone(weights, ('dp', 'ep')).reshape(groups, lanes * tokens)]
    ppermute x28 -> x31, waiting for transfers between devices: 35.1 us -> 53.7 us  [swap(): return lax.ppermute(x, axis, [(i, i ^ d) for i in range(size)])]
    all_to_all x3 -> x0, waiting for transfers between devices: 16.2 us -> none  [the longest x1 11.3 us: shards(): arrived = everyone(packed, 'ep')]
    all_to_all x0 -> x1, blocking collectives: none -> 14.9 us  [shards(): got = lax.all_to_all(sent, 'ep', split_axis=0, concat_axis=0, tiled=True)]
    all_gather x1 -> x0, blocking collectives: 9.61 us -> none  [shards(): group_core = lax.all_gather(core, 'ep', axis=0, tiled=True)]
    ppermute x28 -> x31, starting transfers between devices: 20 us -> 23.2 us  [swap(): return lax.ppermute(x, axis, [(i, i ^ d) for i in range(size)])]
    all_to_all x3 -> x0, local copies, waits for them, and re-layouts: 2.33 us -> none  [the longest x2 1.82 us: shards(): lax.all_to_all(residual.reshape(tokens, width), 'ep', split_axis=1, conca...]
    add x2, other arithmetic: 2.14 us -> 0.16 us  [summed(): return functools.reduce(lambda p, q: p + q, [t.astype(F32) for t in terms])]
  transfers between devices with their start and end apart: 31 -> 31, of which waited for: 9 -> 12; matrix products, arithmetic and copies ran while one was open for 5% -> 2% of each run, Pallas kernels for 20% -> 15%
where the time goes in v4:
time: 136 us
  waiting for transfers between devices  53.7 us (39%)
  Pallas kernels  31.5 us (23%)
  starting transfers between devices  23.2 us (17%)
  blocking collectives  14.9 us (11%)
  local copies, waits for them, and re-layouts  9.82 us (7%)
    ppermute x31, waiting for transfers between devices, swap(): return lax.ppermute(x, axis, [(i, i ^ d) for i in range(size)])  53.7 us
    ppermute x31, starting transfers between devices, swap(): return lax.ppermute(x, axis, [(i, i ^ d) for i in range(size)])  23.2 us
    all_to_all x1, blocking collectives, shards(): got = lax.all_to_all(sent, 'ep', split_axis=0, concat_axis=0, tiled=True)  14.9 us
    pallas_call x2, Pallas kernels, landed_states(): pl.pallas_call(functools.partial(state_kernel, key_heads, heads, steps, l...  11.4 us
    pallas_call x1, Pallas kernels, core_rows(): pl.pallas_call(functools.partial(core_kernel, lanes, experts), in_specs=[...  11.1 us
    pallas_call x4, Pallas kernels, expert_chunk(): pl.pallas_call(functools.partial(expert_kernel, sides, own_out, experts),...  9.1 us
    unnamed x34, local copies, waits for them, and re-layouts  7.44 us
  transfers between devices with their start and end apart: 31, of which 12 were waited for; matrix products, arithmetic and copies ran while one was open for 2% of the time, Pallas kernels for 15%

profile of v4, /device:TPU:0, one launch (start us, length us, event | category | flops | bytes accessed | tf_op | source)
XLA Modules:
  0.0 135.6 jit_solution(662880748421218811)
XLA Ops:
  0.7 11.1 %core_rows.1 = (bf16[4,32,2688]{2,1,0:T(8,128)(2,1)}, bf16[2,2160,128]{2,1,0:T(8,128)(2,1)}, bf16[2,2160,128]{2,1,0:T(8,128)(2,1)}, bf16[2,2160,128]{2,1,0:T(8,128)(2,1)}, bf16[2,2160,128]{2,1,0:T(8,128)(2,1)}) custom-call(s32[8]{0:T(128)} %home_ref.1, s32[1]{0:T(128)} %bitcast.lane_ref, bf16[8,2048,128]{2,1,0:T(8,128)(2,1)} %bitcast.63, ...), custom_call_target="tpu_custom_call" | custom-call | flops 20000000 | bytes 9437184 | tf_op jit(solution)/shard_map/core/core_rows/pallas_call | solution.py:192
  11.7 14.9 %all_to_all.5 = bf16[4,32,2688]{2,1,0:T(8,128)(2,1)S(1)} all-to-all(bf16[4,32,2688]{2,1,0:T(8,128)(2,1)} %get-tuple-element.40), channel_id=1, replica_groups=mesh['dp'=8,'ep'=4] {'ep'}, dimensions={0} | all-to-all | bytes 1376256 | tf_op jit(solution)/shard_map/core/all_to_all | solution.py:441
  27.4 5.0 %collective-permute-done = bf16[128,512]{1,0:T(8,128)(2,1)S(1)} collective-permute-done((bf16[128,512]{1,0:T(8,128)(2,1)S(1)}, bf16[128,512]{1,0:T(8,128)(2,1)S(1)}, u32[]{:S(2)}, u32[]{:S(2)}) %collective-permute-start) | collective-permute-done | bytes 131104 | tf_op jit(solution)/shard_map/attention/ppermute | solution.py:410
  32.5 3.3 %collective-permute-start.5 = (bf16[128,1152]{1,0:T(8,128)(2,1)S(1)}, bf16[128,1152]{1,0:T(8,128)(2,1)S(1)}, u32[]{:S(2)}, u32[]{:S(2)}) collective-permute-start(bf16[128,1152]{1,0:T(8,128)(2,1)S(1)} %pad_maximum_fusion.rest_0_), channel_id=1, source_target_pairs={{0,16},{4,20},{8,24},{12,28},{16,0},{20,4},{24,8},{28,12},{1,17},{... | collective-permute-start | bytes 884744 | tf_op jit(solution)/shard_map/tokens/ppermute | solution.py:410
  35.8 1.5 %collective-permute-start.2 = (bf16[128,1152]{1,0:T(8,128)(2,1)S(1)}, bf16[128,1152]{1,0:T(8,128)(2,1)S(1)}, u32[]{:S(2)}, u32[]{:S(2)}) collective-permute-start(bf16[128,1152]{1,0:T(8,128)(2,1)S(1)} %pad_maximum_fusion.rest_0_), channel_id=1, source_target_pairs={{0,4},{4,0},{8,12},{12,8},{16,20},{20,16},{24,28},{28,24},{1,5},{5... | collective-permute-start | bytes 884744 | tf_op jit(solution)/shard_map/tokens/ppermute | solution.py:410
  37.3 1.3 collective-permute-start.9
  38.9 17.1 %collective-permute-done.5.rest_0_ = bf16[128,1152]{1,0:T(8,128)(2,1)S(1)} collective-permute-done((bf16[128,1152]{1,0:T(8,128)(2,1)S(1)}, bf16[128,1152]{1,0:T(8,128)(2,1)S(1)}, u32[]{:S(2)}, u32[]{:S(2)}) %collective-permute-start.5) | collective-permute-done | bytes 294944 | tf_op jit(solution)/shard_map/tokens/ppermute | solution.py:410
  56.7 1.5 %collective-permute-start.7 = (bf16[128,1152]{1,0:T(8,128)(2,1)S(1)}, bf16[128,1152]{1,0:T(8,128)(2,1)S(1)}, u32[]{:S(2)}, u32[]{:S(2)}) collective-permute-start(bf16[128,1152]{1,0:T(8,128)(2,1)S(1)} %collective-permute-done.5.rest_0_), channel_id=1, source_target_pairs={{0,4},{4,0},{8,12},{12,8},{16,20},{20,16},{24,28},{28,24},{1,5},{5... | collective-permute-start | bytes 884744 | tf_op jit(solution)/shard_map/tokens/ppermute | solution.py:410
  59.9 6.7 %collective-permute-done.7.rest_2_ = bf16[128,1152]{1,0:T(8,128)(2,1)S(1)} collective-permute-done((bf16[128,1152]{1,0:T(8,128)(2,1)S(1)}, bf16[128,1152]{1,0:T(8,128)(2,1)S(1)}, u32[]{:S(2)}, u32[]{:S(2)}) %collective-permute-start.7) | collective-permute-done | bytes 294944 | tf_op jit(solution)/shard_map/tokens/ppermute | solution.py:410
  68.0 1.5 %collective-permute-start.16 = (bf16[128,1152]{1,0:T(8,128)(2,1)}, bf16[128,1152]{1,0:T(8,128)(2,1)}, u32[]{:S(2)}, u32[]{:S(2)}) collective-permute-start(bf16[128,1152]{1,0:T(8,128)(2,1)} %collective-permute-done.14.rest_0_), channel_id=1, source_target_pairs={{0,4},{4,0},{8,12},{12,8},{16,20},{20,16},{24,28},{28,24},{1,5},{5... | collective-permute-start | bytes 884744 | tf_op jit(solution)/shard_map/tokens/ppermute | solution.py:410
  69.5 3.4 %collective-permute-done.11.rest_2_ = bf16[128,1152]{1,0:T(8,128)(2,1)} collective-permute-done((bf16[128,1152]{1,0:T(8,128)(2,1)}, bf16[128,1152]{1,0:T(8,128)(2,1)}, u32[]{:S(2)}, u32[]{:S(2)}) %collective-permute-start.11) | collective-permute-done | bytes 294944 | tf_op jit(solution)/shard_map/tokens/ppermute | solution.py:410
  73.1 1.6 %copy-done.1 = bf16[1,2048,512]{2,1,0:T(8,128)(2,1)S(1)} copy-done((bf16[1,2048,512]{2,1,0:T(8,128)(2,1)S(1)}, bf16[1,2048,512]{2,1,0:T(8,128)(2,1)}, u32[]{:S(2)}) %copy-start.1) | copy-done | bytes 2097176
  74.7 1.0 copy-done.10
  75.6 1.0 copy-done.12
  76.6 1.0 copy-done.14
  77.5 2.0 %expert_chunk.4 = (bf16[2,32,2048]{2,1,0:T(8,128)(2,1)S(1)}, bf16[2,32,2048]{2,1,0:T(8,128)(2,1)S(1)}, bf16[2,2,32,2048]{3,2,1,0:T(8,128)(2,1)S(1)}, bf16[32,2048]{1,0:T(8,128)(2,1)S(1)}) custom-call(s32[2]{0:T(128)S(1)} %pad_add_fusion.where_ref, bf16[128,1152]{1,0:T(8,128)(2,1)S(1)} %pad_maximum_fusion.rest_0_, bf16[128,1152]{1,0:T(8,128)(2,1)S(1)} %copy-done.10, ...), custom_call_target="tpu_custom_call" | custom-call | flops 805306368 | bytes 6291456 | tf_op jit(solution)/shard_map/experts/expert_chunk/pallas_call | solution.py:393
  80.7 2.7 %expert_chunk.5 = (bf16[2,32,2048]{2,1,0:T(8,128)(2,1)S(1)}, bf16[2,32,2048]{2,1,0:T(8,128)(2,1)S(1)}, bf16[2,2,32,2048]{3,2,1,0:T(8,128)(2,1)S(1)}) custom-call(s32[2]{0:T(128)S(1)} %pad_add_fusion.where_ref, bf16[128,1152]{1,0:T(8,128)(2,1)} %collective-permute-done.9.rest_0_, bf16[128,1152]{1,0:T(8,128)(2,1)} %collective-permute-done.10.rest_1_, ...), custom_call_target="tpu_custom_call" | custom-call | flops 805306368 | bytes 6291456 | tf_op jit(solution)/shard_map/experts/expert_chunk/pallas_call | solution.py:393
  84.1 2.5 %expert_chunk.6 = (bf16[2,32,2048]{2,1,0:T(8,128)(2,1)S(1)}, bf16[2,32,2048]{2,1,0:T(8,128)(2,1)S(1)}, bf16[2,2,32,2048]{3,2,1,0:T(8,128)(2,1)S(1)}) custom-call(s32[2]{0:T(128)S(1)} %pad_add_fusion.where_ref, bf16[128,1152]{1,0:T(8,128)(2,1)} %collective-permute-done.14.rest_0_, bf16[128,1152]{1,0:T(8,128)(2,1)S(1)} %collective-permute-done.15.rest_1_, ...), custom_call_target="tpu_custom_call" | custom-call | flops 805306368 | bytes 6291456 | tf_op jit(solution)/shard_map/experts/expert_chunk/pallas_call | solution.py:393
  88.6 0.9 collective-permute-done.18
  89.6 1.6 %collective-permute-start.20 = (bf16[2,32,2048]{2,1,0:T(8,128)(2,1)S(1)}, bf16[2,32,2048]{2,1,0:T(8,128)(2,1)S(1)}, u32[]{:S(2)}, u32[]{:S(2)}) collective-permute-start(bf16[2,32,2048]{2,1,0:T(8,128)(2,1)S(1)} %fusion.13), channel_id=1, source_target_pairs={{0,4},{4,0},{8,12},{12,8},{16,20},{20,16},{24,28},{28,24},{1,5},{5... | collective-permute-start | bytes 786440 | tf_op jit(solution)/shard_map/way_back/ppermute | solution.py:410
  91.7 1.5 %collective-permute-start.23 = (bf16[2,32,2048]{2,1,0:T(8,128)(2,1)S(1)}, bf16[2,32,2048]{2,1,0:T(8,128)(2,1)S(1)}, u32[]{:S(2)}, u32[]{:S(2)}) collective-permute-start(bf16[2,32,2048]{2,1,0:T(8,128)(2,1)S(1)} %fusion.11), channel_id=1, source_target_pairs={{0,4},{4,0},{8,12},{12,8},{16,20},{20,16},{24,28},{28,24},{1,5},{5... | collective-permute-start | bytes 786440 | tf_op jit(solution)/shard_map/way_back/ppermute | solution.py:410
  93.2 1.9 %expert_chunk.7 = (bf16[2,32,2048]{2,1,0:T(8,128)(2,1)S(1)}, bf16[2,32,2048]{2,1,0:T(8,128)(2,1)S(1)}, bf16[2,2,32,2048]{3,2,1,0:T(8,128)(2,1)S(1)}) custom-call(s32[2]{0:T(128)S(1)} %pad_add_fusion.where_ref, bf16[128,1152]{1,0:T(8,128)(2,1)S(1)} %copy-done.6, bf16[128,1152]{1,0:T(8,128)(2,1)S(1)} %collective-permute-done.6.rest_1_, ...), custom_call_target="tpu_custom_call" | custom-call | flops 805306368 | bytes 6291456 | tf_op jit(solution)/shard_map/experts/expert_chunk/pallas_call | solution.py:393
  96.1 7.8 %landed_states.2.rest_1_ = bf16[8,2048,128]{2,1,0:T(8,128)(2,1)} custom-call(s32[6]{0:T(128)S(1)} %maximum_convert_fusion.place_ref, bf16[2,2160,128]{2,1,0:T(8,128)(2,1)S(1)} %copy-done.4, bf16[2,2160,128]{2,1,0:T(8,128)(2,1)} %collective-permute-done.28.rest_1_, bf16[2,2160,128]{2,1,0:T(8,128)(2,1)} %collective-permute-done.19.rest_2_), custom_call_target="tpu_custom_call" | custom-call | flops 20000000 | bytes 6291456 | tf_op jit(solution)/shard_map/landed/landed_states/pallas_call | solution.py:306
  104.5 2.5 %collective-permute-start.22 = (bf16[2,32,2048]{2,1,0:T(8,128)(2,1)S(1)}, bf16[2,32,2048]{2,1,0:T(8,128)(2,1)S(1)}, u32[]{:S(2)}, u32[]{:S(2)}) collective-permute-start(bf16[2,32,2048]{2,1,0:T(8,128)(2,1)S(1)} %fusion.10), channel_id=1, source_target_pairs={{0,24},{4,28},{8,16},{12,20},{16,8},{20,12},{24,0},{28,4},{1,25},{... | collective-permute-start | bytes 786440 | tf_op jit(solution)/shard_map/way_back/ppermute | solution.py:410
  107.1 1.6 %collective-permute-start.26 = (bf16[2,32,2048]{2,1,0:T(8,128)(2,1)S(1)}, bf16[2,32,2048]{2,1,0:T(8,128)(2,1)S(1)}, u32[]{:S(2)}, u32[]{:S(2)}) collective-permute-start(bf16[2,32,2048]{2,1,0:T(8,128)(2,1)S(1)} %fusion.4), channel_id=1, source_target_pairs={{0,4},{4,0},{8,12},{12,8},{16,20},{20,16},{24,28},{28,24},{1,5},{5... | collective-permute-start | bytes 786440 | tf_op jit(solution)/shard_map/way_back/ppermute | solution.py:410
  108.7 0.8 collective-permute-done.23
  109.7 5.4 %collective-permute-done.26 = bf16[2,32,2048]{2,1,0:T(8,128)(2,1)S(1)} collective-permute-done((bf16[2,32,2048]{2,1,0:T(8,128)(2,1)S(1)}, bf16[2,32,2048]{2,1,0:T(8,128)(2,1)S(1)}, u32[]{:S(2)}, u32[]{:S(2)}) %collective-permute-start.26) | collective-permute-done | bytes 262176 | tf_op jit(solution)/shard_map/way_back/ppermute | solution.py:410
  115.2 1.8 %collective-permute-start.27 = (bf16[2,32,2048]{2,1,0:T(8,128)(2,1)S(1)}, bf16[2,32,2048]{2,1,0:T(8,128)(2,1)S(1)}, u32[]{:S(2)}, u32[]{:S(2)}) collective-permute-start(bf16[2,32,2048]{2,1,0:T(8,128)(2,1)S(1)} %fusion.6), channel_id=1, source_target_pairs={{0,16},{4,20},{8,24},{12,28},{16,0},{20,4},{24,8},{28,12},{1,17},{... | collective-permute-start | bytes 786440 | tf_op jit(solution)/shard_map/way_back/ppermute | solution.py:410
  117.1 5.2 %collective-permute-done.24 = bf16[2,32,2048]{2,1,0:T(8,128)(2,1)S(1)} collective-permute-done((bf16[2,32,2048]{2,1,0:T(8,128)(2,1)S(1)}, bf16[2,32,2048]{2,1,0:T(8,128)(2,1)S(1)}, u32[]{:S(2)}, u32[]{:S(2)}) %collective-permute-start.24) | collective-permute-done | bytes 262176 | tf_op jit(solution)/shard_map/way_back/ppermute | solution.py:410
  122.3 7.4 %collective-permute-done.27 = bf16[2,32,2048]{2,1,0:T(8,128)(2,1)S(1)} collective-permute-done((bf16[2,32,2048]{2,1,0:T(8,128)(2,1)S(1)}, bf16[2,32,2048]{2,1,0:T(8,128)(2,1)S(1)}, u32[]{:S(2)}, u32[]{:S(2)}) %collective-permute-start.27) | collective-permute-done | bytes 262176 | tf_op jit(solution)/shard_map/way_back/ppermute | solution.py:410
  130.3 3.6 %landed_states.3 = bf16[8,2048,128]{2,1,0:T(8,128)(2,1)} custom-call(s32[2]{0:T(128)S(1)} %fusion.18.place_ref, bf16[2,2160,128]{2,1,0:T(8,128)(2,1)S(1)} %collective-permute-done.30.rest_0_, bf16[8,2048,128]{2,1,0:T(8,128)(2,1)} %landed_states.2.rest_1_), custom_call_target="tpu_custom_call", output_to_operand_aliasing={{}: (2, {})} | custom-call | flops 20000000 | bytes 2097152 | tf_op jit(solution)/shard_map/landed/landed_states/pallas_call | solution.py:306
  133.8 0.9 collective-permute-done.29
  (93 shorter events, 12.8 us)
Async XLA Ops:
  26.6 46.5 %copy-start.3 = (bf16[1,256,2048]{2,1,0:T(8,128)(2,1)S(1)}, bf16[1,256,2048]{2,1,0:T(8,128)(2,1)}, u32[]{:S(2)}) copy-start(bf16[1,256,2048]{2,1,0:T(8,128)(2,1)} %rest_6_.7) | copy-start | bytes 3145732
  27.1 5.4 %collective-permute-start = (bf16[128,512]{1,0:T(8,128)(2,1)S(1)}, bf16[128,512]{1,0:T(8,128)(2,1)S(1)}, u32[]{:S(2)}, u32[]{:S(2)}) collective-permute-start(bf16[128,512]{1,0:T(8,128)(2,1)S(1)} %fusion.2), channel_id=1, source_target_pairs={{0,2},{1,3},{2,0},{3,1},{4,6},{5,7},{6,4},{7,5},{8,10},{9,11},{10,... | collective-permute-start | bytes 393224 | tf_op jit(solution)/shard_map/attention/ppermute | solution.py:410
  32.5 23.5 %collective-permute-start.5 = (bf16[128,1152]{1,0:T(8,128)(2,1)S(1)}, bf16[128,1152]{1,0:T(8,128)(2,1)S(1)}, u32[]{:S(2)}, u32[]{:S(2)}) collective-permute-start(bf16[128,1152]{1,0:T(8,128)(2,1)S(1)} %pad_maximum_fusion.rest_0_), channel_id=1, source_target_pairs={{0,16},{4,20},{8,24},{12,28},{16,0},{20,4},{24,8},{28,12},{1,17},{... | collective-permute-start | bytes 884744 | tf_op jit(solution)/shard_map/tokens/ppermute | solution.py:410
  35.8 20.2 %collective-permute-start.1 = (bf16[128,1152]{1,0:T(8,128)(2,1)S(1)}, bf16[128,1152]{1,0:T(8,128)(2,1)S(1)}, u32[]{:S(2)}, u32[]{:S(2)}) collective-permute-start(bf16[128,1152]{1,0:T(8,128)(2,1)S(1)} %pad_maximum_fusion.rest_0_), channel_id=1, source_target_pairs={{0,1},{1,0},{2,3},{3,2},{4,5},{5,4},{6,7},{7,6},{8,9},{9,8},{10,11... | collective-permute-start | bytes 884744 | tf_op jit(solution)/shard_map/tokens/ppermute | solution.py:410
  35.8 22.4 %collective-permute-start.2 = (bf16[128,1152]{1,0:T(8,128)(2,1)S(1)}, bf16[128,1152]{1,0:T(8,128)(2,1)S(1)}, u32[]{:S(2)}, u32[]{:S(2)}) collective-permute-start(bf16[128,1152]{1,0:T(8,128)(2,1)S(1)} %pad_maximum_fusion.rest_0_), channel_id=1, source_target_pairs={{0,4},{4,0},{8,12},{12,8},{16,20},{20,16},{24,28},{28,24},{1,5},{5... | collective-permute-start | bytes 884744 | tf_op jit(solution)/shard_map/tokens/ppermute | solution.py:410
  37.3 21.3 %collective-permute-start.9 = (bf16[128,1152]{1,0:T(8,128)(2,1)S(1)}, bf16[128,1152]{1,0:T(8,128)(2,1)}, u32[]{:S(2)}, u32[]{:S(2)}) collective-permute-start(bf16[128,1152]{1,0:T(8,128)(2,1)S(1)} %pad_maximum_fusion.rest_0_), channel_id=1, source_target_pairs={{0,24},{4,28},{8,16},{12,20},{16,8},{20,12},{24,0},{28,4},{1,25},{... | collective-permute-start | bytes 884744 | tf_op jit(solution)/shard_map/tokens/ppermute | solution.py:410
  38.7 20.7 %collective-permute-start.14 = (bf16[128,1152]{1,0:T(8,128)(2,1)S(1)}, bf16[128,1152]{1,0:T(8,128)(2,1)}, u32[]{:S(2)}, u32[]{:S(2)}) collective-permute-start(bf16[128,1152]{1,0:T(8,128)(2,1)S(1)} %pad_maximum_fusion.rest_0_), channel_id=1, source_target_pairs={{0,8},{4,12},{8,0},{12,4},{16,24},{20,28},{24,16},{28,20},{1,9},{5... | collective-permute-start | bytes 884744 | tf_op jit(solution)/shard_map/tokens/ppermute | solution.py:410
  56.0 30.6 %collective-permute-start.28 = (bf16[2,2160,128]{2,1,0:T(8,128)(2,1)}, bf16[2,2160,128]{2,1,0:T(8,128)(2,1)}, u32[]{:S(2)}, u32[]{:S(2)}) collective-permute-start(bf16[2,2160,128]{2,1,0:T(8,128)(2,1)} %get-tuple-element.55), channel_id=1, source_target_pairs={{0,1},{1,0},{2,3},{3,2},{4,5},{5,4},{6,7},{7,6},{8,9},{9,8},{10,11... | collective-permute-start | bytes 3317768 | tf_op jit(solution)/shard_map/send_states/ppermute | solution.py:410
  56.7 9.8 %collective-permute-start.7 = (bf16[128,1152]{1,0:T(8,128)(2,1)S(1)}, bf16[128,1152]{1,0:T(8,128)(2,1)S(1)}, u32[]{:S(2)}, u32[]{:S(2)}) collective-permute-start(bf16[128,1152]{1,0:T(8,128)(2,1)S(1)} %collective-permute-done.5.rest_0_), channel_id=1, source_target_pairs={{0,4},{4,0},{8,12},{12,8},{16,20},{20,16},{24,28},{28,24},{1,5},{5... | collective-permute-start | bytes 884744 | tf_op jit(solution)/shard_map/tokens/ppermute | solution.py:410
  58.3 29.2 %collective-permute-start.19 = (bf16[2,2160,128]{2,1,0:T(8,128)(2,1)}, bf16[2,2160,128]{2,1,0:T(8,128)(2,1)}, u32[]{:S(2)}, u32[]{:S(2)}) collective-permute-start(bf16[2,2160,128]{2,1,0:T(8,128)(2,1)} %get-tuple-element.56), channel_id=1, source_target_pairs={{0,2},{1,3},{2,0},{3,1},{4,6},{5,7},{6,4},{7,5},{8,10},{9,11},{10,... | collective-permute-start | bytes 3317768 | tf_op jit(solution)/shard_map/send_states/ppermute | solution.py:410
  58.6 8.6 %collective-permute-start.3 = (bf16[128,1152]{1,0:T(8,128)(2,1)S(1)}, bf16[128,1152]{1,0:T(8,128)(2,1)S(1)}, u32[]{:S(2)}, u32[]{:S(2)}) collective-permute-start(bf16[128,1152]{1,0:T(8,128)(2,1)S(1)} %collective-permute-done.2.rest_2_), channel_id=1, source_target_pairs={{0,1},{1,0},{2,3},{3,2},{4,5},{5,4},{6,7},{7,6},{8,9},{9,8},{10,11... | collective-permute-start | bytes 884744 | tf_op jit(solution)/shard_map/tokens/ppermute | solution.py:410
  59.4 13.6 %collective-permute-start.11 = (bf16[128,1152]{1,0:T(8,128)(2,1)}, bf16[128,1152]{1,0:T(8,128)(2,1)}, u32[]{:S(2)}, u32[]{:S(2)}) collective-permute-start(bf16[128,1152]{1,0:T(8,128)(2,1)} %collective-permute-done.9.rest_0_), channel_id=1, source_target_pairs={{0,4},{4,0},{8,12},{12,8},{16,20},{20,16},{24,28},{28,24},{1,5},{5... | collective-permute-start | bytes 884744 | tf_op jit(solution)/shard_map/tokens/ppermute | solution.py:410
  67.3 12.3 %collective-permute-start.10 = (bf16[128,1152]{1,0:T(8,128)(2,1)}, bf16[128,1152]{1,0:T(8,128)(2,1)}, u32[]{:S(2)}, u32[]{:S(2)}) collective-permute-start(bf16[128,1152]{1,0:T(8,128)(2,1)} %collective-permute-done.9.rest_0_), channel_id=1, source_target_pairs={{0,1},{1,0},{2,3},{3,2},{4,5},{5,4},{6,7},{7,6},{8,9},{9,8},{10,11... | collective-permute-start | bytes 884744 | tf_op jit(solution)/shard_map/tokens/ppermute | solution.py:410
  68.0 12.1 %collective-permute-start.16 = (bf16[128,1152]{1,0:T(8,128)(2,1)}, bf16[128,1152]{1,0:T(8,128)(2,1)}, u32[]{:S(2)}, u32[]{:S(2)}) collective-permute-start(bf16[128,1152]{1,0:T(8,128)(2,1)} %collective-permute-done.14.rest_0_), channel_id=1, source_target_pairs={{0,4},{4,0},{8,12},{12,8},{16,20},{20,16},{24,28},{28,24},{1,5},{5... | collective-permute-start | bytes 884744 | tf_op jit(solution)/shard_map/tokens/ppermute | solution.py:410
  73.0 7.2 %collective-permute-start.12 = (bf16[128,1152]{1,0:T(8,128)(2,1)}, bf16[128,1152]{1,0:T(8,128)(2,1)}, u32[]{:S(2)}, u32[]{:S(2)}) collective-permute-start(bf16[128,1152]{1,0:T(8,128)(2,1)} %collective-permute-done.11.rest_2_), channel_id=1, source_target_pairs={{0,1},{1,0},{2,3},{3,2},{4,5},{5,4},{6,7},{7,6},{8,9},{9,8},{10,11... | collective-permute-start | bytes 884744 | tf_op jit(solution)/shard_map/tokens/ppermute | solution.py:410
  79.5 8.4 %collective-permute-start.4 = (bf16[2,2,32,2048]{3,2,1,0:T(8,128)(2,1)S(1)}, bf16[2,2,32,2048]{3,2,1,0:T(8,128)(2,1)S(1)}, u32[]{:S(2)}, u32[]{:S(2)}) collective-permute-start(bf16[2,2,32,2048]{3,2,1,0:T(8,128)(2,1)S(1)} %get-tuple-element.48), channel_id=1, source_target_pairs={{0,1},{1,0},{2,3},{3,2},{4,5},{5,4},{6,7},{7,6},{8,9},{9,8},{10,11... | collective-permute-start | bytes 1572872 | tf_op jit(solution)/shard_map/way_back/ppermute | solution.py:410
  80.1 3.4 %collective-permute-start.15 = (bf16[128,1152]{1,0:T(8,128)(2,1)}, bf16[128,1152]{1,0:T(8,128)(2,1)S(1)}, u32[]{:S(2)}, u32[]{:S(2)}) collective-permute-start(bf16[128,1152]{1,0:T(8,128)(2,1)} %collective-permute-done.14.rest_0_), channel_id=1, source_target_pairs={{0,1},{1,0},{2,3},{3,2},{4,5},{5,4},{6,7},{7,6},{8,9},{9,8},{10,11... | collective-permute-start | bytes 884744 | tf_op jit(solution)/shard_map/tokens/ppermute | solution.py:410
  80.2 3.5 %collective-permute-start.17 = (bf16[128,1152]{1,0:T(8,128)(2,1)}, bf16[128,1152]{1,0:T(8,128)(2,1)S(1)}, u32[]{:S(2)}, u32[]{:S(2)}) collective-permute-start(bf16[128,1152]{1,0:T(8,128)(2,1)} %collective-permute-done.16.rest_2_), channel_id=1, source_target_pairs={{0,1},{1,0},{2,3},{3,2},{4,5},{5,4},{6,7},{7,6},{8,9},{9,8},{10,11... | collective-permute-start | bytes 884744 | tf_op jit(solution)/shard_map/tokens/ppermute | solution.py:410
  83.5 6.1 %collective-permute-start.6 = (bf16[128,1152]{1,0:T(8,128)(2,1)S(1)}, bf16[128,1152]{1,0:T(8,128)(2,1)S(1)}, u32[]{:S(2)}, u32[]{:S(2)}) collective-permute-start(bf16[128,1152]{1,0:T(8,128)(2,1)S(1)} %copy-done.6), channel_id=1, source_target_pairs={{0,1},{1,0},{2,3},{3,2},{4,5},{5,4},{6,7},{7,6},{8,9},{9,8},{10,11... | collective-permute-start | bytes 884744 | tf_op jit(solution)/shard_map/tokens/ppermute | solution.py:410
  83.6 5.9 %collective-permute-start.8 = (bf16[128,1152]{1,0:T(8,128)(2,1)S(1)}, bf16[128,1152]{1,0:T(8,128)(2,1)S(1)}, u32[]{:S(2)}, u32[]{:S(2)}) collective-permute-start(bf16[128,1152]{1,0:T(8,128)(2,1)S(1)} %copy-done.8), channel_id=1, source_target_pairs={{0,1},{1,0},{2,3},{3,2},{4,5},{5,4},{6,7},{7,6},{8,9},{9,8},{10,11... | collective-permute-start | bytes 884744 | tf_op jit(solution)/shard_map/tokens/ppermute | solution.py:410
  86.6 2.0 %collective-permute-start.13 = (bf16[2,2,32,2048]{3,2,1,0:T(8,128)(2,1)S(1)}, bf16[2,2,32,2048]{3,2,1,0:T(8,128)(2,1)S(1)}, u32[]{:S(2)}, u32[]{:S(2)}) collective-permute-start(bf16[2,2,32,2048]{3,2,1,0:T(8,128)(2,1)S(1)} %get-tuple-element.51), channel_id=1, source_target_pairs={{0,1},{1,0},{2,3},{3,2},{4,5},{5,4},{6,7},{7,6},{8,9},{9,8},{10,11... | collective-permute-start | bytes 1572872 | tf_op jit(solution)/shard_map/way_back/ppermute | solution.py:410
  87.5 2.0 %collective-permute-start.18 = (bf16[2,2,32,2048]{3,2,1,0:T(8,128)(2,1)S(1)}, bf16[2,2,32,2048]{3,2,1,0:T(8,128)(2,1)S(1)}, u32[]{:S(2)}, u32[]{:S(2)}) collective-permute-start(bf16[2,2,32,2048]{3,2,1,0:T(8,128)(2,1)S(1)} %get-tuple-element.53), channel_id=1, source_target_pairs={{0,1},{1,0},{2,3},{3,2},{4,5},{5,4},{6,7},{7,6},{8,9},{9,8},{10,11... | collective-permute-start | bytes 1572872 | tf_op jit(solution)/shard_map/way_back/ppermute | solution.py:410
  88.0 42.2 %collective-permute-start.30 = (bf16[2,2160,128]{2,1,0:T(8,128)(2,1)S(1)}, bf16[2,2160,128]{2,1,0:T(8,128)(2,1)S(1)}, u32[]{:S(2)}, u32[]{:S(2)}) collective-permute-start(bf16[2,2160,128]{2,1,0:T(8,128)(2,1)S(1)} %copy-done.16), channel_id=1, source_target_pairs={{0,3},{1,2},{2,1},{3,0},{4,7},{5,6},{6,5},{7,4},{8,11},{9,10},{10,... | collective-permute-start | bytes 3317768 | tf_op jit(solution)/shard_map/send_states/ppermute | solution.py:410
  89.6 27.4 %collective-permute-start.20 = (bf16[2,32,2048]{2,1,0:T(8,128)(2,1)S(1)}, bf16[2,32,2048]{2,1,0:T(8,128)(2,1)S(1)}, u32[]{:S(2)}, u32[]{:S(2)}) collective-permute-start(bf16[2,32,2048]{2,1,0:T(8,128)(2,1)S(1)} %fusion.13), channel_id=1, source_target_pairs={{0,4},{4,0},{8,12},{12,8},{16,20},{20,16},{24,28},{28,24},{1,5},{5... | collective-permute-start | bytes 786440 | tf_op jit(solution)/shard_map/way_back/ppermute | solution.py:410
  91.2 13.2 %collective-permute-start.21 = (bf16[2,32,2048]{2,1,0:T(8,128)(2,1)S(1)}, bf16[2,32,2048]{2,1,0:T(8,128)(2,1)S(1)}, u32[]{:S(2)}, u32[]{:S(2)}) collective-permute-start(bf16[2,32,2048]{2,1,0:T(8,128)(2,1)S(1)} %fusion.12), channel_id=1, source_target_pairs={{0,4},{4,0},{8,12},{12,8},{16,20},{20,16},{24,28},{28,24},{1,5},{5... | collective-permute-start | bytes 786440 | tf_op jit(solution)/shard_map/way_back/ppermute | solution.py:410
  91.7 17.8 %collective-permute-start.23 = (bf16[2,32,2048]{2,1,0:T(8,128)(2,1)S(1)}, bf16[2,32,2048]{2,1,0:T(8,128)(2,1)S(1)}, u32[]{:S(2)}, u32[]{:S(2)}) collective-permute-start(bf16[2,32,2048]{2,1,0:T(8,128)(2,1)S(1)} %fusion.11), channel_id=1, source_target_pairs={{0,4},{4,0},{8,12},{12,8},{16,20},{20,16},{24,28},{28,24},{1,5},{5... | collective-permute-start | bytes 786440 | tf_op jit(solution)/shard_map/way_back/ppermute | solution.py:410
  95.2 11.8 %collective-permute-start.25 = (bf16[2,2,32,2048]{3,2,1,0:T(8,128)(2,1)S(1)}, bf16[2,2,32,2048]{3,2,1,0:T(8,128)(2,1)S(1)}, u32[]{:S(2)}, u32[]{:S(2)}) collective-permute-start(bf16[2,2,32,2048]{3,2,1,0:T(8,128)(2,1)S(1)} %get-tuple-element.69), channel_id=1, source_target_pairs={{0,1},{1,0},{2,3},{3,2},{4,5},{5,4},{6,7},{7,6},{8,9},{9,8},{10,11... | collective-permute-start | bytes 1572872 | tf_op jit(solution)/shard_map/way_back/ppermute | solution.py:410
  104.5 12.6 %collective-permute-start.22 = (bf16[2,32,2048]{2,1,0:T(8,128)(2,1)S(1)}, bf16[2,32,2048]{2,1,0:T(8,128)(2,1)S(1)}, u32[]{:S(2)}, u32[]{:S(2)}) collective-permute-start(bf16[2,32,2048]{2,1,0:T(8,128)(2,1)S(1)} %fusion.10), channel_id=1, source_target_pairs={{0,24},{4,28},{8,16},{12,20},{16,8},{20,12},{24,0},{28,4},{1,25},{... | collective-permute-start | bytes 786440 | tf_op jit(solution)/shard_map/way_back/ppermute | solution.py:410
  107.1 8.0 %collective-permute-start.26 = (bf16[2,32,2048]{2,1,0:T(8,128)(2,1)S(1)}, bf16[2,32,2048]{2,1,0:T(8,128)(2,1)S(1)}, u32[]{:S(2)}, u32[]{:S(2)}) collective-permute-start(bf16[2,32,2048]{2,1,0:T(8,128)(2,1)S(1)} %fusion.4), channel_id=1, source_target_pairs={{0,4},{4,0},{8,12},{12,8},{16,20},{20,16},{24,28},{28,24},{1,5},{5... | collective-permute-start | bytes 786440 | tf_op jit(solution)/shard_map/way_back/ppermute | solution.py:410
  109.6 12.7 %collective-permute-start.24 = (bf16[2,32,2048]{2,1,0:T(8,128)(2,1)S(1)}, bf16[2,32,2048]{2,1,0:T(8,128)(2,1)S(1)}, u32[]{:S(2)}, u32[]{:S(2)}) collective-permute-start(bf16[2,32,2048]{2,1,0:T(8,128)(2,1)S(1)} %fusion.8), channel_id=1, source_target_pairs={{0,8},{4,12},{8,0},{12,4},{16,24},{20,28},{24,16},{28,20},{1,9},{5... | collective-permute-start | bytes 786440 | tf_op jit(solution)/shard_map/way_back/ppermute | solution.py:410
  115.2 14.4 %collective-permute-start.27 = (bf16[2,32,2048]{2,1,0:T(8,128)(2,1)S(1)}, bf16[2,32,2048]{2,1,0:T(8,128)(2,1)S(1)}, u32[]{:S(2)}, u32[]{:S(2)}) collective-permute-start(bf16[2,32,2048]{2,1,0:T(8,128)(2,1)S(1)} %fusion.6), channel_id=1, source_target_pairs={{0,16},{4,20},{8,24},{12,28},{16,0},{20,4},{24,8},{28,12},{1,17},{... | collective-permute-start | bytes 786440 | tf_op jit(solution)/shard_map/way_back/ppermute | solution.py:410
  129.7 5.0 %collective-permute-start.29 = (bf16[32,2048]{1,0:T(8,128)(2,1)S(1)}, bf16[32,2048]{1,0:T(8,128)(2,1)S(1)}, u32[]{:S(2)}, u32[]{:S(2)}) collective-permute-start(bf16[32,2048]{1,0:T(8,128)(2,1)S(1)} %fusion.17), channel_id=1, source_target_pairs={{0,2},{1,3},{2,0},{3,1},{4,6},{5,7},{6,4},{7,5},{8,10},{9,11},{10,... | collective-permute-start | bytes 393224 | tf_op jit(solution)/shard_map/mixed/ppermute | solution.py:410
  (16 other events, 99.6 us)

commit v5 on v4

--- a/solution.py
+++ b/solution.py
@@ -332,11 +332,16 @@
 
 
 def expert_kernel(sides, own_out, experts, where_ref, *rest):
-    pieces = rest[: 2 * sides]
+    sources = rest[: 2 * sides]
     gain_ref, up_ref, down_ref = rest[2 * sides : 2 * sides + 3]
     keeps = rest[2 * sides + 3 : 3 * sides + 3]
     give_ref = rest[3 * sides + 3]
-    result_s = rest[-1]
+    pieces, result_s, sems = rest[-3 - 2 * sides + 1 : -2], rest[-2], rest[-1]
+    copies = [pltpu.make_async_copy(a, b, sems.at[i]) for i, (a, b) in enumerate(zip(sources, pieces))]
+    for c in copies:
+        c.start()
+    for c in copies:
+        c.wait()
     group_rows = pieces[0].shape[0]
     cols = gain_ref.shape[-1]
     spans = give_ref.shape[1]
@@ -386,16 +391,18 @@
     spans, group_rows = gain.shape[0] // 2, pieces[0].shape[0]
     width = down_weight.shape[-1]
     vmem = pl.BlockSpec(memory_space=pltpu.VMEM)
+    hbm = pl.BlockSpec(memory_space=pltpu.HBM)
     keep = jax.ShapeDtypeStruct((spans, tokens, width), BF16)
     give = jax.ShapeDtypeStruct((sides, spans, tokens, width), BF16)
     own = [jax.ShapeDtypeStruct((tokens, width), BF16)] if own_out else []
     rows = sides * group_rows
     outs = pl.pallas_call(
         functools.partial(expert_kernel, sides, own_out, experts),
-        in_specs=[pl.BlockSpec(memory_space=pltpu.SMEM)] + [vmem] * (len(pieces) + 3),
+        in_specs=[pl.BlockSpec(memory_space=pltpu.SMEM)] + [hbm] * len(pieces) + [vmem] * 3,
         out_specs=[vmem] * (sides + 1 + len(own)),
         out_shape=[keep] * sides + [give] + own,
-        scratch_shapes=[pltpu.VMEM((rows, width), BF16)],
+        scratch_shapes=[pltpu.VMEM(p.shape, BF16) for p in pieces]
+        + [pltpu.VMEM((rows, width), BF16), pltpu.SemaphoreType.DMA((len(pieces),))],
         compiler_params=pltpu.CompilerParams(vmem_limit_bytes=32 * MIB),
         cost_estimate=pl.CostEstimate(
             flops=6 * rows * width * down_weight.shape[1], bytes_accessed=6 * MIB, transcendentals=0
@@ -462,11 +469,18 @@
     sums, asides = {}, []
     own_rows = None
     with jax.named_scope("tokens"):
-        near = {d: swap(held, "dp", d) if d else held for d in chunks}
+        near = {d: swap(held, "dp", d) if d else held for d in chunks[:-1]}
+        across = {d: swap(near[d], "dp", 1) for d in chunks[:-1]}
+        later, near[chunks[1]] = lax.optimization_barrier((held, near[chunks[1]]))
+        near[far] = swap(later, "dp", far)
     for d in chunks:
         with jax.named_scope("tokens"):
-            across = swap(near[d], "dp", 1)
-            pieces = [near[d], swap(near[d], "ep", 1), across, swap(across, "ep", 1)]
+            if d == far:
+                near[d], asides[0], across[chunks[1]] = lax.optimization_barrier(
+                    (near[d], asides[0], across[chunks[1]])
+                )
+                across[d] = swap(near[d], "dp", 1)
+            pieces = [near[d], swap(near[d], "ep", 1), across[d], swap(across[d], "ep", 1)]
             if d == far:
                 pieces, asides, arrived[2:3] = lax.optimization_barrier((pieces, asides, arrived[2:3]))
         with jax.named_scope("experts"):
@@ -482,8 +496,9 @@
         for d, aside in zip(chunks, asides):
             keep_near, taken = sums[d]
             chunk = summed(keep_near, taken[0], swap(aside, "dp", 1))
-            sums[d] = swap(chunk.astype(BF16), "dp", d) if d else chunk
-        sums = [sums[d] for d in chunks]
+            sums[d] = chunk.astype(BF16) if d else chunk
+        sums, arrived[:-1] = lax.optimization_barrier((sums, arrived[:-1]))
+        sums = [swap(sums[d], "dp", d) if d else sums[d] for d in chunks]
     with jax.named_scope("landed"):
         sizes = (requests, kw // hd, heads, steps)
         moved_out = landed_states(arrived[:-1], [], *sizes)

time: 136 us -> 142 us (1.044)
  starting transfers between devices: 23.2 us -> 34.7 us
  local copies, waits for them, and re-layouts: 9.82 us -> 2.55 us
    ppermute x31, starting transfers between devices: 23.2 us -> 34.7 us  [swap(): return lax.ppermute(x, axis, [(i, i ^ d) for i in range(size)])]
    unnamed x34 -> x18, local copies, waits for them, and re-layouts: 7.44 us -> 1.62 us
    pallas_call x4, Pallas kernels: 9.1 us -> 10.8 us  [expert_chunk(): pl.pallas_call(functools.partial(expert_kernel, sides, own_out, experts),...]
    slice x3 -> x2, local copies, waits for them, and re-layouts: 1.66 us -> 0.21 us  [landed_states(): a[:, place_row, 0]]
  transfers between devices with their start and end apart: 31 -> 31, of which waited for: 12 -> 14; matrix products, arithmetic and copies ran while one was open for 2% -> 1% of each run, Pallas kernels for 15% -> 15%
where the time goes in v5:
time: 142 us; the launch traced here: 141 us
  waiting for transfers between devices  53.9 us (38%)
  starting transfers between devices  34.7 us (24%)
  Pallas kernels  32.9 us (23%)
  blocking collectives  14.8 us (10%)
  local copies, waits for them, and re-layouts  2.55 us (2%)
    ppermute x31, waiting for transfers between devices, swap(): return lax.ppermute(x, axis, [(i, i ^ d) for i in range(size)])  53.9 us
    ppermute x31, starting transfers between devices, swap(): return lax.ppermute(x, axis, [(i, i ^ d) for i in range(size)])  34.7 us
    all_to_all x1, blocking collectives, shards(): got = lax.all_to_all(sent, 'ep', split_axis=0, concat_axis=0, tiled=True)  14.8 us
    pallas_call x1, Pallas kernels, core_rows(): pl.pallas_call(functools.partial(core_kernel, lanes, experts), in_specs=[...  11.1 us
    pallas_call x2, Pallas kernels, landed_states(): pl.pallas_call(functools.partial(state_kernel, key_heads, heads, steps, l...  11 us
    pallas_call x4, Pallas kernels, expert_chunk(): pl.pallas_call(functools.partial(expert_kernel, sides, own_out, experts),...  10.8 us
  transfers between devices with their start and end apart: 31, of which 14 were waited for; matrix products, arithmetic and copies ran while one was open for 1% of the time, Pallas kernels for 15%

profile of v5, /device:TPU:0, one launch (start us, length us, event | category | flops | bytes accessed | tf_op | source)
XLA Modules:
  0.0 141.4 jit_solution(10972984288534934266)
XLA Ops:
  0.7 11.1 %core_rows.1 = (bf16[4,32,2688]{2,1,0:T(8,128)(2,1)}, bf16[2,2160,128]{2,1,0:T(8,128)(2,1)}, bf16[2,2160,128]{2,1,0:T(8,128)(2,1)}, bf16[2,2160,128]{2,1,0:T(8,128)(2,1)}, bf16[2,2160,128]{2,1,0:T(8,128)(2,1)}) custom-call(s32[8]{0:T(128)} %home_ref.1, s32[1]{0:T(128)} %bitcast.lane_ref, bf16[8,2048,128]{2,1,0:T(8,128)(2,1)} %bitcast.63, ...), custom_call_target="tpu_custom_call" | custom-call | flops 20000000 | bytes 9437184 | tf_op jit(solution)/shard_map/core/core_rows/pallas_call | solution.py:192
  11.7 14.8 %all_to_all.5 = bf16[4,32,2688]{2,1,0:T(8,128)(2,1)S(1)} all-to-all(bf16[4,32,2688]{2,1,0:T(8,128)(2,1)} %get-tuple-element.51), channel_id=1, replica_groups=mesh['dp'=8,'ep'=4] {'ep'}, dimensions={0} | all-to-all | bytes 1376256 | tf_op jit(solution)/shard_map/core/all_to_all | solution.py:448
  27.4 5.0 %collective-permute-done = bf16[128,512]{1,0:T(8,128)(2,1)S(1)} collective-permute-done((bf16[128,512]{1,0:T(8,128)(2,1)S(1)}, bf16[128,512]{1,0:T(8,128)(2,1)S(1)}, u32[]{:S(2)}, u32[]{:S(2)}) %collective-permute-start) | collective-permute-done | bytes 131104 | tf_op jit(solution)/shard_map/attention/ppermute | solution.py:417
  32.5 2.3 %collective-permute-start.2 = (bf16[128,1152]{1,0:T(8,128)(2,1)S(1)}, bf16[128,1152]{1,0:T(8,128)(2,1)}, u32[]{:S(2)}, u32[]{:S(2)}) collective-permute-start(bf16[128,1152]{1,0:T(8,128)(2,1)S(1)} %pad_maximum_fusion.rest_0_), channel_id=1, source_target_pairs={{0,4},{4,0},{8,12},{12,8},{16,20},{20,16},{24,28},{28,24},{1,5},{5... | collective-permute-start | bytes 884744 | tf_op jit(solution)/shard_map/tokens/ppermute | solution.py:417
  34.7 3.6 %collective-permute-start.5 = (bf16[128,1152]{1,0:T(8,128)(2,1)S(1)}, bf16[128,1152]{1,0:T(8,128)(2,1)}, u32[]{:S(2)}, u32[]{:S(2)}) collective-permute-start(bf16[128,1152]{1,0:T(8,128)(2,1)S(1)} %pad_maximum_fusion.rest_0_), channel_id=1, source_target_pairs={{0,24},{4,28},{8,16},{12,20},{16,8},{20,12},{24,0},{28,4},{1,25},{... | collective-permute-start | bytes 884744 | tf_op jit(solution)/shard_map/tokens/ppermute | solution.py:417
  38.3 2.8 %collective-permute-done.2.rest_2_ = bf16[128,1152]{1,0:T(8,128)(2,1)} collective-permute-done((bf16[128,1152]{1,0:T(8,128)(2,1)S(1)}, bf16[128,1152]{1,0:T(8,128)(2,1)}, u32[]{:S(2)}, u32[]{:S(2)}) %collective-permute-start.2) | collective-permute-done | bytes 294944 | tf_op jit(solution)/shard_map/tokens/ppermute | solution.py:417
  41.1 1.9 %collective-permute-start.14 = (bf16[128,1152]{1,0:T(8,128)(2,1)S(1)}, bf16[128,1152]{1,0:T(8,128)(2,1)S(1)}, u32[]{:S(2)}, u32[]{:S(2)}) collective-permute-start(bf16[128,1152]{1,0:T(8,128)(2,1)S(1)} %pad_maximum_fusion.rest_0_), channel_id=1, source_target_pairs={{0,8},{4,12},{8,0},{12,4},{16,24},{20,28},{24,16},{28,20},{1,9},{5... | collective-permute-start | bytes 884744 | tf_op jit(solution)/shard_map/tokens/ppermute | solution.py:417
  43.0 1.5 %collective-permute-done.5.rest_0_ = bf16[128,1152]{1,0:T(8,128)(2,1)} collective-permute-done((bf16[128,1152]{1,0:T(8,128)(2,1)S(1)}, bf16[128,1152]{1,0:T(8,128)(2,1)}, u32[]{:S(2)}, u32[]{:S(2)}) %collective-permute-start.5) | collective-permute-done | bytes 294944 | tf_op jit(solution)/shard_map/tokens/ppermute | solution.py:417
  45.1 1.6 %copy-done.1 = bf16[1,2048,512]{2,1,0:T(8,128)(2,1)S(1)} copy-done((bf16[1,2048,512]{2,1,0:T(8,128)(2,1)S(1)}, bf16[1,2048,512]{2,1,0:T(8,128)(2,1)}, u32[]{:S(2)}) %copy-start.1) | copy-done | bytes 2097176
  46.7 3.5 %expert_chunk.4 = (bf16[2,32,2048]{2,1,0:T(8,128)(2,1)S(1)}, bf16[2,32,2048]{2,1,0:T(8,128)(2,1)S(1)}, bf16[2,2,32,2048]{3,2,1,0:T(8,128)(2,1)S(1)}, bf16[32,2048]{1,0:T(8,128)(2,1)S(1)}) custom-call(s32[2]{0:T(128)S(1)} %pad_add_fusion.where_ref, bf16[128,1152]{1,0:T(8,128)(2,1)S(1)} %pad_maximum_fusion.rest_0_, ...), custom_call_target="tpu_custom_call" | custom-call | flops 805306368 | bytes 6291456 | tf_op jit(solution)/shard_map/experts/expert_chunk/pallas_call | solution.py:399
  52.8 7.0 %collective-permute-start.6 = (bf16[128,1152]{1,0:T(8,128)(2,1)S(1)}, bf16[128,1152]{1,0:T(8,128)(2,1)S(1)}, u32[]{:S(2)}, u32[]{:S(2)}) collective-permute-start(bf16[128,1152]{1,0:T(8,128)(2,1)S(1)} %pad_maximum_fusion.rest_0_), channel_id=1, source_target_pairs={{0,16},{4,20},{8,24},{12,28},{16,0},{20,4},{24,8},{28,12},{1,17},{... | collective-permute-start | bytes 884744 | tf_op jit(solution)/shard_map/tokens/ppermute | solution.py:417
  60.2 2.9 %expert_chunk.5 = (bf16[2,32,2048]{2,1,0:T(8,128)(2,1)S(1)}, bf16[2,32,2048]{2,1,0:T(8,128)(2,1)S(1)}, bf16[2,2,32,2048]{3,2,1,0:T(8,128)(2,1)S(1)}) custom-call(s32[2]{0:T(128)S(1)} %pad_add_fusion.where_ref, bf16[128,1152]{1,0:T(8,128)(2,1)} %collective-permute-done.5.rest_0_, bf16[128,1152]{1,0:T(8,128)(2,1)S(1)} %collective-permute-done.11.rest_1_, ...), custom_call_target="tpu_custom_call" | custom-call | flops 805306368 | bytes 6291456 | tf_op jit(solution)/shard_map/experts/expert_chunk/pallas_call | solution.py:399
  63.4 9.9 %collective-permute-done.6.rest_0_ = bf16[128,1152]{1,0:T(8,128)(2,1)S(1)} collective-permute-done((bf16[128,1152]{1,0:T(8,128)(2,1)S(1)}, bf16[128,1152]{1,0:T(8,128)(2,1)S(1)}, u32[]{:S(2)}, u32[]{:S(2)}) %collective-permute-start.6) | collective-permute-done | bytes 294944 | tf_op jit(solution)/shard_map/tokens/ppermute | solution.py:417
  73.3 1.5 %collective-permute-start.9 = (bf16[128,1152]{1,0:T(8,128)(2,1)S(1)}, bf16[128,1152]{1,0:T(8,128)(2,1)S(1)}, u32[]{:S(2)}, u32[]{:S(2)}) collective-permute-start(bf16[128,1152]{1,0:T(8,128)(2,1)S(1)} %collective-permute-done.6.rest_0_), channel_id=1, source_target_pairs={{0,4},{4,0},{8,12},{12,8},{16,20},{20,16},{24,28},{28,24},{1,5},{5... | collective-permute-start | bytes 884744 | tf_op jit(solution)/shard_map/tokens/ppermute | solution.py:417
  74.9 2.2 %expert_chunk.6 = (bf16[2,32,2048]{2,1,0:T(8,128)(2,1)S(1)}, bf16[2,32,2048]{2,1,0:T(8,128)(2,1)S(1)}, bf16[2,2,32,2048]{3,2,1,0:T(8,128)(2,1)S(1)}) custom-call(s32[2]{0:T(128)S(1)} %pad_add_fusion.where_ref, bf16[128,1152]{1,0:T(8,128)(2,1)S(1)} %collective-permute-done.14.rest_0_, bf16[128,1152]{1,0:T(8,128)(2,1)S(1)} %collective-permute-done.15.rest_1_, ...), custom_call_target="tpu_custom_call" | custom-call | flops 805306368 | bytes 6291456 | tf_op jit(solution)/shard_map/experts/expert_chunk/pallas_call | solution.py:399
  77.2 1.9 %collective-permute-done.19.rest_2_ = bf16[2,2160,128]{2,1,0:T(8,128)(2,1)S(1)} collective-permute-done((bf16[2,2160,128]{2,1,0:T(8,128)(2,1)S(1)}, bf16[2,2160,128]{2,1,0:T(8,128)(2,1)S(1)}, u32[]{:S(2)}, u32[]{:S(2)}) %collective-permute-start.19) | collective-permute-done | bytes 1105952 | tf_op jit(solution)/shard_map/send_states/ppermute | solution.py:417
  79.1 2.8 %collective-permute-done.9.rest_2_ = bf16[128,1152]{1,0:T(8,128)(2,1)S(1)} collective-permute-done((bf16[128,1152]{1,0:T(8,128)(2,1)S(1)}, bf16[128,1152]{1,0:T(8,128)(2,1)S(1)}, u32[]{:S(2)}, u32[]{:S(2)}) %collective-permute-start.9) | collective-permute-done | bytes 294944 | tf_op jit(solution)/shard_map/tokens/ppermute | solution.py:417
  83.5 1.5 %collective-permute-start.21 = (bf16[2,32,2048]{2,1,0:T(8,128)(2,1)S(1)}, bf16[2,32,2048]{2,1,0:T(8,128)(2,1)S(1)}, u32[]{:S(2)}, u32[]{:S(2)}) collective-permute-start(bf16[2,32,2048]{2,1,0:T(8,128)(2,1)S(1)} %fusion.11), channel_id=1, source_target_pairs={{0,4},{4,0},{8,12},{12,8},{16,20},{20,16},{24,28},{28,24},{1,5},{5... | collective-permute-start | bytes 786440 | tf_op jit(solution)/shard_map/way_back/ppermute | solution.py:417
  85.7 1.5 %collective-permute-start.20 = (bf16[2,32,2048]{2,1,0:T(8,128)(2,1)S(1)}, bf16[2,32,2048]{2,1,0:T(8,128)(2,1)S(1)}, u32[]{:S(2)}, u32[]{:S(2)}) collective-permute-start(bf16[2,32,2048]{2,1,0:T(8,128)(2,1)S(1)} %fusion.13), channel_id=1, source_target_pairs={{0,4},{4,0},{8,12},{12,8},{16,20},{20,16},{24,28},{28,24},{1,5},{5... | collective-permute-start | bytes 786440 | tf_op jit(solution)/shard_map/way_back/ppermute | solution.py:417
  87.3 2.2 %expert_chunk.7 = (bf16[2,32,2048]{2,1,0:T(8,128)(2,1)S(1)}, bf16[2,32,2048]{2,1,0:T(8,128)(2,1)S(1)}, bf16[2,2,32,2048]{3,2,1,0:T(8,128)(2,1)S(1)}) custom-call(s32[2]{0:T(128)S(1)} %pad_add_fusion.where_ref, bf16[128,1152]{1,0:T(8,128)(2,1)S(1)} %collective-permute-done.6.rest_0_, bf16[128,1152]{1,0:T(8,128)(2,1)S(1)} %collective-permute-done.8.rest_1_, ...), custom_call_target="tpu_custom_call" | custom-call | flops 805306368 | bytes 6291456 | tf_op jit(solution)/shard_map/experts/expert_chunk/pallas_call | solution.py:399
  89.6 3.0 %collective-permute-done.21 = bf16[2,32,2048]{2,1,0:T(8,128)(2,1)S(1)} collective-permute-done((bf16[2,32,2048]{2,1,0:T(8,128)(2,1)S(1)}, bf16[2,32,2048]{2,1,0:T(8,128)(2,1)S(1)}, u32[]{:S(2)}, u32[]{:S(2)}) %collective-permute-start.21) | collective-permute-done | bytes 262176 | tf_op jit(solution)/shard_map/way_back/ppermute | solution.py:417
  94.3 4.0 %collective-permute-done.20 = bf16[2,32,2048]{2,1,0:T(8,128)(2,1)S(1)} collective-permute-done((bf16[2,32,2048]{2,1,0:T(8,128)(2,1)S(1)}, bf16[2,32,2048]{2,1,0:T(8,128)(2,1)S(1)}, u32[]{:S(2)}, u32[]{:S(2)}) %collective-permute-start.20) | collective-permute-done | bytes 262176 | tf_op jit(solution)/shard_map/way_back/ppermute | solution.py:417
  98.4 1.6 %collective-permute-start.23 = (bf16[2,32,2048]{2,1,0:T(8,128)(2,1)S(1)}, bf16[2,32,2048]{2,1,0:T(8,128)(2,1)S(1)}, u32[]{:S(2)}, u32[]{:S(2)}) collective-permute-start(bf16[2,32,2048]{2,1,0:T(8,128)(2,1)S(1)} %fusion.6), channel_id=1, source_target_pairs={{0,4},{4,0},{8,12},{12,8},{16,20},{20,16},{24,28},{28,24},{1,5},{5... | collective-permute-start | bytes 786440 | tf_op jit(solution)/shard_map/way_back/ppermute | solution.py:417
  100.0 3.8 %collective-permute-done.24 = bf16[2,32,2048]{2,1,0:T(8,128)(2,1)S(1)} collective-permute-done((bf16[2,32,2048]{2,1,0:T(8,128)(2,1)S(1)}, bf16[2,32,2048]{2,1,0:T(8,128)(2,1)S(1)}, u32[]{:S(2)}, u32[]{:S(2)}) %collective-permute-start.24) | collective-permute-done | bytes 262176 | tf_op jit(solution)/shard_map/way_back/ppermute | solution.py:417
  103.9 4.7 %collective-permute-done.23 = bf16[2,32,2048]{2,1,0:T(8,128)(2,1)S(1)} collective-permute-done((bf16[2,32,2048]{2,1,0:T(8,128)(2,1)S(1)}, bf16[2,32,2048]{2,1,0:T(8,128)(2,1)S(1)}, u32[]{:S(2)}, u32[]{:S(2)}) %collective-permute-start.23) | collective-permute-done | bytes 262176 | tf_op jit(solution)/shard_map/way_back/ppermute | solution.py:417
  108.8 2.0 %collective-permute-start.26 = (bf16[2,32,2048]{2,1,0:T(8,128)(2,1)S(1)}, bf16[2,32,2048]{2,1,0:T(8,128)(2,1)S(1)}, u32[]{:S(2)}, u32[]{:S(2)}) collective-permute-start(bf16[2,32,2048]{2,1,0:T(8,128)(2,1)S(1)} %fusion.5), channel_id=1, source_target_pairs={{0,24},{4,28},{8,16},{12,20},{16,8},{20,12},{24,0},{28,4},{1,25},{... | collective-permute-start | bytes 786440 | tf_op jit(solution)/shard_map/way_back/ppermute | solution.py:417
  110.8 3.2 %collective-permute-start.27 = (bf16[2,32,2048]{2,1,0:T(8,128)(2,1)S(1)}, bf16[2,32,2048]{2,1,0:T(8,128)(2,1)S(1)}, u32[]{:S(2)}, u32[]{:S(2)}) collective-permute-start(bf16[2,32,2048]{2,1,0:T(8,128)(2,1)S(1)} %fusion.10), channel_id=1, source_target_pairs={{0,8},{4,12},{8,0},{12,4},{16,24},{20,28},{24,16},{28,20},{1,9},{5... | collective-permute-start | bytes 786440 | tf_op jit(solution)/shard_map/way_back/ppermute | solution.py:417
  114.7 7.4 %landed_states.2.rest_1_ = bf16[8,2048,128]{2,1,0:T(8,128)(2,1)} custom-call(s32[6]{0:T(128)S(1)} %maximum_convert_fusion.place_ref, bf16[2,2160,128]{2,1,0:T(8,128)(2,1)S(1)} %copy-done.4, bf16[2,2160,128]{2,1,0:T(8,128)(2,1)S(1)} %collective-permute-done.25.rest_1_, bf16[2,2160,128]{2,1,0:T(8,128)(2,1)S(1)} %collective-permute-done.19.rest_2_), custom_call_target="tpu_custom_call" | custom-call | flops 20000000 | bytes 6291456 | tf_op jit(solution)/shard_map/landed/landed_states/pallas_call | solution.py:306
  122.1 1.7 %collective-permute-done.27 = bf16[2,32,2048]{2,1,0:T(8,128)(2,1)S(1)} collective-permute-done((bf16[2,32,2048]{2,1,0:T(8,128)(2,1)S(1)}, bf16[2,32,2048]{2,1,0:T(8,128)(2,1)S(1)}, u32[]{:S(2)}, u32[]{:S(2)}) %collective-permute-start.27) | collective-permute-done | bytes 262176 | tf_op jit(solution)/shard_map/way_back/ppermute | solution.py:417
  123.8 11.2 %collective-permute-done.28 = bf16[2,32,2048]{2,1,0:T(8,128)(2,1)S(1)} collective-permute-done((bf16[2,32,2048]{2,1,0:T(8,128)(2,1)S(1)}, bf16[2,32,2048]{2,1,0:T(8,128)(2,1)S(1)}, u32[]{:S(2)}, u32[]{:S(2)}) %collective-permute-start.28) | collective-permute-done | bytes 262176 | tf_op jit(solution)/shard_map/way_back/ppermute | solution.py:417
  135.1 1.7 %collective-permute-start.29 = (bf16[32,2048]{1,0:T(8,128)(2,1)S(1)}, bf16[32,2048]{1,0:T(8,128)(2,1)S(1)}, u32[]{:S(2)}, u32[]{:S(2)}) collective-permute-start(bf16[32,2048]{1,0:T(8,128)(2,1)S(1)} %fusion.17), channel_id=1, source_target_pairs={{0,2},{1,3},{2,0},{3,1},{4,6},{5,7},{6,4},{7,5},{8,10},{9,11},{10,... | collective-permute-start | bytes 393224 | tf_op jit(solution)/shard_map/mixed/ppermute | solution.py:417
  136.9 3.6 %landed_states.3 = bf16[8,2048,128]{2,1,0:T(8,128)(2,1)} custom-call(s32[2]{0:T(128)S(1)} %fusion.18.place_ref, bf16[2,2160,128]{2,1,0:T(8,128)(2,1)S(1)} %collective-permute-done.30.rest_0_, bf16[8,2048,128]{2,1,0:T(8,128)(2,1)} %landed_states.2.rest_1_), custom_call_target="tpu_custom_call", output_to_operand_aliasing={{}: (2, {})} | custom-call | flops 20000000 | bytes 2097152 | tf_op jit(solution)/shard_map/landed/landed_states/pallas_call | solution.py:306
  (76 shorter events, 11.0 us)
Async XLA Ops:
  0.6 25.9 %copy-start = (bf16[2048,512]{1,0:T(8,128)(2,1)S(1)}, bf16[2048,512]{1,0:T(8,128)(2,1)}, u32[]{:S(2)}) copy-start(bf16[2048,512]{1,0:T(8,128)(2,1)} %param.26) | copy-start | bytes 6291460
  27.0 5.4 %collective-permute-start = (bf16[128,512]{1,0:T(8,128)(2,1)S(1)}, bf16[128,512]{1,0:T(8,128)(2,1)S(1)}, u32[]{:S(2)}, u32[]{:S(2)}) collective-permute-start(bf16[128,512]{1,0:T(8,128)(2,1)S(1)} %fusion.2), channel_id=1, source_target_pairs={{0,2},{1,3},{2,0},{3,1},{4,6},{5,7},{6,4},{7,5},{8,10},{9,11},{10,... | collective-permute-start | bytes 393224 | tf_op jit(solution)/shard_map/attention/ppermute | solution.py:417
  32.5 8.6 %collective-permute-start.2 = (bf16[128,1152]{1,0:T(8,128)(2,1)S(1)}, bf16[128,1152]{1,0:T(8,128)(2,1)}, u32[]{:S(2)}, u32[]{:S(2)}) collective-permute-start(bf16[128,1152]{1,0:T(8,128)(2,1)S(1)} %pad_maximum_fusion.rest_0_), channel_id=1, source_target_pairs={{0,4},{4,0},{8,12},{12,8},{16,20},{20,16},{24,28},{28,24},{1,5},{5... | collective-permute-start | bytes 884744 | tf_op jit(solution)/shard_map/tokens/ppermute | solution.py:417
  34.7 9.8 %collective-permute-start.5 = (bf16[128,1152]{1,0:T(8,128)(2,1)S(1)}, bf16[128,1152]{1,0:T(8,128)(2,1)}, u32[]{:S(2)}, u32[]{:S(2)}) collective-permute-start(bf16[128,1152]{1,0:T(8,128)(2,1)S(1)} %pad_maximum_fusion.rest_0_), channel_id=1, source_target_pairs={{0,24},{4,28},{8,16},{12,20},{16,8},{20,12},{24,0},{28,4},{1,25},{... | collective-permute-start | bytes 884744 | tf_op jit(solution)/shard_map/tokens/ppermute | solution.py:417
  38.3 6.8 %collective-permute-start.1 = (bf16[128,1152]{1,0:T(8,128)(2,1)S(1)}, bf16[128,1152]{1,0:T(8,128)(2,1)}, u32[]{:S(2)}, u32[]{:S(2)}) collective-permute-start(bf16[128,1152]{1,0:T(8,128)(2,1)S(1)} %pad_maximum_fusion.rest_0_), channel_id=1, source_target_pairs={{0,1},{1,0},{2,3},{3,2},{4,5},{5,4},{6,7},{7,6},{8,9},{9,8},{10,11... | collective-permute-start | bytes 884744 | tf_op jit(solution)/shard_map/tokens/ppermute | solution.py:417
  41.1 4.0 %collective-permute-start.3 = (bf16[128,1152]{1,0:T(8,128)(2,1)}, bf16[128,1152]{1,0:T(8,128)(2,1)}, u32[]{:S(2)}, u32[]{:S(2)}) collective-permute-start(bf16[128,1152]{1,0:T(8,128)(2,1)} %collective-permute-done.2.rest_2_), channel_id=1, source_target_pairs={{0,1},{1,0},{2,3},{3,2},{4,5},{5,4},{6,7},{7,6},{8,9},{9,8},{10,11... | collective-permute-start | bytes 884744 | tf_op jit(solution)/shard_map/tokens/ppermute | solution.py:417
  41.1 9.6 %collective-permute-start.14 = (bf16[128,1152]{1,0:T(8,128)(2,1)S(1)}, bf16[128,1152]{1,0:T(8,128)(2,1)S(1)}, u32[]{:S(2)}, u32[]{:S(2)}) collective-permute-start(bf16[128,1152]{1,0:T(8,128)(2,1)S(1)} %pad_maximum_fusion.rest_0_), channel_id=1, source_target_pairs={{0,8},{4,12},{8,0},{12,4},{16,24},{20,28},{24,16},{28,20},{1,9},{5... | collective-permute-start | bytes 884744 | tf_op jit(solution)/shard_map/tokens/ppermute | solution.py:417
  44.5 7.8 %collective-permute-start.7 = (bf16[128,1152]{1,0:T(8,128)(2,1)}, bf16[128,1152]{1,0:T(8,128)(2,1)S(1)}, u32[]{:S(2)}, u32[]{:S(2)}) collective-permute-start(bf16[128,1152]{1,0:T(8,128)(2,1)} %collective-permute-done.5.rest_0_), channel_id=1, source_target_pairs={{0,4},{4,0},{8,12},{12,8},{16,20},{20,16},{24,28},{28,24},{1,5},{5... | collective-permute-start | bytes 884744 | tf_op jit(solution)/shard_map/tokens/ppermute | solution.py:417
  50.1 13.0 %collective-permute-start.4 = (bf16[2,2,32,2048]{3,2,1,0:T(8,128)(2,1)S(1)}, bf16[2,2,32,2048]{3,2,1,0:T(8,128)(2,1)S(1)}, u32[]{:S(2)}, u32[]{:S(2)}) collective-permute-start(bf16[2,2,32,2048]{3,2,1,0:T(8,128)(2,1)S(1)} %get-tuple-element.59), channel_id=1, source_target_pairs={{0,1},{1,0},{2,3},{3,2},{4,5},{5,4},{6,7},{7,6},{8,9},{9,8},{10,11... | collective-permute-start | bytes 1572872 | tf_op jit(solution)/shard_map/way_back/ppermute | solution.py:417
  50.2 2.5 %collective-permute-start.11 = (bf16[128,1152]{1,0:T(8,128)(2,1)}, bf16[128,1152]{1,0:T(8,128)(2,1)S(1)}, u32[]{:S(2)}, u32[]{:S(2)}) collective-permute-start(bf16[128,1152]{1,0:T(8,128)(2,1)} %collective-permute-done.5.rest_0_), channel_id=1, source_target_pairs={{0,1},{1,0},{2,3},{3,2},{4,5},{5,4},{6,7},{7,6},{8,9},{9,8},{10,11... | collective-permute-start | bytes 884744 | tf_op jit(solution)/shard_map/tokens/ppermute | solution.py:417
  50.7 9.0 %collective-permute-start.16 = (bf16[128,1152]{1,0:T(8,128)(2,1)S(1)}, bf16[128,1152]{1,0:T(8,128)(2,1)S(1)}, u32[]{:S(2)}, u32[]{:S(2)}) collective-permute-start(bf16[128,1152]{1,0:T(8,128)(2,1)S(1)} %collective-permute-done.14.rest_0_), channel_id=1, source_target_pairs={{0,4},{4,0},{8,12},{12,8},{16,20},{20,16},{24,28},{28,24},{1,5},{5... | collective-permute-start | bytes 884744 | tf_op jit(solution)/shard_map/tokens/ppermute | solution.py:417
  52.3 7.5 %collective-permute-start.12 = (bf16[128,1152]{1,0:T(8,128)(2,1)S(1)}, bf16[128,1152]{1,0:T(8,128)(2,1)S(1)}, u32[]{:S(2)}, u32[]{:S(2)}) collective-permute-start(bf16[128,1152]{1,0:T(8,128)(2,1)S(1)} %collective-permute-done.7.rest_2_), channel_id=1, source_target_pairs={{0,1},{1,0},{2,3},{3,2},{4,5},{5,4},{6,7},{7,6},{8,9},{9,8},{10,11... | collective-permute-start | bytes 884744 | tf_op jit(solution)/shard_map/tokens/ppermute | solution.py:417
  52.3 26.8 %collective-permute-start.19 = (bf16[2,2160,128]{2,1,0:T(8,128)(2,1)S(1)}, bf16[2,2160,128]{2,1,0:T(8,128)(2,1)S(1)}, u32[]{:S(2)}, u32[]{:S(2)}) collective-permute-start(bf16[2,2160,128]{2,1,0:T(8,128)(2,1)S(1)} %copy-done.8), channel_id=1, source_target_pairs={{0,2},{1,3},{2,0},{3,1},{4,6},{5,7},{6,4},{7,5},{8,10},{9,11},{10,... | collective-permute-start | bytes 3317768 | tf_op jit(solution)/shard_map/send_states/ppermute | solution.py:417
  52.8 20.6 %collective-permute-start.6 = (bf16[128,1152]{1,0:T(8,128)(2,1)S(1)}, bf16[128,1152]{1,0:T(8,128)(2,1)S(1)}, u32[]{:S(2)}, u32[]{:S(2)}) collective-permute-start(bf16[128,1152]{1,0:T(8,128)(2,1)S(1)} %pad_maximum_fusion.rest_0_), channel_id=1, source_target_pairs={{0,16},{4,20},{8,24},{12,28},{16,0},{20,4},{24,8},{28,12},{1,17},{... | collective-permute-start | bytes 884744 | tf_op jit(solution)/shard_map/tokens/ppermute | solution.py:417
  59.7 15.2 %collective-permute-start.15 = (bf16[128,1152]{1,0:T(8,128)(2,1)S(1)}, bf16[128,1152]{1,0:T(8,128)(2,1)S(1)}, u32[]{:S(2)}, u32[]{:S(2)}) collective-permute-start(bf16[128,1152]{1,0:T(8,128)(2,1)S(1)} %collective-permute-done.14.rest_0_), channel_id=1, source_target_pairs={{0,1},{1,0},{2,3},{3,2},{4,5},{5,4},{6,7},{7,6},{8,9},{9,8},{10,11... | collective-permute-start | bytes 884744 | tf_op jit(solution)/shard_map/tokens/ppermute | solution.py:417
  59.7 15.2 %collective-permute-start.17 = (bf16[128,1152]{1,0:T(8,128)(2,1)S(1)}, bf16[128,1152]{1,0:T(8,128)(2,1)S(1)}, u32[]{:S(2)}, u32[]{:S(2)}) collective-permute-start(bf16[128,1152]{1,0:T(8,128)(2,1)S(1)} %collective-permute-done.16.rest_2_), channel_id=1, source_target_pairs={{0,1},{1,0},{2,3},{3,2},{4,5},{5,4},{6,7},{7,6},{8,9},{9,8},{10,11... | collective-permute-start | bytes 884744 | tf_op jit(solution)/shard_map/tokens/ppermute | solution.py:417
  63.2 18.7 %collective-permute-start.13 = (bf16[2,2,32,2048]{3,2,1,0:T(8,128)(2,1)S(1)}, bf16[2,2,32,2048]{3,2,1,0:T(8,128)(2,1)S(1)}, u32[]{:S(2)}, u32[]{:S(2)}) collective-permute-start(bf16[2,2,32,2048]{3,2,1,0:T(8,128)(2,1)S(1)} %get-tuple-element.66), channel_id=1, source_target_pairs={{0,1},{1,0},{2,3},{3,2},{4,5},{5,4},{6,7},{7,6},{8,9},{9,8},{10,11... | collective-permute-start | bytes 1572872 | tf_op jit(solution)/shard_map/way_back/ppermute | solution.py:417
  73.3 8.5 %collective-permute-start.9 = (bf16[128,1152]{1,0:T(8,128)(2,1)S(1)}, bf16[128,1152]{1,0:T(8,128)(2,1)S(1)}, u32[]{:S(2)}, u32[]{:S(2)}) collective-permute-start(bf16[128,1152]{1,0:T(8,128)(2,1)S(1)} %collective-permute-done.6.rest_0_), channel_id=1, source_target_pairs={{0,4},{4,0},{8,12},{12,8},{16,20},{20,16},{24,28},{28,24},{1,5},{5... | collective-permute-start | bytes 884744 | tf_op jit(solution)/shard_map/tokens/ppermute | solution.py:417
  77.1 4.8 %collective-permute-start.18 = (bf16[2,2,32,2048]{3,2,1,0:T(8,128)(2,1)S(1)}, bf16[2,2,32,2048]{3,2,1,0:T(8,128)(2,1)S(1)}, u32[]{:S(2)}, u32[]{:S(2)}) collective-permute-start(bf16[2,2,32,2048]{3,2,1,0:T(8,128)(2,1)S(1)} %get-tuple-element.68), channel_id=1, source_target_pairs={{0,1},{1,0},{2,3},{3,2},{4,5},{5,4},{6,7},{7,6},{8,9},{9,8},{10,11... | collective-permute-start | bytes 1572872 | tf_op jit(solution)/shard_map/way_back/ppermute | solution.py:417
  79.1 3.0 %collective-permute-start.8 = (bf16[128,1152]{1,0:T(8,128)(2,1)S(1)}, bf16[128,1152]{1,0:T(8,128)(2,1)S(1)}, u32[]{:S(2)}, u32[]{:S(2)}) collective-permute-start(bf16[128,1152]{1,0:T(8,128)(2,1)S(1)} %collective-permute-done.6.rest_0_), channel_id=1, source_target_pairs={{0,1},{1,0},{2,3},{3,2},{4,5},{5,4},{6,7},{7,6},{8,9},{9,8},{10,11... | collective-permute-start | bytes 884744 | tf_op jit(solution)/shard_map/tokens/ppermute | solution.py:417
  81.9 1.6 %collective-permute-start.10 = (bf16[128,1152]{1,0:T(8,128)(2,1)S(1)}, bf16[128,1152]{1,0:T(8,128)(2,1)S(1)}, u32[]{:S(2)}, u32[]{:S(2)}) collective-permute-start(bf16[128,1152]{1,0:T(8,128)(2,1)S(1)} %collective-permute-done.9.rest_2_), channel_id=1, source_target_pairs={{0,1},{1,0},{2,3},{3,2},{4,5},{5,4},{6,7},{7,6},{8,9},{9,8},{10,11... | collective-permute-start | bytes 884744 | tf_op jit(solution)/shard_map/tokens/ppermute | solution.py:417
  83.5 9.1 %collective-permute-start.21 = (bf16[2,32,2048]{2,1,0:T(8,128)(2,1)S(1)}, bf16[2,32,2048]{2,1,0:T(8,128)(2,1)S(1)}, u32[]{:S(2)}, u32[]{:S(2)}) collective-permute-start(bf16[2,32,2048]{2,1,0:T(8,128)(2,1)S(1)} %fusion.11), channel_id=1, source_target_pairs={{0,4},{4,0},{8,12},{12,8},{16,20},{20,16},{24,28},{28,24},{1,5},{5... | collective-permute-start | bytes 786440 | tf_op jit(solution)/shard_map/way_back/ppermute | solution.py:417
  85.0 23.8 %collective-permute-start.25 = (bf16[2,2160,128]{2,1,0:T(8,128)(2,1)S(1)}, bf16[2,2160,128]{2,1,0:T(8,128)(2,1)S(1)}, u32[]{:S(2)}, u32[]{:S(2)}) collective-permute-start(bf16[2,2160,128]{2,1,0:T(8,128)(2,1)S(1)} %copy-done.7), channel_id=1, source_target_pairs={{0,1},{1,0},{2,3},{3,2},{4,5},{5,4},{6,7},{7,6},{8,9},{9,8},{10,11... | collective-permute-start | bytes 3317768 | tf_op jit(solution)/shard_map/send_states/ppermute | solution.py:417
  85.0 51.8 %collective-permute-start.30 = (bf16[2,2160,128]{2,1,0:T(8,128)(2,1)S(1)}, bf16[2,2160,128]{2,1,0:T(8,128)(2,1)S(1)}, u32[]{:S(2)}, u32[]{:S(2)}) collective-permute-start(bf16[2,2160,128]{2,1,0:T(8,128)(2,1)S(1)} %copy-done.6), channel_id=1, source_target_pairs={{0,3},{1,2},{2,1},{3,0},{4,7},{5,6},{6,5},{7,4},{8,11},{9,10},{10,... | collective-permute-start | bytes 3317768 | tf_op jit(solution)/shard_map/send_states/ppermute | solution.py:417
  85.7 12.5 %collective-permute-start.20 = (bf16[2,32,2048]{2,1,0:T(8,128)(2,1)S(1)}, bf16[2,32,2048]{2,1,0:T(8,128)(2,1)S(1)}, u32[]{:S(2)}, u32[]{:S(2)}) collective-permute-start(bf16[2,32,2048]{2,1,0:T(8,128)(2,1)S(1)} %fusion.13), channel_id=1, source_target_pairs={{0,4},{4,0},{8,12},{12,8},{16,20},{20,16},{24,28},{28,24},{1,5},{5... | collective-permute-start | bytes 786440 | tf_op jit(solution)/shard_map/way_back/ppermute | solution.py:417
  89.5 8.8 %collective-permute-start.22 = (bf16[2,2,32,2048]{3,2,1,0:T(8,128)(2,1)S(1)}, bf16[2,2,32,2048]{3,2,1,0:T(8,128)(2,1)S(1)}, u32[]{:S(2)}, u32[]{:S(2)}) collective-permute-start(bf16[2,2,32,2048]{3,2,1,0:T(8,128)(2,1)S(1)} %get-tuple-element.82), channel_id=1, source_target_pairs={{0,1},{1,0},{2,3},{3,2},{4,5},{5,4},{6,7},{7,6},{8,9},{9,8},{10,11... | collective-permute-start | bytes 1572872 | tf_op jit(solution)/shard_map/way_back/ppermute | solution.py:417
  92.6 11.2 %collective-permute-start.24 = (bf16[2,32,2048]{2,1,0:T(8,128)(2,1)S(1)}, bf16[2,32,2048]{2,1,0:T(8,128)(2,1)S(1)}, u32[]{:S(2)}, u32[]{:S(2)}) collective-permute-start(bf16[2,32,2048]{2,1,0:T(8,128)(2,1)S(1)} %fusion.12), channel_id=1, source_target_pairs={{0,4},{4,0},{8,12},{12,8},{16,20},{20,16},{24,28},{28,24},{1,5},{5... | collective-permute-start | bytes 786440 | tf_op jit(solution)/shard_map/way_back/ppermute | solution.py:417
  98.4 10.2 %collective-permute-start.23 = (bf16[2,32,2048]{2,1,0:T(8,128)(2,1)S(1)}, bf16[2,32,2048]{2,1,0:T(8,128)(2,1)S(1)}, u32[]{:S(2)}, u32[]{:S(2)}) collective-permute-start(bf16[2,32,2048]{2,1,0:T(8,128)(2,1)S(1)} %fusion.6), channel_id=1, source_target_pairs={{0,4},{4,0},{8,12},{12,8},{16,20},{20,16},{24,28},{28,24},{1,5},{5... | collective-permute-start | bytes 786440 | tf_op jit(solution)/shard_map/way_back/ppermute | solution.py:417
  108.8 13.3 %collective-permute-start.26 = (bf16[2,32,2048]{2,1,0:T(8,128)(2,1)S(1)}, bf16[2,32,2048]{2,1,0:T(8,128)(2,1)S(1)}, u32[]{:S(2)}, u32[]{:S(2)}) collective-permute-start(bf16[2,32,2048]{2,1,0:T(8,128)(2,1)S(1)} %fusion.5), channel_id=1, source_target_pairs={{0,24},{4,28},{8,16},{12,20},{16,8},{20,12},{24,0},{28,4},{1,25},{... | collective-permute-start | bytes 786440 | tf_op jit(solution)/shard_map/way_back/ppermute | solution.py:417
  110.8 13.0 %collective-permute-start.27 = (bf16[2,32,2048]{2,1,0:T(8,128)(2,1)S(1)}, bf16[2,32,2048]{2,1,0:T(8,128)(2,1)S(1)}, u32[]{:S(2)}, u32[]{:S(2)}) collective-permute-start(bf16[2,32,2048]{2,1,0:T(8,128)(2,1)S(1)} %fusion.10), channel_id=1, source_target_pairs={{0,8},{4,12},{8,0},{12,4},{16,24},{20,28},{24,16},{28,20},{1,9},{5... | collective-permute-start | bytes 786440 | tf_op jit(solution)/shard_map/way_back/ppermute | solution.py:417
  114.0 21.0 %collective-permute-start.28 = (bf16[2,32,2048]{2,1,0:T(8,128)(2,1)S(1)}, bf16[2,32,2048]{2,1,0:T(8,128)(2,1)S(1)}, u32[]{:S(2)}, u32[]{:S(2)}) collective-permute-start(bf16[2,32,2048]{2,1,0:T(8,128)(2,1)S(1)} %fusion.8), channel_id=1, source_target_pairs={{0,16},{4,20},{8,24},{12,28},{16,0},{20,4},{24,8},{28,12},{1,17},{... | collective-permute-start | bytes 786440 | tf_op jit(solution)/shard_map/way_back/ppermute | solution.py:417
  135.1 5.5 %collective-permute-start.29 = (bf16[32,2048]{1,0:T(8,128)(2,1)S(1)}, bf16[32,2048]{1,0:T(8,128)(2,1)S(1)}, u32[]{:S(2)}, u32[]{:S(2)}) collective-permute-start(bf16[32,2048]{1,0:T(8,128)(2,1)S(1)} %fusion.17), channel_id=1, source_target_pairs={{0,2},{1,3},{2,0},{3,1},{4,6},{5,7},{6,4},{7,5},{8,10},{9,11},{10,... | collective-permute-start | bytes 393224 | tf_op jit(solution)/shard_map/mixed/ppermute | solution.py:417
  (8 other events, 87.8 us)

commit v6 on v5

--- a/solution.py
+++ b/solution.py
@@ -77,16 +77,15 @@
 
 
 def core_kernel(
-    lanes, experts, home_ref, lane_ref, state_ref, q_ref, k_ref, v_ref, g_ref, b_ref, a_ref, gain_ref,
-    res_ref, ids_ref, prob_ref, out_ref, *rest,
+    lanes, experts, lane_ref, state_ref, q_ref, k_ref, v_ref, g_ref, b_ref, a_ref, gain_ref,
+    res_ref, ids_ref, prob_ref, *rest,
 ):
-    packed = rest[:lanes]
-    k_s, q_s, v_s, g_s, a_s, b_s, m_s, o_s, r_s, w_s, held, pay_f, pay_s, in_sem, out_sem = rest[lanes:]
+    outs = rest[:lanes]
+    k_s, q_s, v_s, g_s, a_s, b_s, m_s, o_s, r_s, w_s, held, in_sem = rest[lanes:]
     requests, steps, _ = k_ref.shape
     hd = held.shape[-1]
     heads, key_heads = v_s.shape[0], k_s.shape[0]
     repeats = heads // key_heads
-    cap = requests // lanes
     copies = []
     for r in range(requests):
         copies.append(pltpu.make_async_copy(state_ref.at[r], held.at[r], in_sem.at[r]))
@@ -97,60 +96,6 @@
     spread_rows(g_ref, g_s, requests, steps)
     sigmoid_rows(a_ref, a_s, requests, steps)
     sigmoid_rows(b_ref, b_s, requests, steps)
-    target = [lax.rem(lax.div(home_ref[r], requests), lanes) ^ lane_ref[0] for r in range(requests)]
-    ranks = [
-        sum([(target[p] == target[r]).astype(jnp.int32) for p in range(r)], jnp.int32(0))
-        for r in range(requests)
-    ]
-    state_rows = heads * hd
-
-    def send(source, r, start, kind):
-        rows = pl.ds(start, source.shape[0])
-        for d in range(lanes):
-
-            @pl.when(target[r] == d)
-            def _():
-                pltpu.make_async_copy(
-                    source, packed[d].at[ranks[r], rows], out_sem.at[kind, r]
-                ).start()
-
-        return pltpu.make_async_copy(source, packed[0].at[0, rows], out_sem.at[kind, r])
-
-    sent = []
-    pay_f[...] = jnp.zeros_like(pay_f)
-    for r in range(requests):
-        rows = slice(r * steps, (r + 1) * steps)
-        for kh in range(key_heads):
-            pay_f[kh * steps : (kh + 1) * steps, :] = k_s[kh, rows, :]
-        for h in range(heads):
-            at = (key_heads + h) * steps
-            pay_f[at : at + steps, :] = v_s[h, rows, :]
-        at = (key_heads + heads) * steps
-        pay_f[at : at + steps, :heads] = a_ref[r].astype(F32)
-        pay_f[at + steps : at + 2 * steps, :heads] = b_ref[r].astype(F32)
-        place = lax.rem(home_ref[r], requests).astype(F32)
-        pay_f[at + 2 * steps : at + 3 * steps, :] = jnp.full((steps, hd), place, F32)
-        pay_s[r] = pay_f[...].astype(BF16)
-        sent.append(send(pay_s.at[r], r, state_rows, 0))
-    for r in range(requests):
-        copies[r].wait()
-        rows = slice(r * steps, (r + 1) * steps)
-        for kh in range(key_heads):
-            left = jnp.concatenate([k_s[kh, rows, :], q_s[kh, rows, :]], axis=0).astype(BF16)
-            for h in range(kh * repeats, (kh + 1) * repeats):
-                m_s[h, r * 2 * steps : (r + 1) * 2 * steps, :] = jnp.dot(
-                    left, held[r, h * hd : (h + 1) * hd, :], preferred_element_type=F32
-                )
-        sent.append(send(held.at[r], r, 0, 1))
-    gain = gain_ref[...]
-
-    def emit(t, h, o):
-        gate = at_step(g_s, t, requests, steps, h)
-        scaled = o * lax.rsqrt(row_sum(o * o) * (1.0 / hd) + EPS)
-        o_s[h, pl.ds(t, requests, stride=steps), :] = scaled * gain * jax.nn.silu(gate)
-
-    for kh in range(key_heads):
-        recurrence(kh, repeats, steps, requests, hd, k_s, q_s, v_s, a_s, b_s, m_s, emit, None)
     top = ids_ref.shape[-1]
     place = lax.broadcasted_iota(jnp.int32, (steps, w_s.shape[-1]), 1)
     for r in range(requests):
@@ -165,36 +110,53 @@
             weight = jnp.where(place == ids[:, j : j + 1], high, weight)
             weight = jnp.where(place == ids[:, j : j + 1] + experts, prob[:, j : j + 1] - high, weight)
         w_s[rows, :] = weight
+    for r in range(requests):
+        copies[r].wait()
+        rows = slice(r * steps, (r + 1) * steps)
+        for kh in range(key_heads):
+            left = jnp.concatenate([k_s[kh, rows, :], q_s[kh, rows, :]], axis=0).astype(BF16)
+            for h in range(kh * repeats, (kh + 1) * repeats):
+                m_s[h, r * 2 * steps : (r + 1) * 2 * steps, :] = jnp.dot(
+                    left, held[r, h * hd : (h + 1) * hd, :], preferred_element_type=F32
+                )
+    gain = gain_ref[...]
+
+    def emit(t, h, o):
+        gate = at_step(g_s, t, requests, steps, h)
+        scaled = o * lax.rsqrt(row_sum(o * o) * (1.0 / hd) + EPS)
+        o_s[h, pl.ds(t, requests, stride=steps), :] = scaled * gain * jax.nn.silu(gate)
+
+    for kh in range(key_heads):
+        recurrence(kh, repeats, steps, requests, hd, k_s, q_s, v_s, a_s, b_s, m_s, emit, None)
     width = heads * hd
     cols = res_ref.shape[-1] // lanes
-    for p in range(lanes):
-        for h in range(heads):
-            out_ref[p, :, h * hd : (h + 1) * hd] = o_s[h].astype(BF16)
-        out_ref[p, :, width : width + cols] = r_s[:, p * cols : (p + 1) * cols].astype(BF16)
-        out_ref[p, :, width + cols :] = w_s[...].astype(BF16)
-    for c in sent:
-        c.wait()
+    for h in range(heads):
+        part = o_s[h].astype(BF16)
+        for j in range(lanes):
+            outs[j][:, h * hd : (h + 1) * hd] = part
+    marks = w_s[...].astype(BF16)
+    for j in range(lanes):
+        start = pl.multiple_of((lane_ref[0] ^ j) * cols, cols)
+        outs[j][:, width : width + cols] = r_s[:, pl.ds(start, cols)].astype(BF16)
+        outs[j][:, width + cols :] = marks
 
 
 def core_rows(
-    home, lane, lanes, experts, states, query_rows, key_rows, value_rows, gate_rows, beta_logit, decay_logit,
+    lane, lanes, experts, states, query_rows, key_rows, value_rows, gate_rows, beta_logit, decay_logit,
     core_gain, residual, route_ids, route_prob,
 ):
     requests, heads, hd, _ = states.shape
     steps = key_rows.shape[1]
     kw, vw = key_rows.shape[-1], value_rows.shape[-1]
     tokens = requests * steps
-    _, pay_rows = packed_rows(kw // hd, heads, steps)
     width = residual.shape[-1]
     weight_lanes = -(-2 * experts // 128) * 128
     vmem, hbm = pl.BlockSpec(memory_space=pltpu.VMEM), pl.BlockSpec(memory_space=pl.ANY)
-    smem = pl.BlockSpec(memory_space=pltpu.SMEM)
     return pl.pallas_call(
         functools.partial(core_kernel, lanes, experts),
-        in_specs=[smem, smem, hbm] + [vmem] * 10,
-        out_specs=[vmem] + [hbm] * lanes,
-        out_shape=[jax.ShapeDtypeStruct((lanes, tokens, vw + width // lanes + weight_lanes), BF16)]
-        + [jax.ShapeDtypeStruct((requests // lanes, heads * hd + pay_rows, hd), BF16)] * lanes,
+        in_specs=[pl.BlockSpec(memory_space=pltpu.SMEM), hbm] + [vmem] * 10,
+        out_specs=[vmem] * lanes,
+        out_shape=[jax.ShapeDtypeStruct((tokens, vw + width // lanes + weight_lanes), BF16)] * lanes,
         scratch_shapes=[
             pltpu.VMEM((kw // hd, tokens, hd), F32),
             pltpu.VMEM((kw // hd, tokens, hd), F32),
@@ -207,18 +169,121 @@
             pltpu.VMEM((tokens, width), F32),
             pltpu.VMEM((tokens, weight_lanes), F32),
             pltpu.VMEM((requests, heads * hd, hd), BF16),
-            pltpu.VMEM((pay_rows, hd), F32),
-            pltpu.VMEM((requests, pay_rows, hd), BF16),
             pltpu.SemaphoreType.DMA((requests,)),
-            pltpu.SemaphoreType.DMA((2, requests)),
         ],
         compiler_params=pltpu.CompilerParams(vmem_limit_bytes=60 * MIB),
         cost_estimate=pl.CostEstimate(flops=20_000_000, bytes_accessed=9 * MIB, transcendentals=100_000),
         name="core_rows",
     )(
-        home, lane, states.reshape(requests, heads * hd, hd), query_rows, key_rows, value_rows, gate_rows,
+        lane, states.reshape(requests, heads * hd, hd), query_rows, key_rows, value_rows, gate_rows,
         beta_logit, decay_logit, core_gain.reshape(1, hd), residual, route_ids, route_prob,
     )
+
+
+def pack_kernel(lanes, key_heads, home_ref, lane_ref, state_ref, k_ref, v_ref, b_ref, a_ref, *rest):
+    outs = rest[:-4]
+    held, pay_f, in_sem, out_sem = rest[-4:]
+    requests, steps, _ = k_ref.shape
+    hd = held.shape[-1]
+    heads = v_ref.shape[-1] // hd
+    state_rows = heads * hd
+    cap = requests // lanes
+    copies = []
+    for r in range(requests):
+        source = state_ref.at[r]
+        copies.append(pltpu.make_async_copy(source, held.at[r, pl.ds(0, state_rows)], in_sem.at[r]))
+        copies[-1].start()
+    target = [lax.rem(lax.div(home_ref[r], requests), lanes) ^ lane_ref[0] for r in range(requests)]
+    ranks = [
+        sum([(target[p] == target[r]).astype(jnp.int32) for p in range(r)], jnp.int32(0))
+        for r in range(requests)
+    ]
+    pay_f[...] = jnp.zeros_like(pay_f)
+    for r in range(requests):
+        keys, vals = k_ref[r].astype(F32), v_ref[r].astype(F32)
+        for kh in range(key_heads):
+            pay_f[kh * steps : (kh + 1) * steps, :] = keys[:, kh * hd : (kh + 1) * hd]
+        for h in range(heads):
+            at = (key_heads + h) * steps
+            pay_f[at : at + steps, :] = vals[:, h * hd : (h + 1) * hd]
+        at = (key_heads + heads) * steps
+        pay_f[at : at + steps, :heads] = a_ref[r].astype(F32)
+        pay_f[at + steps : at + 2 * steps, :heads] = b_ref[r].astype(F32)
+        place = lax.rem(home_ref[r], requests).astype(F32)
+        pay_f[at + 2 * steps : at + 3 * steps, :] = jnp.full((steps, hd), place, F32)
+        held[r, state_rows:, :] = pay_f[...].astype(BF16)
+    for r in range(requests):
+        copies[r].wait()
+        for d in range(lanes):
+            for q in range(cap if d > 1 else 1):
+                dest = outs[d].at[ranks[r]] if d < 2 else outs[2 + (d - 2) * cap + q].at[0]
+                chosen = (target[r] == d) & (ranks[r] == q) if d > 1 else target[r] == d
+
+                @pl.when(chosen)
+                def _():
+                    pltpu.make_async_copy(held.at[r], dest, out_sem.at[r]).start()
+
+    for r in range(requests):
+        pltpu.make_async_copy(held.at[r], outs[0].at[0], out_sem.at[r]).wait()
+
+
+def pack_states(home, lane, lanes, states, key_rows, value_rows, beta_logit, decay_logit):
+    requests, heads, hd, _ = states.shape
+    steps = key_rows.shape[1]
+    key_heads = key_rows.shape[-1] // hd
+    cap = requests // lanes
+    _, pay_rows = packed_rows(key_heads, heads, steps)
+    all_rows = heads * hd + pay_rows
+    vmem, hbm = pl.BlockSpec(memory_space=pltpu.VMEM), pl.BlockSpec(memory_space=pl.ANY)
+    smem = pl.BlockSpec(memory_space=pltpu.SMEM)
+    sizes = [cap] * 2 + [1] * (cap * (lanes - 2))
+    return pl.pallas_call(
+        functools.partial(pack_kernel, lanes, key_heads),
+        in_specs=[smem, smem, hbm] + [vmem] * 4,
+        out_specs=[hbm] * len(sizes),
+        out_shape=[jax.ShapeDtypeStruct((n, all_rows, hd), BF16) for n in sizes],
+        scratch_shapes=[
+            pltpu.VMEM((requests, all_rows, hd), BF16),
+            pltpu.VMEM((pay_rows, hd), F32),
+            pltpu.SemaphoreType.DMA((requests,)),
+            pltpu.SemaphoreType.DMA((requests,)),
+        ],
+        compiler_params=pltpu.CompilerParams(vmem_limit_bytes=48 * MIB),
+        cost_estimate=pl.CostEstimate(flops=0, bytes_accessed=9 * MIB, transcendentals=0),
+        name="pack_states",
+    )(home, lane, states.reshape(requests, heads * hd, hd), key_rows, value_rows, beta_logit, decay_logit)
+
+
+def project_kernel(*refs):
+    lanes = len(refs) - 3
+    weight_ref, out_ref, marks_ref = refs[lanes:]
+    depth, cols = weight_ref.shape
+    rows = jnp.concatenate([refs[j][...] for j in range(lanes)], axis=0)
+    attention = jnp.dot(rows[:, :depth], weight_ref[...], preferred_element_type=F32).astype(BF16)
+    before = rows[:, depth : depth + cols].astype(F32)
+    out_ref[...] = (before + attention.astype(F32)).astype(BF16)
+    marks_ref[...] = rows[:, depth + cols :]
+
+
+def project(got, out_weight):
+    tokens, wide = got[0].shape
+    depth, cols = out_weight.shape
+    rows = tokens * len(got)
+    vmem = pl.BlockSpec(memory_space=pltpu.VMEM)
+    return pl.pallas_call(
+        project_kernel,
+        in_specs=[vmem] * (len(got) + 1),
+        out_specs=[vmem] * 2,
+        out_shape=[
+            jax.ShapeDtypeStruct((rows, cols), BF16),
+            jax.ShapeDtypeStruct((rows, wide - depth - cols), BF16),
+        ],
+        compiler_params=pltpu.CompilerParams(vmem_limit_bytes=24 * MIB),
+        cost_estimate=pl.CostEstimate(
+            flops=2 * rows * depth * cols, bytes_accessed=3 * MIB, transcendentals=0
+        ),
+        name="project",
+    )(*got, out_weight)
 
 
 def state_kernel(
@@ -227,20 +292,20 @@
     arrived = rest[:count]
     out_ref, k_s, v_s, a_s, b_s, m_s, u_s, c_s, held, pay_s, ready, in_sem, pay_sem, out_sem = rest[-14:]
     requests, state_rows, hd = held.shape
-    cap = requests // count
+    origin = [(a, j) for a in arrived for j in range(a.shape[0])]
     repeats = heads // key_heads
     pays, copies = [], []
     for r in range(requests):
         pays.append(
             pltpu.make_async_copy(
-                arrived[r // cap].at[r % cap, pl.ds(state_rows, pay_s.shape[1])], pay_s.at[r], pay_sem.at[r]
+                origin[r][0].at[origin[r][1], pl.ds(state_rows, pay_s.shape[1])], pay_s.at[r], pay_sem.at[r]
             )
         )
         pays[-1].start()
     for r in range(requests):
         copies.append(
             pltpu.make_async_copy(
-                arrived[r // cap].at[r % cap, pl.ds(0, state_rows)], held.at[r], in_sem.at[r]
+                origin[r][0].at[origin[r][1], pl.ds(0, state_rows)], held.at[r], in_sem.at[r]
             )
         )
         copies[-1].start()
@@ -296,10 +361,10 @@
 
 
 def landed_states(arrived, before, total, key_heads, heads, steps):
-    cap, all_rows, hd = arrived[0].shape
+    _, all_rows, hd = arrived[0].shape
     place_row = heads * hd + (key_heads + heads + 2) * steps
     place = jnp.concatenate([a[:, place_row, 0] for a in arrived]).astype(jnp.int32)
-    requests = cap * len(arrived)
+    requests = place.shape[0]
     tokens = requests * steps
     state_rows = heads * hd
     hbm = pl.BlockSpec(memory_space=pl.ANY)
@@ -352,7 +417,12 @@
     blocks = [(x, c) for x in range(spans) for c in range(2)]
     values = {}
     for x, c in blocks:
-        parts = [pieces[2 * y + c][:, x * cols : (x + 1) * cols] for y in range(sides)]
+        span = slice(x * cols, (x + 1) * cols)
+        parts = [
+            pieces[2 * y + c][(p ^ c) * tokens : ((p ^ c) + 1) * tokens, span]
+            for y in range(sides)
+            for p in range(2 * spans)
+        ]
         values[x, c] = jnp.concatenate(parts, axis=0).astype(F32)
     total = sum(row_sum(values[b] * values[b]) for b in blocks)
     scale = lax.rsqrt(total * (1.0 / width) + EPS)
@@ -364,9 +434,8 @@
         term = jnp.dot(normed, up, preferred_element_type=F32)
         joined = term if joined is None else joined + term
         if own_out:
-            rest[3 * sides + 4][:, pl.ds(pl.multiple_of(block * cols, cols), cols)] = pieces[c][
-                pl.ds(pl.multiple_of(e * tokens, tokens), tokens), x * cols : (x + 1) * cols
-            ]
+            own = values[x, c][:tokens].astype(BF16)
+            rest[3 * sides + 4][:, pl.ds(pl.multiple_of(block * cols, cols), cols)] = own
     active = (jax.nn.silu(joined[:, :hidden_units]) * joined[:, hidden_units:]).astype(BF16)
     result = jnp.dot(active, down_ref[0], preferred_element_type=F32).astype(BF16)
     marks = [pieces[2 * y][:, spans * cols :].astype(F32) for y in range(sides)]
@@ -378,8 +447,8 @@
     for y in range(sides):
         for x in range(spans):
             for c in range(2):
-                start = y * group_rows + (e ^ (2 * x + c)) * tokens
-                rows = result_s[pl.ds(pl.multiple_of(start, tokens), tokens), :]
+                start = y * group_rows + (2 * x + c) * tokens
+                rows = result_s[start : start + tokens, :]
                 if c:
                     give_ref[y, x] = rows
                 else:
@@ -441,69 +510,82 @@
     me = my_group * lanes + my_lane
 
     with jax.named_scope("core"):
-        sent, *packed = core_rows(
-            new_home, my_lane.reshape(1), lanes, experts, states, query_rows, key_rows, value_rows,
+        sent = core_rows(
+            my_lane.reshape(1), lanes, experts, states, query_rows, key_rows, value_rows,
             gate_rows, beta_logit, decay_logit, core_gain, residual, route_ids, route_prob,
         )
-        got = lax.all_to_all(sent, "ep", split_axis=0, concat_axis=0, tiled=True)
-        got = got.reshape(lanes * tokens, got.shape[-1])
+        sent, new_home = lax.optimization_barrier((sent, new_home))
+        got = {j: swap(sent[j], "ep", j) for j in range(lanes - 1, 0, -1)}
+        got = [sent[0]] + [got[j] for j in range(1, lanes)]
+    with jax.named_scope("send_states"):
+        packed = pack_states(
+            new_home, my_lane.reshape(1), lanes, states, key_rows, value_rows, beta_logit, decay_logit
+        )
     with jax.named_scope("attention"):
-        attention = jnp.dot(got[:, :vw], out_weight, preferred_element_type=F32).astype(BF16)
-        before = got[:, vw : vw + cols]
-        hidden_cols = (before.astype(F32) + attention.astype(F32)).astype(BF16)
-        others = [swap(hidden_cols, "ep", d) for d in range(2, lanes, 2)]
-        held = jnp.concatenate([hidden_cols] + others + [got[:, vw + cols :]], axis=1)
+        got, packed = lax.optimization_barrier((got, packed))
+        hidden_cols, marks = project(got, out_weight)
+        others = []
+        for d in range(2, lanes, 2):
+            other = swap(hidden_cols, "ep", d).reshape(lanes, tokens, cols)
+            others.append(jnp.concatenate([other[j ^ d] for j in range(lanes)], axis=0))
+        held = jnp.concatenate([hidden_cols] + others + [marks], axis=1)
         held, packed = lax.optimization_barrier((held, packed))
-
     with jax.named_scope("send_states"):
-        arrived = [packed[0]]
-        for d in range(1, lanes):
-            if d > 2:
-                packed, arrived[-1] = lax.optimization_barrier((packed, arrived[-1]))
-            arrived.append(swap(packed[d], "ep", d))
+        cap = requests // lanes
+        near_states = [packed[0], swap(packed[1], "ep", 1)]
+        far_states = []
+        for i, piece in enumerate(packed[2:]):
+            if i:
+                piece, far_states[-1] = lax.optimization_barrier((piece, far_states[-1]))
+            far_states.append(swap(piece, "ep", 2 + i // cap))
 
     gain = moe_gain.reshape(lanes, cols)
     where = jnp.stack([my_lane, me])
     far = groups // 2
     chunks = [0] + [d for d in range(groups - 2, 0, -2) if d != far] + [far]
-    sums, asides = {}, []
+    tie = lax.optimization_barrier
     own_rows = None
     with jax.named_scope("tokens"):
         near = {d: swap(held, "dp", d) if d else held for d in chunks[:-1]}
+        later, near[chunks[1]] = tie((held, near[chunks[1]]))
         across = {d: swap(near[d], "dp", 1) for d in chunks[:-1]}
-        later, near[chunks[1]] = lax.optimization_barrier((held, near[chunks[1]]))
         near[far] = swap(later, "dp", far)
+        pieces = {}
+        for d in chunks:
+            aside = across.get(d)
+            if d == far:
+                near[d], pieces[chunks[-2]][2] = tie((near[d], pieces[chunks[-2]][2]))
+                aside = swap(near[d], "dp", 1)
+            pieces[d] = [near[d], swap(near[d], "ep", 1), aside, swap(aside, "ep", 1)]
+        pieces[0], pieces[chunks[1]][2] = tie((pieces[0], pieces[chunks[1]][2]))
+        pieces[0], far_states[0] = tie((pieces[0], far_states[0]))
+        pieces[far], far_states[1] = tie((pieces[far], far_states[1]))
+    sums = {}
     for d in chunks:
-        with jax.named_scope("tokens"):
-            if d == far:
-                near[d], asides[0], across[chunks[1]] = lax.optimization_barrier(
-                    (near[d], asides[0], across[chunks[1]])
-                )
-                across[d] = swap(near[d], "dp", 1)
-            pieces = [near[d], swap(near[d], "ep", 1), across[d], swap(across[d], "ep", 1)]
-            if d == far:
-                pieces, asides, arrived[2:3] = lax.optimization_barrier((pieces, asides, arrived[2:3]))
         with jax.named_scope("experts"):
-            outs = expert_chunk(where, pieces, gain, gate_up, down_weight, tokens, experts, d == 0)
+            outs = expert_chunk(where, pieces[d], gain, gate_up, down_weight, tokens, experts, d == 0)
             keep_near, keep_across, give = outs[:3]
             if d == 0:
                 own_rows = outs[3]
         with jax.named_scope("way_back"):
             taken = swap(give, "ep", 1)
-            asides.append(summed(keep_across, taken[1]).astype(BF16))
-            sums[d] = (keep_near, taken)
-    with jax.named_scope("way_back"):
-        for d, aside in zip(chunks, asides):
-            keep_near, taken = sums[d]
-            chunk = summed(keep_near, taken[0], swap(aside, "dp", 1))
+            aside = summed(keep_across, taken[1]).astype(BF16)
+            if d == far:
+                aside, sums[0], sums[chunks[1]] = tie((aside, sums[0], sums[chunks[1]]))
+            back = swap(aside, "dp", 1)
+            if d == far:
+                back, far_states[2] = tie((back, far_states[2]))
+            chunk = summed(keep_near, taken[0], back)
             sums[d] = chunk.astype(BF16) if d else chunk
-        sums, arrived[:-1] = lax.optimization_barrier((sums, arrived[:-1]))
-        sums = [swap(sums[d], "dp", d) if d else sums[d] for d in chunks]
     with jax.named_scope("landed"):
         sizes = (requests, kw // hd, heads, steps)
-        moved_out = landed_states(arrived[:-1], [], *sizes)
-        sums, moved_out = lax.optimization_barrier((sums, moved_out))
-        moved_out = landed_states(arrived[-1:], [moved_out], *sizes)
+        sums[far], arrived = tie((sums[far], near_states + far_states[:-2]))
+        moved_out = landed_states(arrived, [], *sizes)
+    with jax.named_scope("way_back"):
+        sums = [swap(sums[d], "dp", d) if d else sums[d] for d in chunks]
+        sums, moved_out = tie((sums, moved_out))
+    with jax.named_scope("landed"):
+        moved_out = landed_states(far_states[-2:], [moved_out], *sizes)
         moved_out = moved_out.reshape(requests, heads, hd, hd)
     with jax.named_scope("mixed"):
         mixed = summed(own_rows, *[s[0] for s in sums])

time: 142 us -> 131 us (0.923)
  blocking collectives: 14.8 us -> 0 us
  starting transfers between devices: 34.7 us -> 30.6 us
  Pallas kernels: 32.9 us -> 35.9 us
  other arithmetic: 1.12 us -> 3.69 us
  local copies, waits for them, and re-layouts: 2.55 us -> 4.49 us
    all_to_all x1 -> x0, blocking collectives: 14.8 us -> none  [shards(): got = lax.all_to_all(sent, 'ep', split_axis=0, concat_axis=0, tiled=True)]
    ppermute x31 -> x36, starting transfers between devices: 34.7 us -> 30.6 us  [swap(): return lax.ppermute(x, axis, [(i, i ^ d) for i in range(size)])]
    pallas_call x0 -> x2, Pallas kernels: none -> 3.93 us  [the longest x1 3.48 us: pack_states(): pl.pallas_call(functools.partial(pack_kernel, lanes, key_heads), in_specs...]
    slice x2 -> x5, local copies, waits for them, and re-layouts: 0.21 us -> 2.88 us  [landed_states(): a[:, place_row, 0]]
    convert_element_type x2, other arithmetic: 0.2 us -> 2.76 us  [landed_states(): jnp.concatenate([a[:, place_row, 0] for a in arrived]).astype(jnp.int32)]
    pallas_call x1, Pallas kernels: 11.1 us -> 9.5 us  [core_rows(): pl.pallas_call(functools.partial(core_kernel, lanes, experts), in_specs=[...]
    ppermute x31 -> x36, waiting for transfers between devices: 53.9 us -> 54.9 us  [swap(): return lax.ppermute(x, axis, [(i, i ^ d) for i in range(size)])]
  transfers between devices with their start and end apart: 31 -> 36, of which waited for: 14 -> 13; matrix products, arithmetic and copies ran while one was open for 1% -> 5% of each run, Pallas kernels for 15% -> 20%
where the time goes in v6:
time: 131 us
  waiting for transfers between devices  54.9 us (42%)
  Pallas kernels  35.9 us (27%)
  starting transfers between devices  30.6 us (23%)
  local copies, waits for them, and re-layouts  4.49 us (3%)
  other arithmetic  3.69 us (3%)
    ppermute x36, waiting for transfers between devices, swap(): return lax.ppermute(x, axis, [(i, i ^ d) for i in range(size)])  54.9 us
    ppermute x36, starting transfers between devices, swap(): return lax.ppermute(x, axis, [(i, i ^ d) for i in range(size)])  30.6 us
    pallas_call x2, Pallas kernels, landed_states(): pl.pallas_call(functools.partial(state_kernel, key_heads, heads, steps, l...  11.4 us
    pallas_call x4, Pallas kernels, expert_chunk(): pl.pallas_call(functools.partial(expert_kernel, sides, own_out, experts),...  11 us
    pallas_call x1, Pallas kernels, core_rows(): pl.pallas_call(functools.partial(core_kernel, lanes, experts), in_specs=[...  9.5 us
    pallas_call x1, Pallas kernels, pack_states(): pl.pallas_call(functools.partial(pack_kernel, lanes, key_heads), in_specs...  3.48 us
    slice x5, local copies, waits for them, and re-layouts, landed_states(): a[:, place_row, 0]  2.88 us
    convert_element_type x2, other arithmetic, landed_states(): jnp.concatenate([a[:, place_row, 0] for a in arrived]).astype(jnp.int32)  2.76 us
  transfers between devices with their start and end apart: 36, of which 13 were waited for; matrix products, arithmetic and copies ran while one was open for 5% of the time, Pallas kernels for 20%

profile of v6, /device:TPU:0, one launch (start us, length us, event | category | flops | bytes accessed | tf_op | source)
XLA Modules:
  0.0 130.6 jit_solution(16654108575707337976)
XLA Ops:
  0.7 9.5 %core_rows.1 = (bf16[32,2688]{1,0:T(8,128)(2,1)}, bf16[32,2688]{1,0:T(8,128)(2,1)}, bf16[32,2688]{1,0:T(8,128)(2,1)}, bf16[32,2688]{1,0:T(8,128)(2,1)}) custom-call(s32[1]{0:T(128)} %bitcast.lane_ref, bf16[8,2048,128]{2,1,0:T(8,128)(2,1)} %bitcast.64, bf16[8,4,1024]{2,1,0:T(4,128)(2,1)} %q_ref.1, bf16[8,4,1024]{2,1,0:T(4,128)(2,1)} %k_ref.3, ...), custom_call_target="tpu_custom_call" | custom-call | flops 20000000 | bytes 9437184 | tf_op jit(solution)/shard_map/core/core_rows/pallas_call | solution.py:155
  10.7 2.6 %collective-permute-start.1 = (bf16[32,2688]{1,0:T(8,128)(2,1)}, bf16[32,2688]{1,0:T(8,128)(2,1)S(1)}, u32[]{:S(2)}, u32[]{:S(2)}) collective-permute-start(bf16[32,2688]{1,0:T(8,128)(2,1)} %get-tuple-element.95), channel_id=1, source_target_pairs={{0,2},{1,3},{2,0},{3,1},{4,6},{5,7},{6,4},{7,5},{8,10},{9,11},{10,... | collective-permute-start | bytes 516104 | tf_op jit(solution)/shard_map/core/ppermute | solution.py:486
  13.4 3.5 %pack_states.1 = (bf16[2,2160,128]{2,1,0:T(8,128)(2,1)S(1)}, bf16[2,2160,128]{2,1,0:T(8,128)(2,1)S(1)}, bf16[1,2160,128]{2,1,0:T(8,128)(2,1)}, bf16[1,2160,128]{...) custom-call(s32[8]{0:T(128)S(1)} %copy-done.10, s32[1]{0:T(128)} %bitcast.lane_ref, ...), custom_call_target="tpu_custom_call" | custom-call | bytes 9437184 | tf_op jit(solution)/shard_map/send_states/pack_states/pallas_call | solution.py:240
  18.7 3.2 %collective-permute-done.2.refs_3_ = bf16[32,2688]{1,0:T(8,128)(2,1)S(1)} collective-permute-done((bf16[32,2688]{1,0:T(8,128)(2,1)}, bf16[32,2688]{1,0:T(8,128)(2,1)S(1)}, u32[]{:S(2)}, u32[]{:S(2)}) %collective-permute-start.2) | collective-permute-done | bytes 172064 | tf_op jit(solution)/shard_map/core/ppermute | solution.py:486
  22.4 1.6 %collective-permute-start.3 = (bf16[128,512]{1,0:T(8,128)(2,1)S(1)}, bf16[128,512]{1,0:T(8,128)(2,1)S(1)}, u32[]{:S(2)}, u32[]{:S(2)}) collective-permute-start(bf16[128,512]{1,0:T(8,128)(2,1)S(1)} %get-tuple-element.108), channel_id=1, source_target_pairs={{0,2},{1,3},{2,0},{3,1},{4,6},{5,7},{6,4},{7,5},{8,10},{9,11},{10,... | collective-permute-start | bytes 393224 | tf_op jit(solution)/shard_map/attention/ppermute | solution.py:486
  24.0 4.0 %collective-permute-done.3 = bf16[128,512]{1,0:T(8,128)(2,1)S(1)} collective-permute-done((bf16[128,512]{1,0:T(8,128)(2,1)S(1)}, bf16[128,512]{1,0:T(8,128)(2,1)S(1)}, u32[]{:S(2)}, u32[]{:S(2)}) %collective-permute-start.3) | collective-permute-done | bytes 131104 | tf_op jit(solution)/shard_map/attention/ppermute | solution.py:486
  28.0 3.9 %collective-permute-start.7 = (bf16[128,1152]{1,0:T(8,128)(2,1)S(1)}, bf16[128,1152]{1,0:T(8,128)(2,1)}, u32[]{:S(2)}, u32[]{:S(2)}) collective-permute-start(bf16[128,1152]{1,0:T(8,128)(2,1)S(1)} %pad_maximum_fusion.rest_0_), channel_id=1, source_target_pairs={{0,24},{4,28},{8,16},{12,20},{16,8},{20,12},{24,0},{28,4},{1,25},{... | collective-permute-start | bytes 884744 | tf_op jit(solution)/shard_map/tokens/ppermute | solution.py:486
  31.9 1.5 %collective-permute-start.5 = (bf16[128,1152]{1,0:T(8,128)(2,1)S(1)}, bf16[128,1152]{1,0:T(8,128)(2,1)}, u32[]{:S(2)}, u32[]{:S(2)}) collective-permute-start(bf16[128,1152]{1,0:T(8,128)(2,1)S(1)} %pad_maximum_fusion.rest_0_), channel_id=1, source_target_pairs={{0,4},{4,0},{8,12},{12,8},{16,20},{20,16},{24,28},{28,24},{1,5},{5... | collective-permute-start | bytes 884744 | tf_op jit(solution)/shard_map/tokens/ppermute | solution.py:486
  33.4 1.5 %collective-permute-start.9 = (bf16[1,2160,128]{2,1,0:T(8,128)(2,1)}, bf16[1,2160,128]{2,1,0:T(8,128)(2,1)}, u32[]{:S(2)}, u32[]{:S(2)}) collective-permute-start(bf16[1,2160,128]{2,1,0:T(8,128)(2,1)} %get-tuple-element.123), channel_id=1, source_target_pairs={{0,2},{1,3},{2,0},{3,1},{4,6},{5,7},{6,4},{7,5},{8,10},{9,11},{10,... | collective-permute-start | bytes 1658888 | tf_op jit(solution)/shard_map/send_states/ppermute | solution.py:486
  34.9 5.0 %collective-permute-done.7.rest_0_ = bf16[128,1152]{1,0:T(8,128)(2,1)} collective-permute-done((bf16[128,1152]{1,0:T(8,128)(2,1)S(1)}, bf16[128,1152]{1,0:T(8,128)(2,1)}, u32[]{:S(2)}, u32[]{:S(2)}) %collective-permute-start.7) | collective-permute-done | bytes 294944 | tf_op jit(solution)/shard_map/tokens/ppermute | solution.py:486
  40.1 1.7 %collective-permute-start.8 = (bf16[128,1152]{1,0:T(8,128)(2,1)}, bf16[128,1152]{1,0:T(8,128)(2,1)}, u32[]{:S(2)}, u32[]{:S(2)}) collective-permute-start(bf16[128,1152]{1,0:T(8,128)(2,1)} %collective-permute-done.7.rest_0_), channel_id=1, source_target_pairs={{0,4},{4,0},{8,12},{12,8},{16,20},{20,16},{24,28},{28,24},{1,5},{5... | collective-permute-start | bytes 884744 | tf_op jit(solution)/shard_map/tokens/ppermute | solution.py:486
  41.9 3.2 %collective-permute-done.11.rest_0_ = bf16[128,1152]{1,0:T(8,128)(2,1)} collective-permute-done((bf16[128,1152]{1,0:T(8,128)(2,1)S(1)}, bf16[128,1152]{1,0:T(8,128)(2,1)}, u32[]{:S(2)}, u32[]{:S(2)}) %collective-permute-start.11) | collective-permute-done | bytes 294944 | tf_op jit(solution)/shard_map/tokens/ppermute | solution.py:486
  45.1 2.4 %collective-permute-start.10 = (bf16[128,1152]{1,0:T(8,128)(2,1)S(1)}, bf16[128,1152]{1,0:T(8,128)(2,1)S(1)}, u32[]{:S(2)}, u32[]{:S(2)}) collective-permute-start(bf16[128,1152]{1,0:T(8,128)(2,1)S(1)} %pad_maximum_fusion.rest_0_), channel_id=1, source_target_pairs={{0,16},{4,20},{8,24},{12,28},{16,0},{20,4},{24,8},{28,12},{1,17},{... | collective-permute-start | bytes 884744 | tf_op jit(solution)/shard_map/tokens/ppermute | solution.py:486
  47.9 2.0 %collective-permute-done.8.rest_2_ = bf16[128,1152]{1,0:T(8,128)(2,1)} collective-permute-done((bf16[128,1152]{1,0:T(8,128)(2,1)}, bf16[128,1152]{1,0:T(8,128)(2,1)}, u32[]{:S(2)}, u32[]{:S(2)}) %collective-permute-start.8) | collective-permute-done | bytes 294944 | tf_op jit(solution)/shard_map/tokens/ppermute | solution.py:486
  49.9 3.2 %expert_chunk.4 = (bf16[2,32,2048]{2,1,0:T(8,128)(2,1)S(1)}, bf16[2,32,2048]{2,1,0:T(8,128)(2,1)S(1)}, bf16[2,2,32,2048]{3,2,1,0:T(8,128)(2,1)S(1)}, bf16[32,2048]{1,0:T(8,128)(2,1)S(1)}) custom-call(s32[2]{0:T(128)S(1)} %pad_add_fusion.where_ref, bf16[128,1152]{1,0:T(8,128)(2,1)S(1)} %pad_maximum_fusion.rest_0_, ...), custom_call_target="tpu_custom_call" | custom-call | flops 805306368 | bytes 6291456 | tf_op jit(solution)/shard_map/experts/expert_chunk/pallas_call | solution.py:468
  53.8 7.3 %collective-permute-done.10.rest_0_ = bf16[128,1152]{1,0:T(8,128)(2,1)S(1)} collective-permute-done((bf16[128,1152]{1,0:T(8,128)(2,1)S(1)}, bf16[128,1152]{1,0:T(8,128)(2,1)S(1)}, u32[]{:S(2)}, u32[]{:S(2)}) %collective-permute-start.10) | collective-permute-done | bytes 294944 | tf_op jit(solution)/shard_map/tokens/ppermute | solution.py:486
  61.1 1.6 %collective-permute-start.14 = (bf16[128,1152]{1,0:T(8,128)(2,1)S(1)}, bf16[128,1152]{1,0:T(8,128)(2,1)S(1)}, u32[]{:S(2)}, u32[]{:S(2)}) collective-permute-start(bf16[128,1152]{1,0:T(8,128)(2,1)S(1)} %collective-permute-done.10.rest_0_), channel_id=1, source_target_pairs={{0,4},{4,0},{8,12},{12,8},{16,20},{20,16},{24,28},{28,24},{1,5},{5... | collective-permute-start | bytes 884744 | tf_op jit(solution)/shard_map/tokens/ppermute | solution.py:486
  62.7 1.5 %collective-permute-start.16 = (bf16[1,2160,128]{2,1,0:T(8,128)(2,1)S(1)}, bf16[1,2160,128]{2,1,0:T(8,128)(2,1)S(1)}, u32[]{:S(2)}, u32[]{:S(2)}) collective-permute-start(bf16[1,2160,128]{2,1,0:T(8,128)(2,1)S(1)} %copy-done.18), channel_id=1, source_target_pairs={{0,2},{1,3},{2,0},{3,1},{4,6},{5,7},{6,4},{7,5},{8,10},{9,11},{10,... | collective-permute-start | bytes 1658888 | tf_op jit(solution)/shard_map/send_states/ppermute | solution.py:486
  64.7 5.1 %collective-permute-done.14.rest_2_ = bf16[128,1152]{1,0:T(8,128)(2,1)S(1)} collective-permute-done((bf16[128,1152]{1,0:T(8,128)(2,1)S(1)}, bf16[128,1152]{1,0:T(8,128)(2,1)S(1)}, u32[]{:S(2)}, u32[]{:S(2)}) %collective-permute-start.14) | collective-permute-done | bytes 294944 | tf_op jit(solution)/shard_map/tokens/ppermute | solution.py:486
  70.4 1.8 %collective-permute-start.19 = (bf16[2,32,2048]{2,1,0:T(8,128)(2,1)S(1)}, bf16[2,32,2048]{2,1,0:T(8,128)(2,1)S(1)}, u32[]{:S(2)}, u32[]{:S(2)}) collective-permute-start(bf16[2,32,2048]{2,1,0:T(8,128)(2,1)S(1)} %fusion.8), channel_id=1, source_target_pairs={{0,4},{4,0},{8,12},{12,8},{16,20},{20,16},{24,28},{28,24},{1,5},{5... | collective-permute-start | bytes 786440 | tf_op jit(solution)/shard_map/way_back/ppermute | solution.py:486
  72.2 2.9 %expert_chunk.6 = (bf16[2,32,2048]{2,1,0:T(8,128)(2,1)S(1)}, bf16[2,32,2048]{2,1,0:T(8,128)(2,1)S(1)}, bf16[2,2,32,2048]{3,2,1,0:T(8,128)(2,1)S(1)}) custom-call(s32[2]{0:T(128)S(1)} %pad_add_fusion.where_ref, bf16[128,1152]{1,0:T(8,128)(2,1)} %collective-permute-done.7.rest_0_, bf16[128,1152]{1,0:T(8,128)(2,1)S(1)} %collective-permute-done.20.rest_1_, ...), custom_call_target="tpu_custom_call" | custom-call | flops 805306368 | bytes 6291456 | tf_op jit(solution)/shard_map/experts/expert_chunk/pallas_call | solution.py:468
  75.2 2.8 %expert_chunk.7 = (bf16[2,32,2048]{2,1,0:T(8,128)(2,1)S(1)}, bf16[2,32,2048]{2,1,0:T(8,128)(2,1)S(1)}, bf16[2,2,32,2048]{3,2,1,0:T(8,128)(2,1)S(1)}) custom-call(s32[2]{0:T(128)S(1)} %pad_add_fusion.where_ref, bf16[128,1152]{1,0:T(8,128)(2,1)} %collective-permute-done.11.rest_0_, bf16[128,1152]{1,0:T(8,128)(2,1)S(1)} %collective-permute-done.25.rest_1_, ...), custom_call_target="tpu_custom_call" | custom-call | flops 805306368 | bytes 6291456 | tf_op jit(solution)/shard_map/experts/expert_chunk/pallas_call | solution.py:468
  78.7 1.7 %collective-permute-start.31 = (bf16[1,2160,128]{2,1,0:T(8,128)(2,1)S(1)}, bf16[1,2160,128]{2,1,0:T(8,128)(2,1)S(1)}, u32[]{:S(2)}, u32[]{:S(2)}) collective-permute-start(bf16[1,2160,128]{2,1,0:T(8,128)(2,1)S(1)} %copy-done.16), channel_id=1, source_target_pairs={{0,3},{1,2},{2,1},{3,0},{4,7},{5,6},{6,5},{7,4},{8,11},{9,10},{10,... | collective-permute-start | bytes 1658888 | tf_op jit(solution)/shard_map/send_states/ppermute | solution.py:486
  80.3 2.1 %expert_chunk.5 = (bf16[2,32,2048]{2,1,0:T(8,128)(2,1)S(1)}, bf16[2,32,2048]{2,1,0:T(8,128)(2,1)S(1)}, bf16[2,2,32,2048]{3,2,1,0:T(8,128)(2,1)S(1)}) custom-call(s32[2]{0:T(128)S(1)} %pad_add_fusion.where_ref, bf16[128,1152]{1,0:T(8,128)(2,1)S(1)} %collective-permute-done.10.rest_0_, bf16[128,1152]{1,0:T(8,128)(2,1)S(1)} %collective-permute-done.13.rest_1_, ...), custom_call_target="tpu_custom_call" | custom-call | flops 805306368 | bytes 6291456 | tf_op jit(solution)/shard_map/experts/expert_chunk/pallas_call | solution.py:468
  83.2 1.8 %collective-permute-start.28 = (bf16[2,32,2048]{2,1,0:T(8,128)(2,1)S(1)}, bf16[2,32,2048]{2,1,0:T(8,128)(2,1)S(1)}, u32[]{:S(2)}, u32[]{:S(2)}) collective-permute-start(bf16[2,32,2048]{2,1,0:T(8,128)(2,1)S(1)} %fusion.2), channel_id=1, source_target_pairs={{0,4},{4,0},{8,12},{12,8},{16,20},{20,16},{24,28},{28,24},{1,5},{5... | collective-permute-start | bytes 786440 | tf_op jit(solution)/shard_map/way_back/ppermute | solution.py:486
  85.0 7.9 %collective-permute-done.31.rest_0_ = bf16[1,2160,128]{2,1,0:T(8,128)(2,1)S(1)} collective-permute-done((bf16[1,2160,128]{2,1,0:T(8,128)(2,1)S(1)}, bf16[1,2160,128]{2,1,0:T(8,128)(2,1)S(1)}, u32[]{:S(2)}, u32[]{:S(2)}) %collective-permute-start.31) | collective-permute-done | bytes 552992 | tf_op jit(solution)/shard_map/send_states/ppermute | solution.py:486
  93.5 4.1 %collective-permute-done.28 = bf16[2,32,2048]{2,1,0:T(8,128)(2,1)S(1)} collective-permute-done((bf16[2,32,2048]{2,1,0:T(8,128)(2,1)S(1)}, bf16[2,32,2048]{2,1,0:T(8,128)(2,1)S(1)}, u32[]{:S(2)}, u32[]{:S(2)}) %collective-permute-start.28) | collective-permute-done | bytes 262176 | tf_op jit(solution)/shard_map/way_back/ppermute | solution.py:486
  97.7 1.7 %collective-permute-start.24 = (bf16[2,32,2048]{2,1,0:T(8,128)(2,1)S(1)}, bf16[2,32,2048]{2,1,0:T(8,128)(2,1)S(1)}, u32[]{:S(2)}, u32[]{:S(2)}) collective-permute-start(bf16[2,32,2048]{2,1,0:T(8,128)(2,1)S(1)} %fusion.7), channel_id=1, source_target_pairs={{0,24},{4,28},{8,16},{12,20},{16,8},{20,12},{24,0},{28,4},{1,25},{... | collective-permute-start | bytes 786440 | tf_op jit(solution)/shard_map/way_back/ppermute | solution.py:486
  99.4 3.3 %collective-permute-done.30 = bf16[2,32,2048]{2,1,0:T(8,128)(2,1)S(1)} collective-permute-done((bf16[2,32,2048]{2,1,0:T(8,128)(2,1)S(1)}, bf16[2,32,2048]{2,1,0:T(8,128)(2,1)S(1)}, u32[]{:S(2)}, u32[]{:S(2)}) %collective-permute-start.30) | collective-permute-done | bytes 262176 | tf_op jit(solution)/shard_map/way_back/ppermute | solution.py:486
  106.6 7.8 %landed_states.2.rest_2_ = bf16[8,2048,128]{2,1,0:T(8,128)(2,1)} custom-call(s32[6]{0:T(128)S(1)} %maximum_convert_fusion.place_ref, bf16[2,2160,128]{2,1,0:T(8,128)(2,1)S(1)} %copy-done.4, bf16[2,2160,128]{2,1,0:T(8,128)(2,1)S(1)} %collective-permute-done.32.rest_1_, bf16[1,2160,128]{2,1,0:T(8,128)(2,1)} %collective-permute-done.9.rest_2_, ...), custom_call_target="tpu_custom_call" | custom-call | flops 20000000 | bytes 6291456 | tf_op jit(solution)/shard_map/landed/landed_states/pallas_call | solution.py:371
  114.4 8.7 %collective-permute-done.33 = bf16[2,32,2048]{2,1,0:T(8,128)(2,1)S(1)} collective-permute-done((bf16[2,32,2048]{2,1,0:T(8,128)(2,1)S(1)}, bf16[2,32,2048]{2,1,0:T(8,128)(2,1)S(1)}, u32[]{:S(2)}, u32[]{:S(2)}) %collective-permute-start.33) | collective-permute-done | bytes 262176 | tf_op jit(solution)/shard_map/way_back/ppermute | solution.py:486
  126.2 3.6 %landed_states.3 = bf16[8,2048,128]{2,1,0:T(8,128)(2,1)} custom-call(s32[2]{0:T(128)S(1)} %maximum_convert_fusion.1.place_ref, bf16[1,2160,128]{2,1,0:T(8,128)(2,1)S(1)} %collective-permute-done.31.rest_0_, bf16[1,2160,128]{2,1,0:T(8,128)(2,1)S(1)} %collective-permute-done.35.rest_1_, ...), custom_call_target="tpu_custom_call", output_to_operand_aliasing={{}: (3, {})} | custom-call | flops 20000000 | bytes 2097152 | tf_op jit(solution)/shard_map/landed/landed_states/pallas_call | solution.py:371
  (111 shorter events, 15.3 us)
Async XLA Ops:
  10.2 7.5 %collective-permute-start = (bf16[32,2688]{1,0:T(8,128)(2,1)}, bf16[32,2688]{1,0:T(8,128)(2,1)S(1)}, u32[]{:S(2)}, u32[]{:S(2)}) collective-permute-start(bf16[32,2688]{1,0:T(8,128)(2,1)} %get-tuple-element.94), channel_id=1, source_target_pairs={{0,1},{1,0},{2,3},{3,2},{4,5},{5,4},{6,7},{7,6},{8,9},{9,8},{10,11... | collective-permute-start | bytes 516104 | tf_op jit(solution)/shard_map/core/ppermute | solution.py:486
  10.7 8.0 %collective-permute-start.1 = (bf16[32,2688]{1,0:T(8,128)(2,1)}, bf16[32,2688]{1,0:T(8,128)(2,1)S(1)}, u32[]{:S(2)}, u32[]{:S(2)}) collective-permute-start(bf16[32,2688]{1,0:T(8,128)(2,1)} %get-tuple-element.95), channel_id=1, source_target_pairs={{0,2},{1,3},{2,0},{3,1},{4,6},{5,7},{6,4},{7,5},{8,10},{9,11},{10,... | collective-permute-start | bytes 516104 | tf_op jit(solution)/shard_map/core/ppermute | solution.py:486
  13.3 8.6 %collective-permute-start.2 = (bf16[32,2688]{1,0:T(8,128)(2,1)}, bf16[32,2688]{1,0:T(8,128)(2,1)S(1)}, u32[]{:S(2)}, u32[]{:S(2)}) collective-permute-start(bf16[32,2688]{1,0:T(8,128)(2,1)} %get-tuple-element.96), channel_id=1, source_target_pairs={{0,3},{1,2},{2,1},{3,0},{4,7},{5,6},{6,5},{7,4},{8,11},{9,10},{10,... | collective-permute-start | bytes 516104 | tf_op jit(solution)/shard_map/core/ppermute | solution.py:486
  28.0 11.9 %collective-permute-start.7 = (bf16[128,1152]{1,0:T(8,128)(2,1)S(1)}, bf16[128,1152]{1,0:T(8,128)(2,1)}, u32[]{:S(2)}, u32[]{:S(2)}) collective-permute-start(bf16[128,1152]{1,0:T(8,128)(2,1)S(1)} %pad_maximum_fusion.rest_0_), channel_id=1, source_target_pairs={{0,24},{4,28},{8,16},{12,20},{16,8},{20,12},{24,0},{28,4},{1,25},{... | collective-permute-start | bytes 884744 | tf_op jit(solution)/shard_map/tokens/ppermute | solution.py:486
  31.9 8.2 %collective-permute-start.5 = (bf16[128,1152]{1,0:T(8,128)(2,1)S(1)}, bf16[128,1152]{1,0:T(8,128)(2,1)}, u32[]{:S(2)}, u32[]{:S(2)}) collective-permute-start(bf16[128,1152]{1,0:T(8,128)(2,1)S(1)} %pad_maximum_fusion.rest_0_), channel_id=1, source_target_pairs={{0,4},{4,0},{8,12},{12,8},{16,20},{20,16},{24,28},{28,24},{1,5},{5... | collective-permute-start | bytes 884744 | tf_op jit(solution)/shard_map/tokens/ppermute | solution.py:486
  33.4 14.0 %collective-permute-start.9 = (bf16[1,2160,128]{2,1,0:T(8,128)(2,1)}, bf16[1,2160,128]{2,1,0:T(8,128)(2,1)}, u32[]{:S(2)}, u32[]{:S(2)}) collective-permute-start(bf16[1,2160,128]{2,1,0:T(8,128)(2,1)} %get-tuple-element.123), channel_id=1, source_target_pairs={{0,2},{1,3},{2,0},{3,1},{4,6},{5,7},{6,4},{7,5},{8,10},{9,11},{10,... | collective-permute-start | bytes 1658888 | tf_op jit(solution)/shard_map/send_states/ppermute | solution.py:486
  34.9 10.1 %collective-permute-start.11 = (bf16[128,1152]{1,0:T(8,128)(2,1)S(1)}, bf16[128,1152]{1,0:T(8,128)(2,1)}, u32[]{:S(2)}, u32[]{:S(2)}) collective-permute-start(bf16[128,1152]{1,0:T(8,128)(2,1)S(1)} %pad_maximum_fusion.rest_0_), channel_id=1, source_target_pairs={{0,8},{4,12},{8,0},{12,4},{16,24},{20,28},{24,16},{28,20},{1,9},{5... | collective-permute-start | bytes 884744 | tf_op jit(solution)/shard_map/tokens/ppermute | solution.py:486
  34.9 13.0 %collective-permute-start.4 = (bf16[128,1152]{1,0:T(8,128)(2,1)S(1)}, bf16[128,1152]{1,0:T(8,128)(2,1)}, u32[]{:S(2)}, u32[]{:S(2)}) collective-permute-start(bf16[128,1152]{1,0:T(8,128)(2,1)S(1)} %pad_maximum_fusion.rest_0_), channel_id=1, source_target_pairs={{0,1},{1,0},{2,3},{3,2},{4,5},{5,4},{6,7},{7,6},{8,9},{9,8},{10,11... | collective-permute-start | bytes 884744 | tf_op jit(solution)/shard_map/tokens/ppermute | solution.py:486
  40.1 7.8 %collective-permute-start.6 = (bf16[128,1152]{1,0:T(8,128)(2,1)}, bf16[128,1152]{1,0:T(8,128)(2,1)}, u32[]{:S(2)}, u32[]{:S(2)}) collective-permute-start(bf16[128,1152]{1,0:T(8,128)(2,1)} %collective-permute-done.5.rest_2_), channel_id=1, source_target_pairs={{0,1},{1,0},{2,3},{3,2},{4,5},{5,4},{6,7},{7,6},{8,9},{9,8},{10,11... | collective-permute-start | bytes 884744 | tf_op jit(solution)/shard_map/tokens/ppermute | solution.py:486
  40.1 9.8 %collective-permute-start.8 = (bf16[128,1152]{1,0:T(8,128)(2,1)}, bf16[128,1152]{1,0:T(8,128)(2,1)}, u32[]{:S(2)}, u32[]{:S(2)}) collective-permute-start(bf16[128,1152]{1,0:T(8,128)(2,1)} %collective-permute-done.7.rest_0_), channel_id=1, source_target_pairs={{0,4},{4,0},{8,12},{12,8},{16,20},{20,16},{24,28},{28,24},{1,5},{5... | collective-permute-start | bytes 884744 | tf_op jit(solution)/shard_map/tokens/ppermute | solution.py:486
  45.1 16.1 %collective-permute-start.10 = (bf16[128,1152]{1,0:T(8,128)(2,1)S(1)}, bf16[128,1152]{1,0:T(8,128)(2,1)S(1)}, u32[]{:S(2)}, u32[]{:S(2)}) collective-permute-start(bf16[128,1152]{1,0:T(8,128)(2,1)S(1)} %pad_maximum_fusion.rest_0_), channel_id=1, source_target_pairs={{0,16},{4,20},{8,24},{12,28},{16,0},{20,4},{24,8},{28,12},{1,17},{... | collective-permute-start | bytes 884744 | tf_op jit(solution)/shard_map/tokens/ppermute | solution.py:486
  47.4 13.7 %collective-permute-start.12 = (bf16[128,1152]{1,0:T(8,128)(2,1)}, bf16[128,1152]{1,0:T(8,128)(2,1)S(1)}, u32[]{:S(2)}, u32[]{:S(2)}) collective-permute-start(bf16[128,1152]{1,0:T(8,128)(2,1)} %collective-permute-done.11.rest_0_), channel_id=1, source_target_pairs={{0,4},{4,0},{8,12},{12,8},{16,20},{20,16},{24,28},{28,24},{1,5},{5... | collective-permute-start | bytes 884744 | tf_op jit(solution)/shard_map/tokens/ppermute | solution.py:486
  53.2 16.6 %collective-permute-start.18 = (bf16[2,2,32,2048]{3,2,1,0:T(8,128)(2,1)S(1)}, bf16[2,2,32,2048]{3,2,1,0:T(8,128)(2,1)S(1)}, u32[]{:S(2)}, u32[]{:S(2)}) collective-permute-start(bf16[2,2,32,2048]{3,2,1,0:T(8,128)(2,1)S(1)} %get-tuple-element.142), channel_id=1, source_target_pairs={{0,1},{1,0},{2,3},{3,2},{4,5},{5,4},{6,7},{7,6},{8,9},{9,8},{10,11... | collective-permute-start | bytes 1572872 | tf_op jit(solution)/shard_map/way_back/ppermute | solution.py:486
  53.2 11.0 %collective-permute-start.20 = (bf16[128,1152]{1,0:T(8,128)(2,1)}, bf16[128,1152]{1,0:T(8,128)(2,1)S(1)}, u32[]{:S(2)}, u32[]{:S(2)}) collective-permute-start(bf16[128,1152]{1,0:T(8,128)(2,1)} %collective-permute-done.7.rest_0_), channel_id=1, source_target_pairs={{0,1},{1,0},{2,3},{3,2},{4,5},{5,4},{6,7},{7,6},{8,9},{9,8},{10,11... | collective-permute-start | bytes 884744 | tf_op jit(solution)/shard_map/tokens/ppermute | solution.py:486
  53.7 10.5 %collective-permute-start.25 = (bf16[128,1152]{1,0:T(8,128)(2,1)}, bf16[128,1152]{1,0:T(8,128)(2,1)S(1)}, u32[]{:S(2)}, u32[]{:S(2)}) collective-permute-start(bf16[128,1152]{1,0:T(8,128)(2,1)} %collective-permute-done.11.rest_0_), channel_id=1, source_target_pairs={{0,1},{1,0},{2,3},{3,2},{4,5},{5,4},{6,7},{7,6},{8,9},{9,8},{10,11... | collective-permute-start | bytes 884744 | tf_op jit(solution)/shard_map/tokens/ppermute | solution.py:486
  61.1 8.6 %collective-permute-start.14 = (bf16[128,1152]{1,0:T(8,128)(2,1)S(1)}, bf16[128,1152]{1,0:T(8,128)(2,1)S(1)}, u32[]{:S(2)}, u32[]{:S(2)}) collective-permute-start(bf16[128,1152]{1,0:T(8,128)(2,1)S(1)} %collective-permute-done.10.rest_0_), channel_id=1, source_target_pairs={{0,4},{4,0},{8,12},{12,8},{16,20},{20,16},{24,28},{28,24},{1,5},{5... | collective-permute-start | bytes 884744 | tf_op jit(solution)/shard_map/tokens/ppermute | solution.py:486
  62.7 15.3 %collective-permute-start.16 = (bf16[1,2160,128]{2,1,0:T(8,128)(2,1)S(1)}, bf16[1,2160,128]{2,1,0:T(8,128)(2,1)S(1)}, u32[]{:S(2)}, u32[]{:S(2)}) collective-permute-start(bf16[1,2160,128]{2,1,0:T(8,128)(2,1)S(1)} %copy-done.18), channel_id=1, source_target_pairs={{0,2},{1,3},{2,0},{3,1},{4,6},{5,7},{6,4},{7,5},{8,10},{9,11},{10,... | collective-permute-start | bytes 1658888 | tf_op jit(solution)/shard_map/send_states/ppermute | solution.py:486
  64.2 14.4 %collective-permute-start.13 = (bf16[128,1152]{1,0:T(8,128)(2,1)S(1)}, bf16[128,1152]{1,0:T(8,128)(2,1)S(1)}, u32[]{:S(2)}, u32[]{:S(2)}) collective-permute-start(bf16[128,1152]{1,0:T(8,128)(2,1)S(1)} %collective-permute-done.10.rest_0_), channel_id=1, source_target_pairs={{0,1},{1,0},{2,3},{3,2},{4,5},{5,4},{6,7},{7,6},{8,9},{9,8},{10,11... | collective-permute-start | bytes 884744 | tf_op jit(solution)/shard_map/tokens/ppermute | solution.py:486
  64.2 6.2 %collective-permute-start.21 = (bf16[128,1152]{1,0:T(8,128)(2,1)}, bf16[128,1152]{1,0:T(8,128)(2,1)S(1)}, u32[]{:S(2)}, u32[]{:S(2)}) collective-permute-start(bf16[128,1152]{1,0:T(8,128)(2,1)} %collective-permute-done.8.rest_2_), channel_id=1, source_target_pairs={{0,1},{1,0},{2,3},{3,2},{4,5},{5,4},{6,7},{7,6},{8,9},{9,8},{10,11... | collective-permute-start | bytes 884744 | tf_op jit(solution)/shard_map/tokens/ppermute | solution.py:486
  69.8 8.9 %collective-permute-start.15 = (bf16[128,1152]{1,0:T(8,128)(2,1)S(1)}, bf16[128,1152]{1,0:T(8,128)(2,1)S(1)}, u32[]{:S(2)}, u32[]{:S(2)}) collective-permute-start(bf16[128,1152]{1,0:T(8,128)(2,1)S(1)} %collective-permute-done.14.rest_2_), channel_id=1, source_target_pairs={{0,1},{1,0},{2,3},{3,2},{4,5},{5,4},{6,7},{7,6},{8,9},{9,8},{10,11... | collective-permute-start | bytes 884744 | tf_op jit(solution)/shard_map/tokens/ppermute | solution.py:486
  70.4 12.1 %collective-permute-start.19 = (bf16[2,32,2048]{2,1,0:T(8,128)(2,1)S(1)}, bf16[2,32,2048]{2,1,0:T(8,128)(2,1)S(1)}, u32[]{:S(2)}, u32[]{:S(2)}) collective-permute-start(bf16[2,32,2048]{2,1,0:T(8,128)(2,1)S(1)} %fusion.8), channel_id=1, source_target_pairs={{0,4},{4,0},{8,12},{12,8},{16,20},{20,16},{24,28},{28,24},{1,5},{5... | collective-permute-start | bytes 786440 | tf_op jit(solution)/shard_map/way_back/ppermute | solution.py:486
  75.1 27.7 %collective-permute-start.32 = (bf16[2,2160,128]{2,1,0:T(8,128)(2,1)S(1)}, bf16[2,2160,128]{2,1,0:T(8,128)(2,1)S(1)}, u32[]{:S(2)}, u32[]{:S(2)}) collective-permute-start(bf16[2,2160,128]{2,1,0:T(8,128)(2,1)S(1)} %copy-done.12), channel_id=1, source_target_pairs={{0,1},{1,0},{2,3},{3,2},{4,5},{5,4},{6,7},{7,6},{8,9},{9,8},{10,11... | collective-permute-start | bytes 3317768 | tf_op jit(solution)/shard_map/send_states/ppermute | solution.py:486
  78.7 14.3 %collective-permute-start.31 = (bf16[1,2160,128]{2,1,0:T(8,128)(2,1)S(1)}, bf16[1,2160,128]{2,1,0:T(8,128)(2,1)S(1)}, u32[]{:S(2)}, u32[]{:S(2)}) collective-permute-start(bf16[1,2160,128]{2,1,0:T(8,128)(2,1)S(1)} %copy-done.16), channel_id=1, source_target_pairs={{0,3},{1,2},{2,1},{3,0},{4,7},{5,6},{6,5},{7,4},{8,11},{9,10},{10,... | collective-permute-start | bytes 1658888 | tf_op jit(solution)/shard_map/send_states/ppermute | solution.py:486
  82.4 10.6 %collective-permute-start.17 = (bf16[2,2,32,2048]{3,2,1,0:T(8,128)(2,1)S(1)}, bf16[2,2,32,2048]{3,2,1,0:T(8,128)(2,1)S(1)}, u32[]{:S(2)}, u32[]{:S(2)}) collective-permute-start(bf16[2,2,32,2048]{3,2,1,0:T(8,128)(2,1)S(1)} %get-tuple-element.140), channel_id=1, source_target_pairs={{0,1},{1,0},{2,3},{3,2},{4,5},{5,4},{6,7},{7,6},{8,9},{9,8},{10,11... | collective-permute-start | bytes 1572872 | tf_op jit(solution)/shard_map/way_back/ppermute | solution.py:486
  82.8 10.2 %collective-permute-start.23 = (bf16[2,32,2048]{2,1,0:T(8,128)(2,1)S(1)}, bf16[2,32,2048]{2,1,0:T(8,128)(2,1)S(1)}, u32[]{:S(2)}, u32[]{:S(2)}) collective-permute-start(bf16[2,32,2048]{2,1,0:T(8,128)(2,1)S(1)} %fusion.5), channel_id=1, source_target_pairs={{0,4},{4,0},{8,12},{12,8},{16,20},{20,16},{24,28},{28,24},{1,5},{5... | collective-permute-start | bytes 786440 | tf_op jit(solution)/shard_map/way_back/ppermute | solution.py:486
  83.2 14.4 %collective-permute-start.28 = (bf16[2,32,2048]{2,1,0:T(8,128)(2,1)S(1)}, bf16[2,32,2048]{2,1,0:T(8,128)(2,1)S(1)}, u32[]{:S(2)}, u32[]{:S(2)}) collective-permute-start(bf16[2,32,2048]{2,1,0:T(8,128)(2,1)S(1)} %fusion.2), channel_id=1, source_target_pairs={{0,4},{4,0},{8,12},{12,8},{16,20},{20,16},{24,28},{28,24},{1,5},{5... | collective-permute-start | bytes 786440 | tf_op jit(solution)/shard_map/way_back/ppermute | solution.py:486
  93.1 9.6 %collective-permute-start.30 = (bf16[2,32,2048]{2,1,0:T(8,128)(2,1)S(1)}, bf16[2,32,2048]{2,1,0:T(8,128)(2,1)S(1)}, u32[]{:S(2)}, u32[]{:S(2)}) collective-permute-start(bf16[2,32,2048]{2,1,0:T(8,128)(2,1)S(1)} %fusion.10), channel_id=1, source_target_pairs={{0,4},{4,0},{8,12},{12,8},{16,20},{20,16},{24,28},{28,24},{1,5},{5... | collective-permute-start | bytes 786440 | tf_op jit(solution)/shard_map/way_back/ppermute | solution.py:486
  97.7 16.7 %collective-permute-start.29 = (bf16[2,32,2048]{2,1,0:T(8,128)(2,1)S(1)}, bf16[2,32,2048]{2,1,0:T(8,128)(2,1)S(1)}, u32[]{:S(2)}, u32[]{:S(2)}) collective-permute-start(bf16[2,32,2048]{2,1,0:T(8,128)(2,1)S(1)} %fusion.4), channel_id=1, source_target_pairs={{0,8},{4,12},{8,0},{12,4},{16,24},{20,28},{24,16},{28,20},{1,9},{5... | collective-permute-start | bytes 786440 | tf_op jit(solution)/shard_map/way_back/ppermute | solution.py:486
  97.7 16.7 %collective-permute-start.24 = (bf16[2,32,2048]{2,1,0:T(8,128)(2,1)S(1)}, bf16[2,32,2048]{2,1,0:T(8,128)(2,1)S(1)}, u32[]{:S(2)}, u32[]{:S(2)}) collective-permute-start(bf16[2,32,2048]{2,1,0:T(8,128)(2,1)S(1)} %fusion.7), channel_id=1, source_target_pairs={{0,24},{4,28},{8,16},{12,20},{16,8},{20,12},{24,0},{28,4},{1,25},{... | collective-permute-start | bytes 786440 | tf_op jit(solution)/shard_map/way_back/ppermute | solution.py:486
  102.8 20.3 %collective-permute-start.33 = (bf16[2,32,2048]{2,1,0:T(8,128)(2,1)S(1)}, bf16[2,32,2048]{2,1,0:T(8,128)(2,1)S(1)}, u32[]{:S(2)}, u32[]{:S(2)}) collective-permute-start(bf16[2,32,2048]{2,1,0:T(8,128)(2,1)S(1)} %fusion.1), channel_id=1, source_target_pairs={{0,16},{4,20},{8,24},{12,28},{16,0},{20,4},{24,8},{28,12},{1,17},{... | collective-permute-start | bytes 786440 | tf_op jit(solution)/shard_map/way_back/ppermute | solution.py:486
  103.1 21.2 %collective-permute-start.35 = (bf16[1,2160,128]{2,1,0:T(8,128)(2,1)S(1)}, bf16[1,2160,128]{2,1,0:T(8,128)(2,1)S(1)}, u32[]{:S(2)}, u32[]{:S(2)}) collective-permute-start(bf16[1,2160,128]{2,1,0:T(8,128)(2,1)S(1)} %copy-done.14), channel_id=1, source_target_pairs={{0,3},{1,2},{2,1},{3,0},{4,7},{5,6},{6,5},{7,4},{8,11},{9,10},{10,... | collective-permute-start | bytes 1658888 | tf_op jit(solution)/shard_map/send_states/ppermute | solution.py:486
  123.2 6.5 %collective-permute-start.34 = (bf16[32,2048]{1,0:T(8,128)(2,1)S(1)}, bf16[32,2048]{1,0:T(8,128)(2,1)S(1)}, u32[]{:S(2)}, u32[]{:S(2)}) collective-permute-start(bf16[32,2048]{1,0:T(8,128)(2,1)S(1)} %fusion.13), channel_id=1, source_target_pairs={{0,2},{1,3},{2,0},{3,1},{4,6},{5,7},{6,4},{7,5},{8,10},{9,11},{10,... | collective-permute-start | bytes 393224 | tf_op jit(solution)/shard_map/mixed/ppermute | solution.py:486
  (24 other events, 357.1 us)

commit v7 on v6

--- a/solution.py
+++ b/solution.py
@@ -287,7 +287,7 @@
 
 
 def state_kernel(
-    key_heads, heads, steps, count, place_ref, *rest
+    key_heads, heads, steps, count, *rest
 ):
     arrived = rest[:count]
     out_ref, k_s, v_s, a_s, b_s, m_s, u_s, c_s, held, pay_s, ready, in_sem, pay_sem, out_sem = rest[-14:]
@@ -309,6 +309,7 @@
             )
         )
         copies[-1].start()
+    places = []
     for r in range(requests):
         pays[r].wait()
         rows = slice(r * steps, (r + 1) * steps)
@@ -320,6 +321,7 @@
         at = (key_heads + heads) * steps
         a_s[rows, :] = jax.nn.sigmoid(pay[at : at + steps])
         b_s[rows, :] = jax.nn.sigmoid(pay[at + steps : at + 2 * steps])
+        places.append(jnp.max(pay[at + 2 * steps : at + 3 * steps]).astype(jnp.int32))
     for r in range(requests):
         copies[r].wait()
         rows = slice(r * steps, (r + 1) * steps)
@@ -354,7 +356,7 @@
             )
             kept = held[r, h * hd : (h + 1) * hd, :].astype(F32) * c_s[h, r : r + 1, :]
             ready[slot, h * hd : (h + 1) * hd, :] = (kept + added).astype(BF16)
-        sent.append(pltpu.make_async_copy(ready.at[slot], out_ref.at[place_ref[r]], out_sem.at[slot]))
+        sent.append(pltpu.make_async_copy(ready.at[slot], out_ref.at[places[r]], out_sem.at[slot]))
         sent[-1].start()
     for c in sent[-2:]:
         c.wait()
@@ -362,18 +364,16 @@
 
 def landed_states(arrived, before, total, key_heads, heads, steps):
     _, all_rows, hd = arrived[0].shape
-    place_row = heads * hd + (key_heads + heads + 2) * steps
-    place = jnp.concatenate([a[:, place_row, 0] for a in arrived]).astype(jnp.int32)
-    requests = place.shape[0]
+    requests = sum(a.shape[0] for a in arrived)
     tokens = requests * steps
     state_rows = heads * hd
     hbm = pl.BlockSpec(memory_space=pl.ANY)
     out = pl.pallas_call(
         functools.partial(state_kernel, key_heads, heads, steps, len(arrived)),
-        in_specs=[pl.BlockSpec(memory_space=pltpu.SMEM)] + [hbm] * (len(arrived) + len(before)),
+        in_specs=[hbm] * (len(arrived) + len(before)),
         out_specs=hbm,
         out_shape=jax.ShapeDtypeStruct((total, state_rows, hd), BF16),
-        input_output_aliases={len(arrived) + 1: 0} if before else {},
+        input_output_aliases={len(arrived): 0} if before else {},
         scratch_shapes=[
             pltpu.VMEM((key_heads, tokens, hd), F32),
             pltpu.VMEM((heads, tokens, hd), F32),
@@ -392,7 +392,7 @@
         compiler_params=pltpu.CompilerParams(vmem_limit_bytes=32 * MIB),
         cost_estimate=pl.CostEstimate(flops=20_000_000, bytes_accessed=requests * MIB, transcendentals=10_000),
         name="landed_states",
-    )(place, *arrived, *before)
+    )(*arrived, *before)
     return out
 
 
@@ -544,38 +544,38 @@
     far = groups // 2
     chunks = [0] + [d for d in range(groups - 2, 0, -2) if d != far] + [far]
     tie = lax.optimization_barrier
-    own_rows = None
     with jax.named_scope("tokens"):
-        near = {d: swap(held, "dp", d) if d else held for d in chunks[:-1]}
-        later, near[chunks[1]] = tie((held, near[chunks[1]]))
-        across = {d: swap(near[d], "dp", 1) for d in chunks[:-1]}
-        near[far] = swap(later, "dp", far)
-        pieces = {}
-        for d in chunks:
-            aside = across.get(d)
+        near = {d: swap(held, "dp", d) if d else held for d in chunks}
+        across = {0: swap(held, "dp", 1)}
+    sums, keeps, asides, takens = {}, {}, {}, {}
+    for i, d in enumerate(chunks):
+        with jax.named_scope("tokens"):
+            if i == 1:
+                near[d], keeps[0] = tie((near[d], keeps[0]))
+            if i:
+                across[d] = swap(near[d], "dp", 1)
+            beside = across[d]
             if d == far:
-                near[d], pieces[chunks[-2]][2] = tie((near[d], pieces[chunks[-2]][2]))
-                aside = swap(near[d], "dp", 1)
-            pieces[d] = [near[d], swap(near[d], "ep", 1), aside, swap(aside, "ep", 1)]
-        pieces[0], pieces[chunks[1]][2] = tie((pieces[0], pieces[chunks[1]][2]))
-        pieces[0], far_states[0] = tie((pieces[0], far_states[0]))
-        pieces[far], far_states[1] = tie((pieces[far], far_states[1]))
-    sums = {}
-    for d in chunks:
+                beside, keeps = tie((beside, keeps))
+            pieces = [near[d], swap(near[d], "ep", 1), across[d], swap(beside, "ep", 1)]
+            if i < 2:
+                pieces, far_states[i] = tie((pieces, far_states[i]))
         with jax.named_scope("experts"):
-            outs = expert_chunk(where, pieces[d], gain, gate_up, down_weight, tokens, experts, d == 0)
-            keep_near, keep_across, give = outs[:3]
+            outs = expert_chunk(where, pieces, gain, gate_up, down_weight, tokens, experts, d == 0)
+            keeps[d] = outs[0]
             if d == 0:
                 own_rows = outs[3]
         with jax.named_scope("way_back"):
-            taken = swap(give, "ep", 1)
-            aside = summed(keep_across, taken[1]).astype(BF16)
+            takens[d] = swap(outs[2], "ep", 1)
+            asides[d] = summed(outs[1], takens[d][1]).astype(BF16)
+    for d in chunks:
+        with jax.named_scope("way_back"):
             if d == far:
-                aside, sums[0], sums[chunks[1]] = tie((aside, sums[0], sums[chunks[1]]))
-            back = swap(aside, "dp", 1)
+                asides[d], sums[0] = tie((asides[d], sums[0]))
+            back = swap(asides[d], "dp", 1)
             if d == far:
-                back, far_states[2] = tie((back, far_states[2]))
-            chunk = summed(keep_near, taken[0], back)
+                back, sums[chunks[1]], far_states[2] = tie((back, sums[chunks[1]], far_states[2]))
+            chunk = summed(keeps[d], takens[d][0], back)
             sums[d] = chunk.astype(BF16) if d else chunk
     with jax.named_scope("landed"):
         sizes = (requests, kw // hd, heads, steps)

time: 131 us -> 141 us (1.076)
  waiting for transfers between devices: 54.9 us -> 70.4 us
  local copies, waits for them, and re-layouts: 4.49 us -> 0.82 us
  starting transfers between devices: 30.6 us -> 33.4 us
  other arithmetic: 3.69 us -> 0.92 us
  Pallas kernels: 35.9 us -> 34.1 us
    ppermute x36, waiting for transfers between devices: 54.9 us -> 70.4 us  [swap(): return lax.ppermute(x, axis, [(i, i ^ d) for i in range(size)])]
    slice x5 -> x0, local copies, waits for them, and re-layouts: 2.88 us -> none  [landed_states(): a[:, place_row, 0]]
    ppermute x36, starting transfers between devices: 30.6 us -> 33.4 us  [swap(): return lax.ppermute(x, axis, [(i, i ^ d) for i in range(size)])]
    convert_element_type x6 -> x4, other arithmetic: 3.03 us -> 0.26 us  [shards(): asides[d] = summed(outs[1], takens[d][1]).astype(BF16)]
  transfers between devices with their start and end apart: 36 -> 36, of which waited for: 13 -> 14; matrix products, arithmetic and copies ran while one was open for 5% -> 1% of each run, Pallas kernels for 20% -> 17%
where the time goes in v7:
time: 141 us
  waiting for transfers between devices  70.4 us (50%)
  Pallas kernels  34.1 us (24%)
  starting transfers between devices  33.4 us (24%)
    ppermute x36, waiting for transfers between devices, swap(): return lax.ppermute(x, axis, [(i, i ^ d) for i in range(size)])  70.4 us
    ppermute x36, starting transfers between devices, swap(): return lax.ppermute(x, axis, [(i, i ^ d) for i in range(size)])  33.4 us
    pallas_call x2, Pallas kernels, landed_states(): pl.pallas_call(functools.partial(state_kernel, key_heads, heads, steps, l...  10.7 us
    pallas_call x4, Pallas kernels, expert_chunk(): pl.pallas_call(functools.partial(expert_kernel, sides, own_out, experts),...  10.2 us
    pallas_call x1, Pallas kernels, core_rows(): pl.pallas_call(functools.partial(core_kernel, lanes, experts), in_specs=[...  9.51 us
    pallas_call x1, Pallas kernels, pack_states(): pl.pallas_call(functools.partial(pack_kernel, lanes, key_heads), in_specs...  3.17 us
  transfers between devices with their start and end apart: 36, of which 14 were waited for; matrix products, arithmetic and copies ran while one was open for 1% of the time, Pallas kernels for 17%

profile of v7, /device:TPU:0, one launch (start us, length us, event | category | flops | bytes accessed | tf_op | source)
XLA Modules:
  0.0 140.7 jit_solution(11764990006347048414)
XLA Ops:
  0.7 9.5 %core_rows.1 = (bf16[32,2688]{1,0:T(8,128)(2,1)}, bf16[32,2688]{1,0:T(8,128)(2,1)}, bf16[32,2688]{1,0:T(8,128)(2,1)}, bf16[32,2688]{1,0:T(8,128)(2,1)}) custom-call(s32[1]{0:T(128)} %bitcast.lane_ref, bf16[8,2048,128]{2,1,0:T(8,128)(2,1)} %bitcast.60, bf16[8,4,1024]{2,1,0:T(4,128)(2,1)} %q_ref.1, bf16[8,4,1024]{2,1,0:T(4,128)(2,1)} %k_ref.3, ...), custom_call_target="tpu_custom_call" | custom-call | flops 20000000 | bytes 9437184 | tf_op jit(solution)/shard_map/core/core_rows/pallas_call | solution.py:155
  10.8 2.6 %collective-permute-start.1 = (bf16[32,2688]{1,0:T(8,128)(2,1)}, bf16[32,2688]{1,0:T(8,128)(2,1)S(1)}, u32[]{:S(2)}, u32[]{:S(2)}) collective-permute-start(bf16[32,2688]{1,0:T(8,128)(2,1)} %get-tuple-element.92), channel_id=1, source_target_pairs={{0,2},{1,3},{2,0},{3,1},{4,6},{5,7},{6,4},{7,5},{8,10},{9,11},{10,... | collective-permute-start | bytes 516104 | tf_op jit(solution)/shard_map/core/ppermute | solution.py:486
  13.4 3.2 %pack_states.1 = (bf16[2,2160,128]{2,1,0:T(8,128)(2,1)S(1)}, bf16[2,2160,128]{2,1,0:T(8,128)(2,1)S(1)}, bf16[1,2160,128]{2,1,0:T(8,128)(2,1)}, bf16[1,2160,128]{...) custom-call(s32[8]{0:T(128)S(1)} %copy-done.10, s32[1]{0:T(128)} %bitcast.lane_ref, ...), custom_call_target="tpu_custom_call" | custom-call | bytes 9437184 | tf_op jit(solution)/shard_map/send_states/pack_states/pallas_call | solution.py:240
  16.7 2.1 %collective-permute-done.1.refs_2_ = bf16[32,2688]{1,0:T(8,128)(2,1)S(1)} collective-permute-done((bf16[32,2688]{1,0:T(8,128)(2,1)}, bf16[32,2688]{1,0:T(8,128)(2,1)S(1)}, u32[]{:S(2)}, u32[]{:S(2)}) %collective-permute-start.1) | collective-permute-done | bytes 172064 | tf_op jit(solution)/shard_map/core/ppermute | solution.py:486
  18.8 3.2 %collective-permute-done.2.refs_3_ = bf16[32,2688]{1,0:T(8,128)(2,1)S(1)} collective-permute-done((bf16[32,2688]{1,0:T(8,128)(2,1)}, bf16[32,2688]{1,0:T(8,128)(2,1)S(1)}, u32[]{:S(2)}, u32[]{:S(2)}) %collective-permute-start.2) | collective-permute-done | bytes 172064 | tf_op jit(solution)/shard_map/core/ppermute | solution.py:486
  22.4 1.6 %collective-permute-start.3 = (bf16[128,512]{1,0:T(8,128)(2,1)S(1)}, bf16[128,512]{1,0:T(8,128)(2,1)S(1)}, u32[]{:S(2)}, u32[]{:S(2)}) collective-permute-start(bf16[128,512]{1,0:T(8,128)(2,1)S(1)} %get-tuple-element.105), channel_id=1, source_target_pairs={{0,2},{1,3},{2,0},{3,1},{4,6},{5,7},{6,4},{7,5},{8,10},{9,11},{10,... | collective-permute-start | bytes 393224 | tf_op jit(solution)/shard_map/attention/ppermute | solution.py:486
  24.0 4.0 %collective-permute-done.3 = bf16[128,512]{1,0:T(8,128)(2,1)S(1)} collective-permute-done((bf16[128,512]{1,0:T(8,128)(2,1)S(1)}, bf16[128,512]{1,0:T(8,128)(2,1)S(1)}, u32[]{:S(2)}, u32[]{:S(2)}) %collective-permute-start.3) | collective-permute-done | bytes 131104 | tf_op jit(solution)/shard_map/attention/ppermute | solution.py:486
  28.0 1.8 %collective-permute-start.5 = (bf16[128,1152]{1,0:T(8,128)(2,1)S(1)}, bf16[128,1152]{1,0:T(8,128)(2,1)}, u32[]{:S(2)}, u32[]{:S(2)}) collective-permute-start(bf16[128,1152]{1,0:T(8,128)(2,1)S(1)} %pad_maximum_fusion.rest_0_), channel_id=1, source_target_pairs={{0,4},{4,0},{8,12},{12,8},{16,20},{20,16},{24,28},{28,24},{1,5},{5... | collective-permute-start | bytes 884744 | tf_op jit(solution)/shard_map/tokens/ppermute | solution.py:486
  31.3 1.6 %collective-permute-start.12 = (bf16[128,1152]{1,0:T(8,128)(2,1)S(1)}, bf16[128,1152]{1,0:T(8,128)(2,1)}, u32[]{:S(2)}, u32[]{:S(2)}) collective-permute-start(bf16[128,1152]{1,0:T(8,128)(2,1)S(1)} %pad_maximum_fusion.rest_0_), channel_id=1, source_target_pairs={{0,8},{4,12},{8,0},{12,4},{16,24},{20,28},{24,16},{28,20},{1,9},{5... | collective-permute-start | bytes 884744 | tf_op jit(solution)/shard_map/tokens/ppermute | solution.py:486
  32.9 3.7 %collective-permute-done.5.rest_2_ = bf16[128,1152]{1,0:T(8,128)(2,1)} collective-permute-done((bf16[128,1152]{1,0:T(8,128)(2,1)S(1)}, bf16[128,1152]{1,0:T(8,128)(2,1)}, u32[]{:S(2)}, u32[]{:S(2)}) %collective-permute-start.5) | collective-permute-done | bytes 294944 | tf_op jit(solution)/shard_map/tokens/ppermute | solution.py:486
  36.7 3.9 %collective-permute-start.11 = (bf16[128,1152]{1,0:T(8,128)(2,1)S(1)}, bf16[128,1152]{1,0:T(8,128)(2,1)S(1)}, u32[]{:S(2)}, u32[]{:S(2)}) collective-permute-start(bf16[128,1152]{1,0:T(8,128)(2,1)S(1)} %pad_maximum_fusion.rest_0_), channel_id=1, source_target_pairs={{0,24},{4,28},{8,16},{12,20},{16,8},{20,12},{24,0},{28,4},{1,25},{... | collective-permute-start | bytes 884744 | tf_op jit(solution)/shard_map/tokens/ppermute | solution.py:486
  40.6 1.5 %collective-permute-start.14 = (bf16[128,1152]{1,0:T(8,128)(2,1)}, bf16[128,1152]{1,0:T(8,128)(2,1)S(1)}, u32[]{:S(2)}, u32[]{:S(2)}) collective-permute-start(bf16[128,1152]{1,0:T(8,128)(2,1)} %collective-permute-done.12.rest_0_), channel_id=1, source_target_pairs={{0,4},{4,0},{8,12},{12,8},{16,20},{20,16},{24,28},{28,24},{1,5},{5... | collective-permute-start | bytes 884744 | tf_op jit(solution)/shard_map/tokens/ppermute | solution.py:486
  42.2 1.6 %collective-permute-done.7.rest_2_ = bf16[1,2160,128]{2,1,0:T(8,128)(2,1)} collective-permute-done((bf16[1,2160,128]{2,1,0:T(8,128)(2,1)}, bf16[1,2160,128]{2,1,0:T(8,128)(2,1)}, u32[]{:S(2)}, u32[]{:S(2)}) %collective-permute-start.7) | collective-permute-done | bytes 552992 | tf_op jit(solution)/shard_map/send_states/ppermute | solution.py:486
  43.8 2.6 %collective-permute-start.8 = (bf16[128,1152]{1,0:T(8,128)(2,1)S(1)}, bf16[128,1152]{1,0:T(8,128)(2,1)S(1)}, u32[]{:S(2)}, u32[]{:S(2)}) collective-permute-start(bf16[128,1152]{1,0:T(8,128)(2,1)S(1)} %pad_maximum_fusion.rest_0_), channel_id=1, source_target_pairs={{0,16},{4,20},{8,24},{12,28},{16,0},{20,4},{24,8},{28,12},{1,17},{... | collective-permute-start | bytes 884744 | tf_op jit(solution)/shard_map/tokens/ppermute | solution.py:486
  47.9 3.2 %expert_chunk.4 = (bf16[2,32,2048]{2,1,0:T(8,128)(2,1)S(1)}, bf16[2,32,2048]{2,1,0:T(8,128)(2,1)S(1)}, bf16[2,2,32,2048]{3,2,1,0:T(8,128)(2,1)S(1)}, bf16[32,2048]{1,0:T(8,128)(2,1)S(1)}) custom-call(s32[2]{0:T(128)S(1)} %pad_add_fusion.where_ref, bf16[128,1152]{1,0:T(8,128)(2,1)S(1)} %pad_maximum_fusion.rest_0_, ...), custom_call_target="tpu_custom_call" | custom-call | flops 805306368 | bytes 6291456 | tf_op jit(solution)/shard_map/experts/expert_chunk/pallas_call | solution.py:468
  51.8 14.5 %collective-permute-done.8.rest_0_ = bf16[128,1152]{1,0:T(8,128)(2,1)S(1)} collective-permute-done((bf16[128,1152]{1,0:T(8,128)(2,1)S(1)}, bf16[128,1152]{1,0:T(8,128)(2,1)S(1)}, u32[]{:S(2)}, u32[]{:S(2)}) %collective-permute-start.8) | collective-permute-done | bytes 294944 | tf_op jit(solution)/shard_map/tokens/ppermute | solution.py:486
  68.4 2.8 %expert_chunk.5 = (bf16[2,32,2048]{2,1,0:T(8,128)(2,1)S(1)}, bf16[2,32,2048]{2,1,0:T(8,128)(2,1)S(1)}, bf16[2,2,32,2048]{3,2,1,0:T(8,128)(2,1)S(1)}) custom-call(s32[2]{0:T(128)S(1)} %pad_add_fusion.where_ref, bf16[128,1152]{1,0:T(8,128)(2,1)} %collective-permute-done.12.rest_0_, bf16[128,1152]{1,0:T(8,128)(2,1)S(1)} %collective-permute-done.13.rest_1_, ...), custom_call_target="tpu_custom_call" | custom-call | flops 805306368 | bytes 6291456 | tf_op jit(solution)/shard_map/experts/expert_chunk/pallas_call | solution.py:468
  71.5 4.8 %collective-permute-done.17.rest_2_ = bf16[128,1152]{1,0:T(8,128)(2,1)S(1)} collective-permute-done((bf16[128,1152]{1,0:T(8,128)(2,1)S(1)}, bf16[128,1152]{1,0:T(8,128)(2,1)S(1)}, u32[]{:S(2)}, u32[]{:S(2)}) %collective-permute-start.17) | collective-permute-done | bytes 294944 | tf_op jit(solution)/shard_map/tokens/ppermute | solution.py:486
  76.9 1.7 %collective-permute-done.18.rest_3_ = bf16[128,1152]{1,0:T(8,128)(2,1)S(1)} collective-permute-done((bf16[128,1152]{1,0:T(8,128)(2,1)S(1)}, bf16[128,1152]{1,0:T(8,128)(2,1)S(1)}, u32[]{:S(2)}, u32[]{:S(2)}) %collective-permute-start.18) | collective-permute-done | bytes 294944 | tf_op jit(solution)/shard_map/tokens/ppermute | solution.py:486
  79.8 2.1 %expert_chunk.6 = (bf16[2,32,2048]{2,1,0:T(8,128)(2,1)S(1)}, bf16[2,32,2048]{2,1,0:T(8,128)(2,1)S(1)}, bf16[2,2,32,2048]{3,2,1,0:T(8,128)(2,1)S(1)}) custom-call(s32[2]{0:T(128)S(1)} %pad_add_fusion.where_ref, bf16[128,1152]{1,0:T(8,128)(2,1)S(1)} %collective-permute-done.11.rest_0_, bf16[128,1152]{1,0:T(8,128)(2,1)S(1)} %collective-permute-done.16.rest_1_, ...), custom_call_target="tpu_custom_call" | custom-call | flops 805306368 | bytes 6291456 | tf_op jit(solution)/shard_map/experts/expert_chunk/pallas_call | solution.py:468
  81.9 1.6 %collective-permute-start.23 = (bf16[2,32,2048]{2,1,0:T(8,128)(2,1)S(1)}, bf16[2,32,2048]{2,1,0:T(8,128)(2,1)S(1)}, u32[]{:S(2)}, u32[]{:S(2)}) collective-permute-start(bf16[2,32,2048]{2,1,0:T(8,128)(2,1)S(1)} %fusion.8), channel_id=1, source_target_pairs={{0,4},{4,0},{8,12},{12,8},{16,20},{20,16},{24,28},{28,24},{1,5},{5... | collective-permute-start | bytes 786440 | tf_op jit(solution)/shard_map/way_back/ppermute | solution.py:486
  83.7 6.9 %collective-permute-done.23 = bf16[2,32,2048]{2,1,0:T(8,128)(2,1)S(1)} collective-permute-done((bf16[2,32,2048]{2,1,0:T(8,128)(2,1)S(1)}, bf16[2,32,2048]{2,1,0:T(8,128)(2,1)S(1)}, u32[]{:S(2)}, u32[]{:S(2)}) %collective-permute-start.23) | collective-permute-done | bytes 262176 | tf_op jit(solution)/shard_map/way_back/ppermute | solution.py:486
  92.3 2.1 %expert_chunk.7 = (bf16[2,32,2048]{2,1,0:T(8,128)(2,1)S(1)}, bf16[2,32,2048]{2,1,0:T(8,128)(2,1)S(1)}, bf16[2,2,32,2048]{3,2,1,0:T(8,128)(2,1)S(1)}) custom-call(s32[2]{0:T(128)S(1)} %pad_add_fusion.where_ref, bf16[128,1152]{1,0:T(8,128)(2,1)S(1)} %collective-permute-done.8.rest_0_, bf16[128,1152]{1,0:T(8,128)(2,1)S(1)} %collective-permute-done.9.rest_1_, ...), custom_call_target="tpu_custom_call" | custom-call | flops 805306368 | bytes 6291456 | tf_op jit(solution)/shard_map/experts/expert_chunk/pallas_call | solution.py:468
  94.9 3.4 %collective-permute-done.30 = bf16[2,32,2048]{2,1,0:T(8,128)(2,1)S(1)} collective-permute-done((bf16[2,32,2048]{2,1,0:T(8,128)(2,1)S(1)}, bf16[2,32,2048]{2,1,0:T(8,128)(2,1)S(1)}, u32[]{:S(2)}, u32[]{:S(2)}) %collective-permute-start.30) | collective-permute-done | bytes 262176 | tf_op jit(solution)/shard_map/way_back/ppermute | solution.py:486
  98.6 1.6 %collective-permute-start.26 = (bf16[2,32,2048]{2,1,0:T(8,128)(2,1)S(1)}, bf16[2,32,2048]{2,1,0:T(8,128)(2,1)S(1)}, u32[]{:S(2)}, u32[]{:S(2)}) collective-permute-start(bf16[2,32,2048]{2,1,0:T(8,128)(2,1)S(1)} %fusion.5), channel_id=1, source_target_pairs={{0,4},{4,0},{8,12},{12,8},{16,20},{20,16},{24,28},{28,24},{1,5},{5... | collective-permute-start | bytes 786440 | tf_op jit(solution)/shard_map/way_back/ppermute | solution.py:486
  100.9 7.1 %collective-permute-done.26 = bf16[2,32,2048]{2,1,0:T(8,128)(2,1)S(1)} collective-permute-done((bf16[2,32,2048]{2,1,0:T(8,128)(2,1)S(1)}, bf16[2,32,2048]{2,1,0:T(8,128)(2,1)S(1)}, u32[]{:S(2)}, u32[]{:S(2)}) %collective-permute-start.26) | collective-permute-done | bytes 262176 | tf_op jit(solution)/shard_map/way_back/ppermute | solution.py:486
  108.0 3.1 %collective-permute-done.24 = bf16[2,32,2048]{2,1,0:T(8,128)(2,1)S(1)} collective-permute-done((bf16[2,32,2048]{2,1,0:T(8,128)(2,1)S(1)}, bf16[2,32,2048]{2,1,0:T(8,128)(2,1)S(1)}, u32[]{:S(2)}, u32[]{:S(2)}) %collective-permute-start.24) | collective-permute-done | bytes 262176 | tf_op jit(solution)/shard_map/way_back/ppermute | solution.py:486
  111.2 2.5 %collective-permute-start.28 = (bf16[2,32,2048]{2,1,0:T(8,128)(2,1)S(1)}, bf16[2,32,2048]{2,1,0:T(8,128)(2,1)S(1)}, u32[]{:S(2)}, u32[]{:S(2)}) collective-permute-start(bf16[2,32,2048]{2,1,0:T(8,128)(2,1)S(1)} %fusion.7), channel_id=1, source_target_pairs={{0,24},{4,28},{8,16},{12,20},{16,8},{20,12},{24,0},{28,4},{1,25},{... | collective-permute-start | bytes 786440 | tf_op jit(solution)/shard_map/way_back/ppermute | solution.py:486
  114.5 7.5 %landed_states.2.rest_2_ = bf16[8,2048,128]{2,1,0:T(8,128)(2,1)} custom-call(bf16[2,2160,128]{2,1,0:T(8,128)(2,1)S(1)} %copy-done.4, bf16[2,2160,128]{2,1,0:T(8,128)(2,1)S(1)} %collective-permute-done.32.rest_1_, bf16[1,2160,128]{2,1,0:T(8,128)(2,1)} %collective-permute-done.7.rest_2_, bf16[1,2160,128]{2,1,0:T(8,128)(2,1)S(1)} %collective-permute-done.19.rest_3_), custom_call_target="tpu_custom_call" | custom-call | flops 20000000 | bytes 6291456 | tf_op jit(solution)/shard_map/landed/landed_states/pallas_call | solution.py:371
  122.1 12.8 %collective-permute-done.33 = bf16[2,32,2048]{2,1,0:T(8,128)(2,1)S(1)} collective-permute-done((bf16[2,32,2048]{2,1,0:T(8,128)(2,1)S(1)}, bf16[2,32,2048]{2,1,0:T(8,128)(2,1)S(1)}, u32[]{:S(2)}, u32[]{:S(2)}) %collective-permute-start.33) | collective-permute-done | bytes 262176 | tf_op jit(solution)/shard_map/way_back/ppermute | solution.py:486
  135.0 3.2 %landed_states.3 = bf16[8,2048,128]{2,1,0:T(8,128)(2,1)} custom-call(bf16[1,2160,128]{2,1,0:T(8,128)(2,1)S(1)} %collective-permute-done.27.rest_0_, bf16[1,2160,128]{2,1,0:T(8,128)(2,1)S(1)} %collective-permute-done.35.rest_1_, bf16[8,2048,128]{2,1,0:T(8,128)(2,1)} %landed_states.2.rest_2_), custom_call_target="tpu_custom_call", output_to_operand_aliasing={{}: (2, {})} | custom-call | flops 20000000 | bytes 2097152 | tf_op jit(solution)/shard_map/landed/landed_states/pallas_call | solution.py:371
  138.2 1.7 %collective-permute-done.34 = bf16[32,2048]{1,0:T(8,128)(2,1)S(1)} collective-permute-done((bf16[32,2048]{1,0:T(8,128)(2,1)S(1)}, bf16[32,2048]{1,0:T(8,128)(2,1)S(1)}, u32[]{:S(2)}, u32[]{:S(2)}) %collective-permute-start.34) | collective-permute-done | bytes 131104 | tf_op jit(solution)/shard_map/mixed/ppermute | solution.py:486
  (102 shorter events, 14.4 us)
Async XLA Ops:
  10.2 6.4 %collective-permute-start = (bf16[32,2688]{1,0:T(8,128)(2,1)}, bf16[32,2688]{1,0:T(8,128)(2,1)S(1)}, u32[]{:S(2)}, u32[]{:S(2)}) collective-permute-start(bf16[32,2688]{1,0:T(8,128)(2,1)} %get-tuple-element.91), channel_id=1, source_target_pairs={{0,1},{1,0},{2,3},{3,2},{4,5},{5,4},{6,7},{7,6},{8,9},{9,8},{10,11... | collective-permute-start | bytes 516104 | tf_op jit(solution)/shard_map/core/ppermute | solution.py:486
  10.8 8.0 %collective-permute-start.1 = (bf16[32,2688]{1,0:T(8,128)(2,1)}, bf16[32,2688]{1,0:T(8,128)(2,1)S(1)}, u32[]{:S(2)}, u32[]{:S(2)}) collective-permute-start(bf16[32,2688]{1,0:T(8,128)(2,1)} %get-tuple-element.92), channel_id=1, source_target_pairs={{0,2},{1,3},{2,0},{3,1},{4,6},{5,7},{6,4},{7,5},{8,10},{9,11},{10,... | collective-permute-start | bytes 516104 | tf_op jit(solution)/shard_map/core/ppermute | solution.py:486
  13.3 8.6 %collective-permute-start.2 = (bf16[32,2688]{1,0:T(8,128)(2,1)}, bf16[32,2688]{1,0:T(8,128)(2,1)S(1)}, u32[]{:S(2)}, u32[]{:S(2)}) collective-permute-start(bf16[32,2688]{1,0:T(8,128)(2,1)} %get-tuple-element.93), channel_id=1, source_target_pairs={{0,3},{1,2},{2,1},{3,0},{4,7},{5,6},{6,5},{7,4},{8,11},{9,10},{10,... | collective-permute-start | bytes 516104 | tf_op jit(solution)/shard_map/core/ppermute | solution.py:486
  28.0 8.6 %collective-permute-start.5 = (bf16[128,1152]{1,0:T(8,128)(2,1)S(1)}, bf16[128,1152]{1,0:T(8,128)(2,1)}, u32[]{:S(2)}, u32[]{:S(2)}) collective-permute-start(bf16[128,1152]{1,0:T(8,128)(2,1)S(1)} %pad_maximum_fusion.rest_0_), channel_id=1, source_target_pairs={{0,4},{4,0},{8,12},{12,8},{16,20},{20,16},{24,28},{28,24},{1,5},{5... | collective-permute-start | bytes 884744 | tf_op jit(solution)/shard_map/tokens/ppermute | solution.py:486
  29.8 13.9 %collective-permute-start.7 = (bf16[1,2160,128]{2,1,0:T(8,128)(2,1)}, bf16[1,2160,128]{2,1,0:T(8,128)(2,1)}, u32[]{:S(2)}, u32[]{:S(2)}) collective-permute-start(bf16[1,2160,128]{2,1,0:T(8,128)(2,1)} %get-tuple-element.115), channel_id=1, source_target_pairs={{0,2},{1,3},{2,0},{3,1},{4,6},{5,7},{6,4},{7,5},{8,10},{9,11},{10,... | collective-permute-start | bytes 1658888 | tf_op jit(solution)/shard_map/send_states/ppermute | solution.py:486
  31.3 9.3 %collective-permute-start.12 = (bf16[128,1152]{1,0:T(8,128)(2,1)S(1)}, bf16[128,1152]{1,0:T(8,128)(2,1)}, u32[]{:S(2)}, u32[]{:S(2)}) collective-permute-start(bf16[128,1152]{1,0:T(8,128)(2,1)S(1)} %pad_maximum_fusion.rest_0_), channel_id=1, source_target_pairs={{0,8},{4,12},{8,0},{12,4},{16,24},{20,28},{24,16},{28,20},{1,9},{5... | collective-permute-start | bytes 884744 | tf_op jit(solution)/shard_map/tokens/ppermute | solution.py:486
  32.9 13.5 %collective-permute-start.4 = (bf16[128,1152]{1,0:T(8,128)(2,1)S(1)}, bf16[128,1152]{1,0:T(8,128)(2,1)}, u32[]{:S(2)}, u32[]{:S(2)}) collective-permute-start(bf16[128,1152]{1,0:T(8,128)(2,1)S(1)} %pad_maximum_fusion.rest_0_), channel_id=1, source_target_pairs={{0,1},{1,0},{2,3},{3,2},{4,5},{5,4},{6,7},{7,6},{8,9},{9,8},{10,11... | collective-permute-start | bytes 884744 | tf_op jit(solution)/shard_map/tokens/ppermute | solution.py:486
  36.6 11.3 %collective-permute-start.6 = (bf16[128,1152]{1,0:T(8,128)(2,1)}, bf16[128,1152]{1,0:T(8,128)(2,1)}, u32[]{:S(2)}, u32[]{:S(2)}) collective-permute-start(bf16[128,1152]{1,0:T(8,128)(2,1)} %collective-permute-done.5.rest_2_), channel_id=1, source_target_pairs={{0,1},{1,0},{2,3},{3,2},{4,5},{5,4},{6,7},{7,6},{8,9},{9,8},{10,11... | collective-permute-start | bytes 884744 | tf_op jit(solution)/shard_map/tokens/ppermute | solution.py:486
  36.7 14.5 %collective-permute-start.11 = (bf16[128,1152]{1,0:T(8,128)(2,1)S(1)}, bf16[128,1152]{1,0:T(8,128)(2,1)S(1)}, u32[]{:S(2)}, u32[]{:S(2)}) collective-permute-start(bf16[128,1152]{1,0:T(8,128)(2,1)S(1)} %pad_maximum_fusion.rest_0_), channel_id=1, source_target_pairs={{0,24},{4,28},{8,16},{12,20},{16,8},{20,12},{24,0},{28,4},{1,25},{... | collective-permute-start | bytes 884744 | tf_op jit(solution)/shard_map/tokens/ppermute | solution.py:486
  40.6 11.1 %collective-permute-start.14 = (bf16[128,1152]{1,0:T(8,128)(2,1)}, bf16[128,1152]{1,0:T(8,128)(2,1)S(1)}, u32[]{:S(2)}, u32[]{:S(2)}) collective-permute-start(bf16[128,1152]{1,0:T(8,128)(2,1)} %collective-permute-done.12.rest_0_), channel_id=1, source_target_pairs={{0,4},{4,0},{8,12},{12,8},{16,20},{20,16},{24,28},{28,24},{1,5},{5... | collective-permute-start | bytes 884744 | tf_op jit(solution)/shard_map/tokens/ppermute | solution.py:486
  43.8 22.5 %collective-permute-start.8 = (bf16[128,1152]{1,0:T(8,128)(2,1)S(1)}, bf16[128,1152]{1,0:T(8,128)(2,1)S(1)}, u32[]{:S(2)}, u32[]{:S(2)}) collective-permute-start(bf16[128,1152]{1,0:T(8,128)(2,1)S(1)} %pad_maximum_fusion.rest_0_), channel_id=1, source_target_pairs={{0,16},{4,20},{8,24},{12,28},{16,0},{20,4},{24,8},{28,12},{1,17},{... | collective-permute-start | bytes 884744 | tf_op jit(solution)/shard_map/tokens/ppermute | solution.py:486
  46.4 24.9 %collective-permute-start.19 = (bf16[1,2160,128]{2,1,0:T(8,128)(2,1)}, bf16[1,2160,128]{2,1,0:T(8,128)(2,1)S(1)}, u32[]{:S(2)}, u32[]{:S(2)}) collective-permute-start(bf16[1,2160,128]{2,1,0:T(8,128)(2,1)} %copy-done.17), channel_id=1, source_target_pairs={{0,2},{1,3},{2,0},{3,1},{4,6},{5,7},{6,4},{7,5},{8,10},{9,11},{10,... | collective-permute-start | bytes 1658888 | tf_op jit(solution)/shard_map/send_states/ppermute | solution.py:486
  51.1 25.1 %collective-permute-start.22 = (bf16[2,2,32,2048]{3,2,1,0:T(8,128)(2,1)S(1)}, bf16[2,2,32,2048]{3,2,1,0:T(8,128)(2,1)S(1)}, u32[]{:S(2)}, u32[]{:S(2)}) collective-permute-start(bf16[2,2,32,2048]{3,2,1,0:T(8,128)(2,1)S(1)} %get-tuple-element.138), channel_id=1, source_target_pairs={{0,1},{1,0},{2,3},{3,2},{4,5},{5,4},{6,7},{7,6},{8,9},{9,8},{10,11... | collective-permute-start | bytes 1572872 | tf_op jit(solution)/shard_map/way_back/ppermute | solution.py:486
  51.2 16.6 %collective-permute-start.13 = (bf16[128,1152]{1,0:T(8,128)(2,1)}, bf16[128,1152]{1,0:T(8,128)(2,1)S(1)}, u32[]{:S(2)}, u32[]{:S(2)}) collective-permute-start(bf16[128,1152]{1,0:T(8,128)(2,1)} %collective-permute-done.12.rest_0_), channel_id=1, source_target_pairs={{0,1},{1,0},{2,3},{3,2},{4,5},{5,4},{6,7},{7,6},{8,9},{9,8},{10,11... | collective-permute-start | bytes 884744 | tf_op jit(solution)/shard_map/tokens/ppermute | solution.py:486
  51.7 16.2 %collective-permute-start.15 = (bf16[128,1152]{1,0:T(8,128)(2,1)S(1)}, bf16[128,1152]{1,0:T(8,128)(2,1)S(1)}, u32[]{:S(2)}, u32[]{:S(2)}) collective-permute-start(bf16[128,1152]{1,0:T(8,128)(2,1)S(1)} %collective-permute-done.14.rest_2_), channel_id=1, source_target_pairs={{0,1},{1,0},{2,3},{3,2},{4,5},{5,4},{6,7},{7,6},{8,9},{9,8},{10,11... | collective-permute-start | bytes 884744 | tf_op jit(solution)/shard_map/tokens/ppermute | solution.py:486
  66.3 9.9 %collective-permute-start.17 = (bf16[128,1152]{1,0:T(8,128)(2,1)S(1)}, bf16[128,1152]{1,0:T(8,128)(2,1)S(1)}, u32[]{:S(2)}, u32[]{:S(2)}) collective-permute-start(bf16[128,1152]{1,0:T(8,128)(2,1)S(1)} %collective-permute-done.11.rest_0_), channel_id=1, source_target_pairs={{0,4},{4,0},{8,12},{12,8},{16,20},{20,16},{24,28},{28,24},{1,5},{5... | collective-permute-start | bytes 884744 | tf_op jit(solution)/shard_map/tokens/ppermute | solution.py:486
  67.8 45.9 %collective-permute-start.32 = (bf16[2,2160,128]{2,1,0:T(8,128)(2,1)S(1)}, bf16[2,2160,128]{2,1,0:T(8,128)(2,1)S(1)}, u32[]{:S(2)}, u32[]{:S(2)}) collective-permute-start(bf16[2,2160,128]{2,1,0:T(8,128)(2,1)S(1)} %copy-done.12), channel_id=1, source_target_pairs={{0,1},{1,0},{2,3},{3,2},{4,5},{5,4},{6,7},{7,6},{8,9},{9,8},{10,11... | collective-permute-start | bytes 3317768 | tf_op jit(solution)/shard_map/send_states/ppermute | solution.py:486
  67.9 14.1 %collective-permute-start.10 = (bf16[128,1152]{1,0:T(8,128)(2,1)S(1)}, bf16[128,1152]{1,0:T(8,128)(2,1)S(1)}, u32[]{:S(2)}, u32[]{:S(2)}) collective-permute-start(bf16[128,1152]{1,0:T(8,128)(2,1)S(1)} %collective-permute-done.8.rest_0_), channel_id=1, source_target_pairs={{0,4},{4,0},{8,12},{12,8},{16,20},{20,16},{24,28},{28,24},{1,5},{5... | collective-permute-start | bytes 884744 | tf_op jit(solution)/shard_map/tokens/ppermute | solution.py:486
  76.2 7.3 %collective-permute-start.29 = (bf16[2,2,32,2048]{3,2,1,0:T(8,128)(2,1)S(1)}, bf16[2,2,32,2048]{3,2,1,0:T(8,128)(2,1)S(1)}, u32[]{:S(2)}, u32[]{:S(2)}) collective-permute-start(bf16[2,2,32,2048]{3,2,1,0:T(8,128)(2,1)S(1)} %get-tuple-element.150), channel_id=1, source_target_pairs={{0,1},{1,0},{2,3},{3,2},{4,5},{5,4},{6,7},{7,6},{8,9},{9,8},{10,11... | collective-permute-start | bytes 1572872 | tf_op jit(solution)/shard_map/way_back/ppermute | solution.py:486
  76.8 15.3 %collective-permute-start.9 = (bf16[128,1152]{1,0:T(8,128)(2,1)S(1)}, bf16[128,1152]{1,0:T(8,128)(2,1)S(1)}, u32[]{:S(2)}, u32[]{:S(2)}) collective-permute-start(bf16[128,1152]{1,0:T(8,128)(2,1)S(1)} %collective-permute-done.8.rest_0_), channel_id=1, source_target_pairs={{0,1},{1,0},{2,3},{3,2},{4,5},{5,4},{6,7},{7,6},{8,9},{9,8},{10,11... | collective-permute-start | bytes 884744 | tf_op jit(solution)/shard_map/tokens/ppermute | solution.py:486
  78.6 16.4 %collective-permute-start.27 = (bf16[1,2160,128]{2,1,0:T(8,128)(2,1)S(1)}, bf16[1,2160,128]{2,1,0:T(8,128)(2,1)S(1)}, u32[]{:S(2)}, u32[]{:S(2)}) collective-permute-start(bf16[1,2160,128]{2,1,0:T(8,128)(2,1)S(1)} %copy-done.16), channel_id=1, source_target_pairs={{0,3},{1,2},{2,1},{3,0},{4,7},{5,6},{6,5},{7,4},{8,11},{9,10},{10,... | collective-permute-start | bytes 1658888 | tf_op jit(solution)/shard_map/send_states/ppermute | solution.py:486
  81.9 8.6 %collective-permute-start.23 = (bf16[2,32,2048]{2,1,0:T(8,128)(2,1)S(1)}, bf16[2,32,2048]{2,1,0:T(8,128)(2,1)S(1)}, u32[]{:S(2)}, u32[]{:S(2)}) collective-permute-start(bf16[2,32,2048]{2,1,0:T(8,128)(2,1)S(1)} %fusion.8), channel_id=1, source_target_pairs={{0,4},{4,0},{8,12},{12,8},{16,20},{20,16},{24,28},{28,24},{1,5},{5... | collective-permute-start | bytes 786440 | tf_op jit(solution)/shard_map/way_back/ppermute | solution.py:486
  83.5 8.8 %collective-permute-start.20 = (bf16[128,1152]{1,0:T(8,128)(2,1)S(1)}, bf16[128,1152]{1,0:T(8,128)(2,1)S(1)}, u32[]{:S(2)}, u32[]{:S(2)}) collective-permute-start(bf16[128,1152]{1,0:T(8,128)(2,1)S(1)} %collective-permute-done.10.rest_2_), channel_id=1, source_target_pairs={{0,1},{1,0},{2,3},{3,2},{4,5},{5,4},{6,7},{7,6},{8,9},{9,8},{10,11... | collective-permute-start | bytes 884744 | tf_op jit(solution)/shard_map/tokens/ppermute | solution.py:486
  90.6 7.8 %collective-permute-start.30 = (bf16[2,32,2048]{2,1,0:T(8,128)(2,1)S(1)}, bf16[2,32,2048]{2,1,0:T(8,128)(2,1)S(1)}, u32[]{:S(2)}, u32[]{:S(2)}) collective-permute-start(bf16[2,32,2048]{2,1,0:T(8,128)(2,1)S(1)} %fusion.2), channel_id=1, source_target_pairs={{0,4},{4,0},{8,12},{12,8},{16,20},{20,16},{24,28},{28,24},{1,5},{5... | collective-permute-start | bytes 786440 | tf_op jit(solution)/shard_map/way_back/ppermute | solution.py:486
  92.2 6.4 %collective-permute-start.25 = (bf16[2,2,32,2048]{3,2,1,0:T(8,128)(2,1)S(1)}, bf16[2,2,32,2048]{3,2,1,0:T(8,128)(2,1)S(1)}, u32[]{:S(2)}, u32[]{:S(2)}) collective-permute-start(bf16[2,2,32,2048]{3,2,1,0:T(8,128)(2,1)S(1)} %get-tuple-element.143), channel_id=1, source_target_pairs={{0,1},{1,0},{2,3},{3,2},{4,5},{5,4},{6,7},{7,6},{8,9},{9,8},{10,11... | collective-permute-start | bytes 1572872 | tf_op jit(solution)/shard_map/way_back/ppermute | solution.py:486
  94.4 5.8 %collective-permute-start.21 = (bf16[2,2,32,2048]{3,2,1,0:T(8,128)(2,1)S(1)}, bf16[2,2,32,2048]{3,2,1,0:T(8,128)(2,1)S(1)}, u32[]{:S(2)}, u32[]{:S(2)}) collective-permute-start(bf16[2,2,32,2048]{3,2,1,0:T(8,128)(2,1)S(1)} %get-tuple-element.136), channel_id=1, source_target_pairs={{0,1},{1,0},{2,3},{3,2},{4,5},{5,4},{6,7},{7,6},{8,9},{9,8},{10,11... | collective-permute-start | bytes 1572872 | tf_op jit(solution)/shard_map/way_back/ppermute | solution.py:486
  98.5 23.6 %collective-permute-start.31 = (bf16[2,32,2048]{2,1,0:T(8,128)(2,1)S(1)}, bf16[2,32,2048]{2,1,0:T(8,128)(2,1)S(1)}, u32[]{:S(2)}, u32[]{:S(2)}) collective-permute-start(bf16[2,32,2048]{2,1,0:T(8,128)(2,1)S(1)} %fusion.4), channel_id=1, source_target_pairs={{0,8},{4,12},{8,0},{12,4},{16,24},{20,28},{24,16},{28,20},{1,9},{5... | collective-permute-start | bytes 786440 | tf_op jit(solution)/shard_map/way_back/ppermute | solution.py:486
  98.6 9.3 %collective-permute-start.26 = (bf16[2,32,2048]{2,1,0:T(8,128)(2,1)S(1)}, bf16[2,32,2048]{2,1,0:T(8,128)(2,1)S(1)}, u32[]{:S(2)}, u32[]{:S(2)}) collective-permute-start(bf16[2,32,2048]{2,1,0:T(8,128)(2,1)S(1)} %fusion.5), channel_id=1, source_target_pairs={{0,4},{4,0},{8,12},{12,8},{16,20},{20,16},{24,28},{28,24},{1,5},{5... | collective-permute-start | bytes 786440 | tf_op jit(solution)/shard_map/way_back/ppermute | solution.py:486
  100.3 10.9 %collective-permute-start.24 = (bf16[2,32,2048]{2,1,0:T(8,128)(2,1)S(1)}, bf16[2,32,2048]{2,1,0:T(8,128)(2,1)S(1)}, u32[]{:S(2)}, u32[]{:S(2)}) collective-permute-start(bf16[2,32,2048]{2,1,0:T(8,128)(2,1)S(1)} %fusion.10), channel_id=1, source_target_pairs={{0,4},{4,0},{8,12},{12,8},{16,20},{20,16},{24,28},{28,24},{1,5},{5... | collective-permute-start | bytes 786440 | tf_op jit(solution)/shard_map/way_back/ppermute | solution.py:486
  111.2 10.9 %collective-permute-start.28 = (bf16[2,32,2048]{2,1,0:T(8,128)(2,1)S(1)}, bf16[2,32,2048]{2,1,0:T(8,128)(2,1)S(1)}, u32[]{:S(2)}, u32[]{:S(2)}) collective-permute-start(bf16[2,32,2048]{2,1,0:T(8,128)(2,1)S(1)} %fusion.7), channel_id=1, source_target_pairs={{0,24},{4,28},{8,16},{12,20},{16,8},{20,12},{24,0},{28,4},{1,25},{... | collective-permute-start | bytes 786440 | tf_op jit(solution)/shard_map/way_back/ppermute | solution.py:486
  113.7 21.1 %collective-permute-start.33 = (bf16[2,32,2048]{2,1,0:T(8,128)(2,1)S(1)}, bf16[2,32,2048]{2,1,0:T(8,128)(2,1)S(1)}, u32[]{:S(2)}, u32[]{:S(2)}) collective-permute-start(bf16[2,32,2048]{2,1,0:T(8,128)(2,1)S(1)} %fusion.1), channel_id=1, source_target_pairs={{0,16},{4,20},{8,24},{12,28},{16,0},{20,4},{24,8},{28,12},{1,17},{... | collective-permute-start | bytes 786440 | tf_op jit(solution)/shard_map/way_back/ppermute | solution.py:486
  114.5 20.4 %collective-permute-start.35 = (bf16[1,2160,128]{2,1,0:T(8,128)(2,1)S(1)}, bf16[1,2160,128]{2,1,0:T(8,128)(2,1)S(1)}, u32[]{:S(2)}, u32[]{:S(2)}) collective-permute-start(bf16[1,2160,128]{2,1,0:T(8,128)(2,1)S(1)} %copy-done.14), channel_id=1, source_target_pairs={{0,3},{1,2},{2,1},{3,0},{4,7},{5,6},{6,5},{7,4},{8,11},{9,10},{10,... | collective-permute-start | bytes 1658888 | tf_op jit(solution)/shard_map/send_states/ppermute | solution.py:486
  (23 other events, 372.6 us)

commit v8 on v7

--- a/solution.py
+++ b/solution.py
@@ -544,45 +544,74 @@
     far = groups // 2
     chunks = [0] + [d for d in range(groups - 2, 0, -2) if d != far] + [far]
     tie = lax.optimization_barrier
-    with jax.named_scope("tokens"):
-        near = {d: swap(held, "dp", d) if d else held for d in chunks}
-        across = {0: swap(held, "dp", 1)}
-    sums, keeps, asides, takens = {}, {}, {}, {}
-    for i, d in enumerate(chunks):
-        with jax.named_scope("tokens"):
-            if i == 1:
-                near[d], keeps[0] = tie((near[d], keeps[0]))
-            if i:
-                across[d] = swap(near[d], "dp", 1)
-            beside = across[d]
-            if d == far:
-                beside, keeps = tie((beside, keeps))
-            pieces = [near[d], swap(near[d], "ep", 1), across[d], swap(beside, "ep", 1)]
-            if i < 2:
-                pieces, far_states[i] = tie((pieces, far_states[i]))
+    mid = chunks[1:-1]
+    first, last = mid[0], mid[-1]
+    across, keeps, asides, takens, backs, sums = {}, {}, {}, {}, {}, {}
+
+    def expert(d):
         with jax.named_scope("experts"):
+            pieces = [near[d], swap(near[d], "ep", 1), across[d], swap(across[d], "ep", 1)]
             outs = expert_chunk(where, pieces, gain, gate_up, down_weight, tokens, experts, d == 0)
             keeps[d] = outs[0]
-            if d == 0:
-                own_rows = outs[3]
         with jax.named_scope("way_back"):
             takens[d] = swap(outs[2], "ep", 1)
             asides[d] = summed(outs[1], takens[d][1]).astype(BF16)
-    for d in chunks:
+        return outs[3:]
+
+    def over(d):
+        with jax.named_scope("tokens"):
+            across[d] = swap(near[d], "dp", 1)
+
+    def back(d):
         with jax.named_scope("way_back"):
-            if d == far:
-                asides[d], sums[0] = tie((asides[d], sums[0]))
-            back = swap(asides[d], "dp", 1)
-            if d == far:
-                back, sums[chunks[1]], far_states[2] = tie((back, sums[chunks[1]], far_states[2]))
-            chunk = summed(keeps[d], takens[d][0], back)
+            backs[d] = swap(asides[d], "dp", 1)
+
+    def total(d):
+        with jax.named_scope("way_back"):
+            chunk = summed(keeps[d], takens[d][0], backs[d])
             sums[d] = chunk.astype(BF16) if d else chunk
+
+    with jax.named_scope("tokens"):
+        near = {d: swap(held, "dp", d) if d else held for d in [0] + mid}
+    over(0)
+    near, across = tie((near, across))
+    with jax.named_scope("tokens"):
+        half = near[0].shape[0] // 2
+        upper = swap(near[0][:half], "dp", far)
+        lower = swap(near[0][half:], "dp", far)
+    for d in mid:
+        over(d)
+    near[0], upper = tie((near[0], upper))
+    (own_rows,) = expert(0)
+    for d in mid[:-1]:
+        expert(d)
+    with jax.named_scope("tokens"):
+        near[far] = jnp.concatenate([upper, lower], axis=0)
+    near[far], across[last], keeps, far_states[0] = tie((near[far], across[last], keeps, far_states[0]))
+    over(far)
+    if last not in keeps:
+        expert(last)
+    across[far], keeps, asides[first], far_states[1] = tie(
+        (across[far], keeps, asides[first], far_states[1])
+    )
+    expert(far)
+    back(first)
+    asides[far], backs[first] = tie((asides[far], backs[first]))
+    back(far)
+    total(first)
+    with jax.named_scope("way_back"):
+        sums[first] = swap(sums[first], "dp", first)
+    total(far)
+    sums[far], sums[first] = tie((sums[far], sums[first]))
+    for d in mid[1:] + [0]:
+        back(d)
+        total(d)
     with jax.named_scope("landed"):
         sizes = (requests, kw // hd, heads, steps)
         sums[far], arrived = tie((sums[far], near_states + far_states[:-2]))
         moved_out = landed_states(arrived, [], *sizes)
     with jax.named_scope("way_back"):
-        sums = [swap(sums[d], "dp", d) if d else sums[d] for d in chunks]
+        sums = [swap(sums[d], "dp", d) if d not in (0, first) else sums[d] for d in chunks]
         sums, moved_out = tie((sums, moved_out))
     with jax.named_scope("landed"):
         moved_out = landed_states(far_states[-2:], [moved_out], *sizes)

time: 141 us -> 150 us (1.064)
  waiting for transfers between devices: 70.4 us -> 74 us
  starting transfers between devices: 33.4 us -> 36.5 us
  local copies, waits for them, and re-layouts: 0.82 us -> 2.62 us
    ppermute x36 -> x37, waiting for transfers between devices: 70.4 us -> 74 us  [swap(): return lax.ppermute(x, axis, [(i, i ^ d) for i in range(size)])]
    ppermute x36 -> x37, starting transfers between devices: 33.4 us -> 36.5 us  [swap(): return lax.ppermute(x, axis, [(i, i ^ d) for i in range(size)])]
  transfers between devices with their start and end apart: 36 -> 37, of which waited for: 14 -> 15; matrix products, arithmetic and copies ran while one was open for 1% -> 2% of each run, Pallas kernels for 17% -> 16%
where the time goes in v8:
time: 150 us; the launch traced here: 149 us
  waiting for transfers between devices  74 us (49%)
  starting transfers between devices  36.5 us (24%)
  Pallas kernels  33.4 us (22%)
  local copies, waits for them, and re-layouts  2.62 us (2%)
  other arithmetic  1.86 us (1%)
    ppermute x37, waiting for transfers between devices, swap(): return lax.ppermute(x, axis, [(i, i ^ d) for i in range(size)])  74 us
    ppermute x37, starting transfers between devices, swap(): return lax.ppermute(x, axis, [(i, i ^ d) for i in range(size)])  36.5 us
    pallas_call x2, Pallas kernels, landed_states(): pl.pallas_call(functools.partial(state_kernel, key_heads, heads, steps, l...  10.7 us
    pallas_call x4, Pallas kernels, expert_chunk(): pl.pallas_call(functools.partial(expert_kernel, sides, own_out, experts),...  9.53 us
    pallas_call x1, Pallas kernels, core_rows(): pl.pallas_call(functools.partial(core_kernel, lanes, experts), in_specs=[...  9.51 us
    pallas_call x1, Pallas kernels, pack_states(): pl.pallas_call(functools.partial(pack_kernel, lanes, key_heads), in_specs...  3.17 us
  transfers between devices with their start and end apart: 37, of which 15 were waited for; matrix products, arithmetic and copies ran while one was open for 2% of the time, Pallas kernels for 16%

profile of v8, /device:TPU:0, one launch (start us, length us, event | category | flops | bytes accessed | tf_op | source)
XLA Modules:
  0.0 149.4 jit_solution(13354598167441674337)
XLA Ops:
  0.7 9.5 %core_rows.1 = (bf16[32,2688]{1,0:T(8,128)(2,1)}, bf16[32,2688]{1,0:T(8,128)(2,1)}, bf16[32,2688]{1,0:T(8,128)(2,1)}, bf16[32,2688]{1,0:T(8,128)(2,1)}) custom-call(s32[1]{0:T(128)} %bitcast.lane_ref, bf16[8,2048,128]{2,1,0:T(8,128)(2,1)} %bitcast.60, bf16[8,4,1024]{2,1,0:T(4,128)(2,1)} %q_ref.1, bf16[8,4,1024]{2,1,0:T(4,128)(2,1)} %k_ref.3, ...), custom_call_target="tpu_custom_call" | custom-call | flops 20000000 | bytes 9437184 | tf_op jit(solution)/shard_map/core/core_rows/pallas_call | solution.py:155
  10.7 2.6 %collective-permute-start.1 = (bf16[32,2688]{1,0:T(8,128)(2,1)}, bf16[32,2688]{1,0:T(8,128)(2,1)S(1)}, u32[]{:S(2)}, u32[]{:S(2)}) collective-permute-start(bf16[32,2688]{1,0:T(8,128)(2,1)} %get-tuple-element.92), channel_id=1, source_target_pairs={{0,2},{1,3},{2,0},{3,1},{4,6},{5,7},{6,4},{7,5},{8,10},{9,11},{10,... | collective-permute-start | bytes 516104 | tf_op jit(solution)/shard_map/core/ppermute | solution.py:486
  13.4 3.2 %pack_states.1 = (bf16[2,2160,128]{2,1,0:T(8,128)(2,1)S(1)}, bf16[2,2160,128]{2,1,0:T(8,128)(2,1)S(1)}, bf16[1,2160,128]{2,1,0:T(8,128)(2,1)}, bf16[1,2160,128]{...) custom-call(s32[8]{0:T(128)S(1)} %copy-done.14, s32[1]{0:T(128)} %bitcast.lane_ref, ...), custom_call_target="tpu_custom_call" | custom-call | bytes 9437184 | tf_op jit(solution)/shard_map/send_states/pack_states/pallas_call | solution.py:240
  18.7 3.2 %collective-permute-done.2.refs_3_ = bf16[32,2688]{1,0:T(8,128)(2,1)S(1)} collective-permute-done((bf16[32,2688]{1,0:T(8,128)(2,1)}, bf16[32,2688]{1,0:T(8,128)(2,1)S(1)}, u32[]{:S(2)}, u32[]{:S(2)}) %collective-permute-start.2) | collective-permute-done | bytes 172064 | tf_op jit(solution)/shard_map/core/ppermute | solution.py:486
  22.4 1.6 %collective-permute-start.3 = (bf16[128,512]{1,0:T(8,128)(2,1)S(1)}, bf16[128,512]{1,0:T(8,128)(2,1)S(1)}, u32[]{:S(2)}, u32[]{:S(2)}) collective-permute-start(bf16[128,512]{1,0:T(8,128)(2,1)S(1)} %get-tuple-element.105), channel_id=1, source_target_pairs={{0,2},{1,3},{2,0},{3,1},{4,6},{5,7},{6,4},{7,5},{8,10},{9,11},{10,... | collective-permute-start | bytes 393224 | tf_op jit(solution)/shard_map/attention/ppermute | solution.py:486
  24.0 3.9 %collective-permute-done.3 = bf16[128,512]{1,0:T(8,128)(2,1)S(1)} collective-permute-done((bf16[128,512]{1,0:T(8,128)(2,1)S(1)}, bf16[128,512]{1,0:T(8,128)(2,1)S(1)}, u32[]{:S(2)}, u32[]{:S(2)}) %collective-permute-start.3) | collective-permute-done | bytes 131104 | tf_op jit(solution)/shard_map/attention/ppermute | solution.py:486
  28.0 1.9 %collective-permute-start.4 = (bf16[128,1152]{1,0:T(8,128)(2,1)S(1)}, bf16[128,1152]{1,0:T(8,128)(2,1)S(1)}, u32[]{:S(2)}, u32[]{:S(2)}) collective-permute-start(bf16[128,1152]{1,0:T(8,128)(2,1)S(1)} %pad_maximum_fusion.rest_0_), channel_id=1, source_target_pairs={{0,8},{4,12},{8,0},{12,4},{16,24},{20,28},{24,16},{28,20},{1,9},{5... | collective-permute-start | bytes 884744 | tf_op jit(solution)/shard_map/tokens/ppermute | solution.py:486
  29.9 2.5 %collective-permute-start.5 = (bf16[128,1152]{1,0:T(8,128)(2,1)S(1)}, bf16[128,1152]{1,0:T(8,128)(2,1)}, u32[]{:S(2)}, u32[]{:S(2)}) collective-permute-start(bf16[128,1152]{1,0:T(8,128)(2,1)S(1)} %pad_maximum_fusion.rest_0_), channel_id=1, source_target_pairs={{0,24},{4,28},{8,16},{12,20},{16,8},{20,12},{24,0},{28,4},{1,25},{... | collective-permute-start | bytes 884744 | tf_op jit(solution)/shard_map/tokens/ppermute | solution.py:486
  32.4 1.5 %collective-permute-start.6 = (bf16[128,1152]{1,0:T(8,128)(2,1)S(1)}, bf16[128,1152]{1,0:T(8,128)(2,1)S(1)}, u32[]{:S(2)}, u32[]{:S(2)}) collective-permute-start(bf16[128,1152]{1,0:T(8,128)(2,1)S(1)} %pad_maximum_fusion.rest_0_), channel_id=1, source_target_pairs={{0,4},{4,0},{8,12},{12,8},{16,20},{20,16},{24,28},{28,24},{1,5},{5... | collective-permute-start | bytes 884744 | tf_op jit(solution)/shard_map/tokens/ppermute | solution.py:486
  33.9 3.5 %collective-permute-done.4.rest_0_ = bf16[128,1152]{1,0:T(8,128)(2,1)S(1)} collective-permute-done((bf16[128,1152]{1,0:T(8,128)(2,1)S(1)}, bf16[128,1152]{1,0:T(8,128)(2,1)S(1)}, u32[]{:S(2)}, u32[]{:S(2)}) %collective-permute-start.4) | collective-permute-done | bytes 294944 | tf_op jit(solution)/shard_map/tokens/ppermute | solution.py:486
  37.4 7.9 %collective-permute-done.5.rest_0_ = bf16[128,1152]{1,0:T(8,128)(2,1)} collective-permute-done((bf16[128,1152]{1,0:T(8,128)(2,1)S(1)}, bf16[128,1152]{1,0:T(8,128)(2,1)}, u32[]{:S(2)}, u32[]{:S(2)}) %collective-permute-start.5) | collective-permute-done | bytes 294944 | tf_op jit(solution)/shard_map/tokens/ppermute | solution.py:486
  45.3 1.5 %collective-permute-start.13 = (bf16[128,1152]{1,0:T(8,128)(2,1)}, bf16[128,1152]{1,0:T(8,128)(2,1)}, u32[]{:S(2)}, u32[]{:S(2)}) collective-permute-start(bf16[128,1152]{1,0:T(8,128)(2,1)} %collective-permute-done.5.rest_0_), channel_id=1, source_target_pairs={{0,4},{4,0},{8,12},{12,8},{16,20},{20,16},{24,28},{28,24},{1,5},{5... | collective-permute-start | bytes 884744 | tf_op jit(solution)/shard_map/tokens/ppermute | solution.py:486
  48.3 4.7 %collective-permute-done.13.rest_2_ = bf16[128,1152]{1,0:T(8,128)(2,1)} collective-permute-done((bf16[128,1152]{1,0:T(8,128)(2,1)}, bf16[128,1152]{1,0:T(8,128)(2,1)}, u32[]{:S(2)}, u32[]{:S(2)}) %collective-permute-start.13) | collective-permute-done | bytes 294944 | tf_op jit(solution)/shard_map/tokens/ppermute | solution.py:486
  54.9 1.8 %collective-permute-start.10 = (bf16[64,1152]{1,0:T(8,128)(2,1)}, bf16[64,1152]{1,0:T(8,128)(2,1)S(1)}, u32[]{:S(2)}, u32[]{:S(2)}) collective-permute-start(bf16[64,1152]{1,0:T(8,128)(2,1)} %get-tuple-element.170), channel_id=1, source_target_pairs={{0,16},{4,20},{8,24},{12,28},{16,0},{20,4},{24,8},{28,12},{1,17},{... | collective-permute-start | bytes 442376 | tf_op jit(solution)/shard_map/tokens/ppermute | solution.py:486
  56.9 10.2 %collective-permute-done.7 = bf16[64,1152]{1,0:T(8,128)(2,1)} collective-permute-done((bf16[64,1152]{1,0:T(8,128)(2,1)}, bf16[64,1152]{1,0:T(8,128)(2,1)}, u32[]{:S(2)}, u32[]{:S(2)}) %collective-permute-start.7) | collective-permute-done | bytes 147488 | tf_op jit(solution)/shard_map/tokens/ppermute | solution.py:486
  67.0 1.5 %collective-permute-start.11 = (bf16[128,1152]{1,0:T(8,128)(2,1)}, bf16[128,1152]{1,0:T(8,128)(2,1)S(1)}, u32[]{:S(2)}, u32[]{:S(2)}) collective-permute-start(bf16[128,1152]{1,0:T(8,128)(2,1)} %copy-done.6), channel_id=1, source_target_pairs={{0,4},{4,0},{8,12},{12,8},{16,20},{20,16},{24,28},{28,24},{1,5},{5... | collective-permute-start | bytes 884744 | tf_op jit(solution)/shard_map/tokens/ppermute | solution.py:486
  68.8 1.5 %collective-permute-start.20 = (bf16[1,2160,128]{2,1,0:T(8,128)(2,1)}, bf16[1,2160,128]{2,1,0:T(8,128)(2,1)S(1)}, u32[]{:S(2)}, u32[]{:S(2)}) collective-permute-start(bf16[1,2160,128]{2,1,0:T(8,128)(2,1)} %copy-done.21), channel_id=1, source_target_pairs={{0,2},{1,3},{2,0},{3,1},{4,6},{5,7},{6,4},{7,5},{8,10},{9,11},{10,... | collective-permute-start | bytes 1658888 | tf_op jit(solution)/shard_map/send_states/ppermute | solution.py:486
  70.3 3.1 %expert_chunk.5 = (bf16[2,32,2048]{2,1,0:T(8,128)(2,1)S(1)}, bf16[2,32,2048]{2,1,0:T(8,128)(2,1)S(1)}, bf16[2,2,32,2048]{3,2,1,0:T(8,128)(2,1)S(1)}) custom-call(s32[2]{0:T(128)S(1)} %pad_add_fusion.where_ref, bf16[128,1152]{1,0:T(8,128)(2,1)} %collective-permute-done.5.rest_0_, bf16[128,1152]{1,0:T(8,128)(2,1)} %collective-permute-done.12.rest_1_, ...), custom_call_target="tpu_custom_call" | custom-call | flops 805306368 | bytes 6291456 | tf_op jit(solution)/shard_map/experts/expert_chunk/pallas_call | solution.py:468
  75.0 2.3 %expert_chunk.4 = (bf16[2,32,2048]{2,1,0:T(8,128)(2,1)S(1)}, bf16[2,32,2048]{2,1,0:T(8,128)(2,1)S(1)}, bf16[2,2,32,2048]{3,2,1,0:T(8,128)(2,1)S(1)}, bf16[32,2048]{1,0:T(8,128)(2,1)S(1)}) custom-call(s32[2]{0:T(128)S(1)} %pad_add_fusion.where_ref, bf16[128,1152]{1,0:T(8,128)(2,1)S(1)} %pad_maximum_fusion.rest_0_, ...), custom_call_target="tpu_custom_call" | custom-call | flops 805306368 | bytes 6291456 | tf_op jit(solution)/shard_map/experts/expert_chunk/pallas_call | solution.py:468
  78.2 5.5 %collective-permute-done.20.rest_3_ = bf16[1,2160,128]{2,1,0:T(8,128)(2,1)S(1)} collective-permute-done((bf16[1,2160,128]{2,1,0:T(8,128)(2,1)}, bf16[1,2160,128]{2,1,0:T(8,128)(2,1)S(1)}, u32[]{:S(2)}, u32[]{:S(2)}) %collective-permute-start.20) | collective-permute-done | bytes 552992 | tf_op jit(solution)/shard_map/send_states/ppermute | solution.py:486
  83.8 2.1 %expert_chunk.6 = (bf16[2,32,2048]{2,1,0:T(8,128)(2,1)S(1)}, bf16[2,32,2048]{2,1,0:T(8,128)(2,1)S(1)}, bf16[2,2,32,2048]{3,2,1,0:T(8,128)(2,1)S(1)}) custom-call(s32[2]{0:T(128)S(1)} %pad_add_fusion.where_ref, bf16[128,1152]{1,0:T(8,128)(2,1)S(1)} %copy-done.7, bf16[128,1152]{1,0:T(8,128)(2,1)S(1)} %collective-permute-done.17.rest_1_, ...), custom_call_target="tpu_custom_call" | custom-call | flops 805306368 | bytes 6291456 | tf_op jit(solution)/shard_map/experts/expert_chunk/pallas_call | solution.py:468
  88.7 2.1 %expert_chunk.7 = (bf16[2,32,2048]{2,1,0:T(8,128)(2,1)S(1)}, bf16[2,32,2048]{2,1,0:T(8,128)(2,1)S(1)}, bf16[2,2,32,2048]{3,2,1,0:T(8,128)(2,1)S(1)}) custom-call(s32[2]{0:T(128)S(1)} %pad_add_fusion.where_ref, bf16[128,1152]{1,0:T(8,128)(2,1)S(1)} %pad_maximum_fusion.1.rest_0_, bf16[128,1152]{1,0:T(8,128)(2,1)S(1)} %collective-permute-done.23.rest_1_, ...), custom_call_target="tpu_custom_call" | custom-call | flops 805306368 | bytes 6291456 | tf_op jit(solution)/shard_map/experts/expert_chunk/pallas_call | solution.py:468
  93.3 6.9 %collective-permute-done.30 = bf16[2,32,2048]{2,1,0:T(8,128)(2,1)S(1)} collective-permute-done((bf16[2,32,2048]{2,1,0:T(8,128)(2,1)S(1)}, bf16[2,32,2048]{2,1,0:T(8,128)(2,1)S(1)}, u32[]{:S(2)}, u32[]{:S(2)}) %collective-permute-start.30) | collective-permute-done | bytes 262176 | tf_op jit(solution)/shard_map/way_back/ppermute | solution.py:486
  101.5 9.5 %collective-permute-done.26 = bf16[2,32,2048]{2,1,0:T(8,128)(2,1)S(1)} collective-permute-done((bf16[2,32,2048]{2,1,0:T(8,128)(2,1)S(1)}, bf16[2,32,2048]{2,1,0:T(8,128)(2,1)S(1)}, u32[]{:S(2)}, u32[]{:S(2)}) %collective-permute-start.26) | collective-permute-done | bytes 262176 | tf_op jit(solution)/shard_map/way_back/ppermute | solution.py:486
  112.1 6.7 %collective-permute-done.27 = bf16[2,32,2048]{2,1,0:T(8,128)(2,1)S(1)} collective-permute-done((bf16[2,32,2048]{2,1,0:T(8,128)(2,1)S(1)}, bf16[2,32,2048]{2,1,0:T(8,128)(2,1)S(1)}, u32[]{:S(2)}, u32[]{:S(2)}) %collective-permute-start.27) | collective-permute-done | bytes 262176 | tf_op jit(solution)/shard_map/way_back/ppermute | solution.py:486
  118.9 2.3 %collective-permute-start.28 = (bf16[2,32,2048]{2,1,0:T(8,128)(2,1)S(1)}, bf16[2,32,2048]{2,1,0:T(8,128)(2,1)S(1)}, u32[]{:S(2)}, u32[]{:S(2)}) collective-permute-start(bf16[2,32,2048]{2,1,0:T(8,128)(2,1)S(1)} %fusion.4), channel_id=1, source_target_pairs={{0,24},{4,28},{8,16},{12,20},{16,8},{20,12},{24,0},{28,4},{1,25},{... | collective-permute-start | bytes 786440 | tf_op jit(solution)/shard_map/way_back/ppermute | solution.py:486
  121.3 6.4 %collective-permute-done.28 = bf16[2,32,2048]{2,1,0:T(8,128)(2,1)S(1)} collective-permute-done((bf16[2,32,2048]{2,1,0:T(8,128)(2,1)S(1)}, bf16[2,32,2048]{2,1,0:T(8,128)(2,1)S(1)}, u32[]{:S(2)}, u32[]{:S(2)}) %collective-permute-start.28) | collective-permute-done | bytes 262176 | tf_op jit(solution)/shard_map/way_back/ppermute | solution.py:486
  127.7 3.5 %collective-permute-start.33 = (bf16[2,32,2048]{2,1,0:T(8,128)(2,1)S(1)}, bf16[2,32,2048]{2,1,0:T(8,128)(2,1)S(1)}, u32[]{:S(2)}, u32[]{:S(2)}) collective-permute-start(bf16[2,32,2048]{2,1,0:T(8,128)(2,1)S(1)} %fusion.7), channel_id=1, source_target_pairs={{0,16},{4,20},{8,24},{12,28},{16,0},{20,4},{24,8},{28,12},{1,17},{... | collective-permute-start | bytes 786440 | tf_op jit(solution)/shard_map/way_back/ppermute | solution.py:486
  131.4 7.5 %landed_states.2.rest_2_ = bf16[8,2048,128]{2,1,0:T(8,128)(2,1)} custom-call(bf16[2,2160,128]{2,1,0:T(8,128)(2,1)S(1)} %copy-done.4, bf16[2,2160,128]{2,1,0:T(8,128)(2,1)S(1)} %collective-permute-done.32.rest_1_, bf16[1,2160,128]{2,1,0:T(8,128)(2,1)} %collective-permute-done.15.rest_2_, bf16[1,2160,128]{2,1,0:T(8,128)(2,1)S(1)} %collective-permute-done.20.rest_3_), custom_call_target="tpu_custom_call" | custom-call | flops 20000000 | bytes 6291456 | tf_op jit(solution)/shard_map/landed/landed_states/pallas_call | solution.py:371
  138.9 2.7 %collective-permute-done.33 = bf16[2,32,2048]{2,1,0:T(8,128)(2,1)S(1)} collective-permute-done((bf16[2,32,2048]{2,1,0:T(8,128)(2,1)S(1)}, bf16[2,32,2048]{2,1,0:T(8,128)(2,1)S(1)}, u32[]{:S(2)}, u32[]{:S(2)}) %collective-permute-start.33) | collective-permute-done | bytes 262176 | tf_op jit(solution)/shard_map/way_back/ppermute | solution.py:486
  141.7 2.2 %collective-permute-start.34 = (bf16[32,2048]{1,0:T(8,128)(2,1)S(1)}, bf16[32,2048]{1,0:T(8,128)(2,1)S(1)}, u32[]{:S(2)}, u32[]{:S(2)}) collective-permute-start(bf16[32,2048]{1,0:T(8,128)(2,1)S(1)} %fusion.13), channel_id=1, source_target_pairs={{0,2},{1,3},{2,0},{3,1},{4,6},{5,7},{6,4},{7,5},{8,10},{9,11},{10,... | collective-permute-start | bytes 393224 | tf_op jit(solution)/shard_map/mixed/ppermute | solution.py:486
  143.9 3.2 %landed_states.3 = bf16[8,2048,128]{2,1,0:T(8,128)(2,1)} custom-call(bf16[1,2160,128]{2,1,0:T(8,128)(2,1)S(1)} %collective-permute-done.35.rest_0_, bf16[1,2160,128]{2,1,0:T(8,128)(2,1)S(1)} %collective-permute-done.36.rest_1_, bf16[8,2048,128]{2,1,0:T(8,128)(2,1)} %landed_states.2.rest_2_), custom_call_target="tpu_custom_call", output_to_operand_aliasing={{}: (2, {})} | custom-call | flops 20000000 | bytes 2097152 | tf_op jit(solution)/shard_map/landed/landed_states/pallas_call | solution.py:371
  (114 shorter events, 19.8 us)
Async XLA Ops:
  10.2 7.4 %collective-permute-start = (bf16[32,2688]{1,0:T(8,128)(2,1)}, bf16[32,2688]{1,0:T(8,128)(2,1)S(1)}, u32[]{:S(2)}, u32[]{:S(2)}) collective-permute-start(bf16[32,2688]{1,0:T(8,128)(2,1)} %get-tuple-element.91), channel_id=1, source_target_pairs={{0,1},{1,0},{2,3},{3,2},{4,5},{5,4},{6,7},{7,6},{8,9},{9,8},{10,11... | collective-permute-start | bytes 516104 | tf_op jit(solution)/shard_map/core/ppermute | solution.py:486
  10.7 8.0 %collective-permute-start.1 = (bf16[32,2688]{1,0:T(8,128)(2,1)}, bf16[32,2688]{1,0:T(8,128)(2,1)S(1)}, u32[]{:S(2)}, u32[]{:S(2)}) collective-permute-start(bf16[32,2688]{1,0:T(8,128)(2,1)} %get-tuple-element.92), channel_id=1, source_target_pairs={{0,2},{1,3},{2,0},{3,1},{4,6},{5,7},{6,4},{7,5},{8,10},{9,11},{10,... | collective-permute-start | bytes 516104 | tf_op jit(solution)/shard_map/core/ppermute | solution.py:486
  13.3 8.6 %collective-permute-start.2 = (bf16[32,2688]{1,0:T(8,128)(2,1)}, bf16[32,2688]{1,0:T(8,128)(2,1)S(1)}, u32[]{:S(2)}, u32[]{:S(2)}) collective-permute-start(bf16[32,2688]{1,0:T(8,128)(2,1)} %get-tuple-element.93), channel_id=1, source_target_pairs={{0,3},{1,2},{2,1},{3,0},{4,7},{5,6},{6,5},{7,4},{8,11},{9,10},{10,... | collective-permute-start | bytes 516104 | tf_op jit(solution)/shard_map/core/ppermute | solution.py:486
  28.0 9.3 %collective-permute-start.4 = (bf16[128,1152]{1,0:T(8,128)(2,1)S(1)}, bf16[128,1152]{1,0:T(8,128)(2,1)S(1)}, u32[]{:S(2)}, u32[]{:S(2)}) collective-permute-start(bf16[128,1152]{1,0:T(8,128)(2,1)S(1)} %pad_maximum_fusion.rest_0_), channel_id=1, source_target_pairs={{0,8},{4,12},{8,0},{12,4},{16,24},{20,28},{24,16},{28,20},{1,9},{5... | collective-permute-start | bytes 884744 | tf_op jit(solution)/shard_map/tokens/ppermute | solution.py:486
  29.9 15.4 %collective-permute-start.5 = (bf16[128,1152]{1,0:T(8,128)(2,1)S(1)}, bf16[128,1152]{1,0:T(8,128)(2,1)}, u32[]{:S(2)}, u32[]{:S(2)}) collective-permute-start(bf16[128,1152]{1,0:T(8,128)(2,1)S(1)} %pad_maximum_fusion.rest_0_), channel_id=1, source_target_pairs={{0,24},{4,28},{8,16},{12,20},{16,8},{20,12},{24,0},{28,4},{1,25},{... | collective-permute-start | bytes 884744 | tf_op jit(solution)/shard_map/tokens/ppermute | solution.py:486
  32.4 12.9 %collective-permute-start.6 = (bf16[128,1152]{1,0:T(8,128)(2,1)S(1)}, bf16[128,1152]{1,0:T(8,128)(2,1)S(1)}, u32[]{:S(2)}, u32[]{:S(2)}) collective-permute-start(bf16[128,1152]{1,0:T(8,128)(2,1)S(1)} %pad_maximum_fusion.rest_0_), channel_id=1, source_target_pairs={{0,4},{4,0},{8,12},{12,8},{16,20},{20,16},{24,28},{28,24},{1,5},{5... | collective-permute-start | bytes 884744 | tf_op jit(solution)/shard_map/tokens/ppermute | solution.py:486
  45.3 7.7 %collective-permute-start.13 = (bf16[128,1152]{1,0:T(8,128)(2,1)}, bf16[128,1152]{1,0:T(8,128)(2,1)}, u32[]{:S(2)}, u32[]{:S(2)}) collective-permute-start(bf16[128,1152]{1,0:T(8,128)(2,1)} %collective-permute-done.5.rest_0_), channel_id=1, source_target_pairs={{0,4},{4,0},{8,12},{12,8},{16,20},{20,16},{24,28},{28,24},{1,5},{5... | collective-permute-start | bytes 884744 | tf_op jit(solution)/shard_map/tokens/ppermute | solution.py:486
  46.8 20.3 %collective-permute-start.15 = (bf16[1,2160,128]{2,1,0:T(8,128)(2,1)}, bf16[1,2160,128]{2,1,0:T(8,128)(2,1)}, u32[]{:S(2)}, u32[]{:S(2)}) collective-permute-start(bf16[1,2160,128]{2,1,0:T(8,128)(2,1)} %get-tuple-element.124), channel_id=1, source_target_pairs={{0,2},{1,3},{2,0},{3,1},{4,6},{5,7},{6,4},{7,5},{8,10},{9,11},{10,... | collective-permute-start | bytes 1658888 | tf_op jit(solution)/shard_map/send_states/ppermute | solution.py:486
  48.3 20.3 %collective-permute-start.12 = (bf16[128,1152]{1,0:T(8,128)(2,1)}, bf16[128,1152]{1,0:T(8,128)(2,1)}, u32[]{:S(2)}, u32[]{:S(2)}) collective-permute-start(bf16[128,1152]{1,0:T(8,128)(2,1)} %collective-permute-done.5.rest_0_), channel_id=1, source_target_pairs={{0,1},{1,0},{2,3},{3,2},{4,5},{5,4},{6,7},{7,6},{8,9},{9,8},{10,11... | collective-permute-start | bytes 884744 | tf_op jit(solution)/shard_map/experts/ppermute | solution.py:486
  53.0 15.8 %collective-permute-start.14 = (bf16[128,1152]{1,0:T(8,128)(2,1)}, bf16[128,1152]{1,0:T(8,128)(2,1)}, u32[]{:S(2)}, u32[]{:S(2)}) collective-permute-start(bf16[128,1152]{1,0:T(8,128)(2,1)} %collective-permute-done.13.rest_2_), channel_id=1, source_target_pairs={{0,1},{1,0},{2,3},{3,2},{4,5},{5,4},{6,7},{7,6},{8,9},{9,8},{10,11... | collective-permute-start | bytes 884744 | tf_op jit(solution)/shard_map/experts/ppermute | solution.py:486
  53.8 13.2 %collective-permute-start.7 = (bf16[64,1152]{1,0:T(8,128)(2,1)}, bf16[64,1152]{1,0:T(8,128)(2,1)}, u32[]{:S(2)}, u32[]{:S(2)}) collective-permute-start(bf16[64,1152]{1,0:T(8,128)(2,1)} %get-tuple-element.171), channel_id=1, source_target_pairs={{0,16},{4,20},{8,24},{12,28},{16,0},{20,4},{24,8},{28,12},{1,17},{... | collective-permute-start | bytes 442376 | tf_op jit(solution)/shard_map/tokens/ppermute | solution.py:486
  54.9 18.4 %collective-permute-start.10 = (bf16[64,1152]{1,0:T(8,128)(2,1)}, bf16[64,1152]{1,0:T(8,128)(2,1)S(1)}, u32[]{:S(2)}, u32[]{:S(2)}) collective-permute-start(bf16[64,1152]{1,0:T(8,128)(2,1)} %get-tuple-element.170), channel_id=1, source_target_pairs={{0,16},{4,20},{8,24},{12,28},{16,0},{20,4},{24,8},{28,12},{1,17},{... | collective-permute-start | bytes 442376 | tf_op jit(solution)/shard_map/tokens/ppermute | solution.py:486
  67.0 7.4 %collective-permute-start.9 = (bf16[128,1152]{1,0:T(8,128)(2,1)}, bf16[128,1152]{1,0:T(8,128)(2,1)S(1)}, u32[]{:S(2)}, u32[]{:S(2)}) collective-permute-start(bf16[128,1152]{1,0:T(8,128)(2,1)} %copy-done.8), channel_id=1, source_target_pairs={{0,1},{1,0},{2,3},{3,2},{4,5},{5,4},{6,7},{7,6},{8,9},{9,8},{10,11... | collective-permute-start | bytes 884744 | tf_op jit(solution)/shard_map/experts/ppermute | solution.py:486
  67.0 10.2 %collective-permute-start.11 = (bf16[128,1152]{1,0:T(8,128)(2,1)}, bf16[128,1152]{1,0:T(8,128)(2,1)S(1)}, u32[]{:S(2)}, u32[]{:S(2)}) collective-permute-start(bf16[128,1152]{1,0:T(8,128)(2,1)} %copy-done.6), channel_id=1, source_target_pairs={{0,4},{4,0},{8,12},{12,8},{16,20},{20,16},{24,28},{28,24},{1,5},{5... | collective-permute-start | bytes 884744 | tf_op jit(solution)/shard_map/tokens/ppermute | solution.py:486
  68.6 6.4 %collective-permute-start.8 = (bf16[128,1152]{1,0:T(8,128)(2,1)S(1)}, bf16[128,1152]{1,0:T(8,128)(2,1)S(1)}, u32[]{:S(2)}, u32[]{:S(2)}) collective-permute-start(bf16[128,1152]{1,0:T(8,128)(2,1)S(1)} %pad_maximum_fusion.rest_0_), channel_id=1, source_target_pairs={{0,1},{1,0},{2,3},{3,2},{4,5},{5,4},{6,7},{7,6},{8,9},{9,8},{10,11... | collective-permute-start | bytes 884744 | tf_op jit(solution)/shard_map/experts/ppermute | solution.py:486
  68.8 15.0 %collective-permute-start.20 = (bf16[1,2160,128]{2,1,0:T(8,128)(2,1)}, bf16[1,2160,128]{2,1,0:T(8,128)(2,1)S(1)}, u32[]{:S(2)}, u32[]{:S(2)}) collective-permute-start(bf16[1,2160,128]{2,1,0:T(8,128)(2,1)} %copy-done.21), channel_id=1, source_target_pairs={{0,2},{1,3},{2,0},{3,1},{4,6},{5,7},{6,4},{7,5},{8,10},{9,11},{10,... | collective-permute-start | bytes 1658888 | tf_op jit(solution)/shard_map/send_states/ppermute | solution.py:486
  73.4 13.1 %collective-permute-start.19 = (bf16[2,2,32,2048]{3,2,1,0:T(8,128)(2,1)S(1)}, bf16[2,2,32,2048]{3,2,1,0:T(8,128)(2,1)S(1)}, u32[]{:S(2)}, u32[]{:S(2)}) collective-permute-start(bf16[2,2,32,2048]{3,2,1,0:T(8,128)(2,1)S(1)} %get-tuple-element.132), channel_id=1, source_target_pairs={{0,1},{1,0},{2,3},{3,2},{4,5},{5,4},{6,7},{7,6},{8,9},{9,8},{10,11... | collective-permute-start | bytes 1572872 | tf_op jit(solution)/shard_map/way_back/ppermute | solution.py:486
  74.4 9.3 %collective-permute-start.17 = (bf16[128,1152]{1,0:T(8,128)(2,1)S(1)}, bf16[128,1152]{1,0:T(8,128)(2,1)S(1)}, u32[]{:S(2)}, u32[]{:S(2)}) collective-permute-start(bf16[128,1152]{1,0:T(8,128)(2,1)S(1)} %copy-done.7), channel_id=1, source_target_pairs={{0,1},{1,0},{2,3},{3,2},{4,5},{5,4},{6,7},{7,6},{8,9},{9,8},{10,11... | collective-permute-start | bytes 884744 | tf_op jit(solution)/shard_map/experts/ppermute | solution.py:486
  77.3 6.5 %collective-permute-start.18 = (bf16[128,1152]{1,0:T(8,128)(2,1)S(1)}, bf16[128,1152]{1,0:T(8,128)(2,1)S(1)}, u32[]{:S(2)}, u32[]{:S(2)}) collective-permute-start(bf16[128,1152]{1,0:T(8,128)(2,1)S(1)} %collective-permute-done.11.rest_2_), channel_id=1, source_target_pairs={{0,1},{1,0},{2,3},{3,2},{4,5},{5,4},{6,7},{7,6},{8,9},{9,8},{10,11... | collective-permute-start | bytes 884744 | tf_op jit(solution)/shard_map/experts/ppermute | solution.py:486
  77.4 9.4 %collective-permute-start.16 = (bf16[128,1152]{1,0:T(8,128)(2,1)S(1)}, bf16[128,1152]{1,0:T(8,128)(2,1)S(1)}, u32[]{:S(2)}, u32[]{:S(2)}) collective-permute-start(bf16[128,1152]{1,0:T(8,128)(2,1)S(1)} %pad_maximum_fusion.1.rest_0_), channel_id=1, source_target_pairs={{0,4},{4,0},{8,12},{12,8},{16,20},{20,16},{24,28},{28,24},{1,5},{5... | collective-permute-start | bytes 884744 | tf_op jit(solution)/shard_map/tokens/ppermute | solution.py:486
  86.8 40.9 %collective-permute-start.32 = (bf16[2,2160,128]{2,1,0:T(8,128)(2,1)S(1)}, bf16[2,2160,128]{2,1,0:T(8,128)(2,1)S(1)}, u32[]{:S(2)}, u32[]{:S(2)}) collective-permute-start(bf16[2,2160,128]{2,1,0:T(8,128)(2,1)S(1)} %copy-done.16), channel_id=1, source_target_pairs={{0,1},{1,0},{2,3},{3,2},{4,5},{5,4},{6,7},{7,6},{8,9},{9,8},{10,11... | collective-permute-start | bytes 3317768 | tf_op jit(solution)/shard_map/send_states/ppermute | solution.py:486
  87.3 44.0 %collective-permute-start.35 = (bf16[1,2160,128]{2,1,0:T(8,128)(2,1)S(1)}, bf16[1,2160,128]{2,1,0:T(8,128)(2,1)S(1)}, u32[]{:S(2)}, u32[]{:S(2)}) collective-permute-start(bf16[1,2160,128]{2,1,0:T(8,128)(2,1)S(1)} %copy-done.20), channel_id=1, source_target_pairs={{0,3},{1,2},{2,1},{3,0},{4,7},{5,6},{6,5},{7,4},{8,11},{9,10},{10,... | collective-permute-start | bytes 1658888 | tf_op jit(solution)/shard_map/send_states/ppermute | solution.py:486
  90.8 10.5 %collective-permute-start.25 = (bf16[2,2,32,2048]{3,2,1,0:T(8,128)(2,1)S(1)}, bf16[2,2,32,2048]{3,2,1,0:T(8,128)(2,1)S(1)}, u32[]{:S(2)}, u32[]{:S(2)}) collective-permute-start(bf16[2,2,32,2048]{3,2,1,0:T(8,128)(2,1)S(1)} %get-tuple-element.141), channel_id=1, source_target_pairs={{0,1},{1,0},{2,3},{3,2},{4,5},{5,4},{6,7},{7,6},{8,9},{9,8},{10,11... | collective-permute-start | bytes 1572872 | tf_op jit(solution)/shard_map/way_back/ppermute | solution.py:486
  91.0 9.2 %collective-permute-start.30 = (bf16[2,32,2048]{2,1,0:T(8,128)(2,1)S(1)}, bf16[2,32,2048]{2,1,0:T(8,128)(2,1)S(1)}, u32[]{:S(2)}, u32[]{:S(2)}) collective-permute-start(bf16[2,32,2048]{2,1,0:T(8,128)(2,1)S(1)} %fusion), channel_id=1, source_target_pairs={{0,4},{4,0},{8,12},{12,8},{16,20},{20,16},{24,28},{28,24},{1,5},{5... | collective-permute-start | bytes 786440 | tf_op jit(solution)/shard_map/way_back/ppermute | solution.py:486
  92.2 39.0 %collective-permute-start.22 = (bf16[2,32,2048]{2,1,0:T(8,128)(2,1)S(1)}, bf16[2,32,2048]{2,1,0:T(8,128)(2,1)S(1)}, u32[]{:S(2)}, u32[]{:S(2)}) collective-permute-start(bf16[2,32,2048]{2,1,0:T(8,128)(2,1)S(1)} %fusion.8), channel_id=1, source_target_pairs={{0,4},{4,0},{8,12},{12,8},{16,20},{20,16},{24,28},{28,24},{1,5},{5... | collective-permute-start | bytes 786440 | tf_op jit(solution)/shard_map/way_back/ppermute | solution.py:486
  100.2 10.8 %collective-permute-start.26 = (bf16[2,32,2048]{2,1,0:T(8,128)(2,1)S(1)}, bf16[2,32,2048]{2,1,0:T(8,128)(2,1)S(1)}, u32[]{:S(2)}, u32[]{:S(2)}) collective-permute-start(bf16[2,32,2048]{2,1,0:T(8,128)(2,1)S(1)} %fusion.10), channel_id=1, source_target_pairs={{0,4},{4,0},{8,12},{12,8},{16,20},{20,16},{24,28},{28,24},{1,5},{5... | collective-permute-start | bytes 786440 | tf_op jit(solution)/shard_map/way_back/ppermute | solution.py:486
  101.3 37.6 %collective-permute-start.31 = (bf16[2,32,2048]{2,1,0:T(8,128)(2,1)S(1)}, bf16[2,32,2048]{2,1,0:T(8,128)(2,1)S(1)}, u32[]{:S(2)}, u32[]{:S(2)}) collective-permute-start(bf16[2,32,2048]{2,1,0:T(8,128)(2,1)S(1)} %fusion.2), channel_id=1, source_target_pairs={{0,8},{4,12},{8,0},{12,4},{16,24},{20,28},{24,16},{28,20},{1,9},{5... | collective-permute-start | bytes 786440 | tf_op jit(solution)/shard_map/way_back/ppermute | solution.py:486
  111.0 7.9 %collective-permute-start.27 = (bf16[2,32,2048]{2,1,0:T(8,128)(2,1)S(1)}, bf16[2,32,2048]{2,1,0:T(8,128)(2,1)S(1)}, u32[]{:S(2)}, u32[]{:S(2)}) collective-permute-start(bf16[2,32,2048]{2,1,0:T(8,128)(2,1)S(1)} %fusion.5), channel_id=1, source_target_pairs={{0,4},{4,0},{8,12},{12,8},{16,20},{20,16},{24,28},{28,24},{1,5},{5... | collective-permute-start | bytes 786440 | tf_op jit(solution)/shard_map/way_back/ppermute | solution.py:486
  118.9 8.9 %collective-permute-start.28 = (bf16[2,32,2048]{2,1,0:T(8,128)(2,1)S(1)}, bf16[2,32,2048]{2,1,0:T(8,128)(2,1)S(1)}, u32[]{:S(2)}, u32[]{:S(2)}) collective-permute-start(bf16[2,32,2048]{2,1,0:T(8,128)(2,1)S(1)} %fusion.4), channel_id=1, source_target_pairs={{0,24},{4,28},{8,16},{12,20},{16,8},{20,12},{24,0},{28,4},{1,25},{... | collective-permute-start | bytes 786440 | tf_op jit(solution)/shard_map/way_back/ppermute | solution.py:486
  127.7 13.9 %collective-permute-start.33 = (bf16[2,32,2048]{2,1,0:T(8,128)(2,1)S(1)}, bf16[2,32,2048]{2,1,0:T(8,128)(2,1)S(1)}, u32[]{:S(2)}, u32[]{:S(2)}) collective-permute-start(bf16[2,32,2048]{2,1,0:T(8,128)(2,1)S(1)} %fusion.7), channel_id=1, source_target_pairs={{0,16},{4,20},{8,24},{12,28},{16,0},{20,4},{24,8},{28,12},{1,17},{... | collective-permute-start | bytes 786440 | tf_op jit(solution)/shard_map/way_back/ppermute | solution.py:486
  131.3 12.6 %collective-permute-start.36 = (bf16[1,2160,128]{2,1,0:T(8,128)(2,1)S(1)}, bf16[1,2160,128]{2,1,0:T(8,128)(2,1)S(1)}, u32[]{:S(2)}, u32[]{:S(2)}) collective-permute-start(bf16[1,2160,128]{2,1,0:T(8,128)(2,1)S(1)} %copy-done.18), channel_id=1, source_target_pairs={{0,3},{1,2},{2,1},{3,0},{4,7},{5,6},{6,5},{7,4},{8,11},{9,10},{10,... | collective-permute-start | bytes 1658888 | tf_op jit(solution)/shard_map/send_states/ppermute | solution.py:486
  141.7 6.9 %collective-permute-start.34 = (bf16[32,2048]{1,0:T(8,128)(2,1)S(1)}, bf16[32,2048]{1,0:T(8,128)(2,1)S(1)}, u32[]{:S(2)}, u32[]{:S(2)}) collective-permute-start(bf16[32,2048]{1,0:T(8,128)(2,1)S(1)} %fusion.13), channel_id=1, source_target_pairs={{0,2},{1,3},{2,0},{3,1},{4,6},{5,7},{6,4},{7,5},{8,10},{9,11},{10,... | collective-permute-start | bytes 393224 | tf_op jit(solution)/shard_map/mixed/ppermute | solution.py:486
  (28 other events, 523.3 us)

commit v9 on v6

--- a/solution.py
+++ b/solution.py
@@ -287,7 +287,7 @@
 
 
 def state_kernel(
-    key_heads, heads, steps, count, place_ref, *rest
+    key_heads, heads, steps, count, *rest
 ):
     arrived = rest[:count]
     out_ref, k_s, v_s, a_s, b_s, m_s, u_s, c_s, held, pay_s, ready, in_sem, pay_sem, out_sem = rest[-14:]
@@ -309,6 +309,7 @@
             )
         )
         copies[-1].start()
+    places = []
     for r in range(requests):
         pays[r].wait()
         rows = slice(r * steps, (r + 1) * steps)
@@ -320,6 +321,7 @@
         at = (key_heads + heads) * steps
         a_s[rows, :] = jax.nn.sigmoid(pay[at : at + steps])
         b_s[rows, :] = jax.nn.sigmoid(pay[at + steps : at + 2 * steps])
+        places.append(jnp.max(pay[at + 2 * steps : at + 3 * steps]).astype(jnp.int32))
     for r in range(requests):
         copies[r].wait()
         rows = slice(r * steps, (r + 1) * steps)
@@ -354,7 +356,7 @@
             )
             kept = held[r, h * hd : (h + 1) * hd, :].astype(F32) * c_s[h, r : r + 1, :]
             ready[slot, h * hd : (h + 1) * hd, :] = (kept + added).astype(BF16)
-        sent.append(pltpu.make_async_copy(ready.at[slot], out_ref.at[place_ref[r]], out_sem.at[slot]))
+        sent.append(pltpu.make_async_copy(ready.at[slot], out_ref.at[places[r]], out_sem.at[slot]))
         sent[-1].start()
     for c in sent[-2:]:
         c.wait()
@@ -362,18 +364,16 @@
 
 def landed_states(arrived, before, total, key_heads, heads, steps):
     _, all_rows, hd = arrived[0].shape
-    place_row = heads * hd + (key_heads + heads + 2) * steps
-    place = jnp.concatenate([a[:, place_row, 0] for a in arrived]).astype(jnp.int32)
-    requests = place.shape[0]
+    requests = sum(a.shape[0] for a in arrived)
     tokens = requests * steps
     state_rows = heads * hd
     hbm = pl.BlockSpec(memory_space=pl.ANY)
     out = pl.pallas_call(
         functools.partial(state_kernel, key_heads, heads, steps, len(arrived)),
-        in_specs=[pl.BlockSpec(memory_space=pltpu.SMEM)] + [hbm] * (len(arrived) + len(before)),
+        in_specs=[hbm] * (len(arrived) + len(before)),
         out_specs=hbm,
         out_shape=jax.ShapeDtypeStruct((total, state_rows, hd), BF16),
-        input_output_aliases={len(arrived) + 1: 0} if before else {},
+        input_output_aliases={len(arrived): 0} if before else {},
         scratch_shapes=[
             pltpu.VMEM((key_heads, tokens, hd), F32),
             pltpu.VMEM((heads, tokens, hd), F32),
@@ -392,7 +392,7 @@
         compiler_params=pltpu.CompilerParams(vmem_limit_bytes=32 * MIB),
         cost_estimate=pl.CostEstimate(flops=20_000_000, bytes_accessed=requests * MIB, transcendentals=10_000),
         name="landed_states",
-    )(place, *arrived, *before)
+    )(*arrived, *before)
     return out
 
 
@@ -556,12 +556,18 @@
             if d == far:
                 near[d], pieces[chunks[-2]][2] = tie((near[d], pieces[chunks[-2]][2]))
                 aside = swap(near[d], "dp", 1)
-            pieces[d] = [near[d], swap(near[d], "ep", 1), aside, swap(aside, "ep", 1)]
+                last_across = aside
+            else:
+                pieces[d] = [near[d], swap(near[d], "ep", 1), aside, swap(aside, "ep", 1)]
         pieces[0], pieces[chunks[1]][2] = tie((pieces[0], pieces[chunks[1]][2]))
         pieces[0], far_states[0] = tie((pieces[0], far_states[0]))
-        pieces[far], far_states[1] = tie((pieces[far], far_states[1]))
-    sums = {}
+    sums, keeps, parts = {}, {}, {}
     for d in chunks:
+        if d == far:
+            with jax.named_scope("tokens"):
+                beside, keeps = tie((last_across, keeps))
+                pieces[d] = [near[d], swap(near[d], "ep", 1), last_across, swap(beside, "ep", 1)]
+                pieces[d], far_states[1] = tie((pieces[d], far_states[1]))
         with jax.named_scope("experts"):
             outs = expert_chunk(where, pieces[d], gain, gate_up, down_weight, tokens, experts, d == 0)
             keep_near, keep_across, give = outs[:3]
@@ -570,12 +576,12 @@
         with jax.named_scope("way_back"):
             taken = swap(give, "ep", 1)
             aside = summed(keep_across, taken[1]).astype(BF16)
-            if d == far:
-                aside, sums[0], sums[chunks[1]] = tie((aside, sums[0], sums[chunks[1]]))
-            back = swap(aside, "dp", 1)
-            if d == far:
-                back, far_states[2] = tie((back, far_states[2]))
-            chunk = summed(keep_near, taken[0], back)
+            parts[d] = (taken, swap(aside, "dp", 1))
+            keeps[d] = keep_near
+    for d in chunks:
+        with jax.named_scope("way_back"):
+            taken, back = parts[d]
+            chunk = summed(keeps[d], taken[0], back)
             sums[d] = chunk.astype(BF16) if d else chunk
     with jax.named_scope("landed"):
         sizes = (requests, kw // hd, heads, steps)

time: 131 us -> 125 us (0.954)
  local copies, waits for them, and re-layouts: 4.49 us -> 1.62 us
  waiting for transfers between devices: 54.9 us -> 57.7 us
  other arithmetic: 3.69 us -> 0.93 us
  starting transfers between devices: 30.6 us -> 28.1 us
    slice x5 -> x0, local copies, waits for them, and re-layouts: 2.88 us -> none  [landed_states(): a[:, place_row, 0]]
    convert_element_type x2 -> x0, other arithmetic: 2.76 us -> none  [landed_states(): jnp.concatenate([a[:, place_row, 0] for a in arrived]).astype(jnp.int32)]
    ppermute x36, waiting for transfers between devices: 54.9 us -> 57.7 us  [swap(): return lax.ppermute(x, axis, [(i, i ^ d) for i in range(size)])]
    ppermute x36, starting transfers between devices: 30.6 us -> 28.1 us  [swap(): return lax.ppermute(x, axis, [(i, i ^ d) for i in range(size)])]
  transfers between devices with their start and end apart: 36 -> 36, of which waited for: 13 -> 16; matrix products, arithmetic and copies ran while one was open for 5% -> 1% of each run, Pallas kernels for 20% -> 20%
where the time goes in v9:
time: 125 us
  waiting for transfers between devices  57.7 us (46%)
  Pallas kernels  35.3 us (28%)
  starting transfers between devices  28.1 us (22%)
  local copies, waits for them, and re-layouts  1.62 us (1%)
    ppermute x36, waiting for transfers between devices, swap(): return lax.ppermute(x, axis, [(i, i ^ d) for i in range(size)])  57.7 us
    ppermute x36, starting transfers between devices, swap(): return lax.ppermute(x, axis, [(i, i ^ d) for i in range(size)])  28.1 us
    pallas_call x4, Pallas kernels, expert_chunk(): pl.pallas_call(functools.partial(expert_kernel, sides, own_out, experts),...  11.1 us
    pallas_call x2, Pallas kernels, landed_states(): pl.pallas_call(functools.partial(state_kernel, key_heads, heads, steps, l...  10.7 us
    pallas_call x1, Pallas kernels, core_rows(): pl.pallas_call(functools.partial(core_kernel, lanes, experts), in_specs=[...  9.51 us
    pallas_call x1, Pallas kernels, pack_states(): pl.pallas_call(functools.partial(pack_kernel, lanes, key_heads), in_specs...  3.48 us
  transfers between devices with their start and end apart: 36, of which 16 were waited for; matrix products, arithmetic and copies ran while one was open for 1% of the time, Pallas kernels for 20%

profile of v9, /device:TPU:0, one launch (start us, length us, event | category | flops | bytes accessed | tf_op | source)
XLA Modules:
  0.0 124.7 jit_solution(15943579554217260457)
XLA Ops:
  0.7 9.5 %core_rows.1 = (bf16[32,2688]{1,0:T(8,128)(2,1)}, bf16[32,2688]{1,0:T(8,128)(2,1)}, bf16[32,2688]{1,0:T(8,128)(2,1)}, bf16[32,2688]{1,0:T(8,128)(2,1)}) custom-call(s32[1]{0:T(128)} %bitcast.lane_ref, bf16[8,2048,128]{2,1,0:T(8,128)(2,1)} %bitcast.60, bf16[8,4,1024]{2,1,0:T(4,128)(2,1)} %q_ref.1, bf16[8,4,1024]{2,1,0:T(4,128)(2,1)} %k_ref.3, ...), custom_call_target="tpu_custom_call" | custom-call | flops 20000000 | bytes 9437184 | tf_op jit(solution)/shard_map/core/core_rows/pallas_call | solution.py:155
  10.7 2.6 %collective-permute-start.1 = (bf16[32,2688]{1,0:T(8,128)(2,1)}, bf16[32,2688]{1,0:T(8,128)(2,1)S(1)}, u32[]{:S(2)}, u32[]{:S(2)}) collective-permute-start(bf16[32,2688]{1,0:T(8,128)(2,1)} %get-tuple-element.94), channel_id=1, source_target_pairs={{0,2},{1,3},{2,0},{3,1},{4,6},{5,7},{6,4},{7,5},{8,10},{9,11},{10,... | collective-permute-start | bytes 516104 | tf_op jit(solution)/shard_map/core/ppermute | solution.py:486
  13.4 3.5 %pack_states.1 = (bf16[2,2160,128]{2,1,0:T(8,128)(2,1)S(1)}, bf16[2,2160,128]{2,1,0:T(8,128)(2,1)S(1)}, bf16[1,2160,128]{2,1,0:T(8,128)(2,1)}, bf16[1,2160,128]{...) custom-call(s32[8]{0:T(128)S(1)} %copy-done.10, s32[1]{0:T(128)} %bitcast.lane_ref, ...), custom_call_target="tpu_custom_call" | custom-call | bytes 9437184 | tf_op jit(solution)/shard_map/send_states/pack_states/pallas_call | solution.py:240
  18.7 3.2 %collective-permute-done.2.refs_3_ = bf16[32,2688]{1,0:T(8,128)(2,1)S(1)} collective-permute-done((bf16[32,2688]{1,0:T(8,128)(2,1)}, bf16[32,2688]{1,0:T(8,128)(2,1)S(1)}, u32[]{:S(2)}, u32[]{:S(2)}) %collective-permute-start.2) | collective-permute-done | bytes 172064 | tf_op jit(solution)/shard_map/core/ppermute | solution.py:486
  22.4 1.6 %collective-permute-start.3 = (bf16[128,512]{1,0:T(8,128)(2,1)S(1)}, bf16[128,512]{1,0:T(8,128)(2,1)S(1)}, u32[]{:S(2)}, u32[]{:S(2)}) collective-permute-start(bf16[128,512]{1,0:T(8,128)(2,1)S(1)} %get-tuple-element.107), channel_id=1, source_target_pairs={{0,2},{1,3},{2,0},{3,1},{4,6},{5,7},{6,4},{7,5},{8,10},{9,11},{10,... | collective-permute-start | bytes 393224 | tf_op jit(solution)/shard_map/attention/ppermute | solution.py:486
  24.0 3.9 %collective-permute-done.3 = bf16[128,512]{1,0:T(8,128)(2,1)S(1)} collective-permute-done((bf16[128,512]{1,0:T(8,128)(2,1)S(1)}, bf16[128,512]{1,0:T(8,128)(2,1)S(1)}, u32[]{:S(2)}, u32[]{:S(2)}) %collective-permute-start.3) | collective-permute-done | bytes 131104 | tf_op jit(solution)/shard_map/attention/ppermute | solution.py:486
  28.0 1.8 %collective-permute-start.9 = (bf16[1,2160,128]{2,1,0:T(8,128)(2,1)}, bf16[1,2160,128]{2,1,0:T(8,128)(2,1)}, u32[]{:S(2)}, u32[]{:S(2)}) collective-permute-start(bf16[1,2160,128]{2,1,0:T(8,128)(2,1)} %get-tuple-element.122), channel_id=1, source_target_pairs={{0,2},{1,3},{2,0},{3,1},{4,6},{5,7},{6,4},{7,5},{8,10},{9,11},{10,... | collective-permute-start | bytes 1658888 | tf_op jit(solution)/shard_map/send_states/ppermute | solution.py:486
  29.8 1.5 %collective-permute-start.5 = (bf16[128,1152]{1,0:T(8,128)(2,1)S(1)}, bf16[128,1152]{1,0:T(8,128)(2,1)}, u32[]{:S(2)}, u32[]{:S(2)}) collective-permute-start(bf16[128,1152]{1,0:T(8,128)(2,1)S(1)} %pad_maximum_fusion.rest_0_), channel_id=1, source_target_pairs={{0,4},{4,0},{8,12},{12,8},{16,20},{20,16},{24,28},{28,24},{1,5},{5... | collective-permute-start | bytes 884744 | tf_op jit(solution)/shard_map/tokens/ppermute | solution.py:486
  31.3 3.6 %collective-permute-start.7 = (bf16[128,1152]{1,0:T(8,128)(2,1)S(1)}, bf16[128,1152]{1,0:T(8,128)(2,1)}, u32[]{:S(2)}, u32[]{:S(2)}) collective-permute-start(bf16[128,1152]{1,0:T(8,128)(2,1)S(1)} %pad_maximum_fusion.rest_0_), channel_id=1, source_target_pairs={{0,24},{4,28},{8,16},{12,20},{16,8},{20,12},{24,0},{28,4},{1,25},{... | collective-permute-start | bytes 884744 | tf_op jit(solution)/shard_map/tokens/ppermute | solution.py:486
  34.9 3.1 %collective-permute-done.5.rest_2_ = bf16[128,1152]{1,0:T(8,128)(2,1)} collective-permute-done((bf16[128,1152]{1,0:T(8,128)(2,1)S(1)}, bf16[128,1152]{1,0:T(8,128)(2,1)}, u32[]{:S(2)}, u32[]{:S(2)}) %collective-permute-start.5) | collective-permute-done | bytes 294944 | tf_op jit(solution)/shard_map/tokens/ppermute | solution.py:486
  38.0 5.2 %collective-permute-done.7.rest_0_ = bf16[128,1152]{1,0:T(8,128)(2,1)} collective-permute-done((bf16[128,1152]{1,0:T(8,128)(2,1)S(1)}, bf16[128,1152]{1,0:T(8,128)(2,1)}, u32[]{:S(2)}, u32[]{:S(2)}) %collective-permute-start.7) | collective-permute-done | bytes 294944 | tf_op jit(solution)/shard_map/tokens/ppermute | solution.py:486
  43.7 3.8 %collective-permute-done.11.rest_0_ = bf16[128,1152]{1,0:T(8,128)(2,1)} collective-permute-done((bf16[128,1152]{1,0:T(8,128)(2,1)S(1)}, bf16[128,1152]{1,0:T(8,128)(2,1)}, u32[]{:S(2)}, u32[]{:S(2)}) %collective-permute-start.11) | collective-permute-done | bytes 294944 | tf_op jit(solution)/shard_map/tokens/ppermute | solution.py:486
  48.1 2.2 %collective-permute-start.10 = (bf16[128,1152]{1,0:T(8,128)(2,1)S(1)}, bf16[128,1152]{1,0:T(8,128)(2,1)S(1)}, u32[]{:S(2)}, u32[]{:S(2)}) collective-permute-start(bf16[128,1152]{1,0:T(8,128)(2,1)S(1)} %pad_maximum_fusion.rest_0_), channel_id=1, source_target_pairs={{0,16},{4,20},{8,24},{12,28},{16,0},{20,4},{24,8},{28,12},{1,17},{... | collective-permute-start | bytes 884744 | tf_op jit(solution)/shard_map/tokens/ppermute | solution.py:486
  51.0 5.9 %collective-permute-done.12.rest_2_ = bf16[128,1152]{1,0:T(8,128)(2,1)} collective-permute-done((bf16[128,1152]{1,0:T(8,128)(2,1)}, bf16[128,1152]{1,0:T(8,128)(2,1)}, u32[]{:S(2)}, u32[]{:S(2)}) %collective-permute-start.12) | collective-permute-done | bytes 294944 | tf_op jit(solution)/shard_map/tokens/ppermute | solution.py:486
  56.9 3.2 %expert_chunk.4 = (bf16[2,32,2048]{2,1,0:T(8,128)(2,1)S(1)}, bf16[2,32,2048]{2,1,0:T(8,128)(2,1)S(1)}, bf16[2,2,32,2048]{3,2,1,0:T(8,128)(2,1)S(1)}, bf16[32,2048]{1,0:T(8,128)(2,1)S(1)}) custom-call(s32[2]{0:T(128)S(1)} %pad_add_fusion.where_ref, bf16[128,1152]{1,0:T(8,128)(2,1)S(1)} %pad_maximum_fusion.rest_0_, ...), custom_call_target="tpu_custom_call" | custom-call | flops 805306368 | bytes 6291456 | tf_op jit(solution)/shard_map/experts/expert_chunk/pallas_call | solution.py:468
  60.7 2.8 %collective-permute-done.10.rest_0_ = bf16[128,1152]{1,0:T(8,128)(2,1)S(1)} collective-permute-done((bf16[128,1152]{1,0:T(8,128)(2,1)S(1)}, bf16[128,1152]{1,0:T(8,128)(2,1)S(1)}, u32[]{:S(2)}, u32[]{:S(2)}) %collective-permute-start.10) | collective-permute-done | bytes 294944 | tf_op jit(solution)/shard_map/tokens/ppermute | solution.py:486
  64.0 1.3 %collective-permute-start.13 = (bf16[128,1152]{1,0:T(8,128)(2,1)S(1)}, bf16[128,1152]{1,0:T(8,128)(2,1)S(1)}, u32[]{:S(2)}, u32[]{:S(2)}) collective-permute-start(bf16[128,1152]{1,0:T(8,128)(2,1)S(1)} %collective-permute-done.10.rest_0_), channel_id=1, source_target_pairs={{0,4},{4,0},{8,12},{12,8},{16,20},{20,16},{24,28},{28,24},{1,5},{5... | collective-permute-start | bytes 884744 | tf_op jit(solution)/shard_map/tokens/ppermute | solution.py:486
  65.2 2.9 %expert_chunk.5 = (bf16[2,32,2048]{2,1,0:T(8,128)(2,1)S(1)}, bf16[2,32,2048]{2,1,0:T(8,128)(2,1)S(1)}, bf16[2,2,32,2048]{3,2,1,0:T(8,128)(2,1)S(1)}) custom-call(s32[2]{0:T(128)S(1)} %pad_add_fusion.where_ref, bf16[128,1152]{1,0:T(8,128)(2,1)} %collective-permute-done.11.rest_0_, bf16[128,1152]{1,0:T(8,128)(2,1)S(1)} %collective-permute-done.14.rest_1_, ...), custom_call_target="tpu_custom_call" | custom-call | flops 805306368 | bytes 6291456 | tf_op jit(solution)/shard_map/experts/expert_chunk/pallas_call | solution.py:468
  68.8 2.9 %expert_chunk.6 = (bf16[2,32,2048]{2,1,0:T(8,128)(2,1)S(1)}, bf16[2,32,2048]{2,1,0:T(8,128)(2,1)S(1)}, bf16[2,2,32,2048]{3,2,1,0:T(8,128)(2,1)S(1)}) custom-call(s32[2]{0:T(128)S(1)} %pad_add_fusion.where_ref, bf16[128,1152]{1,0:T(8,128)(2,1)} %collective-permute-done.7.rest_0_, bf16[128,1152]{1,0:T(8,128)(2,1)S(1)} %collective-permute-done.16.rest_1_, ...), custom_call_target="tpu_custom_call" | custom-call | flops 805306368 | bytes 6291456 | tf_op jit(solution)/shard_map/experts/expert_chunk/pallas_call | solution.py:468
  74.3 1.7 %collective-permute-done.27.rest_3_ = bf16[128,1152]{1,0:T(8,128)(2,1)S(1)} collective-permute-done((bf16[128,1152]{1,0:T(8,128)(2,1)S(1)}, bf16[128,1152]{1,0:T(8,128)(2,1)S(1)}, u32[]{:S(2)}, u32[]{:S(2)}) %collective-permute-start.27) | collective-permute-done | bytes 294944 | tf_op jit(solution)/shard_map/tokens/ppermute | solution.py:486
  76.0 1.3 %collective-permute-start.19 = (bf16[2,32,2048]{2,1,0:T(8,128)(2,1)S(1)}, bf16[2,32,2048]{2,1,0:T(8,128)(2,1)S(1)}, u32[]{:S(2)}, u32[]{:S(2)}) collective-permute-start(bf16[2,32,2048]{2,1,0:T(8,128)(2,1)S(1)} %fusion.9), channel_id=1, source_target_pairs={{0,4},{4,0},{8,12},{12,8},{16,20},{20,16},{24,28},{28,24},{1,5},{5... | collective-permute-start | bytes 786440 | tf_op jit(solution)/shard_map/way_back/ppermute | solution.py:486
  77.3 2.1 %expert_chunk.7 = (bf16[2,32,2048]{2,1,0:T(8,128)(2,1)S(1)}, bf16[2,32,2048]{2,1,0:T(8,128)(2,1)S(1)}, bf16[2,2,32,2048]{3,2,1,0:T(8,128)(2,1)S(1)}) custom-call(s32[2]{0:T(128)S(1)} %pad_add_fusion.where_ref, bf16[128,1152]{1,0:T(8,128)(2,1)S(1)} %collective-permute-done.10.rest_0_, bf16[128,1152]{1,0:T(8,128)(2,1)S(1)} %collective-permute-done.26.rest_1_, ...), custom_call_target="tpu_custom_call" | custom-call | flops 805306368 | bytes 6291456 | tf_op jit(solution)/shard_map/experts/expert_chunk/pallas_call | solution.py:468
  80.4 9.5 %collective-permute-done.21 = bf16[2,32,2048]{2,1,0:T(8,128)(2,1)S(1)} collective-permute-done((bf16[2,32,2048]{2,1,0:T(8,128)(2,1)S(1)}, bf16[2,32,2048]{2,1,0:T(8,128)(2,1)S(1)}, u32[]{:S(2)}, u32[]{:S(2)}) %collective-permute-start.21) | collective-permute-done | bytes 262176 | tf_op jit(solution)/shard_map/way_back/ppermute | solution.py:486
  90.0 1.3 %collective-permute-start.24 = (bf16[2,32,2048]{2,1,0:T(8,128)(2,1)S(1)}, bf16[2,32,2048]{2,1,0:T(8,128)(2,1)S(1)}, u32[]{:S(2)}, u32[]{:S(2)}) collective-permute-start(bf16[2,32,2048]{2,1,0:T(8,128)(2,1)S(1)} %fusion.3), channel_id=1, source_target_pairs={{0,4},{4,0},{8,12},{12,8},{16,20},{20,16},{24,28},{28,24},{1,5},{5... | collective-permute-start | bytes 786440 | tf_op jit(solution)/shard_map/way_back/ppermute | solution.py:486
  92.1 5.4 %collective-permute-done.24 = bf16[2,32,2048]{2,1,0:T(8,128)(2,1)S(1)} collective-permute-done((bf16[2,32,2048]{2,1,0:T(8,128)(2,1)S(1)}, bf16[2,32,2048]{2,1,0:T(8,128)(2,1)S(1)}, u32[]{:S(2)}, u32[]{:S(2)}) %collective-permute-start.24) | collective-permute-done | bytes 262176 | tf_op jit(solution)/shard_map/way_back/ppermute | solution.py:486
  97.5 1.3 %collective-permute-start.30 = (bf16[2,32,2048]{2,1,0:T(8,128)(2,1)S(1)}, bf16[2,32,2048]{2,1,0:T(8,128)(2,1)S(1)}, u32[]{:S(2)}, u32[]{:S(2)}) collective-permute-start(bf16[2,32,2048]{2,1,0:T(8,128)(2,1)S(1)} %fusion), channel_id=1, source_target_pairs={{0,4},{4,0},{8,12},{12,8},{16,20},{20,16},{24,28},{28,24},{1,5},{5... | collective-permute-start | bytes 786440 | tf_op jit(solution)/shard_map/way_back/ppermute | solution.py:486
  98.9 5.2 %collective-permute-done.30 = bf16[2,32,2048]{2,1,0:T(8,128)(2,1)S(1)} collective-permute-done((bf16[2,32,2048]{2,1,0:T(8,128)(2,1)S(1)}, bf16[2,32,2048]{2,1,0:T(8,128)(2,1)S(1)}, u32[]{:S(2)}, u32[]{:S(2)}) %collective-permute-start.30) | collective-permute-done | bytes 262176 | tf_op jit(solution)/shard_map/way_back/ppermute | solution.py:486
  104.1 2.2 %collective-permute-start.25 = (bf16[2,32,2048]{2,1,0:T(8,128)(2,1)S(1)}, bf16[2,32,2048]{2,1,0:T(8,128)(2,1)S(1)}, u32[]{:S(2)}, u32[]{:S(2)}) collective-permute-start(bf16[2,32,2048]{2,1,0:T(8,128)(2,1)S(1)} %fusion.5), channel_id=1, source_target_pairs={{0,8},{4,12},{8,0},{12,4},{16,24},{20,28},{24,16},{28,20},{1,9},{5... | collective-permute-start | bytes 786440 | tf_op jit(solution)/shard_map/way_back/ppermute | solution.py:486
  106.7 7.5 %landed_states.2.rest_2_ = bf16[8,2048,128]{2,1,0:T(8,128)(2,1)} custom-call(bf16[2,2160,128]{2,1,0:T(8,128)(2,1)S(1)} %copy-done.4, bf16[2,2160,128]{2,1,0:T(8,128)(2,1)S(1)} %collective-permute-done.31.rest_1_, bf16[1,2160,128]{2,1,0:T(8,128)(2,1)} %collective-permute-done.9.rest_2_, bf16[1,2160,128]{2,1,0:T(8,128)(2,1)S(1)} %collective-permute-done.28.rest_3_), custom_call_target="tpu_custom_call" | custom-call | flops 20000000 | bytes 6291456 | tf_op jit(solution)/shard_map/landed/landed_states/pallas_call | solution.py:371
  114.5 3.9 %collective-permute-done.32 = bf16[2,32,2048]{2,1,0:T(8,128)(2,1)S(1)} collective-permute-done((bf16[2,32,2048]{2,1,0:T(8,128)(2,1)S(1)}, bf16[2,32,2048]{2,1,0:T(8,128)(2,1)S(1)}, u32[]{:S(2)}, u32[]{:S(2)}) %collective-permute-start.32) | collective-permute-done | bytes 262176 | tf_op jit(solution)/shard_map/way_back/ppermute | solution.py:486
  119.1 1.5 %collective-permute-done.35.rest_1_ = bf16[1,2160,128]{2,1,0:T(8,128)(2,1)S(1)} collective-permute-done((bf16[1,2160,128]{2,1,0:T(8,128)(2,1)S(1)}, bf16[1,2160,128]{2,1,0:T(8,128)(2,1)S(1)}, u32[]{:S(2)}, u32[]{:S(2)}) %collective-permute-start.35) | collective-permute-done | bytes 552992 | tf_op jit(solution)/shard_map/send_states/ppermute | solution.py:486
  120.6 3.2 %landed_states.3 = bf16[8,2048,128]{2,1,0:T(8,128)(2,1)} custom-call(bf16[1,2160,128]{2,1,0:T(8,128)(2,1)S(1)} %collective-permute-done.34.rest_0_, bf16[1,2160,128]{2,1,0:T(8,128)(2,1)S(1)} %collective-permute-done.35.rest_1_, bf16[8,2048,128]{2,1,0:T(8,128)(2,1)} %landed_states.2.rest_2_), custom_call_target="tpu_custom_call", output_to_operand_aliasing={{}: (2, {})} | custom-call | flops 20000000 | bytes 2097152 | tf_op jit(solution)/shard_map/landed/landed_states/pallas_call | solution.py:371
  (102 shorter events, 13.0 us)
Async XLA Ops:
  10.2 7.5 %collective-permute-start = (bf16[32,2688]{1,0:T(8,128)(2,1)}, bf16[32,2688]{1,0:T(8,128)(2,1)S(1)}, u32[]{:S(2)}, u32[]{:S(2)}) collective-permute-start(bf16[32,2688]{1,0:T(8,128)(2,1)} %get-tuple-element.93), channel_id=1, source_target_pairs={{0,1},{1,0},{2,3},{3,2},{4,5},{5,4},{6,7},{7,6},{8,9},{9,8},{10,11... | collective-permute-start | bytes 516104 | tf_op jit(solution)/shard_map/core/ppermute | solution.py:486
  10.7 8.0 %collective-permute-start.1 = (bf16[32,2688]{1,0:T(8,128)(2,1)}, bf16[32,2688]{1,0:T(8,128)(2,1)S(1)}, u32[]{:S(2)}, u32[]{:S(2)}) collective-permute-start(bf16[32,2688]{1,0:T(8,128)(2,1)} %get-tuple-element.94), channel_id=1, source_target_pairs={{0,2},{1,3},{2,0},{3,1},{4,6},{5,7},{6,4},{7,5},{8,10},{9,11},{10,... | collective-permute-start | bytes 516104 | tf_op jit(solution)/shard_map/core/ppermute | solution.py:486
  13.3 8.6 %collective-permute-start.2 = (bf16[32,2688]{1,0:T(8,128)(2,1)}, bf16[32,2688]{1,0:T(8,128)(2,1)S(1)}, u32[]{:S(2)}, u32[]{:S(2)}) collective-permute-start(bf16[32,2688]{1,0:T(8,128)(2,1)} %get-tuple-element.95), channel_id=1, source_target_pairs={{0,3},{1,2},{2,1},{3,0},{4,7},{5,6},{6,5},{7,4},{8,11},{9,10},{10,... | collective-permute-start | bytes 516104 | tf_op jit(solution)/shard_map/core/ppermute | solution.py:486
  22.4 5.6 %collective-permute-start.3 = (bf16[128,512]{1,0:T(8,128)(2,1)S(1)}, bf16[128,512]{1,0:T(8,128)(2,1)S(1)}, u32[]{:S(2)}, u32[]{:S(2)}) collective-permute-start(bf16[128,512]{1,0:T(8,128)(2,1)S(1)} %get-tuple-element.107), channel_id=1, source_target_pairs={{0,2},{1,3},{2,0},{3,1},{4,6},{5,7},{6,4},{7,5},{8,10},{9,11},{10,... | collective-permute-start | bytes 393224 | tf_op jit(solution)/shard_map/attention/ppermute | solution.py:486
  28.0 22.3 %collective-permute-start.9 = (bf16[1,2160,128]{2,1,0:T(8,128)(2,1)}, bf16[1,2160,128]{2,1,0:T(8,128)(2,1)}, u32[]{:S(2)}, u32[]{:S(2)}) collective-permute-start(bf16[1,2160,128]{2,1,0:T(8,128)(2,1)} %get-tuple-element.122), channel_id=1, source_target_pairs={{0,2},{1,3},{2,0},{3,1},{4,6},{5,7},{6,4},{7,5},{8,10},{9,11},{10,... | collective-permute-start | bytes 1658888 | tf_op jit(solution)/shard_map/send_states/ppermute | solution.py:486
  29.8 8.2 %collective-permute-start.5 = (bf16[128,1152]{1,0:T(8,128)(2,1)S(1)}, bf16[128,1152]{1,0:T(8,128)(2,1)}, u32[]{:S(2)}, u32[]{:S(2)}) collective-permute-start(bf16[128,1152]{1,0:T(8,128)(2,1)S(1)} %pad_maximum_fusion.rest_0_), channel_id=1, source_target_pairs={{0,4},{4,0},{8,12},{12,8},{16,20},{20,16},{24,28},{28,24},{1,5},{5... | collective-permute-start | bytes 884744 | tf_op jit(solution)/shard_map/tokens/ppermute | solution.py:486
  31.3 11.9 %collective-permute-start.7 = (bf16[128,1152]{1,0:T(8,128)(2,1)S(1)}, bf16[128,1152]{1,0:T(8,128)(2,1)}, u32[]{:S(2)}, u32[]{:S(2)}) collective-permute-start(bf16[128,1152]{1,0:T(8,128)(2,1)S(1)} %pad_maximum_fusion.rest_0_), channel_id=1, source_target_pairs={{0,24},{4,28},{8,16},{12,20},{16,8},{20,12},{24,0},{28,4},{1,25},{... | collective-permute-start | bytes 884744 | tf_op jit(solution)/shard_map/tokens/ppermute | solution.py:486
  34.9 12.6 %collective-permute-start.11 = (bf16[128,1152]{1,0:T(8,128)(2,1)S(1)}, bf16[128,1152]{1,0:T(8,128)(2,1)}, u32[]{:S(2)}, u32[]{:S(2)}) collective-permute-start(bf16[128,1152]{1,0:T(8,128)(2,1)S(1)} %pad_maximum_fusion.rest_0_), channel_id=1, source_target_pairs={{0,8},{4,12},{8,0},{12,4},{16,24},{20,28},{24,16},{28,20},{1,9},{5... | collective-permute-start | bytes 884744 | tf_op jit(solution)/shard_map/tokens/ppermute | solution.py:486
  34.9 13.2 %collective-permute-start.4 = (bf16[128,1152]{1,0:T(8,128)(2,1)S(1)}, bf16[128,1152]{1,0:T(8,128)(2,1)}, u32[]{:S(2)}, u32[]{:S(2)}) collective-permute-start(bf16[128,1152]{1,0:T(8,128)(2,1)S(1)} %pad_maximum_fusion.rest_0_), channel_id=1, source_target_pairs={{0,1},{1,0},{2,3},{3,2},{4,5},{5,4},{6,7},{7,6},{8,9},{9,8},{10,11... | collective-permute-start | bytes 884744 | tf_op jit(solution)/shard_map/tokens/ppermute | solution.py:486
  38.0 12.4 %collective-permute-start.6 = (bf16[128,1152]{1,0:T(8,128)(2,1)}, bf16[128,1152]{1,0:T(8,128)(2,1)}, u32[]{:S(2)}, u32[]{:S(2)}) collective-permute-start(bf16[128,1152]{1,0:T(8,128)(2,1)} %collective-permute-done.5.rest_2_), channel_id=1, source_target_pairs={{0,1},{1,0},{2,3},{3,2},{4,5},{5,4},{6,7},{7,6},{8,9},{9,8},{10,11... | collective-permute-start | bytes 884744 | tf_op jit(solution)/shard_map/tokens/ppermute | solution.py:486
  43.2 7.8 %collective-permute-start.8 = (bf16[128,1152]{1,0:T(8,128)(2,1)}, bf16[128,1152]{1,0:T(8,128)(2,1)}, u32[]{:S(2)}, u32[]{:S(2)}) collective-permute-start(bf16[128,1152]{1,0:T(8,128)(2,1)} %collective-permute-done.7.rest_0_), channel_id=1, source_target_pairs={{0,4},{4,0},{8,12},{12,8},{16,20},{20,16},{24,28},{28,24},{1,5},{5... | collective-permute-start | bytes 884744 | tf_op jit(solution)/shard_map/tokens/ppermute | solution.py:486
  47.5 9.3 %collective-permute-start.12 = (bf16[128,1152]{1,0:T(8,128)(2,1)}, bf16[128,1152]{1,0:T(8,128)(2,1)}, u32[]{:S(2)}, u32[]{:S(2)}) collective-permute-start(bf16[128,1152]{1,0:T(8,128)(2,1)} %collective-permute-done.11.rest_0_), channel_id=1, source_target_pairs={{0,4},{4,0},{8,12},{12,8},{16,20},{20,16},{24,28},{28,24},{1,5},{5... | collective-permute-start | bytes 884744 | tf_op jit(solution)/shard_map/tokens/ppermute | solution.py:486
  48.1 15.3 %collective-permute-start.10 = (bf16[128,1152]{1,0:T(8,128)(2,1)S(1)}, bf16[128,1152]{1,0:T(8,128)(2,1)S(1)}, u32[]{:S(2)}, u32[]{:S(2)}) collective-permute-start(bf16[128,1152]{1,0:T(8,128)(2,1)S(1)} %pad_maximum_fusion.rest_0_), channel_id=1, source_target_pairs={{0,16},{4,20},{8,24},{12,28},{16,0},{20,4},{24,8},{28,12},{1,17},{... | collective-permute-start | bytes 884744 | tf_op jit(solution)/shard_map/tokens/ppermute | solution.py:486
  50.3 13.1 %collective-permute-start.14 = (bf16[128,1152]{1,0:T(8,128)(2,1)}, bf16[128,1152]{1,0:T(8,128)(2,1)S(1)}, u32[]{:S(2)}, u32[]{:S(2)}) collective-permute-start(bf16[128,1152]{1,0:T(8,128)(2,1)} %collective-permute-done.11.rest_0_), channel_id=1, source_target_pairs={{0,1},{1,0},{2,3},{3,2},{4,5},{5,4},{6,7},{7,6},{8,9},{9,8},{10,11... | collective-permute-start | bytes 884744 | tf_op jit(solution)/shard_map/tokens/ppermute | solution.py:486
  50.4 22.5 %collective-permute-start.28 = (bf16[1,2160,128]{2,1,0:T(8,128)(2,1)}, bf16[1,2160,128]{2,1,0:T(8,128)(2,1)S(1)}, u32[]{:S(2)}, u32[]{:S(2)}) collective-permute-start(bf16[1,2160,128]{2,1,0:T(8,128)(2,1)} %copy-done.17), channel_id=1, source_target_pairs={{0,2},{1,3},{2,0},{3,1},{4,6},{5,7},{6,4},{7,5},{8,10},{9,11},{10,... | collective-permute-start | bytes 1658888 | tf_op jit(solution)/shard_map/send_states/ppermute | solution.py:486
  56.9 7.1 %collective-permute-start.15 = (bf16[128,1152]{1,0:T(8,128)(2,1)}, bf16[128,1152]{1,0:T(8,128)(2,1)S(1)}, u32[]{:S(2)}, u32[]{:S(2)}) collective-permute-start(bf16[128,1152]{1,0:T(8,128)(2,1)} %collective-permute-done.12.rest_2_), channel_id=1, source_target_pairs={{0,1},{1,0},{2,3},{3,2},{4,5},{5,4},{6,7},{7,6},{8,9},{9,8},{10,11... | collective-permute-start | bytes 884744 | tf_op jit(solution)/shard_map/tokens/ppermute | solution.py:486
  60.1 13.3 %collective-permute-start.18 = (bf16[2,2,32,2048]{3,2,1,0:T(8,128)(2,1)S(1)}, bf16[2,2,32,2048]{3,2,1,0:T(8,128)(2,1)S(1)}, u32[]{:S(2)}, u32[]{:S(2)}) collective-permute-start(bf16[2,2,32,2048]{3,2,1,0:T(8,128)(2,1)S(1)} %get-tuple-element.137), channel_id=1, source_target_pairs={{0,1},{1,0},{2,3},{3,2},{4,5},{5,4},{6,7},{7,6},{8,9},{9,8},{10,11... | collective-permute-start | bytes 1572872 | tf_op jit(solution)/shard_map/way_back/ppermute | solution.py:486
  64.0 9.0 %collective-permute-start.13 = (bf16[128,1152]{1,0:T(8,128)(2,1)S(1)}, bf16[128,1152]{1,0:T(8,128)(2,1)S(1)}, u32[]{:S(2)}, u32[]{:S(2)}) collective-permute-start(bf16[128,1152]{1,0:T(8,128)(2,1)S(1)} %collective-permute-done.10.rest_0_), channel_id=1, source_target_pairs={{0,4},{4,0},{8,12},{12,8},{16,20},{20,16},{24,28},{28,24},{1,5},{5... | collective-permute-start | bytes 884744 | tf_op jit(solution)/shard_map/tokens/ppermute | solution.py:486
  68.2 38.2 %collective-permute-start.31 = (bf16[2,2160,128]{2,1,0:T(8,128)(2,1)S(1)}, bf16[2,2160,128]{2,1,0:T(8,128)(2,1)S(1)}, u32[]{:S(2)}, u32[]{:S(2)}) collective-permute-start(bf16[2,2160,128]{2,1,0:T(8,128)(2,1)S(1)} %copy-done.12), channel_id=1, source_target_pairs={{0,1},{1,0},{2,3},{3,2},{4,5},{5,4},{6,7},{7,6},{8,9},{9,8},{10,11... | collective-permute-start | bytes 3317768 | tf_op jit(solution)/shard_map/send_states/ppermute | solution.py:486
  72.9 6.5 %collective-permute-start.20 = (bf16[2,2,32,2048]{3,2,1,0:T(8,128)(2,1)S(1)}, bf16[2,2,32,2048]{3,2,1,0:T(8,128)(2,1)S(1)}, u32[]{:S(2)}, u32[]{:S(2)}) collective-permute-start(bf16[2,2,32,2048]{3,2,1,0:T(8,128)(2,1)S(1)} %get-tuple-element.140), channel_id=1, source_target_pairs={{0,1},{1,0},{2,3},{3,2},{4,5},{5,4},{6,7},{7,6},{8,9},{9,8},{10,11... | collective-permute-start | bytes 1572872 | tf_op jit(solution)/shard_map/way_back/ppermute | solution.py:486
  72.9 6.6 %collective-permute-start.23 = (bf16[2,2,32,2048]{3,2,1,0:T(8,128)(2,1)S(1)}, bf16[2,2,32,2048]{3,2,1,0:T(8,128)(2,1)S(1)}, u32[]{:S(2)}, u32[]{:S(2)}) collective-permute-start(bf16[2,2,32,2048]{3,2,1,0:T(8,128)(2,1)S(1)} %get-tuple-element.143), channel_id=1, source_target_pairs={{0,1},{1,0},{2,3},{3,2},{4,5},{5,4},{6,7},{7,6},{8,9},{9,8},{10,11... | collective-permute-start | bytes 1572872 | tf_op jit(solution)/shard_map/way_back/ppermute | solution.py:486
  73.6 33.0 %collective-permute-start.34 = (bf16[1,2160,128]{2,1,0:T(8,128)(2,1)S(1)}, bf16[1,2160,128]{2,1,0:T(8,128)(2,1)S(1)}, u32[]{:S(2)}, u32[]{:S(2)}) collective-permute-start(bf16[1,2160,128]{2,1,0:T(8,128)(2,1)S(1)} %copy-done.16), channel_id=1, source_target_pairs={{0,3},{1,2},{2,1},{3,0},{4,7},{5,6},{6,5},{7,4},{8,11},{9,10},{10,... | collective-permute-start | bytes 1658888 | tf_op jit(solution)/shard_map/send_states/ppermute | solution.py:486
  76.0 30.4 %collective-permute-start.19 = (bf16[2,32,2048]{2,1,0:T(8,128)(2,1)S(1)}, bf16[2,32,2048]{2,1,0:T(8,128)(2,1)S(1)}, u32[]{:S(2)}, u32[]{:S(2)}) collective-permute-start(bf16[2,32,2048]{2,1,0:T(8,128)(2,1)S(1)} %fusion.9), channel_id=1, source_target_pairs={{0,4},{4,0},{8,12},{12,8},{16,20},{20,16},{24,28},{28,24},{1,5},{5... | collective-permute-start | bytes 786440 | tf_op jit(solution)/shard_map/way_back/ppermute | solution.py:486
  79.4 12.0 %collective-permute-start.29 = (bf16[2,2,32,2048]{3,2,1,0:T(8,128)(2,1)S(1)}, bf16[2,2,32,2048]{3,2,1,0:T(8,128)(2,1)S(1)}, u32[]{:S(2)}, u32[]{:S(2)}) collective-permute-start(bf16[2,2,32,2048]{3,2,1,0:T(8,128)(2,1)S(1)} %get-tuple-element.154), channel_id=1, source_target_pairs={{0,1},{1,0},{2,3},{3,2},{4,5},{5,4},{6,7},{7,6},{8,9},{9,8},{10,11... | collective-permute-start | bytes 1572872 | tf_op jit(solution)/shard_map/way_back/ppermute | solution.py:486
  79.6 10.4 %collective-permute-start.21 = (bf16[2,32,2048]{2,1,0:T(8,128)(2,1)S(1)}, bf16[2,32,2048]{2,1,0:T(8,128)(2,1)S(1)}, u32[]{:S(2)}, u32[]{:S(2)}) collective-permute-start(bf16[2,32,2048]{2,1,0:T(8,128)(2,1)S(1)} %fusion.6), channel_id=1, source_target_pairs={{0,4},{4,0},{8,12},{12,8},{16,20},{20,16},{24,28},{28,24},{1,5},{5... | collective-permute-start | bytes 786440 | tf_op jit(solution)/shard_map/way_back/ppermute | solution.py:486
  90.0 7.5 %collective-permute-start.24 = (bf16[2,32,2048]{2,1,0:T(8,128)(2,1)S(1)}, bf16[2,32,2048]{2,1,0:T(8,128)(2,1)S(1)}, u32[]{:S(2)}, u32[]{:S(2)}) collective-permute-start(bf16[2,32,2048]{2,1,0:T(8,128)(2,1)S(1)} %fusion.3), channel_id=1, source_target_pairs={{0,4},{4,0},{8,12},{12,8},{16,20},{20,16},{24,28},{28,24},{1,5},{5... | collective-permute-start | bytes 786440 | tf_op jit(solution)/shard_map/way_back/ppermute | solution.py:486
  91.4 22.8 %collective-permute-start.22 = (bf16[2,32,2048]{2,1,0:T(8,128)(2,1)S(1)}, bf16[2,32,2048]{2,1,0:T(8,128)(2,1)S(1)}, u32[]{:S(2)}, u32[]{:S(2)}) collective-permute-start(bf16[2,32,2048]{2,1,0:T(8,128)(2,1)S(1)} %fusion.8), channel_id=1, source_target_pairs={{0,24},{4,28},{8,16},{12,20},{16,8},{20,12},{24,0},{28,4},{1,25},{... | collective-permute-start | bytes 786440 | tf_op jit(solution)/shard_map/way_back/ppermute | solution.py:486
  97.5 6.6 %collective-permute-start.30 = (bf16[2,32,2048]{2,1,0:T(8,128)(2,1)S(1)}, bf16[2,32,2048]{2,1,0:T(8,128)(2,1)S(1)}, u32[]{:S(2)}, u32[]{:S(2)}) collective-permute-start(bf16[2,32,2048]{2,1,0:T(8,128)(2,1)S(1)} %fusion), channel_id=1, source_target_pairs={{0,4},{4,0},{8,12},{12,8},{16,20},{20,16},{24,28},{28,24},{1,5},{5... | collective-permute-start | bytes 786440 | tf_op jit(solution)/shard_map/way_back/ppermute | solution.py:486
  104.1 10.4 %collective-permute-start.25 = (bf16[2,32,2048]{2,1,0:T(8,128)(2,1)S(1)}, bf16[2,32,2048]{2,1,0:T(8,128)(2,1)S(1)}, u32[]{:S(2)}, u32[]{:S(2)}) collective-permute-start(bf16[2,32,2048]{2,1,0:T(8,128)(2,1)S(1)} %fusion.5), channel_id=1, source_target_pairs={{0,8},{4,12},{8,0},{12,4},{16,24},{20,28},{24,16},{28,20},{1,9},{5... | collective-permute-start | bytes 786440 | tf_op jit(solution)/shard_map/way_back/ppermute | solution.py:486
  106.4 12.0 %collective-permute-start.32 = (bf16[2,32,2048]{2,1,0:T(8,128)(2,1)S(1)}, bf16[2,32,2048]{2,1,0:T(8,128)(2,1)S(1)}, u32[]{:S(2)}, u32[]{:S(2)}) collective-permute-start(bf16[2,32,2048]{2,1,0:T(8,128)(2,1)S(1)} %fusion.2), channel_id=1, source_target_pairs={{0,16},{4,20},{8,24},{12,28},{16,0},{20,4},{24,8},{28,12},{1,17},{... | collective-permute-start | bytes 786440 | tf_op jit(solution)/shard_map/way_back/ppermute | solution.py:486
  106.6 14.0 %collective-permute-start.35 = (bf16[1,2160,128]{2,1,0:T(8,128)(2,1)S(1)}, bf16[1,2160,128]{2,1,0:T(8,128)(2,1)S(1)}, u32[]{:S(2)}, u32[]{:S(2)}) collective-permute-start(bf16[1,2160,128]{2,1,0:T(8,128)(2,1)S(1)} %copy-done.14), channel_id=1, source_target_pairs={{0,3},{1,2},{2,1},{3,0},{4,7},{5,6},{6,5},{7,4},{8,11},{9,10},{10,... | collective-permute-start | bytes 1658888 | tf_op jit(solution)/shard_map/send_states/ppermute | solution.py:486
  118.5 5.4 %collective-permute-start.33 = (bf16[32,2048]{1,0:T(8,128)(2,1)S(1)}, bf16[32,2048]{1,0:T(8,128)(2,1)S(1)}, u32[]{:S(2)}, u32[]{:S(2)}) collective-permute-start(bf16[32,2048]{1,0:T(8,128)(2,1)S(1)} %fusion.13), channel_id=1, source_target_pairs={{0,2},{1,3},{2,0},{3,1},{4,6},{5,7},{6,4},{7,5},{8,10},{9,11},{10,... | collective-permute-start | bytes 393224 | tf_op jit(solution)/shard_map/mixed/ppermute | solution.py:486
  (23 other events, 375.8 us)

commit v10 on v9

--- a/solution.py
+++ b/solution.py
@@ -533,6 +533,9 @@
     with jax.named_scope("send_states"):
         cap = requests // lanes
         near_states = [packed[0], swap(packed[1], "ep", 1)]
+        first_across = swap(held, "dp", 1)
+        packed = list(packed)
+        packed[2], first_across = lax.optimization_barrier((packed[2], first_across))
         far_states = []
         for i, piece in enumerate(packed[2:]):
             if i:
@@ -548,7 +551,7 @@
     with jax.named_scope("tokens"):
         near = {d: swap(held, "dp", d) if d else held for d in chunks[:-1]}
         later, near[chunks[1]] = tie((held, near[chunks[1]]))
-        across = {d: swap(near[d], "dp", 1) for d in chunks[:-1]}
+        across = {d: swap(near[d], "dp", 1) if d else first_across for d in chunks[:-1]}
         near[far] = swap(later, "dp", far)
         pieces = {}
         for d in chunks:
@@ -561,13 +564,15 @@
                 pieces[d] = [near[d], swap(near[d], "ep", 1), aside, swap(aside, "ep", 1)]
         pieces[0], pieces[chunks[1]][2] = tie((pieces[0], pieces[chunks[1]][2]))
         pieces[0], far_states[0] = tie((pieces[0], far_states[0]))
-    sums, keeps, parts = {}, {}, {}
+    sums, keeps, parts, asides = {}, {}, {}, {}
     for d in chunks:
         if d == far:
             with jax.named_scope("tokens"):
                 beside, keeps = tie((last_across, keeps))
                 pieces[d] = [near[d], swap(near[d], "ep", 1), last_across, swap(beside, "ep", 1)]
-                pieces[d], far_states[1] = tie((pieces[d], far_states[1]))
+                pieces[d], far_states[1], asides[chunks[1]] = tie(
+                    (pieces[d], far_states[1], asides[chunks[1]])
+                )
         with jax.named_scope("experts"):
             outs = expert_chunk(where, pieces[d], gain, gate_up, down_weight, tokens, experts, d == 0)
             keep_near, keep_across, give = outs[:3]
@@ -576,16 +581,21 @@
         with jax.named_scope("way_back"):
             taken = swap(give, "ep", 1)
             aside = summed(keep_across, taken[1]).astype(BF16)
-            parts[d] = (taken, swap(aside, "dp", 1))
+            parts[d], asides[d] = taken, aside
             keeps[d] = keep_near
-    for d in chunks:
+    for d in [far, chunks[1], 0] + chunks[2:-1]:
         with jax.named_scope("way_back"):
-            taken, back = parts[d]
-            chunk = summed(keeps[d], taken[0], back)
+            back = swap(asides[d], "dp", 1)
+            if d == far:
+                others = {p: asides[p] for p in chunks if p not in (far, chunks[1])}
+                others, back = tie((others, back))
+                asides.update(others)
+            chunk = summed(keeps[d], parts[d][0], back)
             sums[d] = chunk.astype(BF16) if d else chunk
     with jax.named_scope("landed"):
         sizes = (requests, kw // hd, heads, steps)
         sums[far], arrived = tie((sums[far], near_states + far_states[:-2]))
+        sums[chunks[-2]], arrived = tie((sums[chunks[-2]], arrived))
         moved_out = landed_states(arrived, [], *sizes)
     with jax.named_scope("way_back"):
         sums = [swap(sums[d], "dp", d) if d else sums[d] for d in chunks]

time: 125 us -> 127 us (1.016)
  starting transfers between devices: 28.1 us -> 35.9 us
  waiting for transfers between devices: 57.7 us -> 51.2 us
    ppermute x36, starting transfers between devices: 28.1 us -> 35.9 us  [swap(): return lax.ppermute(x, axis, [(i, i ^ d) for i in range(size)])]
    ppermute x36, waiting for transfers between devices: 57.7 us -> 51.2 us  [swap(): return lax.ppermute(x, axis, [(i, i ^ d) for i in range(size)])]
  transfers between devices with their start and end apart: 36 -> 36, of which waited for: 16 -> 13; matrix products, arithmetic and copies ran while one was open for 1% -> 1% of each run, Pallas kernels for 20% -> 20%
where the time goes in v10:
time: 127 us; the launch traced here: 126 us
  waiting for transfers between devices  51.2 us (40%)
  starting transfers between devices  35.9 us (28%)
  Pallas kernels  35 us (28%)
  local copies, waits for them, and re-layouts  2.33 us (2%)
    ppermute x36, waiting for transfers between devices, swap(): return lax.ppermute(x, axis, [(i, i ^ d) for i in range(size)])  51.2 us
    ppermute x36, starting transfers between devices, swap(): return lax.ppermute(x, axis, [(i, i ^ d) for i in range(size)])  35.9 us
    pallas_call x4, Pallas kernels, expert_chunk(): pl.pallas_call(functools.partial(expert_kernel, sides, own_out, experts),...  11.2 us
    pallas_call x2, Pallas kernels, landed_states(): pl.pallas_call(functools.partial(state_kernel, key_heads, heads, steps, l...  10.7 us
    pallas_call x1, Pallas kernels, core_rows(): pl.pallas_call(functools.partial(core_kernel, lanes, experts), in_specs=[...  9.51 us
    pallas_call x1, Pallas kernels, pack_states(): pl.pallas_call(functools.partial(pack_kernel, lanes, key_heads), in_specs...  3.18 us
  transfers between devices with their start and end apart: 36, of which 13 were waited for; matrix products, arithmetic and copies ran while one was open for 1% of the time, Pallas kernels for 20%

profile of v10, /device:TPU:0, one launch (start us, length us, event | category | flops | bytes accessed | tf_op | source)
XLA Modules:
  0.0 126.4 jit_solution(8736223349299768776)
XLA Ops:
  0.7 9.5 %core_rows.1 = (bf16[32,2688]{1,0:T(8,128)(2,1)}, bf16[32,2688]{1,0:T(8,128)(2,1)}, bf16[32,2688]{1,0:T(8,128)(2,1)}, bf16[32,2688]{1,0:T(8,128)(2,1)}) custom-call(s32[1]{0:T(128)} %bitcast.lane_ref, bf16[8,2048,128]{2,1,0:T(8,128)(2,1)} %bitcast.60, bf16[8,4,1024]{2,1,0:T(4,128)(2,1)} %q_ref.1, bf16[8,4,1024]{2,1,0:T(4,128)(2,1)} %k_ref.3, ...), custom_call_target="tpu_custom_call" | custom-call | flops 20000000 | bytes 9437184 | tf_op jit(solution)/shard_map/core/core_rows/pallas_call | solution.py:155
  10.7 2.6 %collective-permute-start.1 = (bf16[32,2688]{1,0:T(8,128)(2,1)}, bf16[32,2688]{1,0:T(8,128)(2,1)S(1)}, u32[]{:S(2)}, u32[]{:S(2)}) collective-permute-start(bf16[32,2688]{1,0:T(8,128)(2,1)} %get-tuple-element.105), channel_id=1, source_target_pairs={{0,2},{1,3},{2,0},{3,1},{4,6},{5,7},{6,4},{7,5},{8,10},{9,11},{10,... | collective-permute-start | bytes 516104 | tf_op jit(solution)/shard_map/core/ppermute | solution.py:486
  13.4 3.2 %pack_states.1 = (bf16[2,2160,128]{2,1,0:T(8,128)(2,1)S(1)}, bf16[2,2160,128]{2,1,0:T(8,128)(2,1)S(1)}, bf16[1,2160,128]{2,1,0:T(8,128)(2,1)}, bf16[1,2160,128]{...) custom-call(s32[8]{0:T(128)S(1)} %copy-done.12, s32[1]{0:T(128)} %bitcast.lane_ref, ...), custom_call_target="tpu_custom_call" | custom-call | bytes 9437184 | tf_op jit(solution)/shard_map/send_states/pack_states/pallas_call | solution.py:240
  17.5 1.3 %collective-permute-done.1.refs_2_ = bf16[32,2688]{1,0:T(8,128)(2,1)S(1)} collective-permute-done((bf16[32,2688]{1,0:T(8,128)(2,1)}, bf16[32,2688]{1,0:T(8,128)(2,1)S(1)}, u32[]{:S(2)}, u32[]{:S(2)}) %collective-permute-start.1) | collective-permute-done | bytes 172064 | tf_op jit(solution)/shard_map/core/ppermute | solution.py:486
  18.7 3.2 %collective-permute-done.2.refs_3_ = bf16[32,2688]{1,0:T(8,128)(2,1)S(1)} collective-permute-done((bf16[32,2688]{1,0:T(8,128)(2,1)}, bf16[32,2688]{1,0:T(8,128)(2,1)S(1)}, u32[]{:S(2)}, u32[]{:S(2)}) %collective-permute-start.2) | collective-permute-done | bytes 172064 | tf_op jit(solution)/shard_map/core/ppermute | solution.py:486
  22.4 1.6 %collective-permute-start.3 = (bf16[128,512]{1,0:T(8,128)(2,1)S(1)}, bf16[128,512]{1,0:T(8,128)(2,1)S(1)}, u32[]{:S(2)}, u32[]{:S(2)}) collective-permute-start(bf16[128,512]{1,0:T(8,128)(2,1)S(1)} %get-tuple-element.118), channel_id=1, source_target_pairs={{0,2},{1,3},{2,0},{3,1},{4,6},{5,7},{6,4},{7,5},{8,10},{9,11},{10,... | collective-permute-start | bytes 393224 | tf_op jit(solution)/shard_map/attention/ppermute | solution.py:486
  24.0 4.0 %collective-permute-done.3 = bf16[128,512]{1,0:T(8,128)(2,1)S(1)} collective-permute-done((bf16[128,512]{1,0:T(8,128)(2,1)S(1)}, bf16[128,512]{1,0:T(8,128)(2,1)S(1)}, u32[]{:S(2)}, u32[]{:S(2)}) %collective-permute-start.3) | collective-permute-done | bytes 131104 | tf_op jit(solution)/shard_map/attention/ppermute | solution.py:486
  28.0 3.9 %collective-permute-start.7 = (bf16[128,1152]{1,0:T(8,128)(2,1)S(1)}, bf16[128,1152]{1,0:T(8,128)(2,1)}, u32[]{:S(2)}, u32[]{:S(2)}) collective-permute-start(bf16[128,1152]{1,0:T(8,128)(2,1)S(1)} %pad_maximum_fusion.rest_0_), channel_id=1, source_target_pairs={{0,24},{4,28},{8,16},{12,20},{16,8},{20,12},{24,0},{28,4},{1,25},{... | collective-permute-start | bytes 884744 | tf_op jit(solution)/shard_map/tokens/ppermute | solution.py:486
  31.9 1.5 %collective-permute-start.5 = (bf16[128,1152]{1,0:T(8,128)(2,1)S(1)}, bf16[128,1152]{1,0:T(8,128)(2,1)}, u32[]{:S(2)}, u32[]{:S(2)}) collective-permute-start(bf16[128,1152]{1,0:T(8,128)(2,1)S(1)} %pad_maximum_fusion.rest_0_), channel_id=1, source_target_pairs={{0,4},{4,0},{8,12},{12,8},{16,20},{20,16},{24,28},{28,24},{1,5},{5... | collective-permute-start | bytes 884744 | tf_op jit(solution)/shard_map/send_states/ppermute | solution.py:486
  33.4 5.3 %collective-permute-done.7.rest_0_ = bf16[128,1152]{1,0:T(8,128)(2,1)} collective-permute-done((bf16[128,1152]{1,0:T(8,128)(2,1)S(1)}, bf16[128,1152]{1,0:T(8,128)(2,1)}, u32[]{:S(2)}, u32[]{:S(2)}) %collective-permute-start.7) | collective-permute-done | bytes 294944 | tf_op jit(solution)/shard_map/tokens/ppermute | solution.py:486
  38.8 1.5 %collective-permute-start.8 = (bf16[128,1152]{1,0:T(8,128)(2,1)}, bf16[128,1152]{1,0:T(8,128)(2,1)}, u32[]{:S(2)}, u32[]{:S(2)}) collective-permute-start(bf16[128,1152]{1,0:T(8,128)(2,1)} %collective-permute-done.7.rest_0_), channel_id=1, source_target_pairs={{0,4},{4,0},{8,12},{12,8},{16,20},{20,16},{24,28},{28,24},{1,5},{5... | collective-permute-start | bytes 884744 | tf_op jit(solution)/shard_map/tokens/ppermute | solution.py:486
  40.3 1.5 %collective-permute-start.9 = (bf16[1,2160,128]{2,1,0:T(8,128)(2,1)}, bf16[1,2160,128]{2,1,0:T(8,128)(2,1)}, u32[]{:S(2)}, u32[]{:S(2)}) collective-permute-start(bf16[1,2160,128]{2,1,0:T(8,128)(2,1)} %get-tuple-element.135), channel_id=1, source_target_pairs={{0,2},{1,3},{2,0},{3,1},{4,6},{5,7},{6,4},{7,5},{8,10},{9,11},{10,... | collective-permute-start | bytes 1658888 | tf_op jit(solution)/shard_map/send_states/ppermute | solution.py:486
  41.8 5.9 %collective-permute-start.11 = (bf16[128,1152]{1,0:T(8,128)(2,1)S(1)}, bf16[128,1152]{1,0:T(8,128)(2,1)}, u32[]{:S(2)}, u32[]{:S(2)}) collective-permute-start(bf16[128,1152]{1,0:T(8,128)(2,1)S(1)} %pad_maximum_fusion.rest_0_), channel_id=1, source_target_pairs={{0,8},{4,12},{8,0},{12,4},{16,24},{20,28},{24,16},{28,20},{1,9},{5... | collective-permute-start | bytes 884744 | tf_op jit(solution)/shard_map/tokens/ppermute | solution.py:486
  49.0 4.4 %collective-permute-done.11.rest_0_ = bf16[128,1152]{1,0:T(8,128)(2,1)} collective-permute-done((bf16[128,1152]{1,0:T(8,128)(2,1)S(1)}, bf16[128,1152]{1,0:T(8,128)(2,1)}, u32[]{:S(2)}, u32[]{:S(2)}) %collective-permute-start.11) | collective-permute-done | bytes 294944 | tf_op jit(solution)/shard_map/tokens/ppermute | solution.py:486
  54.1 2.2 %collective-permute-start.10 = (bf16[128,1152]{1,0:T(8,128)(2,1)S(1)}, bf16[128,1152]{1,0:T(8,128)(2,1)S(1)}, u32[]{:S(2)}, u32[]{:S(2)}) collective-permute-start(bf16[128,1152]{1,0:T(8,128)(2,1)S(1)} %pad_maximum_fusion.rest_0_), channel_id=1, source_target_pairs={{0,16},{4,20},{8,24},{12,28},{16,0},{20,4},{24,8},{28,12},{1,17},{... | collective-permute-start | bytes 884744 | tf_op jit(solution)/shard_map/tokens/ppermute | solution.py:486
  56.9 3.1 %expert_chunk.6 = (bf16[2,32,2048]{2,1,0:T(8,128)(2,1)S(1)}, bf16[2,32,2048]{2,1,0:T(8,128)(2,1)S(1)}, bf16[2,2,32,2048]{3,2,1,0:T(8,128)(2,1)S(1)}) custom-call(s32[2]{0:T(128)S(1)} %pad_add_fusion.where_ref, bf16[128,1152]{1,0:T(8,128)(2,1)} %collective-permute-done.7.rest_0_, bf16[128,1152]{1,0:T(8,128)(2,1)} %collective-permute-done.16.rest_1_, ...), custom_call_target="tpu_custom_call" | custom-call | flops 805306368 | bytes 6291456 | tf_op jit(solution)/shard_map/experts/expert_chunk/pallas_call | solution.py:468
  60.6 8.3 %collective-permute-done.10.rest_0_ = bf16[128,1152]{1,0:T(8,128)(2,1)S(1)} collective-permute-done((bf16[128,1152]{1,0:T(8,128)(2,1)S(1)}, bf16[128,1152]{1,0:T(8,128)(2,1)S(1)}, u32[]{:S(2)}, u32[]{:S(2)}) %collective-permute-start.10) | collective-permute-done | bytes 294944 | tf_op jit(solution)/shard_map/tokens/ppermute | solution.py:486
  69.4 3.2 %expert_chunk.4 = (bf16[2,32,2048]{2,1,0:T(8,128)(2,1)S(1)}, bf16[2,32,2048]{2,1,0:T(8,128)(2,1)S(1)}, bf16[2,2,32,2048]{3,2,1,0:T(8,128)(2,1)S(1)}, bf16[32,2048]{1,0:T(8,128)(2,1)S(1)}) custom-call(s32[2]{0:T(128)S(1)} %pad_add_fusion.where_ref, bf16[128,1152]{1,0:T(8,128)(2,1)S(1)} %pad_maximum_fusion.rest_0_, bf16[128,1152]{1,0:T(8,128)(2,1)S(1)} %copy-done.7, ...), custom_call_target="tpu_custom_call" | custom-call | flops 805306368 | bytes 6291456 | tf_op jit(solution)/shard_map/experts/expert_chunk/pallas_call | solution.py:468
  73.2 2.8 %expert_chunk.5 = (bf16[2,32,2048]{2,1,0:T(8,128)(2,1)S(1)}, bf16[2,32,2048]{2,1,0:T(8,128)(2,1)S(1)}, bf16[2,2,32,2048]{3,2,1,0:T(8,128)(2,1)S(1)}) custom-call(s32[2]{0:T(128)S(1)} %pad_add_fusion.where_ref, bf16[128,1152]{1,0:T(8,128)(2,1)} %collective-permute-done.11.rest_0_, bf16[128,1152]{1,0:T(8,128)(2,1)S(1)} %collective-permute-done.14.rest_1_, ...), custom_call_target="tpu_custom_call" | custom-call | flops 805306368 | bytes 6291456 | tf_op jit(solution)/shard_map/experts/expert_chunk/pallas_call | solution.py:468
  76.8 2.4 %collective-permute-done.21.rest_3_ = bf16[128,1152]{1,0:T(8,128)(2,1)S(1)} collective-permute-done((bf16[128,1152]{1,0:T(8,128)(2,1)S(1)}, bf16[128,1152]{1,0:T(8,128)(2,1)S(1)}, u32[]{:S(2)}, u32[]{:S(2)}) %collective-permute-start.21) | collective-permute-done | bytes 294944 | tf_op jit(solution)/shard_map/tokens/ppermute | solution.py:486
  79.2 2.1 %expert_chunk.7 = (bf16[2,32,2048]{2,1,0:T(8,128)(2,1)S(1)}, bf16[2,32,2048]{2,1,0:T(8,128)(2,1)S(1)}, bf16[2,2,32,2048]{3,2,1,0:T(8,128)(2,1)S(1)}) custom-call(s32[2]{0:T(128)S(1)} %pad_add_fusion.where_ref, bf16[128,1152]{1,0:T(8,128)(2,1)S(1)} %collective-permute-done.10.rest_0_, bf16[128,1152]{1,0:T(8,128)(2,1)S(1)} %collective-permute-done.20.rest_1_, ...), custom_call_target="tpu_custom_call" | custom-call | flops 805306368 | bytes 6291456 | tf_op jit(solution)/shard_map/experts/expert_chunk/pallas_call | solution.py:468
  81.6 1.9 %collective-permute-start.34 = (bf16[1,2160,128]{2,1,0:T(8,128)(2,1)S(1)}, bf16[1,2160,128]{2,1,0:T(8,128)(2,1)S(1)}, u32[]{:S(2)}, u32[]{:S(2)}) collective-permute-start(bf16[1,2160,128]{2,1,0:T(8,128)(2,1)S(1)} %copy-done.18), channel_id=1, source_target_pairs={{0,3},{1,2},{2,1},{3,0},{4,7},{5,6},{6,5},{7,4},{8,11},{9,10},{10,... | collective-permute-start | bytes 1658888 | tf_op jit(solution)/shard_map/send_states/ppermute | solution.py:486
  83.5 1.1 collective-permute-start.27
  85.8 6.9 %collective-permute-done.27 = bf16[2,32,2048]{2,1,0:T(8,128)(2,1)S(1)} collective-permute-done((bf16[2,32,2048]{2,1,0:T(8,128)(2,1)S(1)}, bf16[2,32,2048]{2,1,0:T(8,128)(2,1)S(1)}, u32[]{:S(2)}, u32[]{:S(2)}) %collective-permute-start.27) | collective-permute-done | bytes 262176 | tf_op jit(solution)/shard_map/way_back/ppermute | solution.py:486
  92.8 1.9 %collective-permute-start.28 = (bf16[2,32,2048]{2,1,0:T(8,128)(2,1)S(1)}, bf16[2,32,2048]{2,1,0:T(8,128)(2,1)S(1)}, u32[]{:S(2)}, u32[]{:S(2)}) collective-permute-start(bf16[2,32,2048]{2,1,0:T(8,128)(2,1)S(1)} %fusion.5), channel_id=1, source_target_pairs={{0,24},{4,28},{8,16},{12,20},{16,8},{20,12},{24,0},{28,4},{1,25},{... | collective-permute-start | bytes 786440 | tf_op jit(solution)/shard_map/way_back/ppermute | solution.py:486
  94.6 1.6 %collective-permute-done.34.rest_0_ = bf16[1,2160,128]{2,1,0:T(8,128)(2,1)S(1)} collective-permute-done((bf16[1,2160,128]{2,1,0:T(8,128)(2,1)S(1)}, bf16[1,2160,128]{2,1,0:T(8,128)(2,1)S(1)}, u32[]{:S(2)}, u32[]{:S(2)}) %collective-permute-start.34) | collective-permute-done | bytes 552992 | tf_op jit(solution)/shard_map/send_states/ppermute | solution.py:486
  96.3 1.8 %collective-permute-start.35 = (bf16[1,2160,128]{2,1,0:T(8,128)(2,1)S(1)}, bf16[1,2160,128]{2,1,0:T(8,128)(2,1)S(1)}, u32[]{:S(2)}, u32[]{:S(2)}) collective-permute-start(bf16[1,2160,128]{2,1,0:T(8,128)(2,1)S(1)} %copy-done.16), channel_id=1, source_target_pairs={{0,3},{1,2},{2,1},{3,0},{4,7},{5,6},{6,5},{7,4},{8,11},{9,10},{10,... | collective-permute-start | bytes 1658888 | tf_op jit(solution)/shard_map/send_states/ppermute | solution.py:486
  98.9 1.2 collective-permute-start.29
  100.3 11.5 %collective-permute-done.29 = bf16[2,32,2048]{2,1,0:T(8,128)(2,1)S(1)} collective-permute-done((bf16[2,32,2048]{2,1,0:T(8,128)(2,1)S(1)}, bf16[2,32,2048]{2,1,0:T(8,128)(2,1)S(1)}, u32[]{:S(2)}, u32[]{:S(2)}) %collective-permute-start.29) | collective-permute-done | bytes 262176 | tf_op jit(solution)/shard_map/way_back/ppermute | solution.py:486
  112.1 7.5 %landed_states.2.rest_2_ = bf16[8,2048,128]{2,1,0:T(8,128)(2,1)} custom-call(bf16[2,2160,128]{2,1,0:T(8,128)(2,1)S(1)} %copy-done.4, bf16[2,2160,128]{2,1,0:T(8,128)(2,1)S(1)} %collective-permute-done.30.rest_1_, bf16[1,2160,128]{2,1,0:T(8,128)(2,1)} %collective-permute-done.9.rest_2_, bf16[1,2160,128]{2,1,0:T(8,128)(2,1)S(1)} %collective-permute-done.22.rest_3_), custom_call_target="tpu_custom_call" | custom-call | flops 20000000 | bytes 6291456 | tf_op jit(solution)/shard_map/landed/landed_states/pallas_call | solution.py:371
  121.0 3.2 %landed_states.3 = bf16[8,2048,128]{2,1,0:T(8,128)(2,1)} custom-call(bf16[1,2160,128]{2,1,0:T(8,128)(2,1)S(1)} %collective-permute-done.34.rest_0_, bf16[1,2160,128]{2,1,0:T(8,128)(2,1)S(1)} %collective-permute-done.35.rest_1_, bf16[8,2048,128]{2,1,0:T(8,128)(2,1)} %landed_states.2.rest_2_), custom_call_target="tpu_custom_call", output_to_operand_aliasing={{}: (2, {})} | custom-call | flops 20000000 | bytes 2097152 | tf_op jit(solution)/shard_map/landed/landed_states/pallas_call | solution.py:371
  124.2 1.3 %collective-permute-done.33 = bf16[32,2048]{1,0:T(8,128)(2,1)S(1)} collective-permute-done((bf16[32,2048]{1,0:T(8,128)(2,1)S(1)}, bf16[32,2048]{1,0:T(8,128)(2,1)S(1)}, u32[]{:S(2)}, u32[]{:S(2)}) %collective-permute-start.33) | collective-permute-done | bytes 131104 | tf_op jit(solution)/shard_map/mixed/ppermute | solution.py:486
  (106 shorter events, 11.8 us)
Async XLA Ops:
  10.2 7.2 %collective-permute-start = (bf16[32,2688]{1,0:T(8,128)(2,1)}, bf16[32,2688]{1,0:T(8,128)(2,1)S(1)}, u32[]{:S(2)}, u32[]{:S(2)}) collective-permute-start(bf16[32,2688]{1,0:T(8,128)(2,1)} %get-tuple-element.104), channel_id=1, source_target_pairs={{0,1},{1,0},{2,3},{3,2},{4,5},{5,4},{6,7},{7,6},{8,9},{9,8},{10,11... | collective-permute-start | bytes 516104 | tf_op jit(solution)/shard_map/core/ppermute | solution.py:486
  10.7 8.0 %collective-permute-start.1 = (bf16[32,2688]{1,0:T(8,128)(2,1)}, bf16[32,2688]{1,0:T(8,128)(2,1)S(1)}, u32[]{:S(2)}, u32[]{:S(2)}) collective-permute-start(bf16[32,2688]{1,0:T(8,128)(2,1)} %get-tuple-element.105), channel_id=1, source_target_pairs={{0,2},{1,3},{2,0},{3,1},{4,6},{5,7},{6,4},{7,5},{8,10},{9,11},{10,... | collective-permute-start | bytes 516104 | tf_op jit(solution)/shard_map/core/ppermute | solution.py:486
  13.3 8.6 %collective-permute-start.2 = (bf16[32,2688]{1,0:T(8,128)(2,1)}, bf16[32,2688]{1,0:T(8,128)(2,1)S(1)}, u32[]{:S(2)}, u32[]{:S(2)}) collective-permute-start(bf16[32,2688]{1,0:T(8,128)(2,1)} %get-tuple-element.106), channel_id=1, source_target_pairs={{0,3},{1,2},{2,1},{3,0},{4,7},{5,6},{6,5},{7,4},{8,11},{9,10},{10,... | collective-permute-start | bytes 516104 | tf_op jit(solution)/shard_map/core/ppermute | solution.py:486
  22.4 5.6 %collective-permute-start.3 = (bf16[128,512]{1,0:T(8,128)(2,1)S(1)}, bf16[128,512]{1,0:T(8,128)(2,1)S(1)}, u32[]{:S(2)}, u32[]{:S(2)}) collective-permute-start(bf16[128,512]{1,0:T(8,128)(2,1)S(1)} %get-tuple-element.118), channel_id=1, source_target_pairs={{0,2},{1,3},{2,0},{3,1},{4,6},{5,7},{6,4},{7,5},{8,10},{9,11},{10,... | collective-permute-start | bytes 393224 | tf_op jit(solution)/shard_map/attention/ppermute | solution.py:486
  28.0 10.7 %collective-permute-start.7 = (bf16[128,1152]{1,0:T(8,128)(2,1)S(1)}, bf16[128,1152]{1,0:T(8,128)(2,1)}, u32[]{:S(2)}, u32[]{:S(2)}) collective-permute-start(bf16[128,1152]{1,0:T(8,128)(2,1)S(1)} %pad_maximum_fusion.rest_0_), channel_id=1, source_target_pairs={{0,24},{4,28},{8,16},{12,20},{16,8},{20,12},{24,0},{28,4},{1,25},{... | collective-permute-start | bytes 884744 | tf_op jit(solution)/shard_map/tokens/ppermute | solution.py:486
  31.9 8.4 %collective-permute-start.5 = (bf16[128,1152]{1,0:T(8,128)(2,1)S(1)}, bf16[128,1152]{1,0:T(8,128)(2,1)}, u32[]{:S(2)}, u32[]{:S(2)}) collective-permute-start(bf16[128,1152]{1,0:T(8,128)(2,1)S(1)} %pad_maximum_fusion.rest_0_), channel_id=1, source_target_pairs={{0,4},{4,0},{8,12},{12,8},{16,20},{20,16},{24,28},{28,24},{1,5},{5... | collective-permute-start | bytes 884744 | tf_op jit(solution)/shard_map/send_states/ppermute | solution.py:486
  33.4 14.3 %collective-permute-start.4 = (bf16[128,1152]{1,0:T(8,128)(2,1)S(1)}, bf16[128,1152]{1,0:T(8,128)(2,1)S(1)}, u32[]{:S(2)}, u32[]{:S(2)}) collective-permute-start(bf16[128,1152]{1,0:T(8,128)(2,1)S(1)} %pad_maximum_fusion.rest_0_), channel_id=1, source_target_pairs={{0,1},{1,0},{2,3},{3,2},{4,5},{5,4},{6,7},{7,6},{8,9},{9,8},{10,11... | collective-permute-start | bytes 884744 | tf_op jit(solution)/shard_map/tokens/ppermute | solution.py:486
  38.8 10.2 %collective-permute-start.8 = (bf16[128,1152]{1,0:T(8,128)(2,1)}, bf16[128,1152]{1,0:T(8,128)(2,1)}, u32[]{:S(2)}, u32[]{:S(2)}) collective-permute-start(bf16[128,1152]{1,0:T(8,128)(2,1)} %collective-permute-done.7.rest_0_), channel_id=1, source_target_pairs={{0,4},{4,0},{8,12},{12,8},{16,20},{20,16},{24,28},{28,24},{1,5},{5... | collective-permute-start | bytes 884744 | tf_op jit(solution)/shard_map/tokens/ppermute | solution.py:486
  40.3 16.0 %collective-permute-start.9 = (bf16[1,2160,128]{2,1,0:T(8,128)(2,1)}, bf16[1,2160,128]{2,1,0:T(8,128)(2,1)}, u32[]{:S(2)}, u32[]{:S(2)}) collective-permute-start(bf16[1,2160,128]{2,1,0:T(8,128)(2,1)} %get-tuple-element.135), channel_id=1, source_target_pairs={{0,2},{1,3},{2,0},{3,1},{4,6},{5,7},{6,4},{7,5},{8,10},{9,11},{10,... | collective-permute-start | bytes 1658888 | tf_op jit(solution)/shard_map/send_states/ppermute | solution.py:486
  41.8 11.7 %collective-permute-start.11 = (bf16[128,1152]{1,0:T(8,128)(2,1)S(1)}, bf16[128,1152]{1,0:T(8,128)(2,1)}, u32[]{:S(2)}, u32[]{:S(2)}) collective-permute-start(bf16[128,1152]{1,0:T(8,128)(2,1)S(1)} %pad_maximum_fusion.rest_0_), channel_id=1, source_target_pairs={{0,8},{4,12},{8,0},{12,4},{16,24},{20,28},{24,16},{28,20},{1,9},{5... | collective-permute-start | bytes 884744 | tf_op jit(solution)/shard_map/tokens/ppermute | solution.py:486
  47.7 6.4 %collective-permute-start.6 = (bf16[128,1152]{1,0:T(8,128)(2,1)}, bf16[128,1152]{1,0:T(8,128)(2,1)}, u32[]{:S(2)}, u32[]{:S(2)}) collective-permute-start(bf16[128,1152]{1,0:T(8,128)(2,1)} %collective-permute-done.5.rest_2_), channel_id=1, source_target_pairs={{0,1},{1,0},{2,3},{3,2},{4,5},{5,4},{6,7},{7,6},{8,9},{9,8},{10,11... | collective-permute-start | bytes 884744 | tf_op jit(solution)/shard_map/tokens/ppermute | solution.py:486
  48.4 8.4 %collective-permute-start.16 = (bf16[128,1152]{1,0:T(8,128)(2,1)}, bf16[128,1152]{1,0:T(8,128)(2,1)}, u32[]{:S(2)}, u32[]{:S(2)}) collective-permute-start(bf16[128,1152]{1,0:T(8,128)(2,1)} %collective-permute-done.7.rest_0_), channel_id=1, source_target_pairs={{0,1},{1,0},{2,3},{3,2},{4,5},{5,4},{6,7},{7,6},{8,9},{9,8},{10,11... | collective-permute-start | bytes 884744 | tf_op jit(solution)/shard_map/tokens/ppermute | solution.py:486
  48.9 7.9 %collective-permute-start.17 = (bf16[128,1152]{1,0:T(8,128)(2,1)}, bf16[128,1152]{1,0:T(8,128)(2,1)}, u32[]{:S(2)}, u32[]{:S(2)}) collective-permute-start(bf16[128,1152]{1,0:T(8,128)(2,1)} %collective-permute-done.8.rest_2_), channel_id=1, source_target_pairs={{0,1},{1,0},{2,3},{3,2},{4,5},{5,4},{6,7},{7,6},{8,9},{9,8},{10,11... | collective-permute-start | bytes 884744 | tf_op jit(solution)/shard_map/tokens/ppermute | solution.py:486
  53.5 7.0 %collective-permute-start.12 = (bf16[128,1152]{1,0:T(8,128)(2,1)}, bf16[128,1152]{1,0:T(8,128)(2,1)S(1)}, u32[]{:S(2)}, u32[]{:S(2)}) collective-permute-start(bf16[128,1152]{1,0:T(8,128)(2,1)} %collective-permute-done.11.rest_0_), channel_id=1, source_target_pairs={{0,4},{4,0},{8,12},{12,8},{16,20},{20,16},{24,28},{28,24},{1,5},{5... | collective-permute-start | bytes 884744 | tf_op jit(solution)/shard_map/tokens/ppermute | solution.py:486
  54.1 14.8 %collective-permute-start.10 = (bf16[128,1152]{1,0:T(8,128)(2,1)S(1)}, bf16[128,1152]{1,0:T(8,128)(2,1)S(1)}, u32[]{:S(2)}, u32[]{:S(2)}) collective-permute-start(bf16[128,1152]{1,0:T(8,128)(2,1)S(1)} %pad_maximum_fusion.rest_0_), channel_id=1, source_target_pairs={{0,16},{4,20},{8,24},{12,28},{16,0},{20,4},{24,8},{28,12},{1,17},{... | collective-permute-start | bytes 884744 | tf_op jit(solution)/shard_map/tokens/ppermute | solution.py:486
  56.3 19.9 %collective-permute-start.22 = (bf16[1,2160,128]{2,1,0:T(8,128)(2,1)}, bf16[1,2160,128]{2,1,0:T(8,128)(2,1)S(1)}, u32[]{:S(2)}, u32[]{:S(2)}) collective-permute-start(bf16[1,2160,128]{2,1,0:T(8,128)(2,1)} %copy-done.19), channel_id=1, source_target_pairs={{0,2},{1,3},{2,0},{3,1},{4,6},{5,7},{6,4},{7,5},{8,10},{9,11},{10,... | collective-permute-start | bytes 1658888 | tf_op jit(solution)/shard_map/send_states/ppermute | solution.py:486
  60.0 16.7 %collective-permute-start.23 = (bf16[2,2,32,2048]{3,2,1,0:T(8,128)(2,1)S(1)}, bf16[2,2,32,2048]{3,2,1,0:T(8,128)(2,1)S(1)}, u32[]{:S(2)}, u32[]{:S(2)}) collective-permute-start(bf16[2,2,32,2048]{3,2,1,0:T(8,128)(2,1)S(1)} %get-tuple-element.159), channel_id=1, source_target_pairs={{0,1},{1,0},{2,3},{3,2},{4,5},{5,4},{6,7},{7,6},{8,9},{9,8},{10,11... | collective-permute-start | bytes 1572872 | tf_op jit(solution)/shard_map/way_back/ppermute | solution.py:486
  60.0 12.6 %collective-permute-start.14 = (bf16[128,1152]{1,0:T(8,128)(2,1)}, bf16[128,1152]{1,0:T(8,128)(2,1)S(1)}, u32[]{:S(2)}, u32[]{:S(2)}) collective-permute-start(bf16[128,1152]{1,0:T(8,128)(2,1)} %collective-permute-done.11.rest_0_), channel_id=1, source_target_pairs={{0,1},{1,0},{2,3},{3,2},{4,5},{5,4},{6,7},{7,6},{8,9},{9,8},{10,11... | collective-permute-start | bytes 884744 | tf_op jit(solution)/shard_map/tokens/ppermute | solution.py:486
  60.5 12.2 %collective-permute-start.15 = (bf16[128,1152]{1,0:T(8,128)(2,1)S(1)}, bf16[128,1152]{1,0:T(8,128)(2,1)S(1)}, u32[]{:S(2)}, u32[]{:S(2)}) collective-permute-start(bf16[128,1152]{1,0:T(8,128)(2,1)S(1)} %collective-permute-done.12.rest_2_), channel_id=1, source_target_pairs={{0,1},{1,0},{2,3},{3,2},{4,5},{5,4},{6,7},{7,6},{8,9},{9,8},{10,11... | collective-permute-start | bytes 884744 | tf_op jit(solution)/shard_map/tokens/ppermute | solution.py:486
  68.9 7.2 %collective-permute-start.13 = (bf16[128,1152]{1,0:T(8,128)(2,1)S(1)}, bf16[128,1152]{1,0:T(8,128)(2,1)S(1)}, u32[]{:S(2)}, u32[]{:S(2)}) collective-permute-start(bf16[128,1152]{1,0:T(8,128)(2,1)S(1)} %collective-permute-done.10.rest_0_), channel_id=1, source_target_pairs={{0,4},{4,0},{8,12},{12,8},{16,20},{20,16},{24,28},{28,24},{1,5},{5... | collective-permute-start | bytes 884744 | tf_op jit(solution)/shard_map/tokens/ppermute | solution.py:486
  72.6 27.6 %collective-permute-start.30 = (bf16[2,2160,128]{2,1,0:T(8,128)(2,1)S(1)}, bf16[2,2160,128]{2,1,0:T(8,128)(2,1)S(1)}, u32[]{:S(2)}, u32[]{:S(2)}) collective-permute-start(bf16[2,2160,128]{2,1,0:T(8,128)(2,1)S(1)} %copy-done.14), channel_id=1, source_target_pairs={{0,1},{1,0},{2,3},{3,2},{4,5},{5,4},{6,7},{7,6},{8,9},{9,8},{10,11... | collective-permute-start | bytes 3317768 | tf_op jit(solution)/shard_map/send_states/ppermute | solution.py:486
  76.1 5.4 %collective-permute-start.18 = (bf16[2,2,32,2048]{3,2,1,0:T(8,128)(2,1)S(1)}, bf16[2,2,32,2048]{3,2,1,0:T(8,128)(2,1)S(1)}, u32[]{:S(2)}, u32[]{:S(2)}) collective-permute-start(bf16[2,2,32,2048]{3,2,1,0:T(8,128)(2,1)S(1)} %get-tuple-element.150), channel_id=1, source_target_pairs={{0,1},{1,0},{2,3},{3,2},{4,5},{5,4},{6,7},{7,6},{8,9},{9,8},{10,11... | collective-permute-start | bytes 1572872 | tf_op jit(solution)/shard_map/way_back/ppermute | solution.py:486
  76.2 8.5 %collective-permute-start.19 = (bf16[2,2,32,2048]{3,2,1,0:T(8,128)(2,1)S(1)}, bf16[2,2,32,2048]{3,2,1,0:T(8,128)(2,1)S(1)}, u32[]{:S(2)}, u32[]{:S(2)}) collective-permute-start(bf16[2,2,32,2048]{3,2,1,0:T(8,128)(2,1)S(1)} %get-tuple-element.153), channel_id=1, source_target_pairs={{0,1},{1,0},{2,3},{3,2},{4,5},{5,4},{6,7},{7,6},{8,9},{9,8},{10,11... | collective-permute-start | bytes 1572872 | tf_op jit(solution)/shard_map/way_back/ppermute | solution.py:486
  81.6 14.7 %collective-permute-start.34 = (bf16[1,2160,128]{2,1,0:T(8,128)(2,1)S(1)}, bf16[1,2160,128]{2,1,0:T(8,128)(2,1)S(1)}, u32[]{:S(2)}, u32[]{:S(2)}) collective-permute-start(bf16[1,2160,128]{2,1,0:T(8,128)(2,1)S(1)} %copy-done.18), channel_id=1, source_target_pairs={{0,3},{1,2},{2,1},{3,0},{4,7},{5,6},{6,5},{7,4},{8,11},{9,10},{10,... | collective-permute-start | bytes 1658888 | tf_op jit(solution)/shard_map/send_states/ppermute | solution.py:486
  83.5 9.2 %collective-permute-start.27 = (bf16[2,32,2048]{2,1,0:T(8,128)(2,1)S(1)}, bf16[2,32,2048]{2,1,0:T(8,128)(2,1)S(1)}, u32[]{:S(2)}, u32[]{:S(2)}) collective-permute-start(bf16[2,32,2048]{2,1,0:T(8,128)(2,1)S(1)} %fusion.7), channel_id=1, source_target_pairs={{0,4},{4,0},{8,12},{12,8},{16,20},{20,16},{24,28},{28,24},{1,5},{5... | collective-permute-start | bytes 786440 | tf_op jit(solution)/shard_map/way_back/ppermute | solution.py:486
  84.8 13.3 %collective-permute-start.25 = (bf16[2,32,2048]{2,1,0:T(8,128)(2,1)S(1)}, bf16[2,32,2048]{2,1,0:T(8,128)(2,1)S(1)}, u32[]{:S(2)}, u32[]{:S(2)}) collective-permute-start(bf16[2,32,2048]{2,1,0:T(8,128)(2,1)S(1)} %fusion.6), channel_id=1, source_target_pairs={{0,4},{4,0},{8,12},{12,8},{16,20},{20,16},{24,28},{28,24},{1,5},{5... | collective-permute-start | bytes 786440 | tf_op jit(solution)/shard_map/way_back/ppermute | solution.py:486
  92.8 26.9 %collective-permute-start.28 = (bf16[2,32,2048]{2,1,0:T(8,128)(2,1)S(1)}, bf16[2,32,2048]{2,1,0:T(8,128)(2,1)S(1)}, u32[]{:S(2)}, u32[]{:S(2)}) collective-permute-start(bf16[2,32,2048]{2,1,0:T(8,128)(2,1)S(1)} %fusion.5), channel_id=1, source_target_pairs={{0,24},{4,28},{8,16},{12,20},{16,8},{20,12},{24,0},{28,4},{1,25},{... | collective-permute-start | bytes 786440 | tf_op jit(solution)/shard_map/way_back/ppermute | solution.py:486
  96.3 24.7 %collective-permute-start.35 = (bf16[1,2160,128]{2,1,0:T(8,128)(2,1)S(1)}, bf16[1,2160,128]{2,1,0:T(8,128)(2,1)S(1)}, u32[]{:S(2)}, u32[]{:S(2)}) collective-permute-start(bf16[1,2160,128]{2,1,0:T(8,128)(2,1)S(1)} %copy-done.16), channel_id=1, source_target_pairs={{0,3},{1,2},{2,1},{3,0},{4,7},{5,6},{6,5},{7,4},{8,11},{9,10},{10,... | collective-permute-start | bytes 1658888 | tf_op jit(solution)/shard_map/send_states/ppermute | solution.py:486
  98.1 21.5 %collective-permute-start.26 = (bf16[2,32,2048]{2,1,0:T(8,128)(2,1)S(1)}, bf16[2,32,2048]{2,1,0:T(8,128)(2,1)S(1)}, u32[]{:S(2)}, u32[]{:S(2)}) collective-permute-start(bf16[2,32,2048]{2,1,0:T(8,128)(2,1)S(1)} %fusion.9), channel_id=1, source_target_pairs={{0,4},{4,0},{8,12},{12,8},{16,20},{20,16},{24,28},{28,24},{1,5},{5... | collective-permute-start | bytes 786440 | tf_op jit(solution)/shard_map/way_back/ppermute | solution.py:486
  98.9 12.9 %collective-permute-start.29 = (bf16[2,32,2048]{2,1,0:T(8,128)(2,1)S(1)}, bf16[2,32,2048]{2,1,0:T(8,128)(2,1)S(1)}, u32[]{:S(2)}, u32[]{:S(2)}) collective-permute-start(bf16[2,32,2048]{2,1,0:T(8,128)(2,1)S(1)} %fusion.8), channel_id=1, source_target_pairs={{0,4},{4,0},{8,12},{12,8},{16,20},{20,16},{24,28},{28,24},{1,5},{5... | collective-permute-start | bytes 786440 | tf_op jit(solution)/shard_map/way_back/ppermute | solution.py:486
  100.3 19.4 %collective-permute-start.32 = (bf16[2,32,2048]{2,1,0:T(8,128)(2,1)S(1)}, bf16[2,32,2048]{2,1,0:T(8,128)(2,1)S(1)}, u32[]{:S(2)}, u32[]{:S(2)}) collective-permute-start(bf16[2,32,2048]{2,1,0:T(8,128)(2,1)S(1)} %fusion.1), channel_id=1, source_target_pairs={{0,16},{4,20},{8,24},{12,28},{16,0},{20,4},{24,8},{28,12},{1,17},{... | collective-permute-start | bytes 786440 | tf_op jit(solution)/shard_map/way_back/ppermute | solution.py:486
  112.0 8.5 %collective-permute-start.31 = (bf16[2,32,2048]{2,1,0:T(8,128)(2,1)S(1)}, bf16[2,32,2048]{2,1,0:T(8,128)(2,1)S(1)}, u32[]{:S(2)}, u32[]{:S(2)}) collective-permute-start(bf16[2,32,2048]{2,1,0:T(8,128)(2,1)S(1)} %fusion.3), channel_id=1, source_target_pairs={{0,8},{4,12},{8,0},{12,4},{16,24},{20,28},{24,16},{28,20},{1,9},{5... | collective-permute-start | bytes 786440 | tf_op jit(solution)/shard_map/way_back/ppermute | solution.py:486
  (25 other events, 397.0 us)

commit v11 on v10

--- a/solution.py
+++ b/solution.py
@@ -534,8 +534,6 @@
         cap = requests // lanes
         near_states = [packed[0], swap(packed[1], "ep", 1)]
         first_across = swap(held, "dp", 1)
-        packed = list(packed)
-        packed[2], first_across = lax.optimization_barrier((packed[2], first_across))
         far_states = []
         for i, piece in enumerate(packed[2:]):
             if i:
@@ -595,7 +593,6 @@
     with jax.named_scope("landed"):
         sizes = (requests, kw // hd, heads, steps)
         sums[far], arrived = tie((sums[far], near_states + far_states[:-2]))
-        sums[chunks[-2]], arrived = tie((sums[chunks[-2]], arrived))
         moved_out = landed_states(arrived, [], *sizes)
     with jax.named_scope("way_back"):
         sums = [swap(sums[d], "dp", d) if d else sums[d] for d in chunks]

time: 127 us -> 130 us (1.024)
  waiting for transfers between devices: 51.2 us -> 54.6 us
  local copies, waits for them, and re-layouts: 2.33 us -> 4.97 us
  starting transfers between devices: 35.9 us -> 34 us
    ppermute x36, waiting for transfers between devices: 51.2 us -> 54.6 us  [swap(): return lax.ppermute(x, axis, [(i, i ^ d) for i in range(size)])]
    unnamed x42, local copies, waits for them, and re-layouts: 1.6 us -> 4.24 us
    ppermute x36, starting transfers between devices: 35.9 us -> 34 us  [swap(): return lax.ppermute(x, axis, [(i, i ^ d) for i in range(size)])]
  transfers between devices with their start and end apart: 36 -> 36, of which waited for: 13 -> 15; matrix products, arithmetic and copies ran while one was open for 1% -> 1% of each run, Pallas kernels for 20% -> 19%
where the time goes in v11:
time: 130 us
  waiting for transfers between devices  54.6 us (42%)
  Pallas kernels  34.3 us (26%)
  starting transfers between devices  34 us (26%)
  local copies, waits for them, and re-layouts  4.97 us (4%)
    ppermute x36, waiting for transfers between devices, swap(): return lax.ppermute(x, axis, [(i, i ^ d) for i in range(size)])  54.6 us
    ppermute x36, starting transfers between devices, swap(): return lax.ppermute(x, axis, [(i, i ^ d) for i in range(size)])  34 us
    pallas_call x2, Pallas kernels, landed_states(): pl.pallas_call(functools.partial(state_kernel, key_heads, heads, steps, l...  10.7 us
    pallas_call x4, Pallas kernels, expert_chunk(): pl.pallas_call(functools.partial(expert_kernel, sides, own_out, experts),...  10.5 us
    pallas_call x1, Pallas kernels, core_rows(): pl.pallas_call(functools.partial(core_kernel, lanes, experts), in_specs=[...  9.51 us
    unnamed x42, local copies, waits for them, and re-layouts  4.24 us
    pallas_call x1, Pallas kernels, pack_states(): pl.pallas_call(functools.partial(pack_kernel, lanes, key_heads), in_specs...  3.14 us
  transfers between devices with their start and end apart: 36, of which 15 were waited for; matrix products, arithmetic and copies ran while one was open for 1% of the time, Pallas kernels for 19%

profile of v11, /device:TPU:0, one launch (start us, length us, event | category | flops | bytes accessed | tf_op | source)
XLA Modules:
  0.0 129.9 jit_solution(15700188255256101974)
XLA Ops:
  0.7 9.5 %core_rows.1 = (bf16[32,2688]{1,0:T(8,128)(2,1)}, bf16[32,2688]{1,0:T(8,128)(2,1)}, bf16[32,2688]{1,0:T(8,128)(2,1)}, bf16[32,2688]{1,0:T(8,128)(2,1)}) custom-call(s32[1]{0:T(128)} %bitcast.lane_ref, bf16[8,2048,128]{2,1,0:T(8,128)(2,1)} %bitcast.60, bf16[8,4,1024]{2,1,0:T(4,128)(2,1)} %q_ref.1, bf16[8,4,1024]{2,1,0:T(4,128)(2,1)} %k_ref.3, ...), custom_call_target="tpu_custom_call" | custom-call | flops 20000000 | bytes 9437184 | tf_op jit(solution)/shard_map/core/core_rows/pallas_call | solution.py:155
  10.7 2.6 %collective-permute-start.1 = (bf16[32,2688]{1,0:T(8,128)(2,1)}, bf16[32,2688]{1,0:T(8,128)(2,1)S(1)}, u32[]{:S(2)}, u32[]{:S(2)}) collective-permute-start(bf16[32,2688]{1,0:T(8,128)(2,1)} %get-tuple-element.98), channel_id=1, source_target_pairs={{0,2},{1,3},{2,0},{3,1},{4,6},{5,7},{6,4},{7,5},{8,10},{9,11},{10,... | collective-permute-start | bytes 516104 | tf_op jit(solution)/shard_map/core/ppermute | solution.py:486
  13.4 3.1 %pack_states.1 = (bf16[2,2160,128]{2,1,0:T(8,128)(2,1)S(1)}, bf16[2,2160,128]{2,1,0:T(8,128)(2,1)S(1)}, bf16[1,2160,128]{2,1,0:T(8,128)(2,1)}, bf16[1,2160,128]{...) custom-call(s32[8]{0:T(128)S(1)} %copy-done.12, s32[1]{0:T(128)} %bitcast.lane_ref, ...), custom_call_target="tpu_custom_call" | custom-call | bytes 9437184 | tf_op jit(solution)/shard_map/send_states/pack_states/pallas_call | solution.py:240
  20.1 1.9 %collective-permute-done.2.refs_3_ = bf16[32,2688]{1,0:T(8,128)(2,1)S(1)} collective-permute-done((bf16[32,2688]{1,0:T(8,128)(2,1)}, bf16[32,2688]{1,0:T(8,128)(2,1)S(1)}, u32[]{:S(2)}, u32[]{:S(2)}) %collective-permute-start.2) | collective-permute-done | bytes 172064 | tf_op jit(solution)/shard_map/core/ppermute | solution.py:486
  22.4 1.6 %collective-permute-start.3 = (bf16[128,512]{1,0:T(8,128)(2,1)S(1)}, bf16[128,512]{1,0:T(8,128)(2,1)S(1)}, u32[]{:S(2)}, u32[]{:S(2)}) collective-permute-start(bf16[128,512]{1,0:T(8,128)(2,1)S(1)} %get-tuple-element.111), channel_id=1, source_target_pairs={{0,2},{1,3},{2,0},{3,1},{4,6},{5,7},{6,4},{7,5},{8,10},{9,11},{10,... | collective-permute-start | bytes 393224 | tf_op jit(solution)/shard_map/attention/ppermute | solution.py:486
  24.0 4.0 %collective-permute-done.3 = bf16[128,512]{1,0:T(8,128)(2,1)S(1)} collective-permute-done((bf16[128,512]{1,0:T(8,128)(2,1)S(1)}, bf16[128,512]{1,0:T(8,128)(2,1)S(1)}, u32[]{:S(2)}, u32[]{:S(2)}) %collective-permute-start.3) | collective-permute-done | bytes 131104 | tf_op jit(solution)/shard_map/attention/ppermute | solution.py:486
  28.0 3.9 %collective-permute-start.7 = (bf16[128,1152]{1,0:T(8,128)(2,1)S(1)}, bf16[128,1152]{1,0:T(8,128)(2,1)}, u32[]{:S(2)}, u32[]{:S(2)}) collective-permute-start(bf16[128,1152]{1,0:T(8,128)(2,1)S(1)} %pad_maximum_fusion.rest_0_), channel_id=1, source_target_pairs={{0,24},{4,28},{8,16},{12,20},{16,8},{20,12},{24,0},{28,4},{1,25},{... | collective-permute-start | bytes 884744 | tf_op jit(solution)/shard_map/tokens/ppermute | solution.py:486
  33.4 1.5 %collective-permute-start.5 = (bf16[128,1152]{1,0:T(8,128)(2,1)S(1)}, bf16[128,1152]{1,0:T(8,128)(2,1)}, u32[]{:S(2)}, u32[]{:S(2)}) collective-permute-start(bf16[128,1152]{1,0:T(8,128)(2,1)S(1)} %pad_maximum_fusion.rest_0_), channel_id=1, source_target_pairs={{0,4},{4,0},{8,12},{12,8},{16,20},{20,16},{24,28},{28,24},{1,5},{5... | collective-permute-start | bytes 884744 | tf_op jit(solution)/shard_map/send_states/ppermute | solution.py:486
  34.9 5.0 %collective-permute-done.7.rest_0_ = bf16[128,1152]{1,0:T(8,128)(2,1)} collective-permute-done((bf16[128,1152]{1,0:T(8,128)(2,1)S(1)}, bf16[128,1152]{1,0:T(8,128)(2,1)}, u32[]{:S(2)}, u32[]{:S(2)}) %collective-permute-start.7) | collective-permute-done | bytes 294944 | tf_op jit(solution)/shard_map/tokens/ppermute | solution.py:486
  39.9 1.8 %collective-permute-start.8 = (bf16[128,1152]{1,0:T(8,128)(2,1)}, bf16[128,1152]{1,0:T(8,128)(2,1)}, u32[]{:S(2)}, u32[]{:S(2)}) collective-permute-start(bf16[128,1152]{1,0:T(8,128)(2,1)} %collective-permute-done.7.rest_0_), channel_id=1, source_target_pairs={{0,4},{4,0},{8,12},{12,8},{16,20},{20,16},{24,28},{28,24},{1,5},{5... | collective-permute-start | bytes 884744 | tf_op jit(solution)/shard_map/tokens/ppermute | solution.py:486
  42.2 2.8 %collective-permute-done.11.rest_0_ = bf16[128,1152]{1,0:T(8,128)(2,1)S(1)} collective-permute-done((bf16[128,1152]{1,0:T(8,128)(2,1)S(1)}, bf16[128,1152]{1,0:T(8,128)(2,1)S(1)}, u32[]{:S(2)}, u32[]{:S(2)}) %collective-permute-start.11) | collective-permute-done | bytes 294944 | tf_op jit(solution)/shard_map/tokens/ppermute | solution.py:486
  45.7 2.0 %collective-permute-done.8.rest_2_ = bf16[128,1152]{1,0:T(8,128)(2,1)} collective-permute-done((bf16[128,1152]{1,0:T(8,128)(2,1)}, bf16[128,1152]{1,0:T(8,128)(2,1)}, u32[]{:S(2)}, u32[]{:S(2)}) %collective-permute-start.8) | collective-permute-done | bytes 294944 | tf_op jit(solution)/shard_map/tokens/ppermute | solution.py:486
  47.7 1.6 %collective-permute-start.12 = (bf16[128,1152]{1,0:T(8,128)(2,1)}, bf16[128,1152]{1,0:T(8,128)(2,1)S(1)}, u32[]{:S(2)}, u32[]{:S(2)}) collective-permute-start(bf16[128,1152]{1,0:T(8,128)(2,1)} %copy-done.6), channel_id=1, source_target_pairs={{0,4},{4,0},{8,12},{12,8},{16,20},{20,16},{24,28},{28,24},{1,5},{5... | collective-permute-start | bytes 884744 | tf_op jit(solution)/shard_map/tokens/ppermute | solution.py:486
  49.3 5.8 %collective-permute-start.10 = (bf16[128,1152]{1,0:T(8,128)(2,1)S(1)}, bf16[128,1152]{1,0:T(8,128)(2,1)S(1)}, u32[]{:S(2)}, u32[]{:S(2)}) collective-permute-start(bf16[128,1152]{1,0:T(8,128)(2,1)S(1)} %pad_maximum_fusion.rest_0_), channel_id=1, source_target_pairs={{0,16},{4,20},{8,24},{12,28},{16,0},{20,4},{24,8},{28,12},{1,17},{... | collective-permute-start | bytes 884744 | tf_op jit(solution)/shard_map/tokens/ppermute | solution.py:486
  55.2 1.5 %collective-permute-start.22 = (bf16[1,2160,128]{2,1,0:T(8,128)(2,1)}, bf16[1,2160,128]{2,1,0:T(8,128)(2,1)S(1)}, u32[]{:S(2)}, u32[]{:S(2)}) collective-permute-start(bf16[1,2160,128]{2,1,0:T(8,128)(2,1)} %copy-done.19), channel_id=1, source_target_pairs={{0,2},{1,3},{2,0},{3,1},{4,6},{5,7},{6,4},{7,5},{8,10},{9,11},{10,... | collective-permute-start | bytes 1658888 | tf_op jit(solution)/shard_map/send_states/ppermute | solution.py:486
  56.7 3.1 %expert_chunk.6 = (bf16[2,32,2048]{2,1,0:T(8,128)(2,1)S(1)}, bf16[2,32,2048]{2,1,0:T(8,128)(2,1)S(1)}, bf16[2,2,32,2048]{3,2,1,0:T(8,128)(2,1)S(1)}) custom-call(s32[2]{0:T(128)S(1)} %pad_add_fusion.where_ref, bf16[128,1152]{1,0:T(8,128)(2,1)} %collective-permute-done.7.rest_0_, bf16[128,1152]{1,0:T(8,128)(2,1)} %collective-permute-done.16.rest_1_, ...), custom_call_target="tpu_custom_call" | custom-call | flops 805306368 | bytes 6291456 | tf_op jit(solution)/shard_map/experts/expert_chunk/pallas_call | solution.py:468
  60.5 8.4 %collective-permute-done.10.rest_0_ = bf16[128,1152]{1,0:T(8,128)(2,1)S(1)} collective-permute-done((bf16[128,1152]{1,0:T(8,128)(2,1)S(1)}, bf16[128,1152]{1,0:T(8,128)(2,1)S(1)}, u32[]{:S(2)}, u32[]{:S(2)}) %collective-permute-start.10) | collective-permute-done | bytes 294944 | tf_op jit(solution)/shard_map/tokens/ppermute | solution.py:486
  69.4 3.2 %expert_chunk.4 = (bf16[2,32,2048]{2,1,0:T(8,128)(2,1)S(1)}, bf16[2,32,2048]{2,1,0:T(8,128)(2,1)S(1)}, bf16[2,2,32,2048]{3,2,1,0:T(8,128)(2,1)S(1)}, bf16[32,2048]{1,0:T(8,128)(2,1)S(1)}) custom-call(s32[2]{0:T(128)S(1)} %pad_add_fusion.where_ref, bf16[128,1152]{1,0:T(8,128)(2,1)S(1)} %pad_maximum_fusion.rest_0_, ...), custom_call_target="tpu_custom_call" | custom-call | flops 805306368 | bytes 6291456 | tf_op jit(solution)/shard_map/experts/expert_chunk/pallas_call | solution.py:468
  73.2 2.1 %expert_chunk.5 = (bf16[2,32,2048]{2,1,0:T(8,128)(2,1)S(1)}, bf16[2,32,2048]{2,1,0:T(8,128)(2,1)S(1)}, bf16[2,2,32,2048]{3,2,1,0:T(8,128)(2,1)S(1)}) custom-call(s32[2]{0:T(128)S(1)} %pad_add_fusion.where_ref, bf16[128,1152]{1,0:T(8,128)(2,1)S(1)} %copy-done.7, bf16[128,1152]{1,0:T(8,128)(2,1)S(1)} %collective-permute-done.14.rest_1_, ...), custom_call_target="tpu_custom_call" | custom-call | flops 805306368 | bytes 6291456 | tf_op jit(solution)/shard_map/experts/expert_chunk/pallas_call | solution.py:468
  75.3 2.2 %collective-permute-done.13.rest_2_ = bf16[128,1152]{1,0:T(8,128)(2,1)S(1)} collective-permute-done((bf16[128,1152]{1,0:T(8,128)(2,1)S(1)}, bf16[128,1152]{1,0:T(8,128)(2,1)S(1)}, u32[]{:S(2)}, u32[]{:S(2)}) %collective-permute-start.13) | collective-permute-done | bytes 294944 | tf_op jit(solution)/shard_map/tokens/ppermute | solution.py:486
  78.2 1.6 %collective-permute-start.34 = (bf16[1,2160,128]{2,1,0:T(8,128)(2,1)S(1)}, bf16[1,2160,128]{2,1,0:T(8,128)(2,1)S(1)}, u32[]{:S(2)}, u32[]{:S(2)}) collective-permute-start(bf16[1,2160,128]{2,1,0:T(8,128)(2,1)S(1)} %copy-done.18), channel_id=1, source_target_pairs={{0,3},{1,2},{2,1},{3,0},{4,7},{5,6},{6,5},{7,4},{8,11},{9,10},{10,... | collective-permute-start | bytes 1658888 | tf_op jit(solution)/shard_map/send_states/ppermute | solution.py:486
  80.6 2.1 %expert_chunk.7 = (bf16[2,32,2048]{2,1,0:T(8,128)(2,1)S(1)}, bf16[2,32,2048]{2,1,0:T(8,128)(2,1)S(1)}, bf16[2,2,32,2048]{3,2,1,0:T(8,128)(2,1)S(1)}) custom-call(s32[2]{0:T(128)S(1)} %pad_add_fusion.where_ref, bf16[128,1152]{1,0:T(8,128)(2,1)S(1)} %collective-permute-done.10.rest_0_, bf16[128,1152]{1,0:T(8,128)(2,1)S(1)} %collective-permute-done.20.rest_1_, ...), custom_call_target="tpu_custom_call" | custom-call | flops 805306368 | bytes 6291456 | tf_op jit(solution)/shard_map/experts/expert_chunk/pallas_call | solution.py:468
  83.6 8.9 %collective-permute-done.34.rest_0_ = bf16[1,2160,128]{2,1,0:T(8,128)(2,1)S(1)} collective-permute-done((bf16[1,2160,128]{2,1,0:T(8,128)(2,1)S(1)}, bf16[1,2160,128]{2,1,0:T(8,128)(2,1)S(1)}, u32[]{:S(2)}, u32[]{:S(2)}) %collective-permute-start.34) | collective-permute-done | bytes 552992 | tf_op jit(solution)/shard_map/send_states/ppermute | solution.py:486
  92.5 1.5 %collective-permute-start.35 = (bf16[1,2160,128]{2,1,0:T(8,128)(2,1)S(1)}, bf16[1,2160,128]{2,1,0:T(8,128)(2,1)S(1)}, u32[]{:S(2)}, u32[]{:S(2)}) collective-permute-start(bf16[1,2160,128]{2,1,0:T(8,128)(2,1)S(1)} %copy-done.16), channel_id=1, source_target_pairs={{0,3},{1,2},{2,1},{3,0},{4,7},{5,6},{6,5},{7,4},{8,11},{9,10},{10,... | collective-permute-start | bytes 1658888 | tf_op jit(solution)/shard_map/send_states/ppermute | solution.py:486
  94.8 2.0 %collective-permute-start.28 = (bf16[2,32,2048]{2,1,0:T(8,128)(2,1)S(1)}, bf16[2,32,2048]{2,1,0:T(8,128)(2,1)S(1)}, u32[]{:S(2)}, u32[]{:S(2)}) collective-permute-start(bf16[2,32,2048]{2,1,0:T(8,128)(2,1)S(1)} %fusion.5), channel_id=1, source_target_pairs={{0,24},{4,28},{8,16},{12,20},{16,8},{20,12},{24,0},{28,4},{1,25},{... | collective-permute-start | bytes 786440 | tf_op jit(solution)/shard_map/way_back/ppermute | solution.py:486
  96.8 5.8 %collective-permute-done.25 = bf16[2,32,2048]{2,1,0:T(8,128)(2,1)S(1)} collective-permute-done((bf16[2,32,2048]{2,1,0:T(8,128)(2,1)S(1)}, bf16[2,32,2048]{2,1,0:T(8,128)(2,1)S(1)}, u32[]{:S(2)}, u32[]{:S(2)}) %collective-permute-start.25) | collective-permute-done | bytes 262176 | tf_op jit(solution)/shard_map/way_back/ppermute | solution.py:486
  103.0 1.5 %collective-permute-start.29 = (bf16[2,32,2048]{2,1,0:T(8,128)(2,1)S(1)}, bf16[2,32,2048]{2,1,0:T(8,128)(2,1)S(1)}, u32[]{:S(2)}, u32[]{:S(2)}) collective-permute-start(bf16[2,32,2048]{2,1,0:T(8,128)(2,1)S(1)} %fusion.8), channel_id=1, source_target_pairs={{0,4},{4,0},{8,12},{12,8},{16,20},{20,16},{24,28},{28,24},{1,5},{5... | collective-permute-start | bytes 786440 | tf_op jit(solution)/shard_map/way_back/ppermute | solution.py:486
  104.8 7.5 %landed_states.2.rest_2_ = bf16[8,2048,128]{2,1,0:T(8,128)(2,1)} custom-call(bf16[2,2160,128]{2,1,0:T(8,128)(2,1)S(1)} %copy-done.4, bf16[2,2160,128]{2,1,0:T(8,128)(2,1)S(1)} %collective-permute-done.31.rest_1_, bf16[1,2160,128]{2,1,0:T(8,128)(2,1)} %collective-permute-done.9.rest_2_, bf16[1,2160,128]{2,1,0:T(8,128)(2,1)S(1)} %collective-permute-done.22.rest_3_), custom_call_target="tpu_custom_call" | custom-call | flops 20000000 | bytes 6291456 | tf_op jit(solution)/shard_map/landed/landed_states/pallas_call | solution.py:371
  112.3 3.4 %collective-permute-done.29 = bf16[2,32,2048]{2,1,0:T(8,128)(2,1)S(1)} collective-permute-done((bf16[2,32,2048]{2,1,0:T(8,128)(2,1)S(1)}, bf16[2,32,2048]{2,1,0:T(8,128)(2,1)S(1)}, u32[]{:S(2)}, u32[]{:S(2)}) %collective-permute-start.29) | collective-permute-done | bytes 262176 | tf_op jit(solution)/shard_map/way_back/ppermute | solution.py:486
  116.0 2.4 %collective-permute-done.32 = bf16[2,32,2048]{2,1,0:T(8,128)(2,1)S(1)} collective-permute-done((bf16[2,32,2048]{2,1,0:T(8,128)(2,1)S(1)}, bf16[2,32,2048]{2,1,0:T(8,128)(2,1)S(1)}, u32[]{:S(2)}, u32[]{:S(2)}) %collective-permute-start.32) | collective-permute-done | bytes 262176 | tf_op jit(solution)/shard_map/way_back/ppermute | solution.py:486
  118.4 5.5 %collective-permute-done.30 = bf16[2,32,2048]{2,1,0:T(8,128)(2,1)S(1)} collective-permute-done((bf16[2,32,2048]{2,1,0:T(8,128)(2,1)S(1)}, bf16[2,32,2048]{2,1,0:T(8,128)(2,1)S(1)}, u32[]{:S(2)}, u32[]{:S(2)}) %collective-permute-start.30) | collective-permute-done | bytes 262176 | tf_op jit(solution)/shard_map/way_back/ppermute | solution.py:486
  124.6 3.2 %landed_states.3 = bf16[8,2048,128]{2,1,0:T(8,128)(2,1)} custom-call(bf16[1,2160,128]{2,1,0:T(8,128)(2,1)S(1)} %collective-permute-done.34.rest_0_, bf16[1,2160,128]{2,1,0:T(8,128)(2,1)S(1)} %collective-permute-done.35.rest_1_, bf16[8,2048,128]{2,1,0:T(8,128)(2,1)} %landed_states.2.rest_2_), custom_call_target="tpu_custom_call", output_to_operand_aliasing={{}: (2, {})} | custom-call | flops 20000000 | bytes 2097152 | tf_op jit(solution)/shard_map/landed/landed_states/pallas_call | solution.py:371
  (106 shorter events, 15.9 us)
Async XLA Ops:
  10.2 9.8 %collective-permute-start = (bf16[32,2688]{1,0:T(8,128)(2,1)}, bf16[32,2688]{1,0:T(8,128)(2,1)S(1)}, u32[]{:S(2)}, u32[]{:S(2)}) collective-permute-start(bf16[32,2688]{1,0:T(8,128)(2,1)} %get-tuple-element.97), channel_id=1, source_target_pairs={{0,1},{1,0},{2,3},{3,2},{4,5},{5,4},{6,7},{7,6},{8,9},{9,8},{10,11... | collective-permute-start | bytes 516104 | tf_op jit(solution)/shard_map/core/ppermute | solution.py:486
  10.7 9.3 %collective-permute-start.1 = (bf16[32,2688]{1,0:T(8,128)(2,1)}, bf16[32,2688]{1,0:T(8,128)(2,1)S(1)}, u32[]{:S(2)}, u32[]{:S(2)}) collective-permute-start(bf16[32,2688]{1,0:T(8,128)(2,1)} %get-tuple-element.98), channel_id=1, source_target_pairs={{0,2},{1,3},{2,0},{3,1},{4,6},{5,7},{6,4},{7,5},{8,10},{9,11},{10,... | collective-permute-start | bytes 516104 | tf_op jit(solution)/shard_map/core/ppermute | solution.py:486
  13.3 8.6 %collective-permute-start.2 = (bf16[32,2688]{1,0:T(8,128)(2,1)}, bf16[32,2688]{1,0:T(8,128)(2,1)S(1)}, u32[]{:S(2)}, u32[]{:S(2)}) collective-permute-start(bf16[32,2688]{1,0:T(8,128)(2,1)} %get-tuple-element.99), channel_id=1, source_target_pairs={{0,3},{1,2},{2,1},{3,0},{4,7},{5,6},{6,5},{7,4},{8,11},{9,10},{10,... | collective-permute-start | bytes 516104 | tf_op jit(solution)/shard_map/core/ppermute | solution.py:486
  22.4 5.6 %collective-permute-start.3 = (bf16[128,512]{1,0:T(8,128)(2,1)S(1)}, bf16[128,512]{1,0:T(8,128)(2,1)S(1)}, u32[]{:S(2)}, u32[]{:S(2)}) collective-permute-start(bf16[128,512]{1,0:T(8,128)(2,1)S(1)} %get-tuple-element.111), channel_id=1, source_target_pairs={{0,2},{1,3},{2,0},{3,1},{4,6},{5,7},{6,4},{7,5},{8,10},{9,11},{10,... | collective-permute-start | bytes 393224 | tf_op jit(solution)/shard_map/attention/ppermute | solution.py:486
  28.0 11.9 %collective-permute-start.7 = (bf16[128,1152]{1,0:T(8,128)(2,1)S(1)}, bf16[128,1152]{1,0:T(8,128)(2,1)}, u32[]{:S(2)}, u32[]{:S(2)}) collective-permute-start(bf16[128,1152]{1,0:T(8,128)(2,1)S(1)} %pad_maximum_fusion.rest_0_), channel_id=1, source_target_pairs={{0,24},{4,28},{8,16},{12,20},{16,8},{20,12},{24,0},{28,4},{1,25},{... | collective-permute-start | bytes 884744 | tf_op jit(solution)/shard_map/tokens/ppermute | solution.py:486
  31.9 15.8 %collective-permute-start.9 = (bf16[1,2160,128]{2,1,0:T(8,128)(2,1)}, bf16[1,2160,128]{2,1,0:T(8,128)(2,1)}, u32[]{:S(2)}, u32[]{:S(2)}) collective-permute-start(bf16[1,2160,128]{2,1,0:T(8,128)(2,1)} %get-tuple-element.126), channel_id=1, source_target_pairs={{0,2},{1,3},{2,0},{3,1},{4,6},{5,7},{6,4},{7,5},{8,10},{9,11},{10,... | collective-permute-start | bytes 1658888 | tf_op jit(solution)/shard_map/send_states/ppermute | solution.py:486
  33.4 8.7 %collective-permute-start.5 = (bf16[128,1152]{1,0:T(8,128)(2,1)S(1)}, bf16[128,1152]{1,0:T(8,128)(2,1)}, u32[]{:S(2)}, u32[]{:S(2)}) collective-permute-start(bf16[128,1152]{1,0:T(8,128)(2,1)S(1)} %pad_maximum_fusion.rest_0_), channel_id=1, source_target_pairs={{0,4},{4,0},{8,12},{12,8},{16,20},{20,16},{24,28},{28,24},{1,5},{5... | collective-permute-start | bytes 884744 | tf_op jit(solution)/shard_map/send_states/ppermute | solution.py:486
  34.9 10.0 %collective-permute-start.11 = (bf16[128,1152]{1,0:T(8,128)(2,1)S(1)}, bf16[128,1152]{1,0:T(8,128)(2,1)S(1)}, u32[]{:S(2)}, u32[]{:S(2)}) collective-permute-start(bf16[128,1152]{1,0:T(8,128)(2,1)S(1)} %pad_maximum_fusion.rest_0_), channel_id=1, source_target_pairs={{0,8},{4,12},{8,0},{12,4},{16,24},{20,28},{24,16},{28,20},{1,9},{5... | collective-permute-start | bytes 884744 | tf_op jit(solution)/shard_map/tokens/ppermute | solution.py:486
  39.9 7.7 %collective-permute-start.8 = (bf16[128,1152]{1,0:T(8,128)(2,1)}, bf16[128,1152]{1,0:T(8,128)(2,1)}, u32[]{:S(2)}, u32[]{:S(2)}) collective-permute-start(bf16[128,1152]{1,0:T(8,128)(2,1)} %collective-permute-done.7.rest_0_), channel_id=1, source_target_pairs={{0,4},{4,0},{8,12},{12,8},{16,20},{20,16},{24,28},{28,24},{1,5},{5... | collective-permute-start | bytes 884744 | tf_op jit(solution)/shard_map/tokens/ppermute | solution.py:486
  41.7 7.7 %collective-permute-start.4 = (bf16[128,1152]{1,0:T(8,128)(2,1)S(1)}, bf16[128,1152]{1,0:T(8,128)(2,1)}, u32[]{:S(2)}, u32[]{:S(2)}) collective-permute-start(bf16[128,1152]{1,0:T(8,128)(2,1)S(1)} %pad_maximum_fusion.rest_0_), channel_id=1, source_target_pairs={{0,1},{1,0},{2,3},{3,2},{4,5},{5,4},{6,7},{7,6},{8,9},{9,8},{10,11... | collective-permute-start | bytes 884744 | tf_op jit(solution)/shard_map/tokens/ppermute | solution.py:486
  42.1 13.1 %collective-permute-start.6 = (bf16[128,1152]{1,0:T(8,128)(2,1)}, bf16[128,1152]{1,0:T(8,128)(2,1)}, u32[]{:S(2)}, u32[]{:S(2)}) collective-permute-start(bf16[128,1152]{1,0:T(8,128)(2,1)} %collective-permute-done.5.rest_2_), channel_id=1, source_target_pairs={{0,1},{1,0},{2,3},{3,2},{4,5},{5,4},{6,7},{7,6},{8,9},{9,8},{10,11... | collective-permute-start | bytes 884744 | tf_op jit(solution)/shard_map/tokens/ppermute | solution.py:486
  45.0 11.7 %collective-permute-start.16 = (bf16[128,1152]{1,0:T(8,128)(2,1)}, bf16[128,1152]{1,0:T(8,128)(2,1)}, u32[]{:S(2)}, u32[]{:S(2)}) collective-permute-start(bf16[128,1152]{1,0:T(8,128)(2,1)} %collective-permute-done.7.rest_0_), channel_id=1, source_target_pairs={{0,1},{1,0},{2,3},{3,2},{4,5},{5,4},{6,7},{7,6},{8,9},{9,8},{10,11... | collective-permute-start | bytes 884744 | tf_op jit(solution)/shard_map/tokens/ppermute | solution.py:486
  47.6 9.0 %collective-permute-start.17 = (bf16[128,1152]{1,0:T(8,128)(2,1)}, bf16[128,1152]{1,0:T(8,128)(2,1)}, u32[]{:S(2)}, u32[]{:S(2)}) collective-permute-start(bf16[128,1152]{1,0:T(8,128)(2,1)} %collective-permute-done.8.rest_2_), channel_id=1, source_target_pairs={{0,1},{1,0},{2,3},{3,2},{4,5},{5,4},{6,7},{7,6},{8,9},{9,8},{10,11... | collective-permute-start | bytes 884744 | tf_op jit(solution)/shard_map/tokens/ppermute | solution.py:486
  47.7 12.7 %collective-permute-start.12 = (bf16[128,1152]{1,0:T(8,128)(2,1)}, bf16[128,1152]{1,0:T(8,128)(2,1)S(1)}, u32[]{:S(2)}, u32[]{:S(2)}) collective-permute-start(bf16[128,1152]{1,0:T(8,128)(2,1)} %copy-done.6), channel_id=1, source_target_pairs={{0,4},{4,0},{8,12},{12,8},{16,20},{20,16},{24,28},{28,24},{1,5},{5... | collective-permute-start | bytes 884744 | tf_op jit(solution)/shard_map/tokens/ppermute | solution.py:486
  49.3 19.5 %collective-permute-start.10 = (bf16[128,1152]{1,0:T(8,128)(2,1)S(1)}, bf16[128,1152]{1,0:T(8,128)(2,1)S(1)}, u32[]{:S(2)}, u32[]{:S(2)}) collective-permute-start(bf16[128,1152]{1,0:T(8,128)(2,1)S(1)} %pad_maximum_fusion.rest_0_), channel_id=1, source_target_pairs={{0,16},{4,20},{8,24},{12,28},{16,0},{20,4},{24,8},{28,12},{1,17},{... | collective-permute-start | bytes 884744 | tf_op jit(solution)/shard_map/tokens/ppermute | solution.py:486
  55.2 22.3 %collective-permute-start.22 = (bf16[1,2160,128]{2,1,0:T(8,128)(2,1)}, bf16[1,2160,128]{2,1,0:T(8,128)(2,1)S(1)}, u32[]{:S(2)}, u32[]{:S(2)}) collective-permute-start(bf16[1,2160,128]{2,1,0:T(8,128)(2,1)} %copy-done.19), channel_id=1, source_target_pairs={{0,2},{1,3},{2,0},{3,1},{4,6},{5,7},{6,4},{7,5},{8,10},{9,11},{10,... | collective-permute-start | bytes 1658888 | tf_op jit(solution)/shard_map/send_states/ppermute | solution.py:486
  59.8 18.2 %collective-permute-start.23 = (bf16[2,2,32,2048]{3,2,1,0:T(8,128)(2,1)S(1)}, bf16[2,2,32,2048]{3,2,1,0:T(8,128)(2,1)S(1)}, u32[]{:S(2)}, u32[]{:S(2)}) collective-permute-start(bf16[2,2,32,2048]{3,2,1,0:T(8,128)(2,1)S(1)} %get-tuple-element.150), channel_id=1, source_target_pairs={{0,1},{1,0},{2,3},{3,2},{4,5},{5,4},{6,7},{7,6},{8,9},{9,8},{10,11... | collective-permute-start | bytes 1572872 | tf_op jit(solution)/shard_map/way_back/ppermute | solution.py:486
  59.9 12.8 %collective-permute-start.14 = (bf16[128,1152]{1,0:T(8,128)(2,1)S(1)}, bf16[128,1152]{1,0:T(8,128)(2,1)S(1)}, u32[]{:S(2)}, u32[]{:S(2)}) collective-permute-start(bf16[128,1152]{1,0:T(8,128)(2,1)S(1)} %copy-done.7), channel_id=1, source_target_pairs={{0,1},{1,0},{2,3},{3,2},{4,5},{5,4},{6,7},{7,6},{8,9},{9,8},{10,11... | collective-permute-start | bytes 884744 | tf_op jit(solution)/shard_map/tokens/ppermute | solution.py:486
  60.4 12.4 %collective-permute-start.15 = (bf16[128,1152]{1,0:T(8,128)(2,1)S(1)}, bf16[128,1152]{1,0:T(8,128)(2,1)S(1)}, u32[]{:S(2)}, u32[]{:S(2)}) collective-permute-start(bf16[128,1152]{1,0:T(8,128)(2,1)S(1)} %collective-permute-done.12.rest_2_), channel_id=1, source_target_pairs={{0,1},{1,0},{2,3},{3,2},{4,5},{5,4},{6,7},{7,6},{8,9},{9,8},{10,11... | collective-permute-start | bytes 884744 | tf_op jit(solution)/shard_map/tokens/ppermute | solution.py:486
  68.9 8.6 %collective-permute-start.13 = (bf16[128,1152]{1,0:T(8,128)(2,1)S(1)}, bf16[128,1152]{1,0:T(8,128)(2,1)S(1)}, u32[]{:S(2)}, u32[]{:S(2)}) collective-permute-start(bf16[128,1152]{1,0:T(8,128)(2,1)S(1)} %collective-permute-done.10.rest_0_), channel_id=1, source_target_pairs={{0,4},{4,0},{8,12},{12,8},{16,20},{20,16},{24,28},{28,24},{1,5},{5... | collective-permute-start | bytes 884744 | tf_op jit(solution)/shard_map/tokens/ppermute | solution.py:486
  72.6 32.0 %collective-permute-start.31 = (bf16[2,2160,128]{2,1,0:T(8,128)(2,1)S(1)}, bf16[2,2160,128]{2,1,0:T(8,128)(2,1)S(1)}, u32[]{:S(2)}, u32[]{:S(2)}) collective-permute-start(bf16[2,2160,128]{2,1,0:T(8,128)(2,1)S(1)} %copy-done.14), channel_id=1, source_target_pairs={{0,1},{1,0},{2,3},{3,2},{4,5},{5,4},{6,7},{7,6},{8,9},{9,8},{10,11... | collective-permute-start | bytes 3317768 | tf_op jit(solution)/shard_map/send_states/ppermute | solution.py:486
  77.5 6.0 %collective-permute-start.19 = (bf16[2,2,32,2048]{3,2,1,0:T(8,128)(2,1)S(1)}, bf16[2,2,32,2048]{3,2,1,0:T(8,128)(2,1)S(1)}, u32[]{:S(2)}, u32[]{:S(2)}) collective-permute-start(bf16[2,2,32,2048]{3,2,1,0:T(8,128)(2,1)S(1)} %get-tuple-element.144), channel_id=1, source_target_pairs={{0,1},{1,0},{2,3},{3,2},{4,5},{5,4},{6,7},{7,6},{8,9},{9,8},{10,11... | collective-permute-start | bytes 1572872 | tf_op jit(solution)/shard_map/way_back/ppermute | solution.py:486
  78.2 14.3 %collective-permute-start.34 = (bf16[1,2160,128]{2,1,0:T(8,128)(2,1)S(1)}, bf16[1,2160,128]{2,1,0:T(8,128)(2,1)S(1)}, u32[]{:S(2)}, u32[]{:S(2)}) collective-permute-start(bf16[1,2160,128]{2,1,0:T(8,128)(2,1)S(1)} %copy-done.18), channel_id=1, source_target_pairs={{0,3},{1,2},{2,1},{3,0},{4,7},{5,6},{6,5},{7,4},{8,11},{9,10},{10,... | collective-permute-start | bytes 1658888 | tf_op jit(solution)/shard_map/send_states/ppermute | solution.py:486
  82.7 11.4 %collective-permute-start.24 = (bf16[2,2,32,2048]{3,2,1,0:T(8,128)(2,1)S(1)}, bf16[2,2,32,2048]{3,2,1,0:T(8,128)(2,1)S(1)}, u32[]{:S(2)}, u32[]{:S(2)}) collective-permute-start(bf16[2,2,32,2048]{3,2,1,0:T(8,128)(2,1)S(1)} %get-tuple-element.156), channel_id=1, source_target_pairs={{0,1},{1,0},{2,3},{3,2},{4,5},{5,4},{6,7},{7,6},{8,9},{9,8},{10,11... | collective-permute-start | bytes 1572872 | tf_op jit(solution)/shard_map/way_back/ppermute | solution.py:486
  83.0 11.7 %collective-permute-start.27 = (bf16[2,32,2048]{2,1,0:T(8,128)(2,1)S(1)}, bf16[2,32,2048]{2,1,0:T(8,128)(2,1)S(1)}, u32[]{:S(2)}, u32[]{:S(2)}) collective-permute-start(bf16[2,32,2048]{2,1,0:T(8,128)(2,1)S(1)} %fusion.7), channel_id=1, source_target_pairs={{0,4},{4,0},{8,12},{12,8},{16,20},{20,16},{24,28},{28,24},{1,5},{5... | collective-permute-start | bytes 786440 | tf_op jit(solution)/shard_map/way_back/ppermute | solution.py:486
  92.5 32.1 %collective-permute-start.35 = (bf16[1,2160,128]{2,1,0:T(8,128)(2,1)S(1)}, bf16[1,2160,128]{2,1,0:T(8,128)(2,1)S(1)}, u32[]{:S(2)}, u32[]{:S(2)}) collective-permute-start(bf16[1,2160,128]{2,1,0:T(8,128)(2,1)S(1)} %copy-done.16), channel_id=1, source_target_pairs={{0,3},{1,2},{2,1},{3,0},{4,7},{5,6},{6,5},{7,4},{8,11},{9,10},{10,... | collective-permute-start | bytes 1658888 | tf_op jit(solution)/shard_map/send_states/ppermute | solution.py:486
  94.1 8.4 %collective-permute-start.25 = (bf16[2,32,2048]{2,1,0:T(8,128)(2,1)S(1)}, bf16[2,32,2048]{2,1,0:T(8,128)(2,1)S(1)}, u32[]{:S(2)}, u32[]{:S(2)}) collective-permute-start(bf16[2,32,2048]{2,1,0:T(8,128)(2,1)S(1)} %fusion.6), channel_id=1, source_target_pairs={{0,4},{4,0},{8,12},{12,8},{16,20},{20,16},{24,28},{28,24},{1,5},{5... | collective-permute-start | bytes 786440 | tf_op jit(solution)/shard_map/way_back/ppermute | solution.py:486
  94.8 21.2 %collective-permute-start.28 = (bf16[2,32,2048]{2,1,0:T(8,128)(2,1)S(1)}, bf16[2,32,2048]{2,1,0:T(8,128)(2,1)S(1)}, u32[]{:S(2)}, u32[]{:S(2)}) collective-permute-start(bf16[2,32,2048]{2,1,0:T(8,128)(2,1)S(1)} %fusion.5), channel_id=1, source_target_pairs={{0,24},{4,28},{8,16},{12,20},{16,8},{20,12},{24,0},{28,4},{1,25},{... | collective-permute-start | bytes 786440 | tf_op jit(solution)/shard_map/way_back/ppermute | solution.py:486
  102.5 13.3 %collective-permute-start.26 = (bf16[2,32,2048]{2,1,0:T(8,128)(2,1)S(1)}, bf16[2,32,2048]{2,1,0:T(8,128)(2,1)S(1)}, u32[]{:S(2)}, u32[]{:S(2)}) collective-permute-start(bf16[2,32,2048]{2,1,0:T(8,128)(2,1)S(1)} %fusion.9), channel_id=1, source_target_pairs={{0,4},{4,0},{8,12},{12,8},{16,20},{20,16},{24,28},{28,24},{1,5},{5... | collective-permute-start | bytes 786440 | tf_op jit(solution)/shard_map/way_back/ppermute | solution.py:486
  103.0 12.6 %collective-permute-start.29 = (bf16[2,32,2048]{2,1,0:T(8,128)(2,1)S(1)}, bf16[2,32,2048]{2,1,0:T(8,128)(2,1)S(1)}, u32[]{:S(2)}, u32[]{:S(2)}) collective-permute-start(bf16[2,32,2048]{2,1,0:T(8,128)(2,1)S(1)} %fusion.8), channel_id=1, source_target_pairs={{0,4},{4,0},{8,12},{12,8},{16,20},{20,16},{24,28},{28,24},{1,5},{5... | collective-permute-start | bytes 786440 | tf_op jit(solution)/shard_map/way_back/ppermute | solution.py:486
  104.7 13.7 %collective-permute-start.32 = (bf16[2,32,2048]{2,1,0:T(8,128)(2,1)S(1)}, bf16[2,32,2048]{2,1,0:T(8,128)(2,1)S(1)}, u32[]{:S(2)}, u32[]{:S(2)}) collective-permute-start(bf16[2,32,2048]{2,1,0:T(8,128)(2,1)S(1)} %fusion.1), channel_id=1, source_target_pairs={{0,16},{4,20},{8,24},{12,28},{16,0},{20,4},{24,8},{28,12},{1,17},{... | collective-permute-start | bytes 786440 | tf_op jit(solution)/shard_map/way_back/ppermute | solution.py:486
  115.8 8.1 %collective-permute-start.30 = (bf16[2,32,2048]{2,1,0:T(8,128)(2,1)S(1)}, bf16[2,32,2048]{2,1,0:T(8,128)(2,1)S(1)}, u32[]{:S(2)}, u32[]{:S(2)}) collective-permute-start(bf16[2,32,2048]{2,1,0:T(8,128)(2,1)S(1)} %fusion.3), channel_id=1, source_target_pairs={{0,8},{4,12},{8,0},{12,4},{16,24},{20,28},{24,16},{28,20},{1,9},{5... | collective-permute-start | bytes 786440 | tf_op jit(solution)/shard_map/way_back/ppermute | solution.py:486
  (25 other events, 300.7 us)
